TPU v7x, 32 devices: a whole 2x2x4 slice. The times are simulated.
32 devices in a mesh: batch: 16 (over z, x, core), seq: 2 (over y).
Axes of the slice: x: 2, y: 2, z: 4, core: 2. Of those that a mesh axis runs over, the one named last changes fastest.
Arguments:
- inputs: bfloat16 [16, 4096, 512], P('batch', 'seq'), may hold values from -6 to 6
- window_lengths: int32 [16, 9], P('batch'), may hold values from 0 to 1024, as said below
- conv_weight: bfloat16 [9, 512, 512], P(None, 'seq', 'batch'), may hold values from -0.09375 to 0.09375
- conv_bias: bfloat16 [512], P(('batch', 'seq')), may hold values from -3 to 3
- norm1_gain: bfloat16 [512], P(('batch', 'seq')), may hold values from 0.25 to 1.75
- norm1_bias: bfloat16 [512], P(('batch', 'seq')), may hold values from -2 to 2
- up_weight: bfloat16 [512, 2048], P('seq', 'batch'), may hold values from -0.25 to 0.25
- up_bias: bfloat16 [2048], P(('batch', 'seq')), may hold values from -3 to 3
- down_weight: bfloat16 [2048, 512], P('batch', 'seq'), may hold values from -0.125 to 0.125
- down_bias: bfloat16 [512], P(('batch', 'seq')), may hold values from -3 to 3
- norm2_gain: bfloat16 [512], P(('batch', 'seq')), may hold values from 0.25 to 1.75
- norm2_bias: bfloat16 [512], P(('batch', 'seq')), may hold values from -2 to 2
- out_grad: bfloat16 [16, 4096, 512], P('batch', 'seq'), may hold values from -6 to 6
Outputs:
- block_output: bfloat16 [16, 4096, 512], P('batch', 'seq')
- input_grad: float32 [16, 4096, 512], P('batch', 'seq')
- conv_weight_grad: float32 [9, 512, 512], P(None, 'seq', 'batch')
- conv_bias_grad: float32 [512], P(('batch', 'seq'))
- norm1_gain_grad: float32 [512], P(('batch', 'seq'))
- norm1_bias_grad: float32 [512], P(('batch', 'seq'))
- up_weight_grad: float32 [512, 2048], P('seq', 'batch')
- up_bias_grad: float32 [2048], P(('batch', 'seq'))
- down_weight_grad: float32 [2048, 512], P('batch', 'seq')
- down_bias_grad: float32 [512], P(('batch', 'seq'))
- norm2_gain_grad: float32 [512], P(('batch', 'seq'))
- norm2_bias_grad: float32 [512], P(('batch', 'seq'))
Inputs may be any that keep to these rules, and one draw needn't show every extreme that they name: `window_lengths`: windows are 256, 512 or 1024 bases long. Each row begins with windows that fill one to three quarters of 1024, continues with whole windows of 1024 bases, and ends with zero or more shorter windows followed by at most 256 bases of padding; unused slots are 0 and come last.
All inputs are finite; a program needn't handle non-finite values.
Results may differ from a plain program's by a relative error of at most 0.008.
Values may be sent and summed in bfloat16 or wider, within the bound.
No kernel may reach another device: no remote copies, remote signals or barrier semaphores. Data moves between devices by JAX's collectives and lax.ppermute only.
A program may use at most 192 MiB of HBM per device.

v0:
```python
import jax
import jax.numpy as jnp
from jax import lax
from jax.sharding import PartitionSpec as P

KERNEL_TAPS = 9
DILATION_STEP = 32


EPSILON = 1e-05


def padded(value, sides, width):
    for axis, dim in sides:
        peers, length = (lax.axis_size(axis), value.shape[dim])
        up = [(i, (i + 1) % peers) for i in range(peers - 1)]
        down = [(j, i) for i, j in up]
        last = lax.slice_in_dim(value, length - width, length, axis=dim)
        leading = lax.slice_in_dim(value, 0, width, axis=dim)
        before = lax.ppermute(last, axis, up)
        after = lax.ppermute(leading, axis, down)
        value = jnp.concatenate([before, value, after], axis=dim)
    return value


def gelu_exact(values):
    return jax.nn.gelu(values, approximate=False)


def layer_norm(values, gain_vec, bias_vec):
    average = jnp.mean(values, -1, keepdims=True)
    centered = values - average
    variance = jnp.mean(centered * centered, -1, keepdims=True)
    return centered * lax.rsqrt(variance + EPSILON) * gain_vec + bias_vec


def first_branch(conv_values, gain_vec, bias_vec):
    return layer_norm(gelu_exact(conv_values), gain_vec, bias_vec)


def window_ids(window_lengths, first_base, count):
    window_end = jnp.cumsum(window_lengths, axis=-1)
    positions = first_base + jnp.arange(count, dtype=jnp.int32)
    window_id = jnp.sum((positions[None, :, None] >= window_end[:, None, :]).astype(jnp.int32), -1)
    valid_mask = positions[None, :] < window_end[:, -1:]
    return (window_id, valid_mask)


def local(
    inputs,
    window_lengths,
    conv_weight,
    conv_bias,
    norm1_gain,
    norm1_bias,
    up_weight,
    up_bias,
    down_weight,
    down_bias,
    norm2_gain,
    norm2_bias,
    out_grad,
):
    row_count, local_length, width = inputs.shape
    border_width = KERNEL_TAPS // 2 * DILATION_STEP
    batch_count = lax.axis_size("batch")
    seq_count = lax.axis_size("seq")
    first_base = lax.axis_index("seq") * local_length
    partial_value = (
        lax.all_gather(conv_weight, "seq", axis=1, tiled=True),
        lax.all_gather(up_weight, "seq", axis=0, tiled=True),
        lax.all_gather(down_weight, "seq", axis=1, tiled=True),
        lax.all_gather(conv_bias.reshape(1, 1, -1), "seq", axis=1, tiled=True),
        lax.all_gather(norm1_gain.reshape(1, 1, -1), "seq", axis=1, tiled=True),
        lax.all_gather(norm1_bias.reshape(1, 1, -1), "seq", axis=1, tiled=True),
        lax.all_gather(up_bias.reshape(1, 1, -1), "seq", axis=1, tiled=True),
        lax.all_gather(down_bias.reshape(1, 1, -1), "seq", axis=1, tiled=True),
        lax.all_gather(norm2_gain.reshape(1, 1, -1), "seq", axis=1, tiled=True),
        lax.all_gather(norm2_bias.reshape(1, 1, -1), "seq", axis=1, tiled=True),
    )
    gathered = (
        lax.all_gather(partial_value[0], "batch", axis=2, tiled=True),
        lax.all_gather(partial_value[1], "batch", axis=1, tiled=True),
        lax.all_gather(partial_value[2], "batch", axis=0, tiled=True),
        lax.all_gather(partial_value[3], "batch", axis=0, tiled=True),
        lax.all_gather(partial_value[4], "batch", axis=0, tiled=True),
        lax.all_gather(partial_value[5], "batch", axis=0, tiled=True),
        lax.all_gather(partial_value[6], "batch", axis=0, tiled=True),
        lax.all_gather(partial_value[7], "batch", axis=0, tiled=True),
        lax.all_gather(partial_value[8], "batch", axis=0, tiled=True),
        lax.all_gather(partial_value[9], "batch", axis=0, tiled=True),
    )
    conv_full, up_full, down_full = (gathered[0], gathered[1], gathered[2])
    conv_bias_full = gathered[3].reshape(-1).astype(jnp.float32)
    gain_one = gathered[4].reshape(-1).astype(jnp.float32)
    shift_one = gathered[5].reshape(-1).astype(jnp.float32)
    up_bias_full = gathered[6].reshape(-1).astype(jnp.float32)
    down_bias_full = gathered[7].reshape(-1).astype(jnp.float32)
    gain_two = gathered[8].reshape(-1).astype(jnp.float32)
    shift_two = gathered[9].reshape(-1).astype(jnp.float32)
    extended_window_id, _ = window_ids(
        window_lengths, first_base - border_width, local_length + 2 * border_width
    )
    self_window_id, own_valid = window_ids(window_lengths, first_base, local_length)
    tap_masks = jnp.stack(
        [
            extended_window_id[
                :,
                kernel_tap_index * DILATION_STEP : kernel_tap_index * DILATION_STEP + local_length,
            ]
            == self_window_id
            for kernel_tap_index in range(KERNEL_TAPS)
        ],
        2,
    )
    valid_low = own_valid.astype(jnp.bfloat16)[..., None]
    masked = inputs * valid_low
    extended_input = padded(masked, (("seq", 1),), border_width)
    stacked = (
        jnp.stack(
            [
                extended_input[
                    :,
                    kernel_tap_index * DILATION_STEP : kernel_tap_index * DILATION_STEP
                    + local_length,
                ]
                for kernel_tap_index in range(KERNEL_TAPS)
            ],
            2,
        )
        * tap_masks.astype(jnp.bfloat16)[..., None]
    )
    conv_out = (
        jnp.einsum("rtki,kio->rto", stacked, conv_full, preferred_element_type=jnp.float32)
        + conv_bias_full
    )
    normed_one, first_pull = jax.vjp(first_branch, conv_out, gain_one, shift_one)
    hidden_one = inputs.astype(jnp.float32) + normed_one
    hidden_low = hidden_one.astype(jnp.bfloat16)
    up_out = (
        jnp.einsum("rti,if->rtf", hidden_low, up_full, preferred_element_type=jnp.float32)
        + up_bias_full
    )
    activated, gelu_pull = jax.vjp(gelu_exact, up_out)
    activated_low = activated.astype(jnp.bfloat16)
    down_out = (
        jnp.einsum("rtf,fo->rto", activated_low, down_full, preferred_element_type=jnp.float32)
        + down_bias_full
    )
    normed_two, second_pull = jax.vjp(layer_norm, down_out, gain_two, shift_two)
    block_output = (hidden_one + normed_two).astype(jnp.bfloat16)
    grad_output = out_grad.astype(jnp.float32)
    grad_down, gain_two_grad, shift_two_grad = second_pull(grad_output)
    grad_down_low = grad_down.astype(jnp.bfloat16)
    down_bias_grad = jnp.sum(grad_down_low.astype(jnp.float32), (0, 1))
    down_weight_grad = jnp.einsum(
        "rtf,rto->fo", activated_low, grad_down_low, preferred_element_type=jnp.float32
    )
    grad_active = jnp.einsum(
        "rto,fo->rtf", grad_down_low, down_full, preferred_element_type=jnp.float32
    )
    (grad_up,) = gelu_pull(grad_active)
    grad_up_low = grad_up.astype(jnp.bfloat16)
    up_bias_grad = jnp.sum(grad_up_low.astype(jnp.float32), (0, 1))
    up_weight_grad = jnp.einsum(
        "rti,rtf->if", hidden_low, grad_up_low, preferred_element_type=jnp.float32
    )
    grad_hidden = grad_output + jnp.einsum(
        "rtf,if->rti", grad_up_low, up_full, preferred_element_type=jnp.float32
    )
    grad_conv, gain_one_grad, shift_one_grad = first_pull(grad_hidden)
    grad_conv_low = grad_conv.astype(jnp.bfloat16)
    conv_bias_grad = jnp.sum(grad_conv_low.astype(jnp.float32), (0, 1))
    conv_weight_grad = jnp.einsum(
        "rtki,rto->kio", stacked, grad_conv_low, preferred_element_type=jnp.float32
    )
    extended_input_grad = padded(grad_conv_low, (("seq", 1),), border_width)
    mirrored = jnp.stack(
        [
            extended_input_grad[
                :,
                (KERNEL_TAPS - 1 - kernel_tap_index)
                * DILATION_STEP : (KERNEL_TAPS - 1 - kernel_tap_index)
                * DILATION_STEP
                + local_length,
            ]
            for kernel_tap_index in range(KERNEL_TAPS)
        ],
        2,
    )
    mirrored = mirrored * tap_masks[:, :, ::-1].astype(jnp.bfloat16)[..., None]
    spread = jnp.einsum("rtko,kio->rti", mirrored, conv_full, preferred_element_type=jnp.float32)
    input_grad = grad_hidden + spread * own_valid.astype(jnp.float32)[..., None]
    cb_grid = conv_bias_grad.reshape(batch_count, seq_count, -1)
    g1_grid = gain_one_grad.reshape(batch_count, seq_count, -1)
    s1_grid = shift_one_grad.reshape(batch_count, seq_count, -1)
    ub_grid = up_bias_grad.reshape(batch_count, seq_count, -1)
    db_grid = down_bias_grad.reshape(batch_count, seq_count, -1)
    g2_grid = gain_two_grad.reshape(batch_count, seq_count, -1)
    s2_grid = shift_two_grad.reshape(batch_count, seq_count, -1)
    halfway = (
        lax.psum_scatter(conv_weight_grad, "batch", scatter_dimension=2, tiled=True),
        lax.psum_scatter(up_weight_grad, "batch", scatter_dimension=1, tiled=True),
        lax.psum_scatter(down_weight_grad, "batch", scatter_dimension=0, tiled=True),
        lax.psum_scatter(cb_grid, "batch", scatter_dimension=0, tiled=True),
        lax.psum_scatter(g1_grid, "batch", scatter_dimension=0, tiled=True),
        lax.psum_scatter(s1_grid, "batch", scatter_dimension=0, tiled=True),
        lax.psum_scatter(ub_grid, "batch", scatter_dimension=0, tiled=True),
        lax.psum_scatter(db_grid, "batch", scatter_dimension=0, tiled=True),
        lax.psum_scatter(g2_grid, "batch", scatter_dimension=0, tiled=True),
        lax.psum_scatter(s2_grid, "batch", scatter_dimension=0, tiled=True),
    )
    finished = (
        lax.psum_scatter(halfway[0], "seq", scatter_dimension=1, tiled=True),
        lax.psum_scatter(halfway[1], "seq", scatter_dimension=0, tiled=True),
        lax.psum_scatter(halfway[2], "seq", scatter_dimension=1, tiled=True),
        lax.psum_scatter(halfway[3], "seq", scatter_dimension=1, tiled=True),
        lax.psum_scatter(halfway[4], "seq", scatter_dimension=1, tiled=True),
        lax.psum_scatter(halfway[5], "seq", scatter_dimension=1, tiled=True),
        lax.psum_scatter(halfway[6], "seq", scatter_dimension=1, tiled=True),
        lax.psum_scatter(halfway[7], "seq", scatter_dimension=1, tiled=True),
        lax.psum_scatter(halfway[8], "seq", scatter_dimension=1, tiled=True),
        lax.psum_scatter(halfway[9], "seq", scatter_dimension=1, tiled=True),
    )
    return (
        block_output,
        input_grad,
        finished[0],
        finished[3].reshape(-1),
        finished[4].reshape(-1),
        finished[5].reshape(-1),
        finished[1],
        finished[6].reshape(-1),
        finished[2],
        finished[7].reshape(-1),
        finished[8].reshape(-1),
        finished[9].reshape(-1),
    )


def solution(mesh):
    in_specs = (
        P("batch", "seq", None),
        P("batch", None),
        P(None, "seq", "batch"),
        P(("batch", "seq")),
        P(("batch", "seq")),
        P(("batch", "seq")),
        P("seq", "batch"),
        P(("batch", "seq")),
        P("batch", "seq"),
        P(("batch", "seq")),
        P(("batch", "seq")),
        P(("batch", "seq")),
        P("batch", "seq", None),
    )
    out_specs = (
        P("batch", "seq", None),
        P("batch", "seq", None),
        P(None, "seq", "batch"),
        P(("batch", "seq")),
        P(("batch", "seq")),
        P(("batch", "seq")),
        P("seq", "batch"),
        P(("batch", "seq")),
        P("batch", "seq"),
        P(("batch", "seq")),
        P(("batch", "seq")),
        P(("batch", "seq")),
    )
    return jax.shard_map(local, mesh=mesh, in_specs=in_specs, out_specs=out_specs, check_vma=False)
```

profile of v0, /device:TPU:0, one launch (start us, length us, event | category | flops | bytes accessed | tf_op | source)
XLA Modules:
  0.0 605.4 jit_solution(9939704971360741419)
XLA Ops:
  7.3 9.5 %all_gather.60 = bf16[9,512,32]{1,2,0:T(8,128)(2,1)} all-gather(bf16[9,256,32]{1,2,0:T(8,128)(2,1)} %param.15), channel_id=1, replica_groups=mesh['batch'=16,'seq'=2] {'seq'}, dimensions={1}, use_global_device_ids=true | all-gather | bytes 442368 | tf_op jit(solution)/shard_map/all_gather | solution.py:70
  16.9 5.3 all_gather.68
  24.3 2.0 broadcast_multiply_fusion
  26.4 3.4 collective-permute-start
  29.7 1.3 collective-permute-start.1
  31.0 6.4 %all_gather.72 = bf16[128,512]{1,0:T(8,128)(2,1)} all-gather(bf16[128,256]{1,0:T(8,128)(2,1)S(1)} %copy-done.13), channel_id=1, replica_groups=mesh['batch'=16,'seq'=2] {'seq'}, dimensions={1}, use_global_device_ids=true | all-gather | bytes 196608 | tf_op jit(solution)/shard_map/all_gather | solution.py:72
  42.5 4.9 all-reduce.23
  47.5 21.7 %all_gather.63 = bf16[16,2,16]{2,1,0:T(2,128)(2,1)S(1)} all-gather(bf16[1,2,16]{2,1,0:T(2,128)(2,1)S(1)} %reshape.883), channel_id=1, replica_groups=mesh['batch'=16,'seq'=2] {'batch'}, dimensions={0}, use_global_device_ids=true | all-gather | bytes 1088 | tf_op jit(solution)/shard_map/all_gather | solution.py:85
  69.4 17.3 %all_gather.65 = bf16[16,2,16]{2,1,0:T(2,128)(2,1)S(1)} all-gather(bf16[1,2,16]{2,1,0:T(2,128)(2,1)S(1)} %reshape.884), channel_id=1, replica_groups=mesh['batch'=16,'seq'=2] {'batch'}, dimensions={0}, use_global_device_ids=true | all-gather | bytes 1088 | tf_op jit(solution)/shard_map/all_gather | solution.py:86
  86.8 18.8 %all_gather.67 = bf16[16,2,16]{2,1,0:T(2,128)(2,1)S(1)} all-gather(bf16[1,2,16]{2,1,0:T(2,128)(2,1)S(1)} %reshape.885), channel_id=1, replica_groups=mesh['batch'=16,'seq'=2] {'batch'}, dimensions={0}, use_global_device_ids=true | all-gather | bytes 1088 | tf_op jit(solution)/shard_map/all_gather | solution.py:87
  105.8 17.3 %all_gather.71 = bf16[16,2,64]{2,1,0:T(2,128)(2,1)S(1)} all-gather(bf16[1,2,64]{2,1,0:T(2,128)(2,1)S(1)} %reshape.886), channel_id=1, replica_groups=mesh['batch'=16,'seq'=2] {'batch'}, dimensions={0}, use_global_device_ids=true | all-gather | bytes 4352 | tf_op jit(solution)/shard_map/all_gather | solution.py:88
  123.3 18.7 %all_gather.75 = bf16[16,2,16]{2,1,0:T(2,128)(2,1)S(1)} all-gather(bf16[1,2,16]{2,1,0:T(2,128)(2,1)S(1)} %reshape.887), channel_id=1, replica_groups=mesh['batch'=16,'seq'=2] {'batch'}, dimensions={0}, use_global_device_ids=true | all-gather | bytes 1088 | tf_op jit(solution)/shard_map/all_gather | solution.py:89
  142.7 17.3 %all_gather.77 = bf16[16,2,16]{2,1,0:T(2,128)(2,1)S(1)} all-gather(bf16[1,2,16]{2,1,0:T(2,128)(2,1)S(1)} %reshape.888), channel_id=1, replica_groups=mesh['batch'=16,'seq'=2] {'batch'}, dimensions={0}, use_global_device_ids=true | all-gather | bytes 1088 | tf_op jit(solution)/shard_map/all_gather | solution.py:90
  160.7 18.7 %all_gather.79 = bf16[16,2,16]{2,1,0:T(2,128)(2,1)S(1)} all-gather(bf16[1,2,16]{2,1,0:T(2,128)(2,1)S(1)} %reshape.889), channel_id=1, replica_groups=mesh['batch'=16,'seq'=2] {'batch'}, dimensions={0}, use_global_device_ids=true | all-gather | bytes 1088 | tf_op jit(solution)/shard_map/all_gather | solution.py:91
  180.0 1.5 fusion.70
  181.4 1.4 fusion.73
  182.9 1.5 fusion.67
  184.4 1.5 fusion.81
  185.8 1.8 bitcast_dynamic-update-slice_fusion.1
  187.7 1.5 fusion.61
  189.1 1.5 fusion.64
  190.6 1.4 fusion.58
  192.0 1.5 fusion.79
  193.5 24.8 %fusion.128 = (f32[2048]{0:T(1024)S(1)}, f32[2048,512]{1,0:T(8,128)S(1)}, f32[2048,512]{1,0:T(8,128)}, f32[2048,512,1]{1,0,2:T(8,128)}) fusion(f32[512]{0:T(512)S(1)} %reshape.875, bf16[9,512,512]{1,2,0:T(8,128)(2,1)} %all-gather.11.cloned.1.call-done, bf16[2048,9,512]{2,0,1:T(8,128)(2,1)} %fusion.79, bf16[2048,9]{0,1:T(8,128)(2,1)S(1)} %convert_element_type.160), kind=kOutput, calls=%fused_computation.224 | convolution fusion | flops 9742317568 | bytes 36222976 | tf_op jit(solution)/shard_map/rtki,kio->rto/dot_general | solution.py:134
  218.3 2.1 copy-done
  221.9 44.9 %multiply_convert_fusion = (bf16[2048,2048]{1,0:T(8,128)(2,1)}, f32[2048,2048]{1,0:T(8,128)}, f32[2048,2048]{1,0:T(8,128)}) fusion(f32[2048]{0:T(1024)S(1)} %reshape.878, bf16[512,2048]{1,0:T(8,128)(2,1)} %all-gather.13.cloned.1.call-done, f32[512]{0:T(512)S(1)} %reshape.877, f32[512]{0:T(512)S(1)} %reshape.876, f32[2048]{0:T(1024)S(1)} %fusion.95, ...), kind=kOutput, calls=%fused_computation.6 | convolution fusion | flops 4579131392 | bytes 50360320 | tf_op jit(solution)/shard_map/rti,if->rtf/dot_general | solution.py:141
  266.8 8.2 %add_reduce_fusion = (f32[2048]{0:T(1024)S(1)}, f32[2048,512]{1,0:T(8,128)S(1)}) fusion(f32[512]{0:T(512)S(1)} %copy-done.25, bf16[2048,2048]{1,0:T(8,128)(2,1)} %get-tuple-element.46, bf16[2048,512]{1,0:T(8,128)(2,1)} %all-gather.15.cloned.1.call-done), kind=kOutput, calls=%fused_computation.78 | convolution fusion | flops 4297062400 | bytes 14690304 | tf_op jit(solution)/shard_map/rtf,fo->rto/dot_general | solution.py:147
  276.6 2.0 fusion.19
  278.6 4.6 fusion.126
  283.7 1.3 copy-done.10
  285.0 6.1 %fusion.83 = f32[2048,512]{1,0:T(8,128)} fusion(bf16[2048,2048]{1,0:T(8,128)(2,1)S(1)} %bitcast.262, bf16[1,2048,512]{2,1,0:T(8,128)(2,1)S(1)} %get-tuple-element.41), kind=kOutput, calls=%fused_computation.142 | convolution fusion | flops 4294967296 | bytes 14680064 | tf_op jit(solution)/shard_map/rtf,rto->fo/dot_general | solution.py:156
  291.2 22.8 %convert_reduce_fusion = (f32[2048]{0:T(1024)S(1)}, bf16[2048,2048]{1,0:T(8,128)(2,1)}) fusion(f32[2048,2048]{1,0:T(8,128)} %get-tuple-element.47, bf16[2048,512]{1,0:T(8,128)(2,1)} %all-gather.15.cloned.1.call-done, bf16[1,2048,512]{2,1,0:T(8,128)(2,1)} %copy-done.10, f32[2048,2048]{1,0:T(8,128)} %get-tuple-element.77, f32[2048]{0:T(1024)S(1)} %reshape.878), kind=kOutput, calls=%fused_computation.4 | convolution fusion | flops 4366268416 | bytes 46153728 | tf_op jit(solution)/shard_map/rto,fo->rtf/dot_general | solution.py:159
  314.0 12.0 %fusion.86 = f32[512,2048]{1,0:T(8,128)} fusion(bf16[2048,2048]{1,0:T(8,128)(2,1)} %get-tuple-element.82, bf16[1,2048,512]{2,1,0:T(8,128)(2,1)S(1)} %copy-done.4, f32[2048,512]{1,0:T(8,128)} %copy-done, f32[512]{0:T(512)S(1)} %reshape.877, f32[512]{0:T(512)S(1)} %reshape.876, f32[2048]{0:T(1024)S(1)} %fusion.95, f32[2048]{0:T(1024)S(1)} %broadcast_multiply_fusion.2), kind=kOutput, calls=%fused_computation.145 | convolution fusion | flops 4302307328 | bytes 18894848 | tf_op jit(solution)/shard_map/rti,rtf->if/dot_general | solution.py:165
  326.2 1.3 copy-done.7
  327.6 10.9 %fusion.124 = (f32[512]{0:T(512)S(1)}, f32[2048]{0:T(1024)S(1)}, f32[1,2048,512]{2,1,0:T(8,128)S(1)}) fusion(f32[512]{0:T(512)S(1)} %reshape.876, f32[2048,512]{1,0:T(8,128)} %copy-done, f32[2048]{0:T(1024)S(1)} %broadcast_multiply_fusion.2, bf16[2048,2048]{1,0:T(8,128)(2,1)} %get-tuple-element.82, bf16[512,2048]{1,0:T(8,128)(2,1)} %all-gather.13.cloned.1.call-done, ...), kind=kOutput, calls=%fused_computation.222 | convolution fusion | flops 4302304768 | bytes 20992000 | tf_op jit(solution)/shard_map/rtf,if->rti/dot_general | solution.py:168
  338.6 2.3 fusion.20
  340.9 1.3 copy-done.8
  342.2 1.3 copy-done.9
  343.6 3.5 convert_reduce_fusion.3
  347.1 16.2 %fusion.8 = f32[9,512,512]{1,2,0:T(8,128)} fusion(bf16[2048,9,512]{2,0,1:T(8,128)(2,1)} %fusion.79, bf16[2048,9]{0,1:T(8,128)(2,1)S(1)} %copy-done.15, bf16[1,2048,512]{2,1,0:T(8,128)(2,1)S(1)} %get-tuple-element.43), kind=kOutput, calls=%fused_computation.20 | convolution fusion | flops 9673113600 | bytes 30445568 | tf_op jit(solution)/shard_map/rtki,rto->kio/dot_general | solution.py:174
  366.6 1.3 collective-permute-start.2
  367.9 59.9 %all-reduce.21 = (f32[16,2,16]{2,1,0:T(2,128)S(1)}, f32[16,2,16]{2,1,0:T(2,128)S(1)}, f32[16,2,16]{2,1,0:T(2,128)S(1)}, f32[16,2,64]{2,1,0:T(2,128)S(1)}, f32[16...) all-reduce(f32[16,2,16]{2,1,0:T(2,128)S(1)} %reshape.861, ...), channel_id=11, replica_groups=mesh['batch'=16,'seq'=2] {'batch'}, use_global_device_ids=true, to_apply=%region_14.15.clone | all-reduce | flops 5120 | bytes 40960
  430.5 5.3 all-reduce.22
  435.8 1.1 fusion.102
  436.9 1.1 fusion.103
  438.0 1.1 fusion.104
  439.2 1.1 fusion.105
  440.3 1.1 fusion.101
  441.4 1.1 fusion.100
  442.6 3.9 collective-permute-start.3
  446.5 1.1 fusion.99
  447.7 1.5 fusion.52
  449.1 1.4 fusion.55
  450.6 1.5 fusion.49
  452.1 1.5 fusion.77
  453.5 1.5 bitcast_dynamic-update-slice_fusion
  455.1 1.5 fusion.43
  456.6 1.5 fusion.46
  458.1 1.4 fusion.40
  459.6 1.5 fusion.75
  461.0 90.6 %reduce-scatter.14.cloned.1.call-done = f32[9,512,32]{1,2,0:T(8,128)} async-done(((f32[9,512,512]{1,2,0:T(8,128)}), f32[9,512,32]{1,2,0:T(8,128)}) %reduce-scatter.14.cloned.1.call-update) | async-done | bytes 589840 | tf_op jit(solution)/shard_map/reduce_scatter | solution.py:202
  551.6 16.7 %bitcast_add_fusion = f32[1,2048,512]{2,1,0:T(8,128)} fusion(f32[1,2048,512]{2,1,0:T(8,128)} %copy-done.5, bf16[9,512,512]{1,2,0:T(8,128)(2,1)} %all-gather.11.cloned.1.call-done, bf16[2048,9,512]{2,0,1:T(8,128)(2,1)} %fusion.75, bf16[2048,9]{0,1:T(8,128)(2,1)S(1)} %convert_bitcast_fusion, f32[2048]{0:T(1024)S(1)} %fusion.97), kind=kOutput, calls=%fused_computation.41 | convolution fusion | flops 9675210752 | bytes 32026624 | tf_op jit(solution)/shard_map/rtko,kio->rti/dot_general | solution.py:192
  568.3 12.1 %reduce-scatter.20.cloned.1.call-done = f32[256,128]{1,0:T(8,128)} async-done(((f32[512,128]{1,0:T(8,128)}), f32[256,128]{1,0:T(8,128)}) %reduce-scatter.20.cloned.1.call-update) | async-done | bytes 131088 | tf_op jit(solution)/shard_map/reduce_scatter | solution.py:215
  580.4 18.2 %reduce-scatter.16.cloned.1.call-done = f32[9,256,32]{1,2,0:T(8,128)} async-done(((f32[9,512,32]{1,2,0:T(8,128)}), f32[9,256,32]{1,2,0:T(8,128)}) %reduce-scatter.16.cloned.1.call-update) | async-done | bytes 294928 | tf_op jit(solution)/shard_map/reduce_scatter | solution.py:214
  (175 shorter events, 18.5 us)
Async XLA Ops:
  7.2 31.6 %copy-start.30 = (u32[32]{0:T(128)S(1)}, u32[32]{0:T(128)}, u32[]{:S(2)}) copy-start(u32[32]{0:T(128)} %constant.28) | copy-start | bytes 388
  7.2 23.8 %copy-start.13 = (bf16[128,256]{1,0:T(8,128)(2,1)S(1)}, bf16[128,256]{1,0:T(8,128)(2,1)}, u32[]{:S(2)}) copy-start(bf16[128,256]{1,0:T(8,128)(2,1)} %param.21) | copy-start | bytes 196612
  7.2 33.5 %copy-start.31 = (bf16[16]{0:T(256)(128)(2,1)S(1)}, bf16[16]{0:T(256)(128)(2,1)}, u32[]{:S(2)}) copy-start(bf16[16]{0:T(256)(128)(2,1)} %param.16) | copy-start | bytes 100
  7.2 33.8 %copy-start.32 = (bf16[16]{0:T(256)(128)(2,1)S(1)}, bf16[16]{0:T(256)(128)(2,1)}, u32[]{:S(2)}) copy-start(bf16[16]{0:T(256)(128)(2,1)} %param.17) | copy-start | bytes 100
  7.2 34.0 %copy-start.33 = (bf16[16]{0:T(256)(128)(2,1)S(1)}, bf16[16]{0:T(256)(128)(2,1)}, u32[]{:S(2)}) copy-start(bf16[16]{0:T(256)(128)(2,1)} %param.18) | copy-start | bytes 100
  7.2 34.3 %copy-start.34 = (bf16[16]{0:T(256)(128)(2,1)S(1)}, bf16[16]{0:T(256)(128)(2,1)}, u32[]{:S(2)}) copy-start(bf16[16]{0:T(256)(128)(2,1)} %param.22) | copy-start | bytes 100
  7.2 34.5 %copy-start.35 = (bf16[16]{0:T(256)(128)(2,1)S(1)}, bf16[16]{0:T(256)(128)(2,1)}, u32[]{:S(2)}) copy-start(bf16[16]{0:T(256)(128)(2,1)} %param.23) | copy-start | bytes 100
  7.3 34.7 %copy-start.36 = (bf16[16]{0:T(256)(128)(2,1)S(1)}, bf16[16]{0:T(256)(128)(2,1)}, u32[]{:S(2)}) copy-start(bf16[16]{0:T(256)(128)(2,1)} %param.24) | copy-start | bytes 100
  7.3 35.0 %copy-start.37 = (bf16[64]{0:T(256)(128)(2,1)S(1)}, bf16[64]{0:T(256)(128)(2,1)}, u32[]{:S(2)}) copy-start(bf16[64]{0:T(256)(128)(2,1)} %param.20) | copy-start | bytes 388
  7.3 186.2 %all-gather.11.cloned.1.call-start = ((), (), s32[]{:S(2)}) async-start(), calls=%async_computation.6 | async-start | bytes 5013504 | tf_op jit(solution)/shard_map/all_gather | solution.py:82
  16.8 205.0 %all-gather.13.cloned.1.call-start = ((), (), s32[]{:S(2)}) async-start(), calls=%async_computation.7 | async-start | bytes 2228224 | tf_op jit(solution)/shard_map/all_gather | solution.py:83
  22.2 244.6 %all-gather.15.cloned.1.call-start = ((), (), s32[]{:S(2)}) async-start(), calls=%async_computation.8 | async-start | bytes 2228224 | tf_op jit(solution)/shard_map/all_gather | solution.py:84
  26.4 153.6 %collective-permute-start = (bf16[1,128,512]{2,1,0:T(8,128)(2,1)S(1)}, bf16[1,128,512]{2,1,0:T(8,128)(2,1)S(1)}, u32[]{:S(2)}, u32[]{:S(2)}) collective-permute-start(bf16[1,128,512]{2,1,0:T(8,128)(2,1)S(1)} %get-tuple-element.55), channel_id=1, source_target_pairs={{0,1},{2,3},{4,5},{6,7},{8,9},{10,11},{12,13},{14,15},{16,17},{18,... | collective-permute-start | bytes 393224 | tf_op jit(solution)/shard_map/ppermute | solution.py:20
  29.7 157.9 %collective-permute-start.1 = (bf16[1,128,512]{2,1,0:T(8,128)(2,1)S(1)}, bf16[1,128,512]{2,1,0:T(8,128)(2,1)S(1)}, u32[]{:S(2)}, u32[]{:S(2)}) collective-permute-start(bf16[1,128,512]{2,1,0:T(8,128)(2,1)S(1)} %get-tuple-element.54), channel_id=1, source_target_pairs={{1,0},{3,2},{5,4},{7,6},{9,8},{11,10},{13,12},{15,14},{17,16},{19,... | collective-permute-start | bytes 393224 | tf_op jit(solution)/shard_map/ppermute | solution.py:21
  37.4 417.6 %reduce-scatter.22.cloned.1.call-start = ((), (), s32[]{:S(2)}) async-start(), calls=%async_computation.13 | async-start | bytes 4456448 | tf_op jit(solution)/shard_map/reduce_scatter | solution.py:204
  38.8 154.7 %copy-start.14 = (bf16[2048,9]{0,1:T(8,128)(2,1)}, bf16[2048,9]{0,1:T(8,128)(2,1)S(1)}, u32[]{:S(2)}) copy-start(bf16[2048,9]{0,1:T(8,128)(2,1)S(1)} %convert_element_type.160) | copy-start | bytes 110596
  69.3 124.2 %copy-start.27 = (f32[512]{0:T(512)}, f32[512]{0:T(512)S(1)}, u32[]{:S(2)}) copy-start(f32[512]{0:T(512)S(1)} %reshape.875) | copy-start | bytes 6148
  182.9 3.0 copy-start.3
  218.3 2.1 copy-start
  218.3 3.6 copy-start.4
  221.3 0.6 copy-start.11
  221.9 44.9 %copy-start.25 = (f32[512]{0:T(512)S(1)}, f32[512]{0:T(512)}, u32[]{:S(2)}) copy-start(f32[512]{0:T(512)} %reshape.879) | copy-start | bytes 6148
  275.0 1.6 copy-start.6
  275.0 1.6 copy-start.26
  275.9 2.7 copy-start.1
  275.9 2.7 copy-start.29
  278.5 6.5 %slice-start = ((s8[8388608]{0:T(1024)(128)(4,1)}), s8[4194304]{0:T(1024)(128)(4,1)S(1)}, s32[]{:S(2)}) async-start(s8[8388608]{0:T(1024)(128)(4,1)} %bitcast.261), calls=%async_computation.15 | async-start | bytes 8388608
  278.6 6.4 %slice-start.1 = ((s8[8388608]{0:T(1024)(128)(4,1)}), s8[4194304]{0:T(1024)(128)(4,1)S(1)}, s32[]{:S(2)}) async-start(s8[8388608]{0:T(1024)(128)(4,1)} %bitcast.261), calls=%async_computation.16 | async-start | bytes 8388608
  283.7 1.3 copy-start.10
  291.2 166.9 %reduce-scatter.18.cloned.1.call-start = ((), (), s32[]{:S(2)}) async-start(), calls=%async_computation.11 | async-start | bytes 4456448 | tf_op jit(solution)/shard_map/reduce_scatter | solution.py:203
  326.0 1.6 copy-start.7
  326.0 12.5 %copy-start.12 = (f32[2048]{0:T(1024)S(1)}, f32[2048]{0:T(1024)}, u32[]{:S(2)}) copy-start(f32[2048]{0:T(1024)} %copy-done.11) | copy-start | bytes 24580
  326.0 225.6 %reduce-scatter.14.cloned.1.call-start = ((), (), s32[]{:S(2)}) async-start(), calls=%async_computation.9 | async-start | bytes 10027008 | tf_op jit(solution)/shard_map/reduce_scatter | solution.py:202
  327.6 10.9 %copy-start.2 = (f32[2048,512]{1,0:T(8,128)S(1)}, f32[2048,512]{1,0:T(8,128)}, u32[]{:S(2)}) copy-start(f32[2048,512]{1,0:T(8,128)} %copy-done) | copy-start | bytes 12582916
  338.5 2.4 copy-start.5
  338.5 3.7 copy-start.8
  338.5 5.0 copy-start.9
  338.5 5.0 copy-start.28
  343.6 3.5 copy-start.15
  363.3 0.7 copy-start.38
  363.3 1.2 copy-start.16
  363.3 1.2 copy-start.17
  363.3 1.2 copy-start.18
  363.3 1.2 copy-start.19
  363.3 1.2 copy-start.20
  363.4 1.2 copy-start.21
  363.4 1.2 copy-start.22
  363.4 1.2 copy-start.23
  363.4 1.2 copy-start.24
  363.4 204.9 %reduce-scatter.24.cloned.1.call-start = ((), (), s32[]{:S(2)}) async-start(), calls=%async_computation.14 | async-start | bytes 393216 | tf_op jit(solution)/shard_map/reduce_scatter | solution.py:216
  366.6 81.0 %collective-permute-start.2 = (bf16[1,128,512]{2,1,0:T(8,128)(2,1)S(1)}, bf16[1,128,512]{2,1,0:T(8,128)(2,1)S(1)}, u32[]{:S(2)}, u32[]{:S(2)}) collective-permute-start(bf16[1,128,512]{2,1,0:T(8,128)(2,1)S(1)} %get-tuple-element.53), channel_id=1, source_target_pairs={{1,0},{3,2},{5,4},{7,6},{9,8},{11,10},{13,12},{15,14},{17,16},{19,... | collective-permute-start | bytes 393224 | tf_op jit(solution)/shard_map/ppermute | solution.py:21
  442.6 12.5 %collective-permute-start.3 = (bf16[1,128,512]{2,1,0:T(8,128)(2,1)S(1)}, bf16[1,128,512]{2,1,0:T(8,128)(2,1)S(1)}, u32[]{:S(2)}, u32[]{:S(2)}) collective-permute-start(bf16[1,128,512]{2,1,0:T(8,128)(2,1)S(1)} %get-tuple-element.52), channel_id=1, source_target_pairs={{0,1},{2,3},{4,5},{6,7},{8,9},{10,11},{12,13},{14,15},{16,17},{18,... | collective-permute-start | bytes 393224 | tf_op jit(solution)/shard_map/ppermute | solution.py:20
  455.1 125.4 %reduce-scatter.20.cloned.1.call-start = ((), (), s32[]{:S(2)}) async-start(), calls=%async_computation.12 | async-start | bytes 393216 | tf_op jit(solution)/shard_map/reduce_scatter | solution.py:215
  458.1 140.6 %reduce-scatter.16.cloned.1.call-start = ((), (), s32[]{:S(2)}) async-start(), calls=%async_computation.10 | async-start | bytes 884736 | tf_op jit(solution)/shard_map/reduce_scatter | solution.py:214
Sparse Core Ops, SparseCore 0:
  17.0 53.6 all-gather.10
  72.8 39.7 all-gather.12
  114.7 40.2 all-gather.14
  291.3 69.3 reduce-scatter.21
  364.9 72.2 reduce-scatter.17
  441.1 110.4 reduce-scatter.13
  554.5 11.4 reduce-scatter.23
  568.7 11.6 reduce-scatter.19
  583.4 15.2 reduce-scatter.15
where the time goes:
time: 612 us; the launch traced here: 605 us
  blocking collectives  221 us (36%)
  matrix products  163 us (27%)
  waiting for transfers between devices  121 us (20%)
  other arithmetic  45.1 us (7%)
  local copies, waits for them, and re-layouts  29.2 us (5%)
  between operations  16.1 us (3%)
  starting transfers between devices  10.4 us (2%)
    reduce_scatter x1, waiting for transfers between devices, local(): lax.psum_scatter(conv_weight_grad, 'batch', scatter_dimension=2, tiled=True)  90.6 us
    unnamed x3, blocking collectives  70.1 us
    dot_general x1, matrix products, local(): jnp.einsum('rti,if->rtf', hidden_low, up_full, preferred_element_type=jnp...  44.9 us
    dot_general x1, matrix products, local(): jnp.einsum('rtki,kio->rto', stacked, conv_full, preferred_element_type=jn...  24.8 us
    dot_general x1, matrix products, local(): jnp.einsum('rto,fo->rtf', grad_down_low, down_full, preferred_element_typ...  22.8 us
    unnamed x16, other arithmetic  22.3 us
    all_gather x1, blocking collectives, local(): lax.all_gather(partial_value[3], 'batch', axis=0, tiled=True)  21.7 us
    all_gather x1, blocking collectives, local(): lax.all_gather(partial_value[5], 'batch', axis=0, tiled=True)  18.8 us
  transfers between devices with their start and end apart: 13, of which 3 were waited for; matrix products, arithmetic and copies ran while one was open for 34% of the time, Pallas kernels for 0%

commit v1 on v0

v1 whole, which is shorter than its diff:
```python
import functools
import jax
import jax.numpy as jnp
from jax import lax
from jax.experimental import pallas as pl
from jax.experimental.pallas import tpu as pltpu
from jax.sharding import PartitionSpec as P

KERNEL_TAPS = 9
DILATION_STEP = 32
EPSILON = 1e-05
SUB = 256
BF = jnp.bfloat16
F32 = jnp.float32
NN = (((1,), (0,)), ((), ()))
NT = (((1,), (1,)), ((), ()))
TN = (((0,), (0,)), ((), ()))


def dot(a, b, dims):
    return lax.dot_general(a, b, dims, preferred_element_type=F32)


def conv_cost(count, width):
    return pl.CostEstimate(flops=2 * count * KERNEL_TAPS * width * width, bytes_accessed=2**24, transcendentals=0)


def gelu_pair(v):
    size = jnp.abs(v)
    t = pl.reciprocal(1.0 + 0.23164189 * size, approx=True)
    poly = t * (0.127414796 + t * (-0.142248368 + t * (0.710706871 + t * (-0.726576013 + t * 0.530702714))))
    bell = jnp.exp2(-0.72134752 * (size * size))
    value = jnp.maximum(v, 0.0) - size * (poly * bell)
    low_side = bell * (poly - 0.39894228 * size)
    return value, jnp.where(v >= 0.0, 1.0 - low_side, low_side)


def row_mean(v):
    return jnp.sum(v, -1, keepdims=True) * (1.0 / v.shape[-1])


def fold(v):
    total = v[0:8]
    for r in range(8, v.shape[0], 8):
        total = total + v[r : r + 8]
    return total


def fill_columns(col, load, flags, block, subs, width):
    for r in range(subs):
        j = block * subs + r
        base = j * SUB
        own = flags[2, j].astype(F32).astype(BF)
        before = flags[0, j].astype(F32).astype(BF)
        after = flags[1, j].astype(F32).astype(BF)
        for k in range(KERNEL_TAPS):
            o = (k - KERNEL_TAPS // 2) * DILATION_STEP
            columns = slice(k * width, (k + 1) * width)
            first = r * SUB
            if o < 0:
                col[first : first - o, columns] = load(base + o, -o) * before
                col[first - o : first + SUB, columns] = load(base, SUB + o) * own
            elif o == 0:
                col[first : first + SUB, columns] = load(base, SUB) * own
            else:
                col[first : first + SUB - o, columns] = load(base + o, SUB - o) * own
                col[first + SUB - o : first + SUB, columns] = load(base + SUB, o) * after


def conv_kernel(subs, flags, prev, x, nxt, w, bias, xhat_out, scale_out, ext, col):
    block = pl.program_id(0)
    width = x.shape[1]
    border = prev.shape[0]

    @pl.when(block == 0)
    def _():
        ext[0:border] = prev[...]
        ext[border : border + x.shape[0]] = x[...]
        ext[border + x.shape[0] :] = nxt[...]

    def load(start, count):
        return ext[pl.ds(pl.multiple_of(start + border, DILATION_STEP), count), :]

    fill_columns(col, load, flags, block, subs, width)
    total = None
    for k in range(KERNEL_TAPS):
        part = dot(col[:, k * width : (k + 1) * width], w[k], NT)
        total = part if total is None else total + part
    value, slope = gelu_pair(total + bias[...])
    centered = value - row_mean(value)
    rstd = lax.rsqrt(row_mean(centered * centered) + EPSILON)
    xhat_out[...] = centered * rstd
    scale_out[...] = slope * rstd


def conv_forward(flags, prev, x, nxt, w, bias, subs):
    count, width = x.shape
    rows = subs * SUB
    whole = lambda shape: pl.BlockSpec(shape, lambda j, f: (0,) * len(shape), pipeline_mode=pl.Buffered(1))
    return pl.pallas_call(
        functools.partial(conv_kernel, subs),
        grid_spec=pltpu.PrefetchScalarGridSpec(
            num_scalar_prefetch=1,
            grid=(count // rows,),
            in_specs=[whole(prev.shape), whole(x.shape), whole(nxt.shape), whole(w.shape), whole(bias.shape)],
            out_specs=[pl.BlockSpec((rows, width), lambda j, f: (j, 0))] * 2,
            scratch_shapes=[
                pltpu.VMEM((count + 2 * prev.shape[0], width), BF),
                pltpu.VMEM((rows, KERNEL_TAPS * width), BF),
            ],
        ),
        out_shape=[jax.ShapeDtypeStruct((count, width), F32)] * 2,
        compiler_params=pltpu.CompilerParams(vmem_limit_bytes=56 * 2**20),
        cost_estimate=conv_cost(count, width),
        name="conv_forward",
    )(flags, prev, x, nxt, w, bias)


def ffn_kernel(chunk, fast, core, x, xhat, scale, og, pair, ub, vec, out, gh_out, gc_out, *rest):
    act, slope, dup, ddown, sums, ub_sums = rest[-6:]
    step = pl.program_id(0)
    last = pl.num_programs(0) - 1
    _, hidden, width = pair.shape
    chunks = hidden // chunk
    gain1, shift1, db, gain2, shift2 = (vec[i : i + 1, :] for i in range(5))

    @pl.when(step == 0)
    def _():
        dup[...] = jnp.zeros_like(dup)
        ddown[...] = jnp.zeros_like(ddown)
        sums[...] = jnp.zeros_like(sums)
        ub_sums[...] = jnp.zeros_like(ub_sums)

    one = x[...].astype(F32) + (xhat[...] * gain1 + shift1)
    low = one.astype(BF)
    total = None
    for f in range(chunks):
        cols = slice(f * chunk, (f + 1) * chunk)
        value, s = gelu_pair(dot(low, pair[0, cols, :], NT) + ub[:, cols])
        a = value.astype(BF)
        act[:, cols] = a
        slope[:, cols] = s
        part = dot(a, pair[1, cols, :], NN)
        total = part if total is None else total + part
    d = total + db
    centered = d - row_mean(d)
    rstd = lax.rsqrt(row_mean(centered * centered) + EPSILON)
    hat = centered * rstd
    out[...] = (one + (hat * gain2 + shift2)).astype(BF)
    g = og[...].astype(F32)
    e = g * gain2
    gd = (rstd * (e - row_mean(e) - hat * row_mean(e * hat))).astype(BF)
    sums[0] += fold(g * hat)
    sums[1] += fold(g)
    sums[2] += fold(gd.astype(F32))
    gh = g
    for f in range(chunks):
        cols = slice(f * chunk, (f + 1) * chunk)
        ddown[:, cols] += dot(gd, act[:, cols], TN)
        gu = dot(gd, pair[1, cols, :], NT) * slope[:, cols]
        gul = gu.astype(BF)
        ub_sums[:, cols] += fold(gul.astype(F32))
        dup[:, cols] += dot(low, gul, TN)
        gh = gh + dot(gul, pair[0, cols, :], NN)
    gh_out[...] = gh
    sums[3] += fold(gh * xhat[...])
    sums[4] += fold(gh)
    e = gh * gain1
    gc = (scale[...] * (e - row_mean(e) - xhat[...] * row_mean(e * xhat[...]))).astype(BF)
    gc_out[...] = gc
    sums[5] += fold(gc.astype(F32))

    @pl.when(step == last)
    def _():
        if not fast:
            up_out, down_out, sums_out, ub_out = rest[:4]
            up_out[...] = dup[...]
            down_out[...] = ddown[...]
            sums_out[...] = jnp.sum(sums[...], 1)
            ub_out[...] = jnp.sum(ub_sums[...], 0, keepdims=True)
            return
        up_send, up_keep, down_send, down_keep = rest[:4]
        mine = core[0] == 0
        block = up_send.shape[3]
        half = width // 2
        devices = 2 * (hidden // block)

        def own(length):
            each = length // devices
            place = lax.broadcasted_iota(jnp.int32, (devices, length), 1) // each
            return place == lax.broadcasted_iota(jnp.int32, (devices, length), 0)

        def pick(length, start):
            each = length // devices
            place = lax.broadcasted_iota(jnp.int32, (length, 128), 0) % each + start
            return (place == lax.broadcasted_iota(jnp.int32, (length, 128), 1)).astype(BF)

        first = None
        for v in range(6):
            line = jnp.sum(sums[v], 0, keepdims=True)
            part = dot(jnp.where(own(width), line, 0.0).astype(BF), pick(width, v * (width // devices)), NN)
            first = part if first is None else first + part
        line = jnp.sum(ub_sums[...], 0, keepdims=True)
        second = dot(jnp.where(own(hidden), line, 0.0).astype(BF), pick(hidden, 0), NN)
        index = lax.broadcasted_iota(jnp.int32, (16, 128), 0)

        def tail(b, s):
            at = 2 * b + s
            return jnp.where(index == 0, first[at : at + 1], jnp.where(index == 1, second[at : at + 1], 0.0)).astype(BF)

        for z in range(up_send.shape[0]):
            for s in range(2):
                take = slice(s * half, (s + 1) * half)
                for acc, send, keep in ((dup, up_send, up_keep), (ddown, down_send, down_keep)):
                    lo = acc[take, 2 * z * block : (2 * z + 1) * block].astype(BF)
                    hi = acc[take, (2 * z + 1) * block : (2 * z + 2) * block].astype(BF)
                    send[z, s, 0:half] = jnp.where(mine, hi, lo)
                    keep[z, s, 0:half] = jnp.where(mine, lo, hi)
                lo, hi = tail(2 * z, s), tail(2 * z + 1, s)
                up_send[z, s, half:] = jnp.where(mine, hi, lo)
                up_keep[z, s, half:] = jnp.where(mine, lo, hi)


def ffn(core, x, xhat, scale, og, pair, ub, vec, rows, chunk, batch, fast):
    count, width = x.shape
    hidden = pair.shape[1]
    whole = lambda shape: pl.BlockSpec(shape, lambda j, f: (0,) * len(shape), pipeline_mode=pl.Buffered(1))
    tile = pl.BlockSpec((rows, width), lambda j, f: (j, 0))
    sds = jax.ShapeDtypeStruct
    if fast:
        shapes = [sds((batch // 2, 2, width // 2 + extra, hidden // batch), BF) for extra in (16, 16, 0, 0)]
    else:
        shapes = [sds(s, F32) for s in ((width, hidden), (width, hidden), (6, width), (1, hidden))]
    return pl.pallas_call(
        functools.partial(ffn_kernel, chunk, fast),
        grid_spec=pltpu.PrefetchScalarGridSpec(
            num_scalar_prefetch=1,
            grid=(count // rows,),
            in_specs=[tile, tile, tile, tile, whole(pair.shape), whole(ub.shape), whole(vec.shape)],
            out_specs=[tile, tile, tile] + [whole(s.shape) for s in shapes],
            scratch_shapes=[
                pltpu.VMEM((rows, hidden), BF),
                pltpu.VMEM((rows, hidden), F32),
                pltpu.VMEM((width, hidden), F32),
                pltpu.VMEM((width, hidden), F32),
                pltpu.VMEM((6, 8, width), F32),
                pltpu.VMEM((8, hidden), F32),
            ],
        ),
        out_shape=[sds((count, width), BF), sds((count, width), F32), sds((count, width), BF)] + shapes,
        compiler_params=pltpu.CompilerParams(vmem_limit_bytes=60 * 2**20),
        cost_estimate=pl.CostEstimate(flops=12 * count * width * hidden, bytes_accessed=2**25, transcendentals=0),
        name="feed_forward",
    )(core, x, xhat, scale, og, pair, ub, vec)


def conv_weight_kernel(fast, flags, prev, x, nxt, g, *rest):
    ext, col = rest[-2:]
    tap = pl.program_id(0)
    count, width = x.shape
    border = prev.shape[0]
    subs = count // SUB

    @pl.when(tap == 0)
    def _():
        ext[0:border] = prev[...]
        ext[border : border + count] = x[...]
        ext[border + count :] = nxt[...]

    o = (tap - KERNEL_TAPS // 2) * DILATION_STEP
    place = lax.broadcasted_iota(jnp.int32, (SUB, 1), 0) + o
    for r in range(subs):
        own = flags[2, r].astype(F32)
        before = flags[0, r].astype(F32)
        after = flags[1, r].astype(F32)
        mask = jnp.where(place < 0, before, jnp.where(place >= SUB, after, own)).astype(BF)
        rows = ext[pl.ds(pl.multiple_of(r * SUB + o + border, DILATION_STEP), SUB), :]
        col[r * SUB : (r + 1) * SUB, :] = rows * mask
    grad = dot(g[...], col[...], TN)
    if not fast:
        rest[0][0] = grad
        return
    send, keep = rest[:2]
    mine = flags[3, 0] == 0
    block = send.shape[3]
    half = width // 2
    for s in range(2):
        for z in range(send.shape[2]):
            lo = grad[2 * z * block : (2 * z + 1) * block, s * half : (s + 1) * half].astype(BF)
            hi = grad[(2 * z + 1) * block : (2 * z + 2) * block, s * half : (s + 1) * half].astype(BF)
            send[s, 0, z] = jnp.where(mine, hi, lo)
            keep[s, 0, z] = jnp.where(mine, lo, hi)


def conv_weight_backward(flags, prev, x, nxt, g, batch, fast):
    count, width = x.shape
    whole = lambda shape: pl.BlockSpec(shape, lambda j, f: (0,) * len(shape), pipeline_mode=pl.Buffered(1))
    if fast:
        part = (2, KERNEL_TAPS, batch // 2, width // batch, width // 2)
        specs = [pl.BlockSpec((2, 1) + part[2:], lambda k, f: (0, k, 0, 0, 0))] * 2
        shapes = [jax.ShapeDtypeStruct(part, BF)] * 2
    else:
        specs = [pl.BlockSpec((1, width, width), lambda k, f: (k, 0, 0))]
        shapes = [jax.ShapeDtypeStruct((KERNEL_TAPS, width, width), F32)]
    return pl.pallas_call(
        functools.partial(conv_weight_kernel, fast),
        grid_spec=pltpu.PrefetchScalarGridSpec(
            num_scalar_prefetch=1,
            grid=(KERNEL_TAPS,),
            in_specs=[whole(prev.shape), whole(x.shape), whole(nxt.shape), whole(g.shape)],
            out_specs=specs,
            scratch_shapes=[pltpu.VMEM((count + 2 * prev.shape[0], width), BF), pltpu.VMEM((count, width), BF)],
        ),
        out_shape=shapes,
        compiler_params=pltpu.CompilerParams(vmem_limit_bytes=56 * 2**20),
        cost_estimate=conv_cost(count, width),
        name="conv_weight_backward",
    )(flags, prev, x, nxt, g)


def conv_input_kernel(subs, flags, prev, g, nxt, w, gh, out, ext, col):
    block = pl.program_id(0)
    count, width = g.shape
    border = prev.shape[0]

    @pl.when(block == 0)
    def _():
        ext[0:border] = prev[...]
        ext[border : border + count] = g[...]
        ext[border + count :] = nxt[...]

    def load(start, size):
        return ext[pl.ds(pl.multiple_of(start + border, DILATION_STEP), size), :]

    fill_columns(col, load, flags, block, subs, width)
    total = gh[...]
    for k in range(KERNEL_TAPS):
        total = total + dot(col[:, k * width : (k + 1) * width], w[KERNEL_TAPS - 1 - k], NN)
    out[...] = total


def conv_input_backward(flags, prev, g, nxt, w, gh, subs):
    count, width = g.shape
    rows = subs * SUB
    whole = lambda shape: pl.BlockSpec(shape, lambda j, f: (0,) * len(shape), pipeline_mode=pl.Buffered(1))
    tile = pl.BlockSpec((rows, width), lambda j, f: (j, 0))
    return pl.pallas_call(
        functools.partial(conv_input_kernel, subs),
        grid_spec=pltpu.PrefetchScalarGridSpec(
            num_scalar_prefetch=1,
            grid=(count // rows,),
            in_specs=[whole(prev.shape), whole(g.shape), whole(nxt.shape), whole(w.shape), tile],
            out_specs=tile,
            scratch_shapes=[
                pltpu.VMEM((count + 2 * prev.shape[0], width), BF),
                pltpu.VMEM((rows, KERNEL_TAPS * width), BF),
            ],
        ),
        out_shape=jax.ShapeDtypeStruct((count, width), F32),
        compiler_params=pltpu.CompilerParams(vmem_limit_bytes=56 * 2**20),
        cost_estimate=conv_cost(count, width),
        name="conv_input_backward",
    )(flags, prev, g, nxt, w, gh)


def swap(value, axis, bit):
    count = lax.axis_size(axis)
    return lax.ppermute(value, axis, [(i, i ^ bit) for i in range(count)])


def half_of(axis, bit):
    return (lax.axis_index(axis) // bit) % 2


def exchange(value, axis, bit, dim):
    mine = half_of(axis, bit)
    give = lax.dynamic_index_in_dim(value, 1 - mine, dim, keepdims=False).astype(BF)
    keep = lax.dynamic_index_in_dim(value, mine, dim, keepdims=False).astype(F32)
    return keep + swap(give, axis, bit).astype(F32)


def gather_pieces(own, batch, seq):
    offsets = [(0, 0)]
    bit = batch // 2
    while bit >= 4:
        own = jnp.concatenate([own, swap(own, "batch", bit)], 0)
        offsets += [(b ^ bit, s) for b, s in offsets]
        bit //= 2
    cut = own.shape[1] // 32 * 16
    over_x = swap(own, "batch", 2)
    over_y = swap(own, "seq", 1)
    top = swap(over_x[:, :cut], "seq", 1)
    bottom = swap(over_y[:, cut:], "batch", 2)
    return [own, over_x, over_y, top, bottom], offsets, cut


def assemble_kernel(pieces, taps, rows, small, where, *refs):
    count = len(pieces)
    sources, targets, stash = refs[:count], refs[count : count + 1 + bool(small)], refs[count + 1 + bool(small) :]
    whole = targets[0]
    wide = sources[0].shape[2]
    if small:
        stash[0][...] = jnp.zeros_like(stash[0])
    for source, (offsets, first) in zip(sources, pieces):
        size = source.shape[1]
        for n, (db, ds) in enumerate(offsets):
            b = where[0] ^ db
            s = where[1] ^ ds
            columns = pl.ds(pl.multiple_of(s * wide, wide), wide)
            at = first
            while at < first + size:
                if at >= taps * rows:
                    row = source[n, at - first : at - first + 1, :].astype(F32) if at == taps * rows else None
                    if row is not None:
                        stash[0][pl.ds(2 * b + s, 1), :] = row
                    break
                tap = at // rows
                upto = min(first + size, (tap + 1) * rows)
                inside = at - tap * rows
                whole[tap, pl.ds(pl.multiple_of(b * rows + inside, 16), upto - at), columns] = source[n, at - first : upto - first, :]
                at = upto
    if small:
        table = stash[0][...]
        out = targets[1]
        devices = table.shape[0]
        for v, (start, each, row) in enumerate(small):
            length = devices * each
            pick = (
                lax.broadcasted_iota(jnp.int32, (wide, length), 1) % each + start
                == lax.broadcasted_iota(jnp.int32, (wide, length), 0)
            ).astype(BF)
            spread = dot(table.astype(BF), pick, NN)
            own = lax.broadcasted_iota(jnp.int32, (devices, length), 1) // each == lax.broadcasted_iota(
                jnp.int32, (devices, length), 0
            )
            out[row : row + 1, :length] = jnp.sum(jnp.where(own, spread, 0.0), 0, keepdims=True)


def assemble(where, arrays, pieces, taps, rows, batch, small, width):
    shape = (taps, rows * batch, arrays[0].shape[2] * 2)
    out_shape = [jax.ShapeDtypeStruct(shape, BF)]
    scratch = []
    if small:
        out_shape.append(jax.ShapeDtypeStruct((8, width), F32))
        scratch.append(pltpu.VMEM((2 * batch, arrays[0].shape[2]), F32))
    return pl.pallas_call(
        functools.partial(assemble_kernel, pieces, taps, rows, small),
        grid_spec=pltpu.PrefetchScalarGridSpec(
            num_scalar_prefetch=1,
            grid=(1,),
            in_specs=[pl.BlockSpec(a.shape, lambda i, f: (0, 0, 0)) for a in arrays],
            out_specs=[pl.BlockSpec(o.shape, lambda i, f, n=len(o.shape): (0,) * n) for o in out_shape],
            scratch_shapes=scratch,
        ),
        out_shape=out_shape,
        compiler_params=pltpu.CompilerParams(vmem_limit_bytes=56 * 2**20),
        name="assemble",
    )(where, *arrays)


def gather_whole(where, own, taps, rows, batch, seq, small, width):
    arrays, offsets, cut = gather_pieces(own, batch, seq)
    shift = lambda b, s: tuple((ob ^ b, os ^ s) for ob, os in offsets)
    plans = [(shift(0, 0), 0), (shift(2, 0), 0), (shift(0, 1), 0), (shift(2, 1), 0), (shift(2, 1), cut)]
    others = [swap(a, "batch", 1) for a in arrays]
    plans = plans + [(tuple((b ^ 1, s) for b, s in o), first) for o, first in plans]
    return assemble(where, arrays + others, tuple(plans), taps, rows, batch, small, width)


def local(inputs, window_lengths, conv_weight, conv_bias, norm1_gain, norm1_bias, up_weight, up_bias, down_weight,
          down_bias, norm2_gain, norm2_bias, out_grad):
    _, count, width = inputs.shape
    batch, seq = lax.axis_size("batch"), lax.axis_size("seq")
    hidden = up_weight.shape[1] * batch
    border = KERNEL_TAPS // 2 * DILATION_STEP
    my_batch, my_seq = lax.axis_index("batch"), lax.axis_index("seq")
    x, og = inputs[0], out_grad[0]

    def ends(value):
        first, final = value[:border], value[count - border :]
        if seq == 2:
            other = swap(jnp.where(my_seq == 0, final, first), "seq", 1)
            return other, other
        up = [(i, i + 1) for i in range(seq - 1)]
        return lax.ppermute(final, "seq", up), lax.ppermute(first, "seq", [(j, i) for i, j in up])

    lengths = window_lengths[0]
    slots = lengths.shape[0]
    window_end = jnp.sum(jnp.where(jnp.arange(slots)[:, None] >= jnp.arange(slots)[None, :], lengths[None, :], 0), 1)
    subs = count // SUB
    starts = my_seq * count + (jnp.arange(subs + 2, dtype=jnp.int32) - 1) * SUB
    ids = jnp.sum((starts[:, None] >= window_end[None, :]).astype(jnp.int32), 1)
    inside = (ids < slots).astype(jnp.int32)[1:-1]
    same = ((ids[1:] == ids[:-1]) & (starts[:-1] >= 0)).astype(jnp.int32)
    core = jnp.full((subs,), my_batch % 2, jnp.int32)
    flags = jnp.stack([same[:-1] * inside, same[1:] * inside, inside, core])

    prev, nxt = ends(x)
    vectors = [conv_bias, norm1_gain, norm1_bias, down_bias, norm2_gain, norm2_bias, up_bias]
    rows = width // batch
    hidden_rows = hidden // batch
    conv_own = conv_weight.transpose(0, 2, 1)
    pair_own = jnp.stack([up_weight.T, down_weight])
    if seq == 2:
        where = jnp.stack([my_batch, my_seq]).astype(jnp.int32)
        wide = conv_own.shape[2]
        each = [v.shape[0] for v in vectors]
        tail = jnp.concatenate(vectors + [jnp.zeros((16 * wide - sum(each),), BF)]).reshape(16, wide)
        conv_block = jnp.concatenate([conv_own.reshape(-1, wide), tail], 0)[None]
        small = []
        for i, n in enumerate(each):
            small.append((sum(each[:i]), n, i))
        conv_full, table = gather_whole(where, conv_block, KERNEL_TAPS, rows, batch, seq, tuple(small), hidden)
        (pair_full,) = gather_whole(
            where, pair_own.reshape(1, -1, wide), 2, hidden_rows, batch, seq, (), hidden
        )
        conv_bias_row = table[0:1, :width]
        vec = jnp.concatenate([table[1:6, :width], jnp.zeros((3, width), F32)])
        up_bias_row = table[6:7]
    else:
        def every(value, dims):
            value = lax.all_gather(value, "seq", axis=dims[0], tiled=True)
            return lax.all_gather(value, "batch", axis=dims[1], tiled=True)
        conv_full = every(conv_own, (2, 1))
        pair_full = every(pair_own, (2, 1))
        full = [lax.all_gather(v, ("batch", "seq"), axis=0, tiled=True).astype(F32) for v in vectors]
        conv_bias_row = full[0][None]
        vec = jnp.stack(full[1:6] + [jnp.zeros((width,), F32)] * 3)
        up_bias_row = full[6][None]

    xhat, scale = conv_forward(flags, prev, x, nxt, conv_full, conv_bias_row, 2)
    fast = seq == 2
    block_output, grad_hidden, grad_conv, *ffn_grads = ffn(
        flags[3, :1], x, xhat, scale, og, pair_full, up_bias_row, vec, 2 * SUB, min(1024, hidden), batch, fast
    )
    grad_prev, grad_next = ends(grad_conv)
    conv_grads = conv_weight_backward(flags, prev, x, nxt, grad_conv, batch, fast)
    input_grad = conv_input_backward(flags, grad_prev, grad_conv, grad_next, conv_full, grad_hidden, 2)
    sums = whole_sums if not fast else pair_sums
    weight_grads = sums(conv_grads, ffn_grads, batch, seq, width, hidden)
    conv_grad, cb, g1, s1, up_grad, ub_grad, down_grad, db, g2, s2 = weight_grads
    return (block_output[None], input_grad[None], conv_grad, cb, g1, s1, up_grad, ub_grad, down_grad, db, g2, s2)


def whole_sums(conv_grads, ffn_grads, batch, seq, width, hidden):
    def total(value, dims):
        value = lax.psum_scatter(value, "batch", scatter_dimension=dims[1], tiled=True)
        return lax.psum_scatter(value, "seq", scatter_dimension=dims[0], tiled=True)

    conv_grad = total(conv_grads[0], (2, 1)).transpose(0, 2, 1)
    up_grad = total(ffn_grads[0], (0, 1))
    down_grad = total(ffn_grads[1], (0, 1)).T
    vec_grads = total(ffn_grads[2].reshape(6, batch, seq, -1), (2, 1)).reshape(6, -1)
    ub_grad = total(ffn_grads[3].reshape(batch, seq, -1), (1, 0)).reshape(-1)
    g2, s2, db, g1, s1, cb = (vec_grads[i] for i in range(6))
    return conv_grad, cb, g1, s1, up_grad, ub_grad, down_grad, db, g2, s2


def pair_sums(conv_grads, ffn_grads, batch, seq, width, hidden):
    z_count = batch // 4

    def finish(value, dim):
        bit, left = 4, z_count
        while left > 1:
            shape = value.shape
            value = exchange(value.reshape(shape[:dim] + (left // 2, 2) + shape[dim + 1 :]), "batch", bit, dim + 1)
            bit, left = bit * 2, left // 2
        return value

    def chip(send, keep):
        return keep.astype(F32) + swap(send, "batch", 1).astype(F32)

    up_send, up_keep, down_send, down_keep = ffn_grads
    block = hidden // batch
    up_sum = chip(up_send, up_keep).reshape(z_count, 2, 2, -1, block)
    down_sum = chip(down_send, down_keep).reshape(z_count, 2, 2, -1, block)
    up_sum = exchange(exchange(up_sum, "batch", 2, 1), "seq", 1, 1)
    down_sum = exchange(exchange(down_sum, "seq", 1, 2), "batch", 2, 1)
    pair_sum = finish(jnp.concatenate([up_sum, down_sum], 1), 0)[0]
    rows = width // batch
    conv_sum = chip(*conv_grads).reshape(2, KERNEL_TAPS, z_count, 2, rows, width // 2)
    upper = exchange(exchange(conv_sum[..., : rows // 2, :], "batch", 2, 3), "seq", 1, 0)
    lower = exchange(exchange(conv_sum[..., rows // 2 :, :], "seq", 1, 0), "batch", 2, 2)
    conv_grad = finish(jnp.concatenate([upper, lower], 2), 1)[:, 0].transpose(0, 2, 1)
    up_rows = up_sum.shape[1]
    head = width // 2
    up_grad = pair_sum[:head]
    down_grad = pair_sum[up_rows : up_rows + head].T
    each = width // (batch * seq)
    g2, s2, db, g1, s1, cb = (pair_sum[head, i * each : (i + 1) * each] for i in range(6))
    ub_grad = pair_sum[head + 1, : hidden // (batch * seq)]
    return conv_grad, cb, g1, s1, up_grad, ub_grad, down_grad, db, g2, s2


def solution(mesh):
    in_specs = (
        P("batch", "seq", None),
        P("batch", None),
        P(None, "seq", "batch"),
        P(("batch", "seq")),
        P(("batch", "seq")),
        P(("batch", "seq")),
        P("seq", "batch"),
        P(("batch", "seq")),
        P("batch", "seq"),
        P(("batch", "seq")),
        P(("batch", "seq")),
        P(("batch", "seq")),
        P("batch", "seq", None),
    )
    out_specs = (
        P("batch", "seq", None),
        P("batch", "seq", None),
        P(None, "seq", "batch"),
        P(("batch", "seq")),
        P(("batch", "seq")),
        P(("batch", "seq")),
        P("seq", "batch"),
        P(("batch", "seq")),
        P("batch", "seq"),
        P(("batch", "seq")),
        P(("batch", "seq")),
        P(("batch", "seq")),
    )
    return jax.shard_map(local, mesh=mesh, in_specs=in_specs, out_specs=out_specs, check_vma=False)
```

time: 612 us -> 261 us (0.43)
  blocking collectives: 221 us -> 0 us
  matrix products: 163 us -> 0 us
  Pallas kernels: 0 us -> 110 us
  waiting for transfers between devices: 121 us -> 78.5 us
  other arithmetic: 45.1 us -> 12.3 us
  starting transfers between devices: 10.4 us -> 40 us
  between operations: 16.1 us -> 1.17 us
  local copies, waits for them, and re-layouts: 29.2 us -> 18.7 us
    dot_general x9 -> x0, matrix products: 163 us -> none  [the longest x1 44.9 us: local(): jnp.einsum('rti,if->rtf', hidden_low, up_full, preferred_element_type=jnp...]
    all_gather x10 -> x0, blocking collectives: 151 us -> none  [the longest x1 21.7 us: local(): lax.all_gather(partial_value[3], 'batch', axis=0, tiled=True)]
    reduce_scatter x6 -> x0, waiting for transfers between devices: 121 us -> none  [the longest x1 90.6 us: local(): lax.psum_scatter(conv_weight_grad, 'batch', scatter_dimension=2, tiled=True)]
    pallas_call x0 -> x6, Pallas kernels: none -> 110 us  [the longest x1 46.9 us: ffn(): pl.pallas_call(functools.partial(ffn_kernel, chunk, fast), grid_spec=pltp...]
    ppermute x4 -> x39, waiting for transfers between devices: 0.01 us -> 78.5 us  [swap(): return lax.ppermute(value, axis, [(i, i ^ bit) for i in range(count)])]
    unnamed x3 -> x0, blocking collectives: 70.1 us -> none
    ppermute x4 -> x39, starting transfers between devices: 9.88 us -> 40 us  [swap(): return lax.ppermute(value, axis, [(i, i ^ bit) for i in range(count)])]
    unnamed x16 -> x0, other arithmetic: 22.3 us -> none
  transfers between devices with their start and end apart: 13 -> 39, of which waited for: 3 -> 20; matrix products, arithmetic and copies ran while one was open for 34% -> 9% of each run, Pallas kernels for 0% -> 16%
where the time goes in v1:
time: 261 us; the launch traced here: 260 us
  Pallas kernels  110 us (42%)
  waiting for transfers between devices  78.5 us (30%)
  starting transfers between devices  40 us (15%)
  local copies, waits for them, and re-layouts  18.7 us (7%)
  other arithmetic  12.3 us (5%)
    ppermute x39, waiting for transfers between devices, swap(): return lax.ppermute(value, axis, [(i, i ^ bit) for i in range(count)])  78.5 us
    pallas_call x1, Pallas kernels, ffn(): pl.pallas_call(functools.partial(ffn_kernel, chunk, fast), grid_spec=pltp...  46.9 us
    ppermute x39, starting transfers between devices, swap(): return lax.ppermute(value, axis, [(i, i ^ bit) for i in range(count)])  40 us
    pallas_call x1, Pallas kernels, conv_forward(): pl.pallas_call(functools.partial(conv_kernel, subs), grid_spec=pltpu.Pref...  20.2 us
    pallas_call x1, Pallas kernels, conv_weight_backward(): pl.pallas_call(functools.partial(conv_weight_kernel, fast), grid_spec=plt...  16.1 us
    pallas_call x1, Pallas kernels, conv_input_backward(): pl.pallas_call(functools.partial(conv_input_kernel, subs), grid_spec=pltp...  15.7 us
    pallas_call x2, Pallas kernels, assemble(): pl.pallas_call(functools.partial(assemble_kernel, pieces, taps, rows, sma...  10.8 us
    unnamed x44, local copies, waits for them, and re-layouts  5.9 us
  transfers between devices with their start and end apart: 39, of which 20 were waited for; matrix products, arithmetic and copies ran while one was open for 9% of the time, Pallas kernels for 16%

profile of v1, /device:TPU:0, one launch (start us, length us, event | category | flops | bytes accessed | tf_op | source)
XLA Modules:
  0.0 260.3 jit_solution(16760839370627621664)
XLA Ops:
  0.7 0.9 copy.35
  1.6 0.9 pad_maximum_fusion.6
  2.5 4.1 %collective-permute-start.12 = (bf16[1,256,256]{2,1,0:T(8,128)(2,1)S(1)}, bf16[1,256,256]{2,1,0:T(8,128)(2,1)S(1)}, u32[]{:S(2)}, u32[]{:S(2)}) collective-permute-start(bf16[1,256,256]{2,1,0:T(8,128)(2,1)S(1)} %bitcast.114), channel_id=1, source_target_pairs={{0,16},{2,18},{4,20},{6,22},{8,24},{10,26},{12,28},{14,30},{16,0},... | collective-permute-start | bytes 393224 | tf_op jit(solution)/shard_map/ppermute | solution.py:368
  6.6 4.8 %concatenate.29 = bf16[4096]{0:T(1024)(128)(2,1)S(1)} concatenate(bf16[16]{0:T(256)(128)(2,1)} %param.16, bf16[16]{0:T(256)(128)(2,1)} %param.17, bf16[16]{0:T(256)(128)(2,1)} %param.18, bf16[16]{0:T(256)(128)(2,1)} %param.22, bf16[16]{0:T(256)(128)(2,1)} %param.23, bf16[16]{0:T(256)(128)(2,1)} %param.24, bf16[64]{0:T(256)(128)(2,1)} %param.20, bf16[3936]{0:T(1024)(128)(2,1)S(1)} %broadcast_in_dim.34), dimensions={0} | concatenate | bytes 16384 | tf_op jit(solution)/shard_map/concatenate | solution.py:508
  11.3 0.9 maximum_bitcast_fusion
  12.9 1.4 collective-permute-start.13
  14.3 7.9 %collective-permute-done.1 = bf16[1,304,256]{2,1,0:T(8,128)(2,1)S(1)} collective-permute-done((bf16[1,304,256]{2,1,0:T(8,128)(2,1)S(1)}, bf16[1,304,256]{2,1,0:T(8,128)(2,1)S(1)}, u32[]{:S(2)}, u32[]{:S(2)}) %collective-permute-start.1) | collective-permute-done | bytes 155680 | tf_op jit(solution)/shard_map/ppermute | solution.py:368
  22.3 1.7 collective-permute-done.13
  24.0 1.2 collective-permute-start.14
  25.2 1.5 collective-permute-start.15
  26.7 3.7 %collective-permute-done.2 = bf16[2,304,256]{2,1,0:T(8,128)(2,1)S(1)} collective-permute-done((bf16[2,304,256]{2,1,0:T(8,128)(2,1)S(1)}, bf16[2,304,256]{2,1,0:T(8,128)(2,1)S(1)}, u32[]{:S(2)}, u32[]{:S(2)}) %collective-permute-start.2) | collective-permute-done | bytes 311328 | tf_op jit(solution)/shard_map/ppermute | solution.py:368
  30.5 1.4 collective-permute-start.4
  31.9 1.5 collective-permute-start.3
  33.5 5.4 %collective-permute-done.14.refs_1_ = bf16[4,256,256]{2,1,0:T(8,128)(2,1)S(1)} collective-permute-done((bf16[4,256,256]{2,1,0:T(8,128)(2,1)S(1)}, bf16[4,256,256]{2,1,0:T(8,128)(2,1)S(1)}, u32[]{:S(2)}, u32[]{:S(2)}) %collective-permute-start.14) | collective-permute-done | bytes 524320 | tf_op jit(solution)/shard_map/ppermute | solution.py:368
  39.0 1.1 collective-permute-done.15.refs_2_
  40.1 1.5 collective-permute-start.16
  41.8 11.6 %collective-permute-done.4.refs_2_ = bf16[4,304,256]{2,1,0:T(8,128)(2,1)S(1)} collective-permute-done((bf16[4,304,256]{2,1,0:T(8,128)(2,1)S(1)}, bf16[4,304,256]{2,1,0:T(8,128)(2,1)S(1)}, u32[]{:S(2)}, u32[]{:S(2)}) %collective-permute-start.4) | collective-permute-done | bytes 622624 | tf_op jit(solution)/shard_map/ppermute | solution.py:368
  53.4 0.9 collective-permute-start.17
  54.5 1.2 collective-permute-start.6
  55.7 1.6 collective-permute-start.5
  57.3 1.8 collective-permute-done.16.refs_3_
  59.6 1.5 collective-permute-done.17.refs_4_
  61.1 2.1 collective-permute-done.5.refs_3_
  63.2 1.3 collective-permute-done.6.refs_4_
  64.5 0.7 copy-done.12
  66.1 1.0 select_bitcast_fusion
  67.3 1.5 collective-permute-start
  69.3 0.7 add_add_fusion.flags
  70.5 5.2 %assemble.3.pair = bf16[2,2048,512]{2,1,0:T(8,128)(2,1)} custom-call(s32[2]{0:T(128)} %pad_add_fusion.where, bf16[4,256,256]{2,1,0:T(8,128)(2,1)} %copy-done.3, bf16[4,256,256]{2,1,0:T(8,128)(2,1)} %copy-done.6, bf16[4,256,256]{2,1,0:T(8,128)(2,1)} %copy-done.7, bf16[4,128,256]{2,1,0:T(8,128)(2,1)} %copy-done.16, ...), custom_call_target="tpu_custom_call" | custom-call | tf_op jit(solution)/shard_map/assemble/pallas_call | solution.py:446
  75.8 0.7 copy-done.15
  76.5 0.7 copy-done.13
  77.2 5.6 %assemble.2 = (bf16[9,512,512]{2,1,0:T(8,128)(2,1)}, f32[8,2048]{1,0:T(8,128)}) custom-call(s32[2]{0:T(128)} %pad_add_fusion.where, bf16[4,304,256]{2,1,0:T(8,128)(2,1)} %copy-done.1, bf16[4,304,256]{2,1,0:T(8,128)(2,1)} %copy-done.5, bf16[4,304,256]{2,1,0:T(8,128)(2,1)} %copy-done.4, bf16[4,144,256]{2,1,0:T(8,128)(2,1)} %copy-done.14, ...), custom_call_target="tpu_custom_call" | custom-call | tf_op jit(solution)/shard_map/assemble/pallas_call | solution.py:446
  82.8 1.3 slice.104.bias
  84.1 0.7 slice.108
  84.9 1.4 slice.107.ub
  87.6 20.2 %conv_forward.1 = (f32[2048,512]{1,0:T(8,128)}, f32[2048,512]{1,0:T(8,128)}) custom-call(s32[4,8]{1,0:T(4,128)} %add_add_fusion.flags, bf16[128,512]{1,0:T(8,128)(2,1)} %copy-done.18, bf16[2048,512]{1,0:T(8,128)(2,1)} %bitcast.122, bf16[128,512]{1,0:T(8,128)(2,1)} %copy-done.18, bf16[9,512,512]{2,1,0:T(8,128)(2,1)} %get-tuple-element.25.w, f32[1,512]{1,0:T(1,128)} %slice.104.bias), custom_call_target="tpu_custom_call" | custom-call | flops 9663676416 | bytes 16777216 | tf_op jit(solution)/shard_map/conv_forward/pallas_call | solution.py:100
  107.8 46.9 %feed_forward.1 = (bf16[2048,512]{1,0:T(8,128)(2,1)}, f32[2048,512]{1,0:T(8,128)}, bf16[2048,512]{1,0:T(8,128)(2,1)}, bf16[8,2,272,128]{3,2,1,0:T(8,128)(2,1)}, ...) custom-call(s32[1]{0:T(128)} %bitcast.core, ...), custom_call_target="tpu_custom_call" | custom-call | flops 25769803776 | bytes 33554432 | tf_op jit(solution)/shard_map/feed_forward/pallas_call | solution.py:234
  155.3 16.1 %conv_weight_backward.1 = (bf16[2,9,8,32,256]{4,3,2,1,0:T(8,128)(2,1)}, bf16[2,9,8,32,256]{4,3,2,1,0:T(8,128)(2,1)}) custom-call(s32[4,8]{1,0:T(4,128)} %add_add_fusion.flags, bf16[128,512]{1,0:T(8,128)(2,1)} %copy-done.18, bf16[2048,512]{1,0:T(8,128)(2,1)} %bitcast.124, bf16[128,512]{1,0:T(8,128)(2,1)} %copy-done.18, bf16[2048,512]{1,0:T(8,128)(2,1)} %get-tuple-element.30.g), custom_call_target="tpu_custom_call" | custom-call | flops 9663676416 | bytes 16777216 | tf_op jit(solution)/shard_map/conv_weight_backward/pallas_call | solution.py:305
  171.8 0.9 fusion.4
  173.6 1.1 collective-permute-start.32
  174.7 12.6 %collective-permute-done.35 = bf16[4,2,256,128]{3,2,0,1:T(8,128)(2,1)} collective-permute-done((bf16[4,2,256,128]{3,2,0,1:T(8,128)(2,1)}, bf16[4,2,256,128]{3,2,0,1:T(8,128)(2,1)}, u32[]{:S(2)}, u32[]{:S(2)}) %collective-permute-start.35) | collective-permute-done | bytes 524320 | tf_op jit(solution)/shard_map/ppermute | solution.py:368
  187.2 1.5 bitcast_add_fusion.2
  189.5 1.1 collective-permute-start.33
  190.6 1.0 slice_select_fusion
  191.6 1.1 collective-permute-start.23
  192.7 4.0 %collective-permute-done.36 = bf16[4,256,128]{2,1,0:T(8,128)(2,1)S(1)} collective-permute-done((bf16[4,256,128]{2,1,0:T(8,128)(2,1)S(1)}, bf16[4,256,128]{2,1,0:T(8,128)(2,1)S(1)}, u32[]{:S(2)}, u32[]{:S(2)}) %collective-permute-start.36) | collective-permute-done | bytes 262176 | tf_op jit(solution)/shard_map/ppermute | solution.py:368
  196.7 2.2 collective-permute-done.33
  199.1 2.8 %convert_add_fusion = f32[2,9,8,32,256]{4,3,2,1,0:T(8,128)S(1)} fusion(bf16[2,9,8,32,256]{4,3,2,1,0:T(8,128)(2,1)} %collective-permute-done.24, bf16[2,9,8,32,256]{4,3,2,1,0:T(8,128)(2,1)S(1)} %copy-done.2), kind=kLoop, calls=%fused_computation | loop fusion | flops 3538944 | bytes 9437184 | tf_op jit(solution)/shard_map/add | solution.py:571
  202.5 1.6 collective-permute-start.25
  204.1 0.7 copy-done.19
  204.7 15.7 %conv_input_backward.1 = f32[2048,512]{1,0:T(8,128)} custom-call(s32[4,8]{1,0:T(4,128)} %add_add_fusion.flags, bf16[128,512]{1,0:T(8,128)(2,1)} %copy-done.19, bf16[2048,512]{1,0:T(8,128)(2,1)} %get-tuple-element.30.g, bf16[128,512]{1,0:T(8,128)(2,1)} %copy-done.19, bf16[9,512,512]{2,1,0:T(8,128)(2,1)} %get-tuple-element.25.w, f32[2048,512]{1,0:T(8,128)} %get-tuple-element.31.gh), custom_call_target="tpu_custom_call" | custom-call | flops 9663676416 | bytes 16777216 | tf_op jit(solution)/shard_map/conv_input_backward/pallas_call | solution.py:347
  221.2 5.2 %collective-permute-start.38 = (bf16[1,528,128]{2,1,0:T(8,128)(2,1)S(1)}, bf16[1,528,128]{2,1,0:T(8,128)(2,1)S(1)}, u32[]{:S(2)}, u32[]{:S(2)}) collective-permute-start(bf16[1,528,128]{2,1,0:T(8,128)(2,1)S(1)} %dynamic-slice_convert_fusion.7), channel_id=1, source_target_pairs={{0,16},{2,18},{4,20},{6,22},{8,24},{10,26},{12,28},{14,30},{16,0},... | collective-permute-start | bytes 405512 | tf_op jit(solution)/shard_map/ppermute | solution.py:368
  226.7 1.6 collective-permute-start.26
  228.3 7.4 %collective-permute-done.27 = bf16[9,4,2,16,256]{4,3,1,0,2:T(8,128)(2,1)S(1)} collective-permute-done((bf16[9,4,2,16,256]{4,3,1,0,2:T(8,128)(2,1)S(1)}, bf16[9,4,2,16,256]{4,3,1,0,2:T(8,128)(2,1)S(1)}, u32[]{:S(2)}, u32[]{:S(2)}) %collective-permute-start.27) | collective-permute-done | bytes 589856 | tf_op jit(solution)/shard_map/ppermute | solution.py:368
  235.9 1.5 collective-permute-start.28
  237.5 1.4 collective-permute-done.26
  238.9 3.8 %collective-permute-done.28 = bf16[9,4,16,256]{3,2,1,0:T(8,128)(2,1)S(1)} collective-permute-done((bf16[9,4,16,256]{3,2,1,0:T(8,128)(2,1)S(1)}, bf16[9,4,16,256]{3,2,1,0:T(8,128)(2,1)S(1)}, u32[]{:S(2)}, u32[]{:S(2)}) %collective-permute-start.28) | collective-permute-done | bytes 294944 | tf_op jit(solution)/shard_map/ppermute | solution.py:368
  243.0 1.8 collective-permute-start.29
  244.8 0.7 slice_bitcast_fusion
  245.5 0.8 copy.42
  246.8 4.5 %collective-permute-done.29 = bf16[9,2,32,256]{3,2,1,0:T(8,128)(2,1)S(1)} collective-permute-done((bf16[9,2,32,256]{3,2,1,0:T(8,128)(2,1)S(1)}, bf16[9,2,32,256]{3,2,1,0:T(8,128)(2,1)S(1)}, u32[]{:S(2)}, u32[]{:S(2)}) %collective-permute-start.29) | collective-permute-done | bytes 294944 | tf_op jit(solution)/shard_map/ppermute | solution.py:368
  251.4 3.5 %collective-permute-start.30 = (bf16[9,1,32,256]{3,2,1,0:T(8,128)(2,1)S(1)}, bf16[9,1,32,256]{3,2,1,0:T(8,128)(2,1)S(1)}, u32[]{:S(2)}, u32[]{:S(2)}) collective-permute-start(bf16[9,1,32,256]{3,2,1,0:T(8,128)(2,1)S(1)} %dynamic-slice_convert_fusion.6), channel_id=1, source_target_pairs={{0,16},{2,18},{4,20},{6,22},{8,24},{10,26},{12,28},{14,30},{16,0},... | collective-permute-start | bytes 442376 | tf_op jit(solution)/shard_map/ppermute | solution.py:368
  255.4 4.2 %collective-permute-done.30 = bf16[9,1,32,256]{3,2,1,0:T(8,128)(2,1)S(1)} collective-permute-done((bf16[9,1,32,256]{3,2,1,0:T(8,128)(2,1)S(1)}, bf16[9,1,32,256]{3,2,1,0:T(8,128)(2,1)S(1)}, u32[]{:S(2)}, u32[]{:S(2)}) %collective-permute-start.30) | collective-permute-done | bytes 147488 | tf_op jit(solution)/shard_map/ppermute | solution.py:368
  259.6 0.7 add_bitcast_fusion
  (126 shorter events, 11.7 us)
Async XLA Ops:
  0.6 32.8 %copy-start.20 = (s32[1,9]{1,0:T(1,128)S(1)}, s32[1,9]{1,0:T(1,128)}, u32[]{:S(2)}) copy-start(s32[1,9]{1,0:T(1,128)} %param.14) | copy-start | bytes 112
  2.5 10.4 %collective-permute-start.12 = (bf16[1,256,256]{2,1,0:T(8,128)(2,1)S(1)}, bf16[1,256,256]{2,1,0:T(8,128)(2,1)S(1)}, u32[]{:S(2)}, u32[]{:S(2)}) collective-permute-start(bf16[1,256,256]{2,1,0:T(8,128)(2,1)S(1)} %bitcast.114), channel_id=1, source_target_pairs={{0,16},{2,18},{4,20},{6,22},{8,24},{10,26},{12,28},{14,30},{16,0},... | collective-permute-start | bytes 393224 | tf_op jit(solution)/shard_map/ppermute | solution.py:368
  12.3 9.9 %collective-permute-start.1 = (bf16[1,304,256]{2,1,0:T(8,128)(2,1)S(1)}, bf16[1,304,256]{2,1,0:T(8,128)(2,1)S(1)}, u32[]{:S(2)}, u32[]{:S(2)}) collective-permute-start(bf16[1,304,256]{2,1,0:T(8,128)(2,1)S(1)} %maximum_bitcast_fusion), channel_id=1, source_target_pairs={{0,16},{2,18},{4,20},{6,22},{8,24},{10,26},{12,28},{14,30},{16,0},... | collective-permute-start | bytes 466952 | tf_op jit(solution)/shard_map/ppermute | solution.py:368
  12.9 11.1 %collective-permute-start.13 = (bf16[2,256,256]{2,1,0:T(8,128)(2,1)S(1)}, bf16[2,256,256]{2,1,0:T(8,128)(2,1)S(1)}, u32[]{:S(2)}, u32[]{:S(2)}) collective-permute-start(bf16[2,256,256]{2,1,0:T(8,128)(2,1)S(1)} %pad_maximum_fusion.5), channel_id=1, source_target_pairs={{0,8},{2,10},{4,12},{6,14},{8,0},{10,2},{12,4},{14,6},{16,24},{18,... | collective-permute-start | bytes 786440 | tf_op jit(solution)/shard_map/ppermute | solution.py:368
  22.2 8.2 %collective-permute-start.2 = (bf16[2,304,256]{2,1,0:T(8,128)(2,1)S(1)}, bf16[2,304,256]{2,1,0:T(8,128)(2,1)S(1)}, u32[]{:S(2)}, u32[]{:S(2)}) collective-permute-start(bf16[2,304,256]{2,1,0:T(8,128)(2,1)S(1)} %pad_maximum_fusion.4), channel_id=1, source_target_pairs={{0,8},{2,10},{4,12},{6,14},{8,0},{10,2},{12,4},{14,6},{16,24},{18,... | collective-permute-start | bytes 933896 | tf_op jit(solution)/shard_map/ppermute | solution.py:368
  24.0 46.5 %copy-start.3 = (bf16[4,256,256]{2,1,0:T(8,128)(2,1)}, bf16[4,256,256]{2,1,0:T(8,128)(2,1)S(1)}, u32[]{:S(2)}) copy-start(bf16[4,256,256]{2,1,0:T(8,128)(2,1)S(1)} %pad_maximum_fusion.3.refs_0_) | copy-start | bytes 1572868
  24.0 14.9 %collective-permute-start.14 = (bf16[4,256,256]{2,1,0:T(8,128)(2,1)S(1)}, bf16[4,256,256]{2,1,0:T(8,128)(2,1)S(1)}, u32[]{:S(2)}, u32[]{:S(2)}) collective-permute-start(bf16[4,256,256]{2,1,0:T(8,128)(2,1)S(1)} %pad_maximum_fusion.3.refs_0_), channel_id=1, source_target_pairs={{0,4},{2,6},{4,0},{6,2},{8,12},{10,14},{12,8},{14,10},{16,20},{18,... | collective-permute-start | bytes 1572872 | tf_op jit(solution)/shard_map/ppermute | solution.py:368
  25.2 14.9 %collective-permute-start.15 = (bf16[4,256,256]{2,1,0:T(8,128)(2,1)S(1)}, bf16[4,256,256]{2,1,0:T(8,128)(2,1)S(1)}, u32[]{:S(2)}, u32[]{:S(2)}) collective-permute-start(bf16[4,256,256]{2,1,0:T(8,128)(2,1)S(1)} %pad_maximum_fusion.3.refs_0_), channel_id=1, source_target_pairs={{0,1},{1,0},{2,3},{3,2},{4,5},{5,4},{6,7},{7,6},{8,9},{9,8},{10,11... | collective-permute-start | bytes 1572872 | tf_op jit(solution)/shard_map/ppermute | solution.py:368
  30.5 45.2 %copy-start.1 = (bf16[4,304,256]{2,1,0:T(8,128)(2,1)}, bf16[4,304,256]{2,1,0:T(8,128)(2,1)S(1)}, u32[]{:S(2)}) copy-start(bf16[4,304,256]{2,1,0:T(8,128)(2,1)S(1)} %pad_maximum_fusion.2.refs_0_) | copy-start | bytes 1867780
  30.5 22.9 %collective-permute-start.4 = (bf16[4,304,256]{2,1,0:T(8,128)(2,1)S(1)}, bf16[4,304,256]{2,1,0:T(8,128)(2,1)S(1)}, u32[]{:S(2)}, u32[]{:S(2)}) collective-permute-start(bf16[4,304,256]{2,1,0:T(8,128)(2,1)S(1)} %pad_maximum_fusion.2.refs_0_), channel_id=1, source_target_pairs={{0,1},{1,0},{2,3},{3,2},{4,5},{5,4},{6,7},{7,6},{8,9},{9,8},{10,11... | collective-permute-start | bytes 1867784 | tf_op jit(solution)/shard_map/ppermute | solution.py:368
  31.9 22.5 %collective-permute-start.3 = (bf16[4,304,256]{2,1,0:T(8,128)(2,1)S(1)}, bf16[4,304,256]{2,1,0:T(8,128)(2,1)S(1)}, u32[]{:S(2)}, u32[]{:S(2)}) collective-permute-start(bf16[4,304,256]{2,1,0:T(8,128)(2,1)S(1)} %pad_maximum_fusion.2.refs_0_), channel_id=1, source_target_pairs={{0,4},{2,6},{4,0},{6,2},{8,12},{10,14},{12,8},{14,10},{16,20},{18,... | collective-permute-start | bytes 1867784 | tf_op jit(solution)/shard_map/ppermute | solution.py:368
  33.4 22.2 %collective-permute-start.18 = (bf16[4,256,256]{2,1,0:T(8,128)(2,1)S(1)}, bf16[4,256,256]{2,1,0:T(8,128)(2,1)S(1)}, u32[]{:S(2)}, u32[]{:S(2)}) collective-permute-start(bf16[4,256,256]{2,1,0:T(8,128)(2,1)S(1)} %pad_maximum_fusion.3.refs_0_), channel_id=1, source_target_pairs={{0,2},{2,0},{4,6},{6,4},{8,10},{10,8},{12,14},{14,12},{16,18},{18,... | collective-permute-start | bytes 1572872 | tf_op jit(solution)/shard_map/ppermute | solution.py:368
  39.0 31.6 %copy-start.6 = (bf16[4,256,256]{2,1,0:T(8,128)(2,1)}, bf16[4,256,256]{2,1,0:T(8,128)(2,1)S(1)}, u32[]{:S(2)}) copy-start(bf16[4,256,256]{2,1,0:T(8,128)(2,1)S(1)} %collective-permute-done.14.refs_1_) | copy-start | bytes 1572868
  39.0 20.1 %collective-permute-start.7 = (bf16[4,304,256]{2,1,0:T(8,128)(2,1)S(1)}, bf16[4,304,256]{2,1,0:T(8,128)(2,1)S(1)}, u32[]{:S(2)}, u32[]{:S(2)}) collective-permute-start(bf16[4,304,256]{2,1,0:T(8,128)(2,1)S(1)} %pad_maximum_fusion.2.refs_0_), channel_id=1, source_target_pairs={{0,2},{2,0},{4,6},{6,4},{8,10},{10,8},{12,14},{14,12},{16,18},{18,... | collective-permute-start | bytes 1867784 | tf_op jit(solution)/shard_map/ppermute | solution.py:368
  40.1 30.5 %copy-start.7 = (bf16[4,256,256]{2,1,0:T(8,128)(2,1)}, bf16[4,256,256]{2,1,0:T(8,128)(2,1)S(1)}, u32[]{:S(2)}) copy-start(bf16[4,256,256]{2,1,0:T(8,128)(2,1)S(1)} %collective-permute-done.15.refs_2_) | copy-start | bytes 1572868
  40.1 19.0 %collective-permute-start.16 = (bf16[4,128,256]{2,1,0:T(8,128)(2,1)S(1)}, bf16[4,128,256]{2,1,0:T(8,128)(2,1)S(1)}, u32[]{:S(2)}, u32[]{:S(2)}) collective-permute-start(bf16[4,128,256]{2,1,0:T(8,128)(2,1)S(1)} %slice.126), channel_id=1, source_target_pairs={{0,1},{1,0},{2,3},{3,2},{4,5},{5,4},{6,7},{7,6},{8,9},{9,8},{10,11... | collective-permute-start | bytes 786440 | tf_op jit(solution)/shard_map/ppermute | solution.py:368
  53.4 22.3 %copy-start.4 = (bf16[4,304,256]{2,1,0:T(8,128)(2,1)}, bf16[4,304,256]{2,1,0:T(8,128)(2,1)S(1)}, u32[]{:S(2)}) copy-start(bf16[4,304,256]{2,1,0:T(8,128)(2,1)S(1)} %collective-permute-done.4.refs_2_) | copy-start | bytes 1867780
  53.4 7.7 %collective-permute-start.17 = (bf16[4,128,256]{2,1,0:T(8,128)(2,1)S(1)}, bf16[4,128,256]{2,1,0:T(8,128)(2,1)}, u32[]{:S(2)}, u32[]{:S(2)}) collective-permute-start(bf16[4,128,256]{2,1,0:T(8,128)(2,1)S(1)} %slice.127), channel_id=1, source_target_pairs={{0,4},{2,6},{4,0},{6,2},{8,12},{10,14},{12,8},{14,10},{16,20},{18,... | collective-permute-start | bytes 786440 | tf_op jit(solution)/shard_map/ppermute | solution.py:368
  54.4 21.3 %copy-start.5 = (bf16[4,304,256]{2,1,0:T(8,128)(2,1)}, bf16[4,304,256]{2,1,0:T(8,128)(2,1)S(1)}, u32[]{:S(2)}) copy-start(bf16[4,304,256]{2,1,0:T(8,128)(2,1)S(1)} %collective-permute-done.3.refs_1_) | copy-start | bytes 1867780
  54.5 10.0 %collective-permute-start.6 = (bf16[4,160,256]{2,1,0:T(8,128)(2,1)S(1)}, bf16[4,160,256]{2,1,0:T(8,128)(2,1)S(1)}, u32[]{:S(2)}, u32[]{:S(2)}) collective-permute-start(bf16[4,160,256]{2,1,0:T(8,128)(2,1)S(1)} %slice.125), channel_id=1, source_target_pairs={{0,4},{2,6},{4,0},{6,2},{8,12},{10,14},{12,8},{14,10},{16,20},{18,... | collective-permute-start | bytes 983048 | tf_op jit(solution)/shard_map/ppermute | solution.py:368
  55.7 8.8 %copy-start.11 = (bf16[4,256,256]{2,1,0:T(8,128)(2,1)}, bf16[4,256,256]{2,1,0:T(8,128)(2,1)S(1)}, u32[]{:S(2)}) copy-start(bf16[4,256,256]{2,1,0:T(8,128)(2,1)S(1)} %collective-permute-done.18.refs_5_) | copy-start | bytes 1572868
  55.7 7.5 %collective-permute-start.5 = (bf16[4,144,256]{2,1,0:T(8,128)(2,1)S(1)}, bf16[4,144,256]{2,1,0:T(8,128)(2,1)S(1)}, u32[]{:S(2)}, u32[]{:S(2)}) collective-permute-start(bf16[4,144,256]{2,1,0:T(8,128)(2,1)S(1)} %slice.124), channel_id=1, source_target_pairs={{0,1},{1,0},{2,3},{3,2},{4,5},{5,4},{6,7},{7,6},{8,9},{9,8},{10,11... | collective-permute-start | bytes 884744 | tf_op jit(solution)/shard_map/ppermute | solution.py:368
  59.0 6.3 %copy-start.16 = (bf16[4,128,256]{2,1,0:T(8,128)(2,1)}, bf16[4,128,256]{2,1,0:T(8,128)(2,1)S(1)}, u32[]{:S(2)}) copy-start(bf16[4,128,256]{2,1,0:T(8,128)(2,1)S(1)} %collective-permute-done.16.refs_3_) | copy-start | bytes 786436
  59.0 6.2 %collective-permute-start.21 = (bf16[4,128,256]{2,1,0:T(8,128)(2,1)S(1)}, bf16[4,128,256]{2,1,0:T(8,128)(2,1)S(1)}, u32[]{:S(2)}, u32[]{:S(2)}) collective-permute-start(bf16[4,128,256]{2,1,0:T(8,128)(2,1)S(1)} %collective-permute-done.16.refs_3_), channel_id=1, source_target_pairs={{0,2},{2,0},{4,6},{6,4},{8,10},{10,8},{12,14},{14,12},{16,18},{18,... | collective-permute-start | bytes 786440 | tf_op jit(solution)/shard_map/ppermute | solution.py:368
  59.1 4.2 %copy-start.10 = (bf16[4,304,256]{2,1,0:T(8,128)(2,1)}, bf16[4,304,256]{2,1,0:T(8,128)(2,1)S(1)}, u32[]{:S(2)}) copy-start(bf16[4,304,256]{2,1,0:T(8,128)(2,1)S(1)} %collective-permute-done.7.refs_5_) | copy-start | bytes 1867780
  59.1 9.7 %collective-permute-start.19 = (bf16[4,256,256]{2,1,0:T(8,128)(2,1)S(1)}, bf16[4,256,256]{2,1,0:T(8,128)(2,1)}, u32[]{:S(2)}, u32[]{:S(2)}) collective-permute-start(bf16[4,256,256]{2,1,0:T(8,128)(2,1)S(1)} %collective-permute-done.14.refs_1_), channel_id=1, source_target_pairs={{0,2},{2,0},{4,6},{6,4},{8,10},{10,8},{12,14},{14,12},{16,18},{18,... | collective-permute-start | bytes 1572872 | tf_op jit(solution)/shard_map/ppermute | solution.py:368
  61.1 7.7 %collective-permute-start.20 = (bf16[4,256,256]{2,1,0:T(8,128)(2,1)S(1)}, bf16[4,256,256]{2,1,0:T(8,128)(2,1)}, u32[]{:S(2)}, u32[]{:S(2)}) collective-permute-start(bf16[4,256,256]{2,1,0:T(8,128)(2,1)S(1)} %collective-permute-done.15.refs_2_), channel_id=1, source_target_pairs={{0,2},{2,0},{4,6},{6,4},{8,10},{10,8},{12,14},{14,12},{16,18},{18,... | collective-permute-start | bytes 1572872 | tf_op jit(solution)/shard_map/ppermute | solution.py:368
  63.2 2.0 copy-start.14
  63.2 12.5 %collective-permute-start.8 = (bf16[4,304,256]{2,1,0:T(8,128)(2,1)S(1)}, bf16[4,304,256]{2,1,0:T(8,128)(2,1)}, u32[]{:S(2)}, u32[]{:S(2)}) collective-permute-start(bf16[4,304,256]{2,1,0:T(8,128)(2,1)S(1)} %collective-permute-done.3.refs_1_), channel_id=1, source_target_pairs={{0,2},{2,0},{4,6},{6,4},{8,10},{10,8},{12,14},{14,12},{16,18},{18,... | collective-permute-start | bytes 1867784 | tf_op jit(solution)/shard_map/ppermute | solution.py:368
  64.5 0.7 copy-start.12
  64.5 11.3 %collective-permute-start.9 = (bf16[4,304,256]{2,1,0:T(8,128)(2,1)S(1)}, bf16[4,304,256]{2,1,0:T(8,128)(2,1)}, u32[]{:S(2)}, u32[]{:S(2)}) collective-permute-start(bf16[4,304,256]{2,1,0:T(8,128)(2,1)S(1)} %collective-permute-done.4.refs_2_), channel_id=1, source_target_pairs={{0,2},{2,0},{4,6},{6,4},{8,10},{10,8},{12,14},{14,12},{16,18},{18,... | collective-permute-start | bytes 1867784 | tf_op jit(solution)/shard_map/ppermute | solution.py:368
  65.2 0.7 copy-start.17
  65.2 2.0 collective-permute-start.22
  67.3 19.7 %collective-permute-start = (bf16[128,512]{1,0:T(8,128)(2,1)S(1)}, bf16[128,512]{1,0:T(8,128)(2,1)S(1)}, u32[]{:S(2)}, u32[]{:S(2)}) collective-permute-start(bf16[128,512]{1,0:T(8,128)(2,1)S(1)} %select_bitcast_fusion), channel_id=1, source_target_pairs={{0,1},{1,0},{2,3},{3,2},{4,5},{5,4},{6,7},{7,6},{8,9},{9,8},{10,11... | collective-permute-start | bytes 393224 | tf_op jit(solution)/shard_map/ppermute | solution.py:368
  68.8 6.9 %collective-permute-start.10 = (bf16[4,144,256]{2,1,0:T(8,128)(2,1)}, bf16[4,144,256]{2,1,0:T(8,128)(2,1)S(1)}, u32[]{:S(2)}, u32[]{:S(2)}) collective-permute-start(bf16[4,144,256]{2,1,0:T(8,128)(2,1)} %copy-done.14), channel_id=1, source_target_pairs={{0,2},{2,0},{4,6},{6,4},{8,10},{10,8},{12,14},{14,12},{16,18},{18,... | collective-permute-start | bytes 884744 | tf_op jit(solution)/shard_map/ppermute | solution.py:368
  68.8 7.0 %collective-permute-start.11 = (bf16[4,160,256]{2,1,0:T(8,128)(2,1)}, bf16[4,160,256]{2,1,0:T(8,128)(2,1)S(1)}, u32[]{:S(2)}, u32[]{:S(2)}) collective-permute-start(bf16[4,160,256]{2,1,0:T(8,128)(2,1)} %copy-done.12), channel_id=1, source_target_pairs={{0,2},{2,0},{4,6},{6,4},{8,10},{10,8},{12,14},{14,12},{16,18},{18,... | collective-permute-start | bytes 983048 | tf_op jit(solution)/shard_map/ppermute | solution.py:368
  75.7 0.8 copy-start.15
  76.5 0.7 copy-start.13
  86.9 0.7 copy-start.18
  154.7 16.8 %collective-permute-start.34 = (bf16[8,2,256,128]{3,2,1,0:T(8,128)(2,1)}, bf16[8,2,256,128]{3,2,1,0:T(8,128)(2,1)S(1)}, u32[]{:S(2)}, u32[]{:S(2)}) collective-permute-start(bf16[8,2,256,128]{3,2,1,0:T(8,128)(2,1)} %get-tuple-element.37), channel_id=1, source_target_pairs={{0,2},{2,0},{4,6},{6,4},{8,10},{10,8},{12,14},{14,12},{16,18},{18,... | collective-permute-start | bytes 3145736 | tf_op jit(solution)/shard_map/ppermute | solution.py:368
  154.8 18.4 %collective-permute-start.31 = (bf16[8,2,272,128]{3,2,1,0:T(8,128)(2,1)}, bf16[8,2,272,128]{3,2,1,0:T(8,128)(2,1)S(1)}, u32[]{:S(2)}, u32[]{:S(2)}) collective-permute-start(bf16[8,2,272,128]{3,2,1,0:T(8,128)(2,1)} %get-tuple-element.35), channel_id=1, source_target_pairs={{0,2},{2,0},{4,6},{6,4},{8,10},{10,8},{12,14},{14,12},{16,18},{18,... | collective-permute-start | bytes 3342344 | tf_op jit(solution)/shard_map/ppermute | solution.py:368
  155.3 16.2 %copy-start.9 = (bf16[8,2,256,128]{3,2,1,0:T(8,128)(2,1)S(1)}, bf16[8,2,256,128]{3,2,1,0:T(8,128)(2,1)}, u32[]{:S(2)}) copy-start(bf16[8,2,256,128]{3,2,1,0:T(8,128)(2,1)} %get-tuple-element.36) | copy-start | bytes 3145732
  171.4 27.7 %collective-permute-start.24 = (bf16[2,9,8,32,256]{4,3,2,1,0:T(8,128)(2,1)}, bf16[2,9,8,32,256]{4,3,2,1,0:T(8,128)(2,1)}, u32[]{:S(2)}, u32[]{:S(2)}) collective-permute-start(bf16[2,9,8,32,256]{4,3,2,1,0:T(8,128)(2,1)} %get-tuple-element.33), channel_id=1, source_target_pairs={{0,2},{2,0},{4,6},{6,4},{8,10},{10,8},{12,14},{14,12},{16,18},{18,... | collective-permute-start | bytes 7077896 | tf_op jit(solution)/shard_map/ppermute | solution.py:368
  171.5 1.7 copy-start.8
  171.8 1.7 copy-start
  172.7 14.5 %collective-permute-start.35 = (bf16[4,2,256,128]{3,2,0,1:T(8,128)(2,1)}, bf16[4,2,256,128]{3,2,0,1:T(8,128)(2,1)}, u32[]{:S(2)}, u32[]{:S(2)}) collective-permute-start(bf16[4,2,256,128]{3,2,0,1:T(8,128)(2,1)} %fusion.4), channel_id=1, source_target_pairs={{0,1},{1,0},{2,3},{3,2},{4,5},{5,4},{6,7},{7,6},{8,9},{9,8},{10,11... | collective-permute-start | bytes 1572872 | tf_op jit(solution)/shard_map/ppermute | solution.py:368
  173.6 15.8 %collective-permute-start.32 = (bf16[4,2,272,128]{3,2,0,1:T(8,128)(2,1)S(1)}, bf16[4,2,272,128]{3,2,0,1:T(8,128)(2,1)S(1)}, u32[]{:S(2)}, u32[]{:S(2)}) collective-permute-start(bf16[4,2,272,128]{3,2,0,1:T(8,128)(2,1)S(1)} %fusion.3), channel_id=1, source_target_pairs={{0,4},{2,6},{4,0},{6,2},{8,12},{10,14},{12,8},{14,10},{16,20},{18,... | collective-permute-start | bytes 1671176 | tf_op jit(solution)/shard_map/ppermute | solution.py:368
  188.8 7.8 %collective-permute-start.36 = (bf16[4,256,128]{2,1,0:T(8,128)(2,1)S(1)}, bf16[4,256,128]{2,1,0:T(8,128)(2,1)S(1)}, u32[]{:S(2)}, u32[]{:S(2)}) collective-permute-start(bf16[4,256,128]{2,1,0:T(8,128)(2,1)S(1)} %fusion.10), channel_id=1, source_target_pairs={{0,4},{2,6},{4,0},{6,2},{8,12},{10,14},{12,8},{14,10},{16,20},{18,... | collective-permute-start | bytes 786440 | tf_op jit(solution)/shard_map/ppermute | solution.py:368
  189.5 9.3 %collective-permute-start.33 = (bf16[4,272,128]{2,1,0:T(8,128)(2,1)S(1)}, bf16[4,272,128]{2,1,0:T(8,128)(2,1)S(1)}, u32[]{:S(2)}, u32[]{:S(2)}) collective-permute-start(bf16[4,272,128]{2,1,0:T(8,128)(2,1)S(1)} %fusion.8), channel_id=1, source_target_pairs={{0,1},{1,0},{2,3},{3,2},{4,5},{5,4},{6,7},{7,6},{8,9},{9,8},{10,11... | collective-permute-start | bytes 835592 | tf_op jit(solution)/shard_map/ppermute | solution.py:368
  191.6 12.5 %collective-permute-start.23 = (bf16[128,512]{1,0:T(8,128)(2,1)S(1)}, bf16[128,512]{1,0:T(8,128)(2,1)S(1)}, u32[]{:S(2)}, u32[]{:S(2)}) collective-permute-start(bf16[128,512]{1,0:T(8,128)(2,1)S(1)} %slice_select_fusion), channel_id=1, source_target_pairs={{0,1},{1,0},{2,3},{3,2},{4,5},{5,4},{6,7},{7,6},{8,9},{9,8},{10,11... | collective-permute-start | bytes 393224 | tf_op jit(solution)/shard_map/ppermute | solution.py:368
  196.7 2.4 copy-start.2
  199.0 22.1 %collective-permute-start.37 = (bf16[2,528,128]{2,1,0:T(8,128)(2,1)S(1)}, bf16[2,528,128]{2,1,0:T(8,128)(2,1)S(1)}, u32[]{:S(2)}, u32[]{:S(2)}) collective-permute-start(bf16[2,528,128]{2,1,0:T(8,128)(2,1)S(1)} %fusion.9), channel_id=1, source_target_pairs={{0,8},{2,10},{4,12},{6,14},{8,0},{10,2},{12,4},{14,6},{16,24},{18,... | collective-permute-start | bytes 811016 | tf_op jit(solution)/shard_map/ppermute | solution.py:368
  202.5 23.9 %collective-permute-start.25 = (bf16[2,9,4,16,256]{4,3,2,1,0:T(8,128)(2,1)S(1)}, bf16[2,9,4,16,256]{4,3,2,1,0:T(8,128)(2,1)S(1)}, u32[]{:S(2)}, u32[]{:S(2)}) collective-permute-start(bf16[2,9,4,16,256]{4,3,2,1,0:T(8,128)(2,1)S(1)} %fusion.2), channel_id=1, source_target_pairs={{0,4},{2,6},{4,0},{6,2},{8,12},{10,14},{12,8},{14,10},{16,20},{18,... | collective-permute-start | bytes 1769480 | tf_op jit(solution)/shard_map/ppermute | solution.py:368
  204.1 0.7 copy-start.19
  220.6 15.1 %collective-permute-start.27 = (bf16[9,4,2,16,256]{4,3,1,0,2:T(8,128)(2,1)S(1)}, bf16[9,4,2,16,256]{4,3,1,0,2:T(8,128)(2,1)S(1)}, u32[]{:S(2)}, u32[]{:S(2)}) collective-permute-start(bf16[9,4,2,16,256]{4,3,1,0,2:T(8,128)(2,1)S(1)} %fusion.1), channel_id=1, source_target_pairs={{0,1},{1,0},{2,3},{3,2},{4,5},{5,4},{6,7},{7,6},{8,9},{9,8},{10,11... | collective-permute-start | bytes 1769480 | tf_op jit(solution)/shard_map/ppermute | solution.py:368
  221.2 16.2 %collective-permute-start.38 = (bf16[1,528,128]{2,1,0:T(8,128)(2,1)S(1)}, bf16[1,528,128]{2,1,0:T(8,128)(2,1)S(1)}, u32[]{:S(2)}, u32[]{:S(2)}) collective-permute-start(bf16[1,528,128]{2,1,0:T(8,128)(2,1)S(1)} %dynamic-slice_convert_fusion.7), channel_id=1, source_target_pairs={{0,16},{2,18},{4,20},{6,22},{8,24},{10,26},{12,28},{14,30},{16,0},... | collective-permute-start | bytes 405512 | tf_op jit(solution)/shard_map/ppermute | solution.py:368
  226.7 12.1 %collective-permute-start.26 = (bf16[9,4,16,256]{3,2,1,0:T(8,128)(2,1)S(1)}, bf16[9,4,16,256]{3,2,1,0:T(8,128)(2,1)S(1)}, u32[]{:S(2)}, u32[]{:S(2)}) collective-permute-start(bf16[9,4,16,256]{3,2,1,0:T(8,128)(2,1)S(1)} %fusion.5), channel_id=1, source_target_pairs={{0,1},{1,0},{2,3},{3,2},{4,5},{5,4},{6,7},{7,6},{8,9},{9,8},{10,11... | collective-permute-start | bytes 884744 | tf_op jit(solution)/shard_map/ppermute | solution.py:368
  235.9 6.8 %collective-permute-start.28 = (bf16[9,4,16,256]{3,2,1,0:T(8,128)(2,1)S(1)}, bf16[9,4,16,256]{3,2,1,0:T(8,128)(2,1)S(1)}, u32[]{:S(2)}, u32[]{:S(2)}) collective-permute-start(bf16[9,4,16,256]{3,2,1,0:T(8,128)(2,1)S(1)} %fusion.6), channel_id=1, source_target_pairs={{0,4},{2,6},{4,0},{6,2},{8,12},{10,14},{12,8},{14,10},{16,20},{18,... | collective-permute-start | bytes 884744 | tf_op jit(solution)/shard_map/ppermute | solution.py:368
  243.0 8.3 %collective-permute-start.29 = (bf16[9,2,32,256]{3,2,1,0:T(8,128)(2,1)S(1)}, bf16[9,2,32,256]{3,2,1,0:T(8,128)(2,1)S(1)}, u32[]{:S(2)}, u32[]{:S(2)}) collective-permute-start(bf16[9,2,32,256]{3,2,1,0:T(8,128)(2,1)S(1)} %fusion.7), channel_id=1, source_target_pairs={{0,8},{2,10},{4,12},{6,14},{8,0},{10,2},{12,4},{14,6},{16,24},{18,... | collective-permute-start | bytes 884744 | tf_op jit(solution)/shard_map/ppermute | solution.py:368
  251.4 8.2 %collective-permute-start.30 = (bf16[9,1,32,256]{3,2,1,0:T(8,128)(2,1)S(1)}, bf16[9,1,32,256]{3,2,1,0:T(8,128)(2,1)S(1)}, u32[]{:S(2)}, u32[]{:S(2)}) collective-permute-start(bf16[9,1,32,256]{3,2,1,0:T(8,128)(2,1)S(1)} %dynamic-slice_convert_fusion.6), channel_id=1, source_target_pairs={{0,16},{2,18},{4,20},{6,22},{8,24},{10,26},{12,28},{14,30},{16,0},... | collective-permute-start | bytes 442376 | tf_op jit(solution)/shard_map/ppermute | solution.py:368

commit v2 on v1

v2 whole, which is shorter than its diff:
```python
import functools
import jax
import jax.numpy as jnp
from jax import lax
from jax.experimental import pallas as pl
from jax.experimental.pallas import tpu as pltpu
from jax.sharding import Mesh, PartitionSpec as P

KERNEL_TAPS = 9
DILATION_STEP = 32
EPSILON = 1e-05
SUB = 256
BF = jnp.bfloat16
F32 = jnp.float32
VMEM_CONV = 28 * 2**20
VMEM_FFN = 46 * 2**20
VMEM_FIRST = 30 * 2**20
VMEM_PACK = 60 * 2**20
VMEM_SUM = 24 * 2**20
COST = 1
BATCH = ("z", "x", "core")
X, Y, Z0, Z1, CORE = ("x", 1), ("seq", 1), ("z", 1), ("z", 2), ("core", 1)
NN = (((1,), (0,)), ((), ()))
NT = (((1,), (1,)), ((), ()))
TN = (((0,), (0,)), ((), ()))


def dot(a, b, dims):
    return lax.dot_general(a, b, dims, preferred_element_type=F32)


def conv_cost(count, width):
    return pl.CostEstimate(flops=2 * count * KERNEL_TAPS * width * width // COST, bytes_accessed=2**20, transcendentals=0)


def gelu_pair(v):
    size = jnp.abs(v)
    t = pl.reciprocal(1.0 + 0.23164189 * size, approx=True)
    poly = t * (0.127414796 + t * (-0.142248368 + t * (0.710706871 + t * (-0.726576013 + t * 0.530702714))))
    bell = jnp.exp2(-0.72134752 * (size * size))
    value = jnp.maximum(v, 0.0) - size * (poly * bell)
    low_side = bell * (poly - 0.39894228 * size)
    return value, jnp.where(v >= 0.0, 1.0 - low_side, low_side)


def row_mean(v):
    return jnp.sum(v, -1, keepdims=True) * (1.0 / v.shape[-1])


def fold(v):
    total = v[0:8]
    for r in range(8, v.shape[0], 8):
        total = total + v[r : r + 8]
    return total


def fill_columns(col, load, flags, block, subs, width):
    for r in range(subs):
        j = block * subs + r
        base = j * SUB
        own = flags[2, j].astype(F32).astype(BF)
        before = flags[0, j].astype(F32).astype(BF)
        after = flags[1, j].astype(F32).astype(BF)
        for k in range(KERNEL_TAPS):
            o = (k - KERNEL_TAPS // 2) * DILATION_STEP
            columns = slice(k * width, (k + 1) * width)
            first = r * SUB
            if o < 0:
                col[first : first - o, columns] = load(base + o, -o) * before
                col[first - o : first + SUB, columns] = load(base, SUB + o) * own
            elif o == 0:
                col[first : first + SUB, columns] = load(base, SUB) * own
            else:
                col[first : first + SUB - o, columns] = load(base + o, SUB - o) * own
                col[first + SUB - o : first + SUB, columns] = load(base + SUB, o) * after


def place(plan, batch_index, seq_index, sources, whole, sems):
    copies = []
    taps = whole.shape[0]
    for source, (offsets, first) in zip(sources, plan):
        if offsets is None:
            copies.append(pltpu.make_async_copy(source, whole, sems.at[len(copies)]))
            continue
        _, span, rows, wide = source.shape
        span = min(span, taps - max(first, 0))
        for n, (db, ds) in enumerate(offsets):
            b, s = (db, ds) if first < 0 else (batch_index ^ db, seq_index ^ ds)
            at_rows = pl.ds(pl.multiple_of(b * rows, rows), rows)
            at_columns = pl.ds(pl.multiple_of(s * wide, wide), wide)
            target = whole.at[pl.ds(max(first, 0), span), at_rows, at_columns]
            copies.append(pltpu.make_async_copy(source.at[n, pl.ds(0, span)], target, sems.at[len(copies)]))
    return copies


def count_copies(plan):
    return sum(1 if offsets is None else len(offsets) for offsets, _ in plan)


def spread_table(small, rows, out):
    devices, wide = rows.shape
    for v, (start, each) in enumerate(small):
        length = devices * each
        place_of = lax.broadcasted_iota(jnp.int32, (wide, length), 1) % each + start
        pick = (place_of == lax.broadcasted_iota(jnp.int32, (wide, length), 0)).astype(BF)
        values = dot(rows, pick, NN)
        owner = lax.broadcasted_iota(jnp.int32, (devices, length), 1) // each
        own = owner == lax.broadcasted_iota(jnp.int32, (devices, length), 0)
        out[v : v + 1, :length] = jnp.sum(jnp.where(own, values, 0.0), 0, keepdims=True)


def conv_kernel(subs, plan, small, taps, flags, prev, x, nxt, *rest):
    block = pl.program_id(0)
    width = x.shape[1]
    border = prev.shape[0]
    sources = rest[: len(plan)]
    if small:
        xhat_out, scale_out, w_out, table, ext, col, w, sems, out_sem, tails, tail_sems = rest[len(plan) :]
    else:
        table, xhat_out, scale_out, w_out, ext, col, w, sems, out_sem = rest[len(plan) :]

    def copies_in():
        copies = place(plan, flags[4, 0], flags[4, 1], sources, w, sems)
        if small:
            for source, (offsets, first) in zip(sources, plan):
                if first + source.shape[1] <= taps:
                    continue
                for db, ds in offsets:
                    n = offsets.index((db, ds))
                    device = 2 * (flags[4, 0] ^ db) + (flags[4, 1] ^ ds)
                    k = len(copies) - count_copies(plan)
                    copies.append(
                        pltpu.make_async_copy(
                            source.at[n, taps - first, pl.ds(0, 16)], tails.at[device], tail_sems.at[k]
                        )
                    )
        return copies

    @pl.when(block == 0)
    def _():
        for copy in copies_in():
            copy.start()
        ext[0:border] = prev[...]
        ext[border : border + x.shape[0]] = x[...]
        ext[border + x.shape[0] :] = nxt[...]

        for copy in copies_in():
            copy.wait()
        pltpu.make_async_copy(w, w_out, out_sem).start()
        if small:
            devices, high, wide = tails.shape
            first_row = lax.broadcasted_iota(jnp.int32, (devices, devices * high), 0) * high
            pick = (first_row == lax.broadcasted_iota(jnp.int32, (devices, devices * high), 1)).astype(BF)
            rows = dot(pick, tails[...].reshape(devices * high, wide), NN).astype(BF)
            spread_table(small, rows, table)

    @pl.when(block == pl.num_programs(0) - 1)
    def _():
        pltpu.make_async_copy(w, w_out, out_sem).wait()

    def load(start, count):
        return ext[pl.ds(pl.multiple_of(start + border, DILATION_STEP), count), :]

    fill_columns(col, load, flags, block, subs, width)
    total = None
    for k in range(KERNEL_TAPS):
        part = dot(col[:, k * width : (k + 1) * width], w[k], NT)
        total = part if total is None else total + part
    value, slope = gelu_pair(total + table[0:1, :width])
    centered = value - row_mean(value)
    rstd = lax.rsqrt(row_mean(centered * centered) + EPSILON)
    xhat_out[...] = centered * rstd
    scale_out[...] = slope * rstd


def whole_block(shape):
    return pl.BlockSpec(shape, lambda *_: (0,) * len(shape), pipeline_mode=pl.Buffered(1))


def conv_forward(flags, prev, x, nxt, sources, plan, small, table, subs, hidden):
    count, width = x.shape
    rows = subs * SUB
    anywhere = [pl.BlockSpec(memory_space=pl.ANY)] * len(sources)
    out_specs = [pl.BlockSpec((rows, width), lambda j, f: (j, 0))] * 2 + [pl.BlockSpec(memory_space=pltpu.HBM)]
    out_shape = [pltpu.HBM((count, width), F32)] * 2 + [pltpu.HBM((KERNEL_TAPS, width, width), BF)]
    scratch = [
        pltpu.VMEM((count + 2 * prev.shape[0], width), BF),
        pltpu.VMEM((rows, KERNEL_TAPS * width), BF),
        pltpu.VMEM((KERNEL_TAPS, width, width), BF),
        pltpu.SemaphoreType.DMA((count_copies(plan),)),
        pltpu.SemaphoreType.DMA,
    ]
    extra_specs, extra = [], []
    if small:
        out_specs = out_specs + [whole_block((8, hidden))]
        out_shape = out_shape + [jax.ShapeDtypeStruct((8, hidden), F32)]
        devices = width // small[0][1]
        scratch += [pltpu.VMEM((devices, 16, width // 2), BF), pltpu.SemaphoreType.DMA((devices,))]
    else:
        extra_specs, extra = [whole_block(table.shape)], [table]
    outs = pl.pallas_call(
        functools.partial(conv_kernel, subs, plan, small, KERNEL_TAPS),
        grid_spec=pltpu.PrefetchScalarGridSpec(
            num_scalar_prefetch=1,
            grid=(count // rows,),
            in_specs=[whole_block(prev.shape), whole_block(x.shape), whole_block(nxt.shape)] + anywhere + extra_specs,
            out_specs=out_specs,
            scratch_shapes=scratch,
        ),
        out_shape=out_shape,
        compiler_params=pltpu.CompilerParams(vmem_limit_bytes=VMEM_FIRST),
        cost_estimate=conv_cost(count, width),
        name="conv_forward",
    )(flags, prev, x, nxt, *sources, *extra)
    return outs if small else (*outs, table)


def ffn_kernel(chunk, fast, plan, flags, x, xhat, scale, og, table, *rest):
    sources, rest = rest[: len(plan)], rest[len(plan) :]
    out, gh_out, gc_out, *rest = rest
    act, slope, dup, ddown, sums, ub_sums, pair, sems = rest[-8:]
    step = pl.program_id(0)
    last = pl.num_programs(0) - 1
    _, hidden, width = pair.shape
    chunks = hidden // chunk
    gain1, shift1, db, gain2, shift2 = (table[i : i + 1, :width] for i in range(1, 6))
    ub = table[6:7, :]

    @pl.when(step == 0)
    def _():
        copies = place(plan, flags[4, 0], flags[4, 1], sources, pair, sems)
        for copy in copies:
            copy.start()
        dup[...] = jnp.zeros_like(dup)
        ddown[...] = jnp.zeros_like(ddown)
        sums[...] = jnp.zeros_like(sums)
        ub_sums[...] = jnp.zeros_like(ub_sums)
        for copy in copies:
            copy.wait()

    one = x[...].astype(F32) + (xhat[...] * gain1 + shift1)
    low = one.astype(BF)
    total = None
    for f in range(chunks):
        cols = slice(f * chunk, (f + 1) * chunk)
        value, s = gelu_pair(dot(low, pair[0, cols, :], NT) + ub[:, cols])
        a = value.astype(BF)
        act[:, cols] = a
        slope[:, cols] = s
        part = dot(a, pair[1, cols, :], NN)
        total = part if total is None else total + part
    d = total + db
    centered = d - row_mean(d)
    rstd = lax.rsqrt(row_mean(centered * centered) + EPSILON)
    hat = centered * rstd
    out[...] = (one + (hat * gain2 + shift2)).astype(BF)
    g = og[...].astype(F32)
    e = g * gain2
    gd = (rstd * (e - row_mean(e) - hat * row_mean(e * hat))).astype(BF)
    sums[0] += fold(g * hat)
    sums[1] += fold(g)
    sums[2] += fold(gd.astype(F32))
    gh = g
    for f in range(chunks):
        cols = slice(f * chunk, (f + 1) * chunk)
        ddown[:, cols] += dot(gd, act[:, cols], TN)
        gu = dot(gd, pair[1, cols, :], NT) * slope[:, cols]
        gul = gu.astype(BF)
        ub_sums[:, cols] += fold(gul.astype(F32))
        dup[:, cols] += dot(low, gul, TN)
        gh = gh + dot(gul, pair[0, cols, :], NN)
    gh_out[...] = gh
    sums[3] += fold(gh * xhat[...])
    sums[4] += fold(gh)
    e = gh * gain1
    gc = (scale[...] * (e - row_mean(e) - xhat[...] * row_mean(e * xhat[...]))).astype(BF)
    gc_out[...] = gc
    sums[5] += fold(gc.astype(F32))

    @pl.when(step == last)
    def _():
        if not fast:
            up_out, down_out, sums_out, ub_out = rest[:4]
            up_out[...] = dup[...]
            down_out[...] = ddown[...]
            sums_out[...] = jnp.sum(sums[...], 1)
            ub_out[...] = jnp.sum(ub_sums[...], 0, keepdims=True)
            return
        send, keep = rest[:2]
        mine = flags[3, 0] == 0
        block = send.shape[-1]
        half = width // 2
        devices = 2 * (hidden // block)

        def own(length):
            each = length // devices
            place = lax.broadcasted_iota(jnp.int32, (devices, length), 1) // each
            return place == lax.broadcasted_iota(jnp.int32, (devices, length), 0)

        def pick(length, start):
            each = length // devices
            place = lax.broadcasted_iota(jnp.int32, (length, 128), 0) % each + start
            return (place == lax.broadcasted_iota(jnp.int32, (length, 128), 1)).astype(BF)

        first = None
        for v in range(6):
            line = jnp.sum(sums[v], 0, keepdims=True)
            part = dot(jnp.where(own(width), line, 0.0).astype(BF), pick(width, v * (width // devices)), NN)
            first = part if first is None else first + part
        line = jnp.sum(ub_sums[...], 0, keepdims=True)
        second = dot(jnp.where(own(hidden), line, 0.0).astype(BF), pick(hidden, 0), NN)
        index = lax.broadcasted_iota(jnp.int32, (16, 128), 0)

        def tail(b, s):
            at = 2 * b + s
            return jnp.where(index == 0, first[at : at + 1], jnp.where(index == 1, second[at : at + 1], 0.0)).astype(BF)

        for b in range(0, hidden // block, 2):
            for s in range(2):
                take = slice(s * half, (s + 1) * half)
                x_bit, z = b // 2 % 2, (b // 4 % 2, b // 8)
                up_at, down_at = (2 * x_bit + s, *z), (2 * s + x_bit, *z)
                for acc, at, start in ((dup, up_at, 0), (ddown, down_at, half + 16)):
                    lo = acc[take, b * block : (b + 1) * block].astype(BF)
                    hi = acc[take, (b + 1) * block : (b + 2) * block].astype(BF)
                    send[(*at, slice(start, start + half))] = jnp.where(mine, hi, lo)
                    keep[(*at, slice(start, start + half))] = jnp.where(mine, lo, hi)
                lo, hi = tail(b, s), tail(b + 1, s)
                send[(*up_at, slice(half, half + 16))] = jnp.where(mine, hi, lo)
                keep[(*up_at, slice(half, half + 16))] = jnp.where(mine, lo, hi)


def ffn(flags, x, xhat, scale, og, table, sources, plan, rows, chunk, batch, fast):
    count, width = x.shape
    hidden = table.shape[1]
    tile = pl.BlockSpec((rows, width), lambda j, f: (j, 0))
    sds = jax.ShapeDtypeStruct
    if fast:
        shapes = [sds((4, 2, 2, width + 16, hidden // batch), BF)] * 2
    else:
        shapes = [sds(s, F32) for s in ((width, hidden), (width, hidden), (6, width), (1, hidden))]
    anywhere = [pl.BlockSpec(memory_space=pl.ANY)] * len(sources)
    return pl.pallas_call(
        functools.partial(ffn_kernel, chunk, fast, plan),
        grid_spec=pltpu.PrefetchScalarGridSpec(
            num_scalar_prefetch=1,
            grid=(count // rows,),
            in_specs=[tile, tile, tile, tile, whole_block(table.shape)] + anywhere,
            out_specs=[tile, tile, tile] + [whole_block(s.shape) for s in shapes],
            scratch_shapes=[
                pltpu.VMEM((rows, hidden), BF),
                pltpu.VMEM((rows, hidden), F32),
                pltpu.VMEM((width, hidden), F32),
                pltpu.VMEM((width, hidden), F32),
                pltpu.VMEM((6, 8, width), F32),
                pltpu.VMEM((8, hidden), F32),
                pltpu.VMEM((2, hidden, width), BF),
                pltpu.SemaphoreType.DMA((count_copies(plan),)),
            ],
        ),
        out_shape=[sds((count, width), BF), sds((count, width), F32), sds((count, width), BF)] + shapes,
        compiler_params=pltpu.CompilerParams(vmem_limit_bytes=VMEM_FFN if fast else VMEM_PACK),
        cost_estimate=pl.CostEstimate(flops=12 * count * width * hidden // COST, bytes_accessed=2**20, transcendentals=0),
        name="feed_forward",
    )(flags, x, xhat, scale, og, table, *sources)


def conv_weight_kernel(fast, flags, prev, x, nxt, g, *rest):
    ext, col = rest[-2:]
    tap = pl.program_id(0)
    count, width = g.shape
    border = prev.shape[0]
    subs = count // SUB

    @pl.when(tap == 0)
    def _():
        ext[0:border] = prev[...]
        ext[border : border + count] = x[...]
        ext[border + count :] = nxt[...]

    o = (tap - KERNEL_TAPS // 2) * DILATION_STEP
    offset = lax.broadcasted_iota(jnp.int32, (SUB, 1), 0) + o
    for r in range(subs):
        own = flags[2, r].astype(F32)
        before = flags[0, r].astype(F32)
        after = flags[1, r].astype(F32)
        mask = jnp.where(offset < 0, before, jnp.where(offset >= SUB, after, own)).astype(BF)
        rows = ext[pl.ds(pl.multiple_of(r * SUB + o + border, DILATION_STEP), SUB), :]
        col[r * SUB : (r + 1) * SUB, :] = rows * mask

    grad = dot(g[...], col[...], TN)
    if not fast:
        rest[0][0] = grad
        return
    mine = flags[3, 0] == 0
    half = width // 2

    send, keep = rest[:2]
    block = send.shape[4]
    early = (tap < (KERNEL_TAPS + 1) // 2).astype(jnp.int32)
    for s in range(2):
        columns = slice(s * half, (s + 1) * half)
        for b in range(0, width // block, 2):
            bit = b // 2 % 2
            at = (early * (2 * bit + s) + (1 - early) * (2 * s + bit), b // 4 % 2, b // 8, 0)
            lo = grad[b * block : (b + 1) * block, columns].astype(BF)
            hi = grad[(b + 1) * block : (b + 2) * block, columns].astype(BF)
            send[at] = jnp.where(mine, hi, lo)
            keep[at] = jnp.where(mine, lo, hi)


def conv_weight_backward(flags, prev, x, nxt, g, batch, fast):
    count, width = x.shape
    if fast:
        block = (4, 2, 2, 1, width // batch, width // 2)
        specs = [pl.BlockSpec(block, lambda k, f: (0, 0, 0, k, 0, 0))] * 2
        shapes = [jax.ShapeDtypeStruct(block[:3] + (KERNEL_TAPS,) + block[4:], BF)] * 2
    else:
        specs = [pl.BlockSpec((1, width, width), lambda k, f: (k, 0, 0))]
        shapes = [jax.ShapeDtypeStruct((KERNEL_TAPS, width, width), F32)]
    return pl.pallas_call(
        functools.partial(conv_weight_kernel, fast),
        grid_spec=pltpu.PrefetchScalarGridSpec(
            num_scalar_prefetch=1,
            grid=(KERNEL_TAPS,),
            in_specs=[whole_block(a.shape) for a in (prev, x, nxt, g)],
            out_specs=specs,
            scratch_shapes=[
                pltpu.VMEM((count + 2 * prev.shape[0], width), BF),
                pltpu.VMEM((count, width), BF),
            ],
        ),
        out_shape=shapes,
        compiler_params=pltpu.CompilerParams(vmem_limit_bytes=VMEM_CONV),
        cost_estimate=conv_cost(count, width),
        name="conv_weight_backward",
    )(flags, prev, x, nxt, g)


def conv_input_kernel(subs, flags, prev, g, nxt, gh, w, out, ext, col):
    step = pl.program_id(0)
    count, width = g.shape
    border = prev.shape[0]

    @pl.when(step == 0)
    def _():
        ext[0:border] = prev[...]
        ext[border : border + count] = g[...]
        ext[border + count :] = nxt[...]

    def load(start, size):
        return ext[pl.ds(pl.multiple_of(start + border, DILATION_STEP), size), :]

    fill_columns(col, load, flags, step, subs, width)
    total = gh[...]
    for k in range(KERNEL_TAPS):
        total = total + dot(col[:, k * width : (k + 1) * width], w[KERNEL_TAPS - 1 - k], NN)
    out[...] = total


def conv_input_backward(flags, prev, g, nxt, gh, weights, subs):
    count, width = g.shape
    rows = subs * SUB
    tile = pl.BlockSpec((rows, width), lambda j, f: (j, 0))
    return pl.pallas_call(
        functools.partial(conv_input_kernel, subs),
        grid_spec=pltpu.PrefetchScalarGridSpec(
            num_scalar_prefetch=1,
            grid=(count // rows,),
            in_specs=[whole_block(a.shape) for a in (prev, g, nxt)] + [tile, whole_block(weights.shape)],
            out_specs=tile,
            scratch_shapes=[
                pltpu.VMEM((count + 2 * prev.shape[0], width), BF),
                pltpu.VMEM((rows, KERNEL_TAPS * width), BF),
            ],
        ),
        out_shape=jax.ShapeDtypeStruct((count, width), F32),
        compiler_params=pltpu.CompilerParams(vmem_limit_bytes=VMEM_CONV),
        cost_estimate=conv_cost(count, width),
        name="conv_input_backward",
    )(flags, prev, g, nxt, gh, weights)


def pack_kernel(small, slots, count, lengths, first, final, conv, up, down, *rest):
    vectors, (flags, halo, conv_out, pair_out) = rest[: len(small)], rest[len(small) :]
    batch_index = lax.axis_index("z") * 4 + lax.axis_index("x") * 2 + lax.axis_index("core")
    seq_index = lax.axis_index("seq")
    taps, rows, wide = conv.shape
    subs = flags.shape[1]
    conv_out[0, 0:taps] = conv[...]
    line = None
    for v, (start, each) in zip(vectors, small):
        pick = (
            lax.broadcasted_iota(jnp.int32, (each, wide), 0) + start == lax.broadcasted_iota(jnp.int32, (each, wide), 1)
        ).astype(BF)
        part = dot(jnp.broadcast_to(v[...], (rows, each)), pick, NN)
        line = part if line is None else line + part
    conv_out[0, taps] = line.astype(BF)
    pair_out[0, 0] = up[...].T
    pair_out[0, 1] = down[...]
    halo[...] = jnp.where(seq_index == 0, final[...], first[...])
    ends = []
    total = 0
    for i in range(slots):
        total = total + lengths[0, i]
        ends.append(total)
    ids = []
    for j in range(-1, subs + 1):
        start = seq_index * count + j * SUB
        number = 0
        for end in ends:
            number = number + (start >= end).astype(jnp.int32)
        ids.append(jnp.where(start >= 0, number, -1))
    for j in range(subs):
        inside = (ids[j + 1] < slots).astype(jnp.int32)
        flags[0, j] = (ids[j] == ids[j + 1]).astype(jnp.int32) * inside
        flags[1, j] = (ids[j + 2] == ids[j + 1]).astype(jnp.int32) * inside
        flags[2, j] = inside
        flags[3, j] = batch_index % 2
        flags[4, j] = batch_index if j == 0 else seq_index
        bits = (lax.axis_index("x"), seq_index, lax.axis_index("z") % 2, lax.axis_index("z") // 2)
        flags[5, j] = bits[min(j, 3)]


def pack(lengths, x, conv, up, down, vectors, small):
    taps, rows, wide = conv.shape
    count, width = x.shape
    border = KERNEL_TAPS // 2 * DILATION_STEP
    smem = pl.BlockSpec(memory_space=pltpu.SMEM)
    arrays = [conv, up, down] + [v[None] for v in vectors]
    end_rows = pl.BlockSpec((border, width), lambda i: (0, 0))
    final_rows = pl.BlockSpec((border, width), lambda i: (count // border - 1, 0))
    sds = jax.ShapeDtypeStruct
    outs = [
        sds((6, count // SUB), jnp.int32),
        sds((border, width), BF),
        sds((1, taps + 1, rows, wide), BF),
        sds((1, 2) + down.shape, BF),
    ]
    return pl.pallas_call(
        functools.partial(pack_kernel, small, lengths.shape[1], count),
        grid=(1,),
        in_specs=[smem, end_rows, final_rows] + [whole_block(a.shape) for a in arrays],
        out_specs=[smem] + [whole_block(o.shape) for o in outs[1:]],
        out_shape=outs,
        compiler_params=pltpu.CompilerParams(vmem_limit_bytes=VMEM_PACK),
        name="pack",
    )(lengths, x, x, *arrays)


def swap(value, link):
    axis, bit = link
    return lax.ppermute(value, axis, [(i, i ^ bit) for i in range(lax.axis_size(axis))])


def half_of(link):
    return (lax.axis_index(link[0]) // link[1]) % 2


def give_half(value, link, dim):
    return lax.dynamic_index_in_dim(value, 1 - half_of(link), dim, keepdims=False).astype(BF)


def keep_half(value, link, dim):
    return lax.dynamic_index_in_dim(value, half_of(link), dim, keepdims=False).astype(F32)


def after(value, *others):
    return lax.optimization_barrier((value, *others))[0]


def shifted(offsets, b, s):
    return tuple((ob ^ b, os ^ s) for ob, os in offsets)


def both_cores(arrays, plan):
    other = [swap(a, CORE) for a in arrays]
    return arrays + other, tuple(plan) + tuple((shifted(o, 1, 0), first) for o, first in plan)


def gather_conv(own):
    cut = own.shape[1] // 2
    top = lambda value: swap(value[:, :cut], Y)
    bottom = lambda value: swap(value[:, cut:], X)
    far, own_x, own_y = lax.optimization_barrier((swap(own, Z1), swap(own, X), swap(own, Y)))
    column = jnp.concatenate([own, far], 0)
    near, far_x, far_y, own_top, own_bottom = lax.optimization_barrier(
        (swap(column, Z0), swap(far, X), swap(far, Y), top(own_x), bottom(own_y))
    )
    near_x, near_y, far_top, far_bottom = lax.optimization_barrier(
        (swap(near, X), swap(near, Y), top(far_x), bottom(far_y))
    )
    near_top, near_bottom = top(near_x), bottom(near_y)
    arrays, plan = [column, near], [(((0, 0), (8, 0)), 0), (((4, 0), (12, 0)), 0)]
    for offsets, members in (
        (((0, 0),), (own_x, own_y, own_top, own_bottom)),
        (((8, 0),), (far_x, far_y, far_top, far_bottom)),
        (((4, 0), (12, 0)), (near_x, near_y, near_top, near_bottom)),
    ):
        arrays += members
        plan += [(shifted(offsets, b, s), first) for b, s, first in ((2, 0, 0), (0, 1, 0), (2, 1, 0), (2, 1, cut))]
    return both_cores(arrays, plan)


def stage_kernel(columns, joined, flags, *refs):
    count = len(columns)
    outs = refs[2 * count :]
    at = 0
    for i, column in enumerate(columns):
        keep, got = refs[2 * i], refs[2 * i + 1]
        if joined is None:
            give_out, keep_out, where = outs[2 * i], outs[2 * i + 1], Ellipsis
        else:
            taps = keep.shape[1 + joined]
            give_out, keep_out = outs
            where = (*(slice(None),) * joined, slice(at, at + taps))
            at += taps
        bit = flags[5, column]
        give_out[where] = (keep[1 - bit].astype(F32) + got[1 - bit].astype(F32)).astype(BF)
        keep_out[where] = keep[bit].astype(F32) + got[bit].astype(F32)


def first_stage_kernel(cut, flags, keep, got, *outs):
    for i, taps in enumerate((slice(0, cut), slice(cut, keep.shape[3]))):
        bit = flags[5, i]
        give_out, keep_out = outs[2 * i], outs[2 * i + 1]
        for n in range(2):
            other, own = 2 * (1 - bit) + n, 2 * bit + n
            give_out[n] = (keep[other, :, :, taps].astype(F32) + got[other, :, :, taps].astype(F32)).astype(BF)
            keep_out[n] = keep[own, :, :, taps].astype(F32) + got[own, :, :, taps].astype(F32)


def first_stage(flags, keep, got, cut):
    tail = keep.shape[4:]
    outs = [jax.ShapeDtypeStruct((2, 2, 2, n) + tail, kind) for n in (cut, keep.shape[3] - cut) for kind in (BF, F32)]
    return pl.pallas_call(
        functools.partial(first_stage_kernel, cut),
        grid_spec=pltpu.PrefetchScalarGridSpec(
            num_scalar_prefetch=1,
            grid=(1,),
            in_specs=[whole_block(keep.shape)] * 2,
            out_specs=[whole_block(o.shape) for o in outs],
        ),
        out_shape=outs,
        compiler_params=pltpu.CompilerParams(vmem_limit_bytes=VMEM_SUM),
        name="stage",
    )(flags, keep, got)


def stage(flags, parts, columns, joined=None):
    shapes = [keep.shape[1:] for keep, _ in parts]
    if joined is not None:
        first = list(shapes[0])
        first[joined] = sum(shape[joined] for shape in shapes)
        shapes = [tuple(first)]
    outs = [jax.ShapeDtypeStruct(shape, kind) for shape in shapes for kind in (BF, F32)]
    arrays = [a for part in parts for a in part]
    return pl.pallas_call(
        functools.partial(stage_kernel, columns, joined),
        grid_spec=pltpu.PrefetchScalarGridSpec(
            num_scalar_prefetch=1,
            grid=(1,),
            in_specs=[whole_block(a.shape) for a in arrays],
            out_specs=[whole_block(o.shape) for o in outs],
        ),
        out_shape=outs,
        compiler_params=pltpu.CompilerParams(vmem_limit_bytes=VMEM_SUM),
        name="stage",
    )(flags, *arrays)


def local(inputs, window_lengths, conv_weight, conv_bias, norm1_gain, norm1_bias, up_weight, up_bias, down_weight,
          down_bias, norm2_gain, norm2_bias, out_grad):
    _, count, width = inputs.shape
    batch, seq = lax.axis_size(BATCH), lax.axis_size("seq")
    hidden = up_weight.shape[1] * batch
    border = KERNEL_TAPS // 2 * DILATION_STEP
    x, og = inputs[0], out_grad[0]
    fast = seq == 2 and batch == 16

    def ends(value):
        first, final = value[:border], value[count - border :]
        if fast:
            other = swap(jnp.where(lax.axis_index("seq") == 0, final, first), Y)
            return other, other
        up = [(i, i + 1) for i in range(seq - 1)]
        return lax.ppermute(final, "seq", up), lax.ppermute(first, "seq", [(j, i) for i, j in up])

    vectors = [conv_bias, norm1_gain, norm1_bias, down_bias, norm2_gain, norm2_bias, up_bias]
    sizes = [v.shape[0] for v in vectors]
    small = tuple((sum(sizes[:i]), n) for i, n in enumerate(sizes))
    conv_own = conv_weight.transpose(0, 2, 1)
    flags, halo, conv_block, pair_block = pack(window_lengths, x, conv_own, up_weight, down_weight, vectors, small)
    if fast:
        prev = nxt = swap(halo, Y)
        conv_pieces, conv_plan = gather_conv(conv_block)
        pair_pieces = [lax.all_gather(pair_block[0], (*BATCH, "seq"), axis=0)]
        pair_plan = ((tuple((d // 2, d % 2) for d in range(2 * batch)), -1),)
        table = None
    else:
        def every(value):
            value = lax.all_gather(value, "seq", axis=2, tiled=True)
            return lax.all_gather(value, BATCH, axis=1, tiled=True)

        prev, nxt = ends(x)
        conv_pieces, conv_plan = [every(conv_own)], ((None, 0),)
        pair_pieces, pair_plan = [every(pair_block[0])], ((None, 0),)
        full = [lax.all_gather(v, (*BATCH, "seq"), axis=0, tiled=True).astype(F32) for v in vectors]
        table = jnp.stack([jnp.pad(v, (0, hidden - v.shape[0])) for v in full + [full[0]]])
        small = ()
    conv_pieces, conv_plan = list(conv_pieces), tuple((None if o is None else tuple(o), f) for o, f in conv_plan)
    xhat, scale, conv_full, table = conv_forward(flags, prev, x, nxt, conv_pieces, conv_plan, small, table, 2, hidden)
    pair_plan = tuple((None if o is None else tuple(o), f) for o, f in pair_plan)
    block_output, grad_hidden, grad_conv, *ffn_grads = ffn(
        flags, x, xhat, scale, og, table, pair_pieces, pair_plan, 2 * SUB, min(1024, hidden), batch, fast
    )
    grad_prev, grad_next = ends(grad_conv)
    grads = (flags, prev, x, nxt, grad_conv, grad_prev, grad_next, grad_hidden, conv_full)
    if fast:
        input_grad, weight_grads = paired(grads, ffn_grads, batch, width, hidden)
    else:
        conv_grads = conv_weight_backward(flags, prev, x, nxt, grad_conv, batch, fast)
        input_grad = conv_input_backward(flags, grad_prev, grad_conv, grad_next, grad_hidden, conv_full, 2)
        weight_grads = whole_sums(conv_grads, ffn_grads, batch, seq, width, hidden)
    conv_grad, cb, g1, s1, up_grad, ub_grad, down_grad, db, g2, s2 = weight_grads
    return (block_output[None], input_grad[None], conv_grad, cb, g1, s1, up_grad, ub_grad, down_grad, db, g2, s2)


def paired(grads, ffn_grads, batch, width, hidden):
    flags, prev, x, nxt, grad_conv, grad_prev, grad_next, grad_hidden, conv_full = grads
    up_rows = width // 2 + 16
    ffn_send, ffn_keep = ffn_grads
    ffn_got = swap(ffn_send, CORE)
    send, keep = conv_weight_backward(flags, prev, x, nxt, grad_conv, batch, True)
    ffn_got, grad_prev, send = lax.optimization_barrier((ffn_got, grad_prev, send))
    got = swap(send, CORE)
    up_give, up_keep, down_give, down_keep = first_stage(flags, ffn_keep, ffn_got, up_rows)
    up_got, down_got = swap(up_give, X), swap(down_give, Y)
    upper_give, upper_keep, lower_give, lower_keep = first_stage(
        flags, keep, after(got, up_give), (KERNEL_TAPS + 1) // 2
    )
    upper_got, lower_got = swap(upper_give, X), swap(lower_give, Y)
    input_grad = conv_input_backward(
        flags, grad_prev, after(grad_conv, upper_give), grad_prev, grad_hidden, conv_full, 2
    )
    up_got, down_got, input_grad = lax.optimization_barrier((up_got, down_got, input_grad))
    parts = [(up_keep, up_got), (down_keep, down_got)]
    up_give, up_keep, down_give, down_keep = stage(flags, parts, (1, 0))
    up_got, down_got = swap(up_give, Y), swap(down_give, X)
    upper_got, lower_got, _ = lax.optimization_barrier((upper_got, lower_got, up_give))
    parts = [(upper_keep, upper_got), (lower_keep, lower_got)]
    upper_give, upper_keep, lower_give, lower_keep = stage(flags, parts, (1, 0))
    upper_got, lower_got = swap(upper_give, Y), swap(lower_give, X)
    up_got, down_got, _ = lax.optimization_barrier((up_got, down_got, upper_give))
    ffn_give, ffn_keep = stage(flags, [(up_keep, up_got), (down_keep, down_got)], (2, 2), 1)
    ffn_got = swap(ffn_give, Z0)
    upper_got, lower_got, _ = lax.optimization_barrier((upper_got, lower_got, ffn_give))
    conv_give, conv_keep = stage(flags, [(upper_keep, upper_got), (lower_keep, lower_got)], (2, 2), 1)
    conv_got = swap(conv_give, Z0)
    ffn_give, ffn_keep = stage(flags, [(ffn_keep, after(ffn_got, conv_give))], (3,))
    ffn_got = swap(ffn_give, Z1)
    conv_give, conv_keep = stage(flags, [(conv_keep, after(conv_got, ffn_give))], (3,))
    conv_got = swap(conv_give, Z1)
    pair_part = ffn_keep + after(ffn_got, conv_give).astype(F32)
    conv_grad = (conv_keep + conv_got.astype(F32)).transpose(0, 2, 1)
    head = width // 2
    up_grad = pair_part[:head]
    down_grad = pair_part[up_rows:].T
    each = width // (batch * 2)
    g2, s2, db, g1, s1, cb = (pair_part[head, i * each : (i + 1) * each] for i in range(6))
    ub_grad = pair_part[head + 1, : hidden // (batch * 2)]
    return input_grad, (conv_grad, cb, g1, s1, up_grad, ub_grad, down_grad, db, g2, s2)


def whole_sums(conv_grads, ffn_grads, batch, seq, width, hidden):
    def total(value, dims):
        value = lax.psum_scatter(value, BATCH, scatter_dimension=dims[1], tiled=True)
        return lax.psum_scatter(value, "seq", scatter_dimension=dims[0], tiled=True)

    conv_grad = total(conv_grads[0], (2, 1)).transpose(0, 2, 1)
    up_grad = total(ffn_grads[0], (0, 1))
    down_grad = total(ffn_grads[1], (0, 1)).T
    vec_grads = total(ffn_grads[2].reshape(6, batch, seq, -1), (2, 1)).reshape(6, -1)
    ub_grad = total(ffn_grads[3].reshape(batch, seq, -1), (1, 0)).reshape(-1)
    g2, s2, db, g1, s1, cb = (vec_grads[i] for i in range(6))
    return conv_grad, cb, g1, s1, up_grad, ub_grad, down_grad, db, g2, s2


def solution(mesh):
    batch, seq = mesh.shape["batch"], mesh.shape["seq"]
    split = Mesh(mesh.devices.reshape(batch // 4, 2, 2, seq), (*BATCH, "seq"))
    both = P((*BATCH, "seq"))
    rows = P(BATCH, "seq", None)
    conv, up, down = P(None, "seq", BATCH), P("seq", BATCH), P(BATCH, "seq")
    in_specs = (rows, P(BATCH, None), conv, both, both, both, up, both, down, both, both, both, rows)
    out_specs = (rows, rows, conv, both, both, both, up, both, down, both, both, both)
    return jax.shard_map(local, mesh=split, in_specs=in_specs, out_specs=out_specs, check_vma=False)
```

time: 261 us -> 222 us (0.85)
  waiting for transfers between devices: 78.5 us -> 55.6 us
  between operations: 1.17 us -> 14.3 us
  other arithmetic: 12.3 us -> 1.76 us
  local copies, waits for them, and re-layouts: 18.7 us -> 8.76 us
  Pallas kernels: 110 us -> 102 us
    ppermute x39 -> x44, waiting for transfers between devices: 78.5 us -> 53.4 us  [swap(): lax.ppermute(value, axis, [(i, i ^ bit) for i in range(lax.axis_size(axis...]
    add x15 -> x1, other arithmetic: 5.68 us -> 0.03 us  [paired(): pair_part = ffn_keep + after(ffn_got, conv_give).astype(F32)]
    concatenate x2 -> x1, local copies, waits for them, and re-layouts: 5.36 us -> 0.01 us  [gather_conv(): column = jnp.concatenate([own, far], 0)]
    slice x8 -> x6, local copies, waits for them, and re-layouts: 4.05 us -> 0.05 us  [the longest x3 0.03 us: gather_conv(): bottom = lambda value: swap(value[:, cut:], X)]
    pallas_call x1, Pallas kernels: 15.7 us -> 12.2 us  [conv_input_backward(): pl.pallas_call(functools.partial(conv_input_kernel, subs), grid_spec=pltp...]
    pallas_call x1, Pallas kernels: 16.1 us -> 13 us  [conv_weight_backward(): pl.pallas_call(functools.partial(conv_weight_kernel, fast), grid_spec=plt...]
    ppermute x39 -> x44, starting transfers between devices: 40 us -> 38.8 us  [swap(): lax.ppermute(value, axis, [(i, i ^ bit) for i in range(lax.axis_size(axis...]
    unnamed x44 -> x22, local copies, waits for them, and re-layouts: 5.9 us -> 6.92 us
  transfers between devices with their start and end apart: 39 -> 45, of which waited for: 20 -> 19; matrix products, arithmetic and copies ran while one was open for 9% -> 1% of each run, Pallas kernels for 16% -> 24%
where the time goes in v2:
time: 222 us
  Pallas kernels  102 us (46%)
  waiting for transfers between devices  55.6 us (25%)
  starting transfers between devices  38.8 us (17%)
  between operations  14.3 us (6%)
  local copies, waits for them, and re-layouts  8.76 us (4%)
    ppermute x44, waiting for transfers between devices, swap(): lax.ppermute(value, axis, [(i, i ^ bit) for i in range(lax.axis_size(axis...  53.4 us
    pallas_call x1, Pallas kernels, ffn(): pl.pallas_call(functools.partial(ffn_kernel, chunk, fast, plan), grid_spe...  47.3 us
    ppermute x44, starting transfers between devices, swap(): lax.ppermute(value, axis, [(i, i ^ bit) for i in range(lax.axis_size(axis...  38.8 us
    pallas_call x1, Pallas kernels, conv_forward(): pl.pallas_call(functools.partial(conv_kernel, subs, plan, small, KERNEL_T...  19.3 us
    pallas_call x1, Pallas kernels, conv_weight_backward(): pl.pallas_call(functools.partial(conv_weight_kernel, fast), grid_spec=plt...  13 us
    pallas_call x1, Pallas kernels, conv_input_backward(): pl.pallas_call(functools.partial(conv_input_kernel, subs), grid_spec=pltp...  12.2 us
    unnamed x22, local copies, waits for them, and re-layouts  6.92 us
  transfers between devices with their start and end apart: 45, of which 19 were waited for; matrix products, arithmetic and copies ran while one was open for 1% of the time, Pallas kernels for 24%

profile of v2, /device:TPU:0, one launch (start us, length us, event | category | flops | bytes accessed | tf_op | source)
XLA Modules:
  0.0 221.6 jit_solution(18366077968178287049)
XLA Ops:
  7.2 2.2 pack.1
  9.5 4.1 %collective-permute-start.1 = (bf16[1,10,32,256]{3,2,1,0:T(8,128)(2,1)}, bf16[1,10,32,256]{3,2,1,0:T(8,128)(2,1)S(1)}, u32[]{:S(2)}, u32[]{:S(2)}) collective-permute-start(bf16[1,10,32,256]{3,2,1,0:T(8,128)(2,1)} %get-tuple-element.82), channel_id=1, source_target_pairs={{0,16},{8,24},{16,0},{24,8},{1,17},{9,25},{17,1},{25,9},{2,18},{10... | collective-permute-start | bytes 491528 | tf_op jit(solution)/shard_map/ppermute | solution.py:553
  13.6 1.5 collective-permute-start.2
  15.1 1.5 collective-permute-start.3
  16.6 1.0 constant_dynamic-update-slice_fusion.1
  17.6 3.9 %collective-permute-done.1 = bf16[1,10,32,256]{3,2,1,0:T(8,128)(2,1)S(1)} collective-permute-done((bf16[1,10,32,256]{3,2,1,0:T(8,128)(2,1)}, bf16[1,10,32,256]{3,2,1,0:T(8,128)(2,1)S(1)}, u32[]{:S(2)}, u32[]{:S(2)}) %collective-permute-start.1) | collective-permute-done | bytes 163872 | tf_op jit(solution)/shard_map/ppermute | solution.py:553
  21.5 0.9 collective-permute-start.4
  22.4 1.5 collective-permute-start.7
  23.9 1.5 collective-permute-start.5
  26.5 1.2 collective-permute-done.7.rest_4_
  27.7 1.6 collective-permute-start
  29.3 2.5 %collective-permute-done.8.rest_5_ = bf16[1,5,32,256]{3,2,1,0:T(8,128)(2,1)S(1)} collective-permute-done((bf16[1,5,32,256]{3,2,1,0:T(8,128)(2,1)S(1)}, bf16[1,5,32,256]{3,2,1,0:T(8,128)(2,1)S(1)}, u32[]{:S(2)}, u32[]{:S(2)}) %collective-permute-start.8) | collective-permute-done | bytes 81952 | tf_op jit(solution)/shard_map/ppermute | solution.py:553
  32.4 1.3 collective-permute-start.10
  33.7 1.6 collective-permute-start.9
  35.9 0.9 collective-permute-done.17.rest_16_
  37.1 0.8 collective-permute-start.12
  37.9 7.8 %collective-permute-done.11.rest_8_ = bf16[1,5,32,256]{3,2,1,0:T(8,128)(2,1)S(1)} collective-permute-done((bf16[1,5,32,256]{3,2,1,0:T(8,128)(2,1)S(1)}, bf16[1,5,32,256]{3,2,1,0:T(8,128)(2,1)S(1)}, u32[]{:S(2)}, u32[]{:S(2)}) %collective-permute-start.11) | collective-permute-done | bytes 81952 | tf_op jit(solution)/shard_map/ppermute | solution.py:553
  45.6 2.2 %collective-permute-done.12.rest_9_ = bf16[1,5,32,256]{3,2,1,0:T(8,128)(2,1)S(1)} collective-permute-done((bf16[1,5,32,256]{3,2,1,0:T(8,128)(2,1)S(1)}, bf16[1,5,32,256]{3,2,1,0:T(8,128)(2,1)S(1)}, u32[]{:S(2)}, u32[]{:S(2)}) %collective-permute-start.12) | collective-permute-done | bytes 81952 | tf_op jit(solution)/shard_map/ppermute | solution.py:553
  48.5 0.9 collective-permute-done.19.rest_18_
  49.6 1.7 collective-permute-start.14
  51.9 3.8 %collective-permute-done.13.rest_12_ = bf16[2,5,32,256]{3,2,1,0:T(8,128)(2,1)S(1)} collective-permute-done((bf16[2,5,32,256]{3,2,1,0:T(8,128)(2,1)S(1)}, bf16[2,5,32,256]{3,2,1,0:T(8,128)(2,1)S(1)}, u32[]{:S(2)}, u32[]{:S(2)}) %collective-permute-start.13) | collective-permute-done | bytes 163872 | tf_op jit(solution)/shard_map/ppermute | solution.py:553
  56.4 1.1 collective-permute-done.24.rest_23_
  57.6 0.7 copy-done.2
  58.3 19.3 %conv_forward.1 = (f32[2048,512]{1,0:T(8,128)}, f32[2048,512]{1,0:T(8,128)}, bf16[9,512,512]{2,1,0:T(8,128)(2,1)}, f32[8,2048]{1,0:T(8,128)S(1)}) custom-call(s32[6,8]{1,0:T(8,128)S(1)} %copy-done.2, bf16[128,512]{1,0:T(8,128)(2,1)S(1)} %collective-permute-done.prev.nxt, bf16[2048,512]{1,0:T(8,128)(2,1)S(1)} %bitcast.32, ...), custom_call_target="tpu_custom_call" | custom-call | flops 9663676416 | bytes 1048576 | tf_op jit(solution)/shard_map/conv_forward/pallas_call | solution.py:201
  77.6 2.2 all-gather.2.cloned.1.call-done.rest_0_
  79.8 1.6 copy-done.7
  81.4 47.3 %feed_forward.1 = (bf16[2048,512]{1,0:T(8,128)(2,1)}, f32[2048,512]{1,0:T(8,128)}, bf16[2048,512]{1,0:T(8,128)(2,1)S(1)}, bf16[4,2,2,528,128]{4,3,2,1,0:T(8,128)(2,1)}, bf16[4,2,2,528,128]{4,3,2,1,0:T(8,128)(2,1)}) custom-call(s32[6,8]{1,0:T(8,128)S(1)} %copy-done.3, bf16[2048,512]{1,0:T(8,128)(2,1)S(1)} %bitcast.33, f32[2048,512]{1,0:T(8,128)} %get-tuple-element.95.xhat, ...), custom_call_target="tpu_custom_call" | custom-call | flops 25769803776 | bytes 1048576 | tf_op jit(solution)/shard_map/feed_forward/pallas_call | solution.py:343
  128.6 1.3 copy-done.4
  130.2 1.0 slice_select_fusion
  131.2 1.5 collective-permute-start.30
  132.8 1.6 copy-done.5
  134.3 13.0 %conv_weight_backward.1 = (bf16[4,2,2,9,32,256]{5,4,3,2,1,0:T(8,128)(2,1)S(1)}, bf16[4,2,2,9,32,256]{5,4,3,2,1,0:T(8,128)(2,1)S(1)}) custom-call(s32[6,8]{1,0:T(8,128)S(1)} %copy-done.3, bf16[128,512]{1,0:T(8,128)(2,1)S(1)} %collective-permute-done.prev.nxt, bf16[2048,512]{1,0:T(8,128)(2,1)S(1)} %bitcast.34, ...), custom_call_target="tpu_custom_call" | custom-call | flops 9663676416 | bytes 1048576 | tf_op jit(solution)/shard_map/conv_weight_backward/pallas_call | solution.py:421
  147.5 3.0 %stage.8 = (bf16[2,2,2,272,128]{4,3,2,1,0:T(8,128)(2,1)S(1)}, f32[2,2,2,272,128]{4,3,2,1,0:T(8,128)S(1)}, bf16[2,2,2,256,128]{4,3,2,1,0:T(8,128)(2,1)S(1)}, f32[2,2,2,256,128]{4,3,2,1,0:T(8,128)S(1)}) custom-call(s32[6,8]{1,0:T(8,128)S(1)} %copy-done.3, bf16[4,2,2,528,128]{4,3,2,1,0:T(8,128)(2,1)S(1)} %copy-done.1, ...), custom_call_target="tpu_custom_call" | custom-call | tf_op jit(solution)/shard_map/stage/pallas_call | solution.py:636
  150.4 0.6 collective-permute-start.31
  151.1 1.2 collective-permute-start.32
  152.3 1.1 stage.9
  153.4 0.9 collective-permute-start.34
  154.4 1.4 collective-permute-start.35
  155.8 12.2 %conv_input_backward.1 = f32[2048,512]{1,0:T(8,128)} custom-call(s32[6,8]{1,0:T(8,128)S(1)} %copy-done.3, bf16[128,512]{1,0:T(8,128)(2,1)S(1)} %collective-permute-done.30.prev.nxt, bf16[2048,512]{1,0:T(8,128)(2,1)S(1)} %copy-done.6, bf16[128,512]{1,0:T(8,128)(2,1)S(1)} %collective-permute-done.30.prev.nxt, f32[2048,512]{1,0:T(8,128)S(1)} %copy-done.9, ...), custom_call_target="tpu_custom_call" | custom-call | flops 9663676416 | bytes 1048576 | tf_op jit(solution)/shard_map/conv_input_backward/pallas_call | solution.py:465
  168.0 0.8 stage.10
  168.8 0.7 collective-permute-start.38
  169.5 1.2 collective-permute-start.39
  170.6 6.5 %collective-permute-done.35.refs_3_ = bf16[2,2,2,4,32,256]{5,4,3,2,1,0:T(8,128)(2,1)S(1)} collective-permute-done((bf16[2,2,2,4,32,256]{5,4,3,2,1,0:T(8,128)(2,1)S(1)}, bf16[2,2,2,4,32,256]{5,4,3,2,1,0:T(8,128)(2,1)S(1)}, u32[]{:S(2)}, u32[]{:S(2)}) %collective-permute-start.35) | collective-permute-done | bytes 524320 | tf_op jit(solution)/shard_map/ppermute | solution.py:553
  177.1 2.9 %collective-permute-done.34.refs_1_ = bf16[2,2,2,5,32,256]{5,4,3,2,1,0:T(8,128)(2,1)S(1)} collective-permute-done((bf16[2,2,2,5,32,256]{5,4,3,2,1,0:T(8,128)(2,1)S(1)}, bf16[2,2,2,5,32,256]{5,4,3,2,1,0:T(8,128)(2,1)S(1)}, u32[]{:S(2)}, u32[]{:S(2)}) %collective-permute-start.34) | collective-permute-done | bytes 655392 | tf_op jit(solution)/shard_map/ppermute | solution.py:553
  180.0 0.8 stage.11
  180.8 0.7 collective-permute-start.36
  181.5 1.1 collective-permute-start.37
  182.6 3.0 %collective-permute-done.39.refs_3_ = bf16[2,2,256,128]{3,2,1,0:T(8,128)(2,1)S(1)} collective-permute-done((bf16[2,2,256,128]{3,2,1,0:T(8,128)(2,1)S(1)}, bf16[2,2,256,128]{3,2,1,0:T(8,128)(2,1)S(1)}, u32[]{:S(2)}, u32[]{:S(2)}) %collective-permute-start.39) | collective-permute-done | bytes 262176 | tf_op jit(solution)/shard_map/ppermute | solution.py:553
  185.6 0.7 stage.12
  186.3 1.5 collective-permute-start.41
  187.8 3.0 %collective-permute-done.37.refs_3_ = bf16[2,2,4,32,256]{4,3,2,1,0:T(8,128)(2,1)S(1)} collective-permute-done((bf16[2,2,4,32,256]{4,3,2,1,0:T(8,128)(2,1)S(1)}, bf16[2,2,4,32,256]{4,3,2,1,0:T(8,128)(2,1)S(1)}, u32[]{:S(2)}, u32[]{:S(2)}) %collective-permute-start.37) | collective-permute-done | bytes 262176 | tf_op jit(solution)/shard_map/ppermute | solution.py:553
  190.8 0.7 stage.13
  191.5 1.5 collective-permute-start.40
  193.0 1.2 collective-permute-done.41.refs_1_
  194.1 0.7 stage.14
  194.8 2.5 %collective-permute-start.43 = (bf16[528,128]{1,0:T(8,128)(2,1)S(1)}, bf16[528,128]{1,0:T(8,128)(2,1)S(1)}, u32[]{:S(2)}, u32[]{:S(2)}) collective-permute-start(bf16[528,128]{1,0:T(8,128)(2,1)S(1)} %get-tuple-element.142), channel_id=1, source_target_pairs={{0,16},{8,24},{16,0},{24,8},{1,17},{9,25},{17,1},{25,9},{2,18},{10... | collective-permute-start | bytes 405512 | tf_op jit(solution)/shard_map/ppermute | solution.py:553
  197.3 6.0 %collective-permute-done.40.refs_1_ = bf16[2,9,32,256]{3,2,1,0:T(8,128)(2,1)S(1)} collective-permute-done((bf16[2,9,32,256]{3,2,1,0:T(8,128)(2,1)S(1)}, bf16[2,9,32,256]{3,2,1,0:T(8,128)(2,1)S(1)}, u32[]{:S(2)}, u32[]{:S(2)}) %collective-permute-start.40) | collective-permute-done | bytes 294944 | tf_op jit(solution)/shard_map/ppermute | solution.py:553
  203.3 0.7 stage.15
  204.0 0.7 slice_bitcast_fusion
  204.6 0.6 slice_bitcast_fusion.1
  205.2 1.7 collective-permute-start.42
  207.0 0.8 copy.26
  208.2 5.8 %collective-permute-done.42 = bf16[9,32,256]{2,1,0:T(8,128)(2,1)S(1)} collective-permute-done((bf16[9,32,256]{2,1,0:T(8,128)(2,1)S(1)}, bf16[9,32,256]{2,1,0:T(8,128)(2,1)S(1)}, u32[]{:S(2)}, u32[]{:S(2)}) %collective-permute-start.42) | collective-permute-done | bytes 147488 | tf_op jit(solution)/shard_map/ppermute | solution.py:553
  214.0 0.7 add_bitcast_fusion
  (75 shorter events, 5.7 us)
Async XLA Ops:
  7.2 72.6 %all-gather.2.cloned.1.call-start = ((), (), s32[]{:S(2)}) async-start(), calls=%async_computation | async-start | bytes 4325376 | tf_op jit(solution)/shard_map/all_gather | solution.py:697
  7.2 50.3 %copy-start = (bf16[1,2048,512]{2,1,0:T(8,128)(2,1)S(1)}, bf16[1,2048,512]{2,1,0:T(8,128)(2,1)}, u32[]{:S(2)}) copy-start(bf16[1,2048,512]{2,1,0:T(8,128)(2,1)} %param.13) | copy-start | bytes 6291460
  9.5 12.0 %collective-permute-start.1 = (bf16[1,10,32,256]{3,2,1,0:T(8,128)(2,1)}, bf16[1,10,32,256]{3,2,1,0:T(8,128)(2,1)S(1)}, u32[]{:S(2)}, u32[]{:S(2)}) collective-permute-start(bf16[1,10,32,256]{3,2,1,0:T(8,128)(2,1)} %get-tuple-element.82), channel_id=1, source_target_pairs={{0,16},{8,24},{16,0},{24,8},{1,17},{9,25},{17,1},{25,9},{2,18},{10... | collective-permute-start | bytes 491528 | tf_op jit(solution)/shard_map/ppermute | solution.py:553
  13.6 7.9 %collective-permute-start.2 = (bf16[1,10,32,256]{3,2,1,0:T(8,128)(2,1)}, bf16[1,10,32,256]{3,2,1,0:T(8,128)(2,1)S(1)}, u32[]{:S(2)}, u32[]{:S(2)}) collective-permute-start(bf16[1,10,32,256]{3,2,1,0:T(8,128)(2,1)} %get-tuple-element.82), channel_id=1, source_target_pairs={{0,4},{4,0},{1,5},{5,1},{2,6},{6,2},{3,7},{7,3},{8,12},{12,8},{9,1... | collective-permute-start | bytes 491528 | tf_op jit(solution)/shard_map/ppermute | solution.py:553
  15.1 6.4 %collective-permute-start.3 = (bf16[1,10,32,256]{3,2,1,0:T(8,128)(2,1)}, bf16[1,10,32,256]{3,2,1,0:T(8,128)(2,1)S(1)}, u32[]{:S(2)}, u32[]{:S(2)}) collective-permute-start(bf16[1,10,32,256]{3,2,1,0:T(8,128)(2,1)} %get-tuple-element.82), channel_id=1, source_target_pairs={{0,1},{1,0},{2,3},{3,2},{4,5},{5,4},{6,7},{7,6},{8,9},{9,8},{10,11... | collective-permute-start | bytes 491528 | tf_op jit(solution)/shard_map/ppermute | solution.py:553
  21.5 10.9 %collective-permute-start.4 = (bf16[2,10,32,256]{3,2,1,0:T(8,128)(2,1)S(1)}, bf16[2,10,32,256]{3,2,1,0:T(8,128)(2,1)S(1)}, u32[]{:S(2)}, u32[]{:S(2)}) collective-permute-start(bf16[2,10,32,256]{3,2,1,0:T(8,128)(2,1)S(1)} %constant_dynamic-update-slice_fusion.rest_0_), channel_id=1, source_target_pairs={{0,8},{8,0},{16,24},{24,16},{1,9},{9,1},{17,25},{25,17},{2,10},{10... | collective-permute-start | bytes 983048 | tf_op jit(solution)/shard_map/ppermute | solution.py:553
  22.4 5.2 %collective-permute-start.7 = (bf16[1,5,32,256]{3,2,1,0:T(8,128)(2,1)S(1)}, bf16[1,5,32,256]{3,2,1,0:T(8,128)(2,1)S(1)}, u32[]{:S(2)}, u32[]{:S(2)}) collective-permute-start(bf16[1,5,32,256]{3,2,1,0:T(8,128)(2,1)S(1)} %slice.51), channel_id=1, source_target_pairs={{0,1},{1,0},{2,3},{3,2},{4,5},{5,4},{6,7},{7,6},{8,9},{9,8},{10,11... | collective-permute-start | bytes 245768 | tf_op jit(solution)/shard_map/ppermute | solution.py:553
  23.9 7.8 %collective-permute-start.5 = (bf16[1,10,32,256]{3,2,1,0:T(8,128)(2,1)S(1)}, bf16[1,10,32,256]{3,2,1,0:T(8,128)(2,1)S(1)}, u32[]{:S(2)}, u32[]{:S(2)}) collective-permute-start(bf16[1,10,32,256]{3,2,1,0:T(8,128)(2,1)S(1)} %collective-permute-done.1), channel_id=1, source_target_pairs={{0,4},{4,0},{1,5},{5,1},{2,6},{6,2},{3,7},{7,3},{8,12},{12,8},{9,1... | collective-permute-start | bytes 491528 | tf_op jit(solution)/shard_map/ppermute | solution.py:553
  25.4 6.9 %collective-permute-start.6 = (bf16[1,10,32,256]{3,2,1,0:T(8,128)(2,1)S(1)}, bf16[1,10,32,256]{3,2,1,0:T(8,128)(2,1)S(1)}, u32[]{:S(2)}, u32[]{:S(2)}) collective-permute-start(bf16[1,10,32,256]{3,2,1,0:T(8,128)(2,1)S(1)} %collective-permute-done.1), channel_id=1, source_target_pairs={{0,1},{1,0},{2,3},{3,2},{4,5},{5,4},{6,7},{7,6},{8,9},{9,8},{10,11... | collective-permute-start | bytes 491528 | tf_op jit(solution)/shard_map/ppermute | solution.py:553
  26.0 5.8 %collective-permute-start.8 = (bf16[1,5,32,256]{3,2,1,0:T(8,128)(2,1)S(1)}, bf16[1,5,32,256]{3,2,1,0:T(8,128)(2,1)S(1)}, u32[]{:S(2)}, u32[]{:S(2)}) collective-permute-start(bf16[1,5,32,256]{3,2,1,0:T(8,128)(2,1)S(1)} %slice.52), channel_id=1, source_target_pairs={{0,4},{4,0},{1,5},{5,1},{2,6},{6,2},{3,7},{7,3},{8,12},{12,8},{9,1... | collective-permute-start | bytes 245768 | tf_op jit(solution)/shard_map/ppermute | solution.py:553
  27.7 7.7 %collective-permute-start = (bf16[128,512]{1,0:T(8,128)(2,1)}, bf16[128,512]{1,0:T(8,128)(2,1)S(1)}, u32[]{:S(2)}, u32[]{:S(2)}) collective-permute-start(bf16[128,512]{1,0:T(8,128)(2,1)} %get-tuple-element.81), channel_id=1, source_target_pairs={{0,1},{1,0},{2,3},{3,2},{4,5},{5,4},{6,7},{7,6},{8,9},{9,8},{10,11... | collective-permute-start | bytes 393224 | tf_op jit(solution)/shard_map/ppermute | solution.py:553
  31.8 6.1 %collective-permute-start.15 = (bf16[2,10,32,256]{3,2,1,0:T(8,128)(2,1)S(1)}, bf16[2,10,32,256]{3,2,1,0:T(8,128)(2,1)S(1)}, u32[]{:S(2)}, u32[]{:S(2)}) collective-permute-start(bf16[2,10,32,256]{3,2,1,0:T(8,128)(2,1)S(1)} %constant_dynamic-update-slice_fusion.rest_0_), channel_id=1, source_target_pairs={{0,2},{2,0},{1,3},{3,1},{4,6},{6,4},{5,7},{7,5},{8,10},{10,8},{9,1... | collective-permute-start | bytes 983048 | tf_op jit(solution)/shard_map/ppermute | solution.py:553
  32.4 15.5 %collective-permute-start.10 = (bf16[2,10,32,256]{3,2,1,0:T(8,128)(2,1)S(1)}, bf16[2,10,32,256]{3,2,1,0:T(8,128)(2,1)S(1)}, u32[]{:S(2)}, u32[]{:S(2)}) collective-permute-start(bf16[2,10,32,256]{3,2,1,0:T(8,128)(2,1)S(1)} %collective-permute-done.4.rest_1_), channel_id=1, source_target_pairs={{0,1},{1,0},{2,3},{3,2},{4,5},{5,4},{6,7},{7,6},{8,9},{9,8},{10,11... | collective-permute-start | bytes 983048 | tf_op jit(solution)/shard_map/ppermute | solution.py:553
  33.7 14.6 %collective-permute-start.9 = (bf16[2,10,32,256]{3,2,1,0:T(8,128)(2,1)S(1)}, bf16[2,10,32,256]{3,2,1,0:T(8,128)(2,1)S(1)}, u32[]{:S(2)}, u32[]{:S(2)}) collective-permute-start(bf16[2,10,32,256]{3,2,1,0:T(8,128)(2,1)S(1)} %collective-permute-done.4.rest_1_), channel_id=1, source_target_pairs={{0,4},{4,0},{1,5},{5,1},{2,6},{6,2},{3,7},{7,3},{8,12},{12,8},{9,1... | collective-permute-start | bytes 983048 | tf_op jit(solution)/shard_map/ppermute | solution.py:553
  35.4 1.4 collective-permute-start.17
  35.4 1.7 collective-permute-start.18
  36.8 8.9 %collective-permute-start.11 = (bf16[1,5,32,256]{3,2,1,0:T(8,128)(2,1)S(1)}, bf16[1,5,32,256]{3,2,1,0:T(8,128)(2,1)S(1)}, u32[]{:S(2)}, u32[]{:S(2)}) collective-permute-start(bf16[1,5,32,256]{3,2,1,0:T(8,128)(2,1)S(1)} %slice.53), channel_id=1, source_target_pairs={{0,1},{1,0},{2,3},{3,2},{4,5},{5,4},{6,7},{7,6},{8,9},{9,8},{10,11... | collective-permute-start | bytes 245768 | tf_op jit(solution)/shard_map/ppermute | solution.py:553
  37.1 10.8 %collective-permute-start.12 = (bf16[1,5,32,256]{3,2,1,0:T(8,128)(2,1)S(1)}, bf16[1,5,32,256]{3,2,1,0:T(8,128)(2,1)S(1)}, u32[]{:S(2)}, u32[]{:S(2)}) collective-permute-start(bf16[1,5,32,256]{3,2,1,0:T(8,128)(2,1)S(1)} %slice.54), channel_id=1, source_target_pairs={{0,4},{4,0},{1,5},{5,1},{2,6},{6,2},{3,7},{7,3},{8,12},{12,8},{9,1... | collective-permute-start | bytes 245768 | tf_op jit(solution)/shard_map/ppermute | solution.py:553
  37.9 14.0 %collective-permute-start.16 = (bf16[2,10,32,256]{3,2,1,0:T(8,128)(2,1)S(1)}, bf16[2,10,32,256]{3,2,1,0:T(8,128)(2,1)S(1)}, u32[]{:S(2)}, u32[]{:S(2)}) collective-permute-start(bf16[2,10,32,256]{3,2,1,0:T(8,128)(2,1)S(1)} %collective-permute-done.4.rest_1_), channel_id=1, source_target_pairs={{0,2},{2,0},{1,3},{3,1},{4,6},{6,4},{5,7},{7,5},{8,10},{10,8},{9,1... | collective-permute-start | bytes 983048 | tf_op jit(solution)/shard_map/ppermute | solution.py:553
  45.6 5.7 %collective-permute-start.21 = (bf16[1,10,32,256]{3,2,1,0:T(8,128)(2,1)S(1)}, bf16[1,10,32,256]{3,2,1,0:T(8,128)(2,1)S(1)}, u32[]{:S(2)}, u32[]{:S(2)}) collective-permute-start(bf16[1,10,32,256]{3,2,1,0:T(8,128)(2,1)S(1)} %collective-permute-done.5.rest_6_), channel_id=1, source_target_pairs={{0,2},{2,0},{1,3},{3,1},{4,6},{6,4},{5,7},{7,5},{8,10},{10,8},{9,1... | collective-permute-start | bytes 491528 | tf_op jit(solution)/shard_map/ppermute | solution.py:553
  47.8 3.5 %collective-permute-start.22 = (bf16[1,10,32,256]{3,2,1,0:T(8,128)(2,1)S(1)}, bf16[1,10,32,256]{3,2,1,0:T(8,128)(2,1)S(1)}, u32[]{:S(2)}, u32[]{:S(2)}) collective-permute-start(bf16[1,10,32,256]{3,2,1,0:T(8,128)(2,1)S(1)} %collective-permute-done.6.rest_7_), channel_id=1, source_target_pairs={{0,2},{2,0},{1,3},{3,1},{4,6},{6,4},{5,7},{7,5},{8,10},{10,8},{9,1... | collective-permute-start | bytes 491528 | tf_op jit(solution)/shard_map/ppermute | solution.py:553
  47.9 1.5 collective-permute-start.19
  48.4 1.3 collective-permute-start.20
  49.4 6.4 %collective-permute-start.13 = (bf16[2,5,32,256]{3,2,1,0:T(8,128)(2,1)S(1)}, bf16[2,5,32,256]{3,2,1,0:T(8,128)(2,1)S(1)}, u32[]{:S(2)}, u32[]{:S(2)}) collective-permute-start(bf16[2,5,32,256]{3,2,1,0:T(8,128)(2,1)S(1)} %slice.55), channel_id=1, source_target_pairs={{0,1},{1,0},{2,3},{3,2},{4,5},{5,4},{6,7},{7,6},{8,9},{9,8},{10,11... | collective-permute-start | bytes 491528 | tf_op jit(solution)/shard_map/ppermute | solution.py:553
  49.6 6.3 %collective-permute-start.14 = (bf16[2,5,32,256]{3,2,1,0:T(8,128)(2,1)S(1)}, bf16[2,5,32,256]{3,2,1,0:T(8,128)(2,1)S(1)}, u32[]{:S(2)}, u32[]{:S(2)}) collective-permute-start(bf16[2,5,32,256]{3,2,1,0:T(8,128)(2,1)S(1)} %slice.56), channel_id=1, source_target_pairs={{0,4},{4,0},{1,5},{5,1},{2,6},{6,2},{3,7},{7,3},{8,12},{12,8},{9,1... | collective-permute-start | bytes 491528 | tf_op jit(solution)/shard_map/ppermute | solution.py:553
  51.3 6.2 %collective-permute-start.25 = (bf16[2,10,32,256]{3,2,1,0:T(8,128)(2,1)S(1)}, bf16[2,10,32,256]{3,2,1,0:T(8,128)(2,1)S(1)}, u32[]{:S(2)}, u32[]{:S(2)}) collective-permute-start(bf16[2,10,32,256]{3,2,1,0:T(8,128)(2,1)S(1)} %collective-permute-done.9.rest_10_), channel_id=1, source_target_pairs={{0,2},{2,0},{1,3},{3,1},{4,6},{6,4},{5,7},{7,5},{8,10},{10,8},{9,1... | collective-permute-start | bytes 983048 | tf_op jit(solution)/shard_map/ppermute | solution.py:553
  51.3 6.2 %collective-permute-start.26 = (bf16[2,10,32,256]{3,2,1,0:T(8,128)(2,1)S(1)}, bf16[2,10,32,256]{3,2,1,0:T(8,128)(2,1)S(1)}, u32[]{:S(2)}, u32[]{:S(2)}) collective-permute-start(bf16[2,10,32,256]{3,2,1,0:T(8,128)(2,1)S(1)} %collective-permute-done.10.rest_11_), channel_id=1, source_target_pairs={{0,2},{2,0},{1,3},{3,1},{4,6},{6,4},{5,7},{7,5},{8,10},{10,8},{9,1... | collective-permute-start | bytes 983048 | tf_op jit(solution)/shard_map/ppermute | solution.py:553
  51.9 4.4 %collective-permute-start.23 = (bf16[1,5,32,256]{3,2,1,0:T(8,128)(2,1)S(1)}, bf16[1,5,32,256]{3,2,1,0:T(8,128)(2,1)S(1)}, u32[]{:S(2)}, u32[]{:S(2)}) collective-permute-start(bf16[1,5,32,256]{3,2,1,0:T(8,128)(2,1)S(1)} %collective-permute-done.11.rest_8_), channel_id=1, source_target_pairs={{0,2},{2,0},{1,3},{3,1},{4,6},{6,4},{5,7},{7,5},{8,10},{10,8},{9,1... | collective-permute-start | bytes 245768 | tf_op jit(solution)/shard_map/ppermute | solution.py:553
  55.7 1.8 collective-permute-start.27
  55.9 1.6 collective-permute-start.28
  56.3 1.3 collective-permute-start.24
  57.6 0.7 copy-start.2
  58.3 21.5 %copy-start.3 = (s32[6,8]{1,0:T(8,128)S(1)}, s32[6,8]{1,0:T(8,128)}, u32[]{:S(2)}) copy-start(s32[6,8]{1,0:T(8,128)} %get-tuple-element.80.flags) | copy-start | bytes 580
  79.8 1.6 copy-start.7
  128.6 1.3 copy-start.4
  129.9 17.4 %collective-permute-start.29 = (bf16[4,2,2,528,128]{4,3,2,1,0:T(8,128)(2,1)}, bf16[4,2,2,528,128]{4,3,2,1,0:T(8,128)(2,1)}, u32[]{:S(2)}, u32[]{:S(2)}) collective-permute-start(bf16[4,2,2,528,128]{4,3,2,1,0:T(8,128)(2,1)} %get-tuple-element.101), channel_id=1, source_target_pairs={{0,2},{2,0},{1,3},{3,1},{4,6},{6,4},{5,7},{7,5},{8,10},{10,8},{9,1... | collective-permute-start | bytes 6488072 | tf_op jit(solution)/shard_map/ppermute | solution.py:553
  131.2 16.3 %copy-start.1 = (bf16[4,2,2,528,128]{4,3,2,1,0:T(8,128)(2,1)S(1)}, bf16[4,2,2,528,128]{4,3,2,1,0:T(8,128)(2,1)}, u32[]{:S(2)}) copy-start(bf16[4,2,2,528,128]{4,3,2,1,0:T(8,128)(2,1)} %get-tuple-element.100.keep) | copy-start | bytes 6488068
  131.2 16.2 %collective-permute-start.30 = (bf16[128,512]{1,0:T(8,128)(2,1)S(1)}, bf16[128,512]{1,0:T(8,128)(2,1)S(1)}, u32[]{:S(2)}, u32[]{:S(2)}) collective-permute-start(bf16[128,512]{1,0:T(8,128)(2,1)S(1)} %slice_select_fusion), channel_id=1, source_target_pairs={{0,1},{1,0},{2,3},{3,2},{4,5},{5,4},{6,7},{7,6},{8,9},{9,8},{10,11... | collective-permute-start | bytes 393224 | tf_op jit(solution)/shard_map/ppermute | solution.py:553
  132.8 1.6 copy-start.5
  134.3 21.4 %copy-start.9 = (f32[2048,512]{1,0:T(8,128)S(1)}, f32[2048,512]{1,0:T(8,128)}, u32[]{:S(2)}) copy-start(f32[2048,512]{1,0:T(8,128)} %get-tuple-element.113.gh) | copy-start | bytes 12582916
  147.4 4.9 %collective-permute-start.33 = (bf16[4,2,2,9,32,256]{5,4,3,2,1,0:T(8,128)(2,1)S(1)}, bf16[4,2,2,9,32,256]{5,4,3,2,1,0:T(8,128)(2,1)S(1)}, u32[]{:S(2)}, u32[]{:S(2)}) collective-permute-start(bf16[4,2,2,9,32,256]{5,4,3,2,1,0:T(8,128)(2,1)S(1)} %get-tuple-element.109), channel_id=1, source_target_pairs={{0,2},{2,0},{1,3},{3,1},{4,6},{6,4},{5,7},{7,5},{8,10},{10,8},{9,1... | collective-permute-start | bytes 7077896 | tf_op jit(solution)/shard_map/ppermute | solution.py:553
  147.5 8.3 %copy-start.8 = (bf16[9,512,512]{2,1,0:T(8,128)(2,1)S(1)}, bf16[9,512,512]{2,1,0:T(8,128)(2,1)}, u32[]{:S(2)}) copy-start(bf16[9,512,512]{2,1,0:T(8,128)(2,1)} %get-tuple-element.114.w) | copy-start | bytes 14155780
  150.4 17.5 %collective-permute-start.31 = (bf16[2,2,2,272,128]{4,3,2,1,0:T(8,128)(2,1)S(1)}, bf16[2,2,2,272,128]{4,3,2,1,0:T(8,128)(2,1)S(1)}, u32[]{:S(2)}, u32[]{:S(2)}) collective-permute-start(bf16[2,2,2,272,128]{4,3,2,1,0:T(8,128)(2,1)S(1)} %get-tuple-element.105), channel_id=1, source_target_pairs={{0,4},{4,0},{1,5},{5,1},{2,6},{6,2},{3,7},{7,3},{8,12},{12,8},{9,1... | collective-permute-start | bytes 1671176 | tf_op jit(solution)/shard_map/ppermute | solution.py:553
  151.1 16.9 %collective-permute-start.32 = (bf16[2,2,2,256,128]{4,3,2,1,0:T(8,128)(2,1)S(1)}, bf16[2,2,2,256,128]{4,3,2,1,0:T(8,128)(2,1)S(1)}, u32[]{:S(2)}, u32[]{:S(2)}) collective-permute-start(bf16[2,2,2,256,128]{4,3,2,1,0:T(8,128)(2,1)S(1)} %get-tuple-element.106), channel_id=1, source_target_pairs={{0,1},{1,0},{2,3},{3,2},{4,5},{5,4},{6,7},{7,6},{8,9},{9,8},{10,11... | collective-permute-start | bytes 1572872 | tf_op jit(solution)/shard_map/ppermute | solution.py:553
  152.3 3.4 %copy-start.6 = (bf16[2048,512]{1,0:T(8,128)(2,1)S(1)}, bf16[2048,512]{1,0:T(8,128)(2,1)}, u32[]{:S(2)}) copy-start(bf16[2048,512]{1,0:T(8,128)(2,1)} %copy-done.4) | copy-start | bytes 6291460
  153.4 26.6 %collective-permute-start.34 = (bf16[2,2,2,5,32,256]{5,4,3,2,1,0:T(8,128)(2,1)S(1)}, bf16[2,2,2,5,32,256]{5,4,3,2,1,0:T(8,128)(2,1)S(1)}, u32[]{:S(2)}, u32[]{:S(2)}) collective-permute-start(bf16[2,2,2,5,32,256]{5,4,3,2,1,0:T(8,128)(2,1)S(1)} %get-tuple-element.111), channel_id=1, source_target_pairs={{0,4},{4,0},{1,5},{5,1},{2,6},{6,2},{3,7},{7,3},{8,12},{12,8},{9,1... | collective-permute-start | bytes 1966088 | tf_op jit(solution)/shard_map/ppermute | solution.py:553
  154.4 22.7 %collective-permute-start.35 = (bf16[2,2,2,4,32,256]{5,4,3,2,1,0:T(8,128)(2,1)S(1)}, bf16[2,2,2,4,32,256]{5,4,3,2,1,0:T(8,128)(2,1)S(1)}, u32[]{:S(2)}, u32[]{:S(2)}) collective-permute-start(bf16[2,2,2,4,32,256]{5,4,3,2,1,0:T(8,128)(2,1)S(1)} %get-tuple-element.117), channel_id=1, source_target_pairs={{0,1},{1,0},{2,3},{3,2},{4,5},{5,4},{6,7},{7,6},{8,9},{9,8},{10,11... | collective-permute-start | bytes 1572872 | tf_op jit(solution)/shard_map/ppermute | solution.py:553
  168.8 16.9 %collective-permute-start.38 = (bf16[2,2,272,128]{3,2,1,0:T(8,128)(2,1)S(1)}, bf16[2,2,272,128]{3,2,1,0:T(8,128)(2,1)S(1)}, u32[]{:S(2)}, u32[]{:S(2)}) collective-permute-start(bf16[2,2,272,128]{3,2,1,0:T(8,128)(2,1)S(1)} %get-tuple-element.122), channel_id=1, source_target_pairs={{0,1},{1,0},{2,3},{3,2},{4,5},{5,4},{6,7},{7,6},{8,9},{9,8},{10,11... | collective-permute-start | bytes 835592 | tf_op jit(solution)/shard_map/ppermute | solution.py:553
  169.5 16.1 %collective-permute-start.39 = (bf16[2,2,256,128]{3,2,1,0:T(8,128)(2,1)S(1)}, bf16[2,2,256,128]{3,2,1,0:T(8,128)(2,1)S(1)}, u32[]{:S(2)}, u32[]{:S(2)}) collective-permute-start(bf16[2,2,256,128]{3,2,1,0:T(8,128)(2,1)S(1)} %get-tuple-element.130), channel_id=1, source_target_pairs={{0,4},{4,0},{1,5},{5,1},{2,6},{6,2},{3,7},{7,3},{8,12},{12,8},{9,1... | collective-permute-start | bytes 786440 | tf_op jit(solution)/shard_map/ppermute | solution.py:553
  180.8 10.0 %collective-permute-start.36 = (bf16[2,2,5,32,256]{4,3,2,1,0:T(8,128)(2,1)S(1)}, bf16[2,2,5,32,256]{4,3,2,1,0:T(8,128)(2,1)S(1)}, u32[]{:S(2)}, u32[]{:S(2)}) collective-permute-start(bf16[2,2,5,32,256]{4,3,2,1,0:T(8,128)(2,1)S(1)} %get-tuple-element.127), channel_id=1, source_target_pairs={{0,1},{1,0},{2,3},{3,2},{4,5},{5,4},{6,7},{7,6},{8,9},{9,8},{10,11... | collective-permute-start | bytes 983048 | tf_op jit(solution)/shard_map/ppermute | solution.py:553
  181.5 9.3 %collective-permute-start.37 = (bf16[2,2,4,32,256]{4,3,2,1,0:T(8,128)(2,1)S(1)}, bf16[2,2,4,32,256]{4,3,2,1,0:T(8,128)(2,1)S(1)}, u32[]{:S(2)}, u32[]{:S(2)}) collective-permute-start(bf16[2,2,4,32,256]{4,3,2,1,0:T(8,128)(2,1)S(1)} %get-tuple-element.128), channel_id=1, source_target_pairs={{0,4},{4,0},{1,5},{5,1},{2,6},{6,2},{3,7},{7,3},{8,12},{12,8},{9,1... | collective-permute-start | bytes 786440 | tf_op jit(solution)/shard_map/ppermute | solution.py:553
  186.3 7.8 %collective-permute-start.41 = (bf16[2,528,128]{2,1,0:T(8,128)(2,1)S(1)}, bf16[2,528,128]{2,1,0:T(8,128)(2,1)S(1)}, u32[]{:S(2)}, u32[]{:S(2)}) collective-permute-start(bf16[2,528,128]{2,1,0:T(8,128)(2,1)S(1)} %get-tuple-element.134), channel_id=1, source_target_pairs={{0,8},{8,0},{16,24},{24,16},{1,9},{9,1},{17,25},{25,17},{2,10},{10... | collective-permute-start | bytes 811016 | tf_op jit(solution)/shard_map/ppermute | solution.py:553
  191.5 11.7 %collective-permute-start.40 = (bf16[2,9,32,256]{3,2,1,0:T(8,128)(2,1)S(1)}, bf16[2,9,32,256]{3,2,1,0:T(8,128)(2,1)S(1)}, u32[]{:S(2)}, u32[]{:S(2)}) collective-permute-start(bf16[2,9,32,256]{3,2,1,0:T(8,128)(2,1)S(1)} %get-tuple-element.139), channel_id=1, source_target_pairs={{0,8},{8,0},{16,24},{24,16},{1,9},{9,1},{17,25},{25,17},{2,10},{10... | collective-permute-start | bytes 884744 | tf_op jit(solution)/shard_map/ppermute | solution.py:553
  194.8 9.1 %collective-permute-start.43 = (bf16[528,128]{1,0:T(8,128)(2,1)S(1)}, bf16[528,128]{1,0:T(8,128)(2,1)S(1)}, u32[]{:S(2)}, u32[]{:S(2)}) collective-permute-start(bf16[528,128]{1,0:T(8,128)(2,1)S(1)} %get-tuple-element.142), channel_id=1, source_target_pairs={{0,16},{8,24},{16,0},{24,8},{1,17},{9,25},{17,1},{25,9},{2,18},{10... | collective-permute-start | bytes 405512 | tf_op jit(solution)/shard_map/ppermute | solution.py:553
  205.2 8.8 %collective-permute-start.42 = (bf16[9,32,256]{2,1,0:T(8,128)(2,1)S(1)}, bf16[9,32,256]{2,1,0:T(8,128)(2,1)S(1)}, u32[]{:S(2)}, u32[]{:S(2)}) collective-permute-start(bf16[9,32,256]{2,1,0:T(8,128)(2,1)S(1)} %get-tuple-element.145), channel_id=1, source_target_pairs={{0,16},{8,24},{16,0},{24,8},{1,17},{9,25},{17,1},{25,9},{2,18},{10... | collective-permute-start | bytes 442376 | tf_op jit(solution)/shard_map/ppermute | solution.py:553
Sparse Core Ops, SparseCore 0:
  11.5 68.2 all-gather.1

commit v3 on v2

--- a/solution.py
+++ b/solution.py
@@ -13,7 +13,7 @@
 BF = jnp.bfloat16
 F32 = jnp.float32
 VMEM_CONV = 28 * 2**20
-VMEM_FFN = 46 * 2**20
+VMEM_FFN = 51 * 2**20
 VMEM_FIRST = 30 * 2**20
 VMEM_PACK = 60 * 2**20
 VMEM_SUM = 24 * 2**20
@@ -275,6 +275,18 @@
     e = gh * gain1
     gc = (scale[...] * (e - row_mean(e) - xhat[...] * row_mean(e * xhat[...]))).astype(BF)
     gc_out[...] = gc
+    if fast:
+        edge = rest[0]
+        border = edge.shape[0]
+
+        @pl.when((step == 0) & (flags[4, 1] == 1))
+        def _():
+            edge[...] = gc[:border]
+
+        @pl.when((step == last) & (flags[4, 1] == 0))
+        def _():
+            edge[...] = gc[gc.shape[0] - border :]
+
     sums[5] += fold(gc.astype(F32))
 
     @pl.when(step == last)
@@ -286,7 +298,7 @@
             sums_out[...] = jnp.sum(sums[...], 1)
             ub_out[...] = jnp.sum(ub_sums[...], 0, keepdims=True)
             return
-        send, keep = rest[:2]
+        send, keep = rest[1:3]
         mine = flags[3, 0] == 0
         block = send.shape[-1]
         half = width // 2
@@ -336,7 +348,8 @@
     tile = pl.BlockSpec((rows, width), lambda j, f: (j, 0))
     sds = jax.ShapeDtypeStruct
     if fast:
-        shapes = [sds((4, 2, 2, width + 16, hidden // batch), BF)] * 2
+        border = KERNEL_TAPS // 2 * DILATION_STEP
+        shapes = [sds((border, width), BF)] + [sds((4, 2, 2, width + 16, hidden // batch), BF)] * 2
     else:
         shapes = [sds(s, F32) for s in ((width, hidden), (width, hidden), (6, width), (1, hidden))]
     anywhere = [pl.BlockSpec(memory_space=pl.ANY)] * len(sources)
@@ -358,21 +371,22 @@
                 pltpu.SemaphoreType.DMA((count_copies(plan),)),
             ],
         ),
-        out_shape=[sds((count, width), BF), sds((count, width), F32), sds((count, width), BF)] + shapes,
+        out_shape=[pltpu.HBM((count, width), BF), pltpu.HBM((count, width), F32), (pltpu.VMEM if fast else pltpu.HBM)((count, width), BF)] + shapes,
         compiler_params=pltpu.CompilerParams(vmem_limit_bytes=VMEM_FFN if fast else VMEM_PACK),
         cost_estimate=pl.CostEstimate(flops=12 * count * width * hidden // COST, bytes_accessed=2**20, transcendentals=0),
         name="feed_forward",
     )(flags, x, xhat, scale, og, table, *sources)
 
 
-def conv_weight_kernel(fast, flags, prev, x, nxt, g, *rest):
+def conv_weight_kernel(fast, first, flags, prev, x, nxt, g, *rest):
     ext, col = rest[-2:]
-    tap = pl.program_id(0)
+    outs = rest[:-2] if first == 0 else rest[2:-2]
+    tap = pl.program_id(0) + first
     count, width = g.shape
     border = prev.shape[0]
     subs = count // SUB
 
-    @pl.when(tap == 0)
+    @pl.when(tap == first)
     def _():
         ext[0:border] = prev[...]
         ext[border : border + count] = x[...]
@@ -390,12 +404,12 @@
 
     grad = dot(g[...], col[...], TN)
     if not fast:
-        rest[0][0] = grad
+        outs[0][0] = grad
         return
     mine = flags[3, 0] == 0
     half = width // 2
 
-    send, keep = rest[:2]
+    send, keep = outs
     block = send.shape[4]
     early = (tap < (KERNEL_TAPS + 1) // 2).astype(jnp.int32)
     for s in range(2):
@@ -409,21 +423,21 @@
             keep[at] = jnp.where(mine, lo, hi)
 
 
-def conv_weight_backward(flags, prev, x, nxt, g, batch, fast):
+def conv_weight_backward(flags, prev, x, nxt, g, batch, fast, first=0, taps=KERNEL_TAPS, into=()):
     count, width = x.shape
     if fast:
         block = (4, 2, 2, 1, width // batch, width // 2)
-        specs = [pl.BlockSpec(block, lambda k, f: (0, 0, 0, k, 0, 0))] * 2
+        specs = [pl.BlockSpec(block, lambda k, f: (0, 0, 0, k + first, 0, 0))] * 2
         shapes = [jax.ShapeDtypeStruct(block[:3] + (KERNEL_TAPS,) + block[4:], BF)] * 2
     else:
         specs = [pl.BlockSpec((1, width, width), lambda k, f: (k, 0, 0))]
         shapes = [jax.ShapeDtypeStruct((KERNEL_TAPS, width, width), F32)]
     return pl.pallas_call(
-        functools.partial(conv_weight_kernel, fast),
+        functools.partial(conv_weight_kernel, fast, first),
         grid_spec=pltpu.PrefetchScalarGridSpec(
             num_scalar_prefetch=1,
-            grid=(KERNEL_TAPS,),
-            in_specs=[whole_block(a.shape) for a in (prev, x, nxt, g)],
+            grid=(taps,),
+            in_specs=[whole_block(a.shape) for a in (prev, x, nxt, g)] + [pl.BlockSpec(memory_space=pl.ANY)] * len(into),
             out_specs=specs,
             scratch_shapes=[
                 pltpu.VMEM((count + 2 * prev.shape[0], width), BF),
@@ -432,9 +446,10 @@
         ),
         out_shape=shapes,
         compiler_params=pltpu.CompilerParams(vmem_limit_bytes=VMEM_CONV),
-        cost_estimate=conv_cost(count, width),
+        cost_estimate=conv_cost(count * taps // KERNEL_TAPS, width),
+        input_output_aliases={5 + i: i for i in range(len(into))},
         name="conv_weight_backward",
-    )(flags, prev, x, nxt, g)
+    )(flags, prev, x, nxt, g, *into)
 
 
 def conv_input_kernel(subs, flags, prev, g, nxt, gh, w, out, ext, col):
@@ -578,19 +593,26 @@
     return arrays + other, tuple(plan) + tuple((shifted(o, 1, 0), first) for o, first in plan)
 
 
-def gather_conv(own):
+def gather(own, pair, halo):
     cut = own.shape[1] // 2
     top = lambda value: swap(value[:, :cut], Y)
     bottom = lambda value: swap(value[:, cut:], X)
-    far, own_x, own_y = lax.optimization_barrier((swap(own, Z1), swap(own, X), swap(own, Y)))
+    halo, own_y, own_x, far = lax.optimization_barrier((swap(halo, Y), swap(own, Y), swap(own, X), swap(own, Z1)))
     column = jnp.concatenate([own, far], 0)
     near, far_x, far_y, own_top, own_bottom = lax.optimization_barrier(
         (swap(column, Z0), swap(far, X), swap(far, Y), top(own_x), bottom(own_y))
     )
-    near_x, near_y, far_top, far_bottom = lax.optimization_barrier(
-        (swap(near, X), swap(near, Y), top(far_x), bottom(far_y))
+    pair = after(pair, near, own_top)
+    near_x, near_y, far_top, far_bottom, pair_far = lax.optimization_barrier(
+        (swap(near, X), swap(near, Y), top(far_x), bottom(far_y), swap(pair, Z1))
     )
     near_top, near_bottom = top(near_x), bottom(near_y)
+    pair = jnp.concatenate([pair, pair_far], 0)
+    pair = jnp.concatenate([pair, swap(pair, Z0)], 0)
+    pair_x, pair_y = swap(pair, X), swap(pair, Y)
+    across = lax.ppermute(pair, ("x", "seq"), [(i, i ^ 3) for i in range(4)])
+    offsets = ((0, 0), (8, 0), (4, 0), (12, 0))
+    pair_plan = [(shifted(offsets, b, s), 0) for b, s in ((0, 0), (2, 0), (0, 1), (2, 1))]
     arrays, plan = [column, near], [(((0, 0), (8, 0)), 0), (((4, 0), (12, 0)), 0)]
     for offsets, members in (
         (((0, 0),), (own_x, own_y, own_top, own_bottom)),
@@ -599,7 +621,7 @@
     ):
         arrays += members
         plan += [(shifted(offsets, b, s), first) for b, s, first in ((2, 0, 0), (0, 1, 0), (2, 1, 0), (2, 1, cut))]
-    return both_cores(arrays, plan)
+    return halo, both_cores(arrays, plan), ([pair, pair_x, pair_y, across], pair_plan)
 
 
 def stage_kernel(columns, joined, flags, *refs):
@@ -675,7 +697,7 @@
     batch, seq = lax.axis_size(BATCH), lax.axis_size("seq")
     hidden = up_weight.shape[1] * batch
     border = KERNEL_TAPS // 2 * DILATION_STEP
-    x, og = inputs[0], out_grad[0]
+    x, og = inputs[0], pltpu.with_memory_space_constraint(out_grad[0], pltpu.HBM)
     fast = seq == 2 and batch == 16
 
     def ends(value):
@@ -692,10 +714,8 @@
     conv_own = conv_weight.transpose(0, 2, 1)
     flags, halo, conv_block, pair_block = pack(window_lengths, x, conv_own, up_weight, down_weight, vectors, small)
     if fast:
-        prev = nxt = swap(halo, Y)
-        conv_pieces, conv_plan = gather_conv(conv_block)
-        pair_pieces = [lax.all_gather(pair_block[0], (*BATCH, "seq"), axis=0)]
-        pair_plan = ((tuple((d // 2, d % 2) for d in range(2 * batch)), -1),)
+        halo, (conv_pieces, conv_plan), (pair_pieces, pair_plan) = gather(conv_block, pair_block, halo)
+        prev = nxt = halo
         table = None
     else:
         def every(value):
@@ -710,15 +730,21 @@
         small = ()
     conv_pieces, conv_plan = list(conv_pieces), tuple((None if o is None else tuple(o), f) for o, f in conv_plan)
     xhat, scale, conv_full, table = conv_forward(flags, prev, x, nxt, conv_pieces, conv_plan, small, table, 2, hidden)
+    if fast:
+        (column, over_x, over_y, across), table = lax.optimization_barrier((pair_pieces, table))
+        others = [swap(a, CORE) for a in (column, over_x, over_y)]
+        others, across = lax.optimization_barrier((others, across))
+        pair_pieces = [column, over_x, over_y, across] + others + [swap(across, CORE)]
+        pair_plan = tuple(pair_plan) + tuple((shifted(o, 1, 0), first) for o, first in pair_plan)
     pair_plan = tuple((None if o is None else tuple(o), f) for o, f in pair_plan)
     block_output, grad_hidden, grad_conv, *ffn_grads = ffn(
         flags, x, xhat, scale, og, table, pair_pieces, pair_plan, 2 * SUB, min(1024, hidden), batch, fast
     )
-    grad_prev, grad_next = ends(grad_conv)
-    grads = (flags, prev, x, nxt, grad_conv, grad_prev, grad_next, grad_hidden, conv_full)
+    grads = (flags, prev, x, nxt, grad_conv, grad_hidden, conv_full)
     if fast:
         input_grad, weight_grads = paired(grads, ffn_grads, batch, width, hidden)
     else:
+        grad_prev, grad_next = ends(grad_conv)
         conv_grads = conv_weight_backward(flags, prev, x, nxt, grad_conv, batch, fast)
         input_grad = conv_input_backward(flags, grad_prev, grad_conv, grad_next, grad_hidden, conv_full, 2)
         weight_grads = whole_sums(conv_grads, ffn_grads, batch, seq, width, hidden)
@@ -727,41 +753,45 @@
 
 
 def paired(grads, ffn_grads, batch, width, hidden):
-    flags, prev, x, nxt, grad_conv, grad_prev, grad_next, grad_hidden, conv_full = grads
+    flags, prev, x, nxt, grad_conv, grad_hidden, conv_full = grads
     up_rows = width // 2 + 16
-    ffn_send, ffn_keep = ffn_grads
-    ffn_got = swap(ffn_send, CORE)
-    send, keep = conv_weight_backward(flags, prev, x, nxt, grad_conv, batch, True)
-    ffn_got, grad_prev, send = lax.optimization_barrier((ffn_got, grad_prev, send))
-    got = swap(send, CORE)
+    edge, ffn_send, ffn_keep = ffn_grads
+    ffn_got, grad_prev = swap(ffn_send, CORE), swap(edge, Y)
+    early = 2
+    parts = conv_weight_backward(flags, prev, x, prev, grad_conv, batch, True, 0, early)
+    ffn_got, grad_prev, parts = lax.optimization_barrier((ffn_got, grad_prev, parts))
     up_give, up_keep, down_give, down_keep = first_stage(flags, ffn_keep, ffn_got, up_rows)
     up_got, down_got = swap(up_give, X), swap(down_give, Y)
+    first = after(prev, up_give)
+    send, keep = conv_weight_backward(
+        flags, first, x, first, grad_conv, batch, True, early, KERNEL_TAPS - early, parts
+    )
+    up_got, down_got, send = lax.optimization_barrier((up_got, down_got, send))
+    got = swap(send, CORE)
+    parts = [(up_keep, up_got), (down_keep, down_got)]
+    up_give, up_keep, down_give, down_keep = stage(flags, parts, (1, 0))
+    up_got, down_got = swap(up_give, Y), swap(down_give, X)
     upper_give, upper_keep, lower_give, lower_keep = first_stage(
         flags, keep, after(got, up_give), (KERNEL_TAPS + 1) // 2
     )
     upper_got, lower_got = swap(upper_give, X), swap(lower_give, Y)
-    input_grad = conv_input_backward(
-        flags, grad_prev, after(grad_conv, upper_give), grad_prev, grad_hidden, conv_full, 2
-    )
+    second = after(grad_prev, upper_give)
+    input_grad = conv_input_backward(flags, second, grad_conv, second, grad_hidden, conv_full, 2)
     up_got, down_got, input_grad = lax.optimization_barrier((up_got, down_got, input_grad))
-    parts = [(up_keep, up_got), (down_keep, down_got)]
-    up_give, up_keep, down_give, down_keep = stage(flags, parts, (1, 0))
-    up_got, down_got = swap(up_give, Y), swap(down_give, X)
-    upper_got, lower_got, _ = lax.optimization_barrier((upper_got, lower_got, up_give))
+    ffn_give, ffn_keep = stage(flags, [(up_keep, up_got), (down_keep, down_got)], (2, 2), 1)
+    ffn_got = swap(ffn_give, Z0)
+    upper_got, lower_got, _ = lax.optimization_barrier((upper_got, lower_got, ffn_give))
     parts = [(upper_keep, upper_got), (lower_keep, lower_got)]
     upper_give, upper_keep, lower_give, lower_keep = stage(flags, parts, (1, 0))
     upper_got, lower_got = swap(upper_give, Y), swap(lower_give, X)
-    up_got, down_got, _ = lax.optimization_barrier((up_got, down_got, upper_give))
-    ffn_give, ffn_keep = stage(flags, [(up_keep, up_got), (down_keep, down_got)], (2, 2), 1)
-    ffn_got = swap(ffn_give, Z0)
+    ffn_give, ffn_keep = stage(flags, [(ffn_keep, after(ffn_got, upper_give))], (3,))
+    ffn_got = swap(ffn_give, Z1)
     upper_got, lower_got, _ = lax.optimization_barrier((upper_got, lower_got, ffn_give))
     conv_give, conv_keep = stage(flags, [(upper_keep, upper_got), (lower_keep, lower_got)], (2, 2), 1)
     conv_got = swap(conv_give, Z0)
-    ffn_give, ffn_keep = stage(flags, [(ffn_keep, after(ffn_got, conv_give))], (3,))
-    ffn_got = swap(ffn_give, Z1)
-    conv_give, conv_keep = stage(flags, [(conv_keep, after(conv_got, ffn_give))], (3,))
+    pair_part = ffn_keep + after(ffn_got, conv_give).astype(F32)
+    conv_give, conv_keep = stage(flags, [(conv_keep, conv_got)], (3,))
     conv_got = swap(conv_give, Z1)
-    pair_part = ffn_keep + after(ffn_got, conv_give).astype(F32)
     conv_grad = (conv_keep + conv_got.astype(F32)).transpose(0, 2, 1)
     head = width // 2
     up_grad = pair_part[:head]

time: 222 us -> 210 us (0.946)
  between operations: 14.3 us -> 0.96 us
  waiting for transfers between devices: 55.6 us -> 60 us
  local copies, waits for them, and re-layouts: 8.76 us -> 4.38 us
    ppermute x44 -> x52, waiting for transfers between devices: 53.4 us -> 60 us  [swap(): lax.ppermute(value, axis, [(i, i ^ bit) for i in range(lax.axis_size(axis...]
    unnamed x22 -> x34, local copies, waits for them, and re-layouts: 6.92 us -> 2.52 us
    pallas_call x1 -> x2, Pallas kernels: 13 us -> 14 us  [conv_weight_backward(): pl.pallas_call(functools.partial(conv_weight_kernel, fast, first), grid_s...]
    ppermute x44 -> x52, starting transfers between devices: 38.8 us -> 39.2 us  [swap(): lax.ppermute(value, axis, [(i, i ^ bit) for i in range(lax.axis_size(axis...]
  transfers between devices with their start and end apart: 45 -> 53, of which waited for: 19 -> 25; matrix products, arithmetic and copies ran while one was open for 1% -> 2% of each run, Pallas kernels for 24% -> 24%
where the time goes in v3:
time: 210 us
  Pallas kernels  102 us (49%)
  waiting for transfers between devices  60 us (29%)
  starting transfers between devices  40.9 us (19%)
  local copies, waits for them, and re-layouts  4.38 us (2%)
    ppermute x52, waiting for transfers between devices, swap(): lax.ppermute(value, axis, [(i, i ^ bit) for i in range(lax.axis_size(axis...  60 us
    pallas_call x1, Pallas kernels, ffn(): pl.pallas_call(functools.partial(ffn_kernel, chunk, fast, plan), grid_spe...  48.1 us
    ppermute x52, starting transfers between devices, swap(): lax.ppermute(value, axis, [(i, i ^ bit) for i in range(lax.axis_size(axis...  39.2 us
    pallas_call x1, Pallas kernels, conv_forward(): pl.pallas_call(functools.partial(conv_kernel, subs, plan, small, KERNEL_T...  19.4 us
    pallas_call x2, Pallas kernels, conv_weight_backward(): pl.pallas_call(functools.partial(conv_weight_kernel, fast, first), grid_s...  14 us
    pallas_call x1, Pallas kernels, conv_input_backward(): pl.pallas_call(functools.partial(conv_input_kernel, subs), grid_spec=pltp...  12.3 us
    pallas_call x6, Pallas kernels, stage(): pl.pallas_call(functools.partial(stage_kernel, columns, joined), grid_spe...  4.27 us
  transfers between devices with their start and end apart: 53, of which 25 were waited for; matrix products, arithmetic and copies ran while one was open for 2% of the time, Pallas kernels for 24%

profile of v3, /device:TPU:0, one launch (start us, length us, event | category | flops | bytes accessed | tf_op | source)
XLA Modules:
  0.0 210.2 jit_solution(206935787328667857)
XLA Ops:
  0.6 2.1 pack.1
  2.8 4.1 %collective-permute-start.3 = (bf16[1,10,32,256]{3,2,1,0:T(8,128)(2,1)}, bf16[1,10,32,256]{3,2,1,0:T(8,128)(2,1)S(1)}, u32[]{:S(2)}, u32[]{:S(2)}) collective-permute-start(bf16[1,10,32,256]{3,2,1,0:T(8,128)(2,1)} %get-tuple-element.99), channel_id=1, source_target_pairs={{0,16},{8,24},{16,0},{24,8},{1,17},{9,25},{17,1},{25,9},{2,18},{10... | collective-permute-start | bytes 491528 | tf_op jit(solution)/shard_map/ppermute | solution.py:568
  6.9 1.5 collective-permute-start.2
  8.4 1.5 collective-permute-start.1
  10.4 0.9 constant_dynamic-update-slice_fusion.1
  11.3 5.4 %collective-permute-done.prev.nxt = bf16[128,512]{1,0:T(8,128)(2,1)S(1)} collective-permute-done((bf16[128,512]{1,0:T(8,128)(2,1)}, bf16[128,512]{1,0:T(8,128)(2,1)S(1)}, u32[]{:S(2)}, u32[]{:S(2)}) %collective-permute-start) | collective-permute-done | bytes 131104 | tf_op jit(solution)/shard_map/ppermute | solution.py:568
  16.8 1.6 collective-permute-start.4
  19.0 1.5 collective-permute-start.6
  20.5 1.5 collective-permute-start.5
  22.0 1.2 collective-permute-done.8.rest_5_
  23.2 1.2 collective-permute-start.7
  24.4 3.3 %collective-permute-done.7.rest_4_ = bf16[1,5,32,256]{3,2,1,0:T(8,128)(2,1)S(1)} collective-permute-done((bf16[1,5,32,256]{3,2,1,0:T(8,128)(2,1)S(1)}, bf16[1,5,32,256]{3,2,1,0:T(8,128)(2,1)S(1)}, u32[]{:S(2)}, u32[]{:S(2)}) %collective-permute-start.7) | collective-permute-done | bytes 81952 | tf_op jit(solution)/shard_map/ppermute | solution.py:568
  27.7 1.2 collective-permute-start.10
  29.1 0.8 collective-permute-start.9
  30.0 1.3 collective-permute-start.12
  31.3 0.9 collective-permute-start.11
  32.2 1.1 collective-permute-start.13
  33.3 7.5 %collective-permute-done.12.rest_9_ = bf16[1,5,32,256]{3,2,1,0:T(8,128)(2,1)S(1)} collective-permute-done((bf16[1,5,32,256]{3,2,1,0:T(8,128)(2,1)S(1)}, bf16[1,5,32,256]{3,2,1,0:T(8,128)(2,1)S(1)}, u32[]{:S(2)}, u32[]{:S(2)}) %collective-permute-start.12) | collective-permute-done | bytes 81952 | tf_op jit(solution)/shard_map/ppermute | solution.py:568
  42.0 0.8 collective-permute-done.21.rest_19_
  42.9 0.8 collective-permute-start.15
  43.8 1.0 collective-permute-start.14
  44.8 0.9 pad_maximum_fusion
  46.8 2.6 %collective-permute-done.15.rest_13_ = bf16[2,5,32,256]{3,2,1,0:T(8,128)(2,1)S(1)} collective-permute-done((bf16[2,5,32,256]{3,2,1,0:T(8,128)(2,1)S(1)}, bf16[2,5,32,256]{3,2,1,0:T(8,128)(2,1)S(1)}, u32[]{:S(2)}, u32[]{:S(2)}) %collective-permute-start.15) | collective-permute-done | bytes 163872 | tf_op jit(solution)/shard_map/ppermute | solution.py:568
  50.0 3.8 %collective-permute-done.30 = bf16[2,2,128,256]{3,2,1,0:T(8,128)(2,1)S(1)} collective-permute-done((bf16[2,2,128,256]{3,2,1,0:T(8,128)(2,1)S(1)}, bf16[2,2,128,256]{3,2,1,0:T(8,128)(2,1)S(1)}, u32[]{:S(2)}, u32[]{:S(2)}) %collective-permute-start.30) | collective-permute-done | bytes 262176 | tf_op jit(solution)/shard_map/ppermute | solution.py:568
  53.8 1.3 collective-permute-done.25.rest_23_
  55.1 1.7 collective-permute-start.33
  56.7 0.9 collective-permute-start.32
  57.6 1.0 collective-permute-start.31
  58.6 19.4 %conv_forward.1 = (f32[2048,512]{1,0:T(8,128)}, f32[2048,512]{1,0:T(8,128)}, bf16[9,512,512]{2,1,0:T(8,128)(2,1)}, f32[8,2048]{1,0:T(8,128)S(1)}) custom-call(s32[6,8]{1,0:T(8,128)S(1)} %copy-done.3, bf16[128,512]{1,0:T(8,128)(2,1)S(1)} %collective-permute-done.prev.nxt, bf16[2048,512]{1,0:T(8,128)(2,1)S(1)} %bitcast.33, ...), custom_call_target="tpu_custom_call" | custom-call | flops 9663676416 | bytes 1048576 | tf_op jit(solution)/shard_map/conv_forward/pallas_call | solution.py:201
  78.0 3.2 %collective-permute-done.32.rest_2_ = bf16[4,2,128,256]{3,2,1,0:T(8,128)(2,1)S(1)} collective-permute-done((bf16[4,2,128,256]{3,2,1,0:T(8,128)(2,1)S(1)}, bf16[4,2,128,256]{3,2,1,0:T(8,128)(2,1)S(1)}, u32[]{:S(2)}, u32[]{:S(2)}) %collective-permute-start.32) | collective-permute-done | bytes 524320 | tf_op jit(solution)/shard_map/ppermute | solution.py:568
  81.9 1.3 collective-permute-done.34.rest_4_
  83.2 0.7 collective-permute-done.35.rest_5_
  83.9 0.7 collective-permute-done.36.rest_6_
  84.8 1.8 collective-permute-done.37.rest_7_
  86.6 0.8 copy-done.12
  87.4 48.1 %feed_forward.1 = (bf16[2048,512]{1,0:T(8,128)(2,1)}, f32[2048,512]{1,0:T(8,128)}, bf16[2048,512]{1,0:T(8,128)(2,1)S(1)}, bf16[128,512]{1,0:T(8,128)(2,1)S(1)}, ...) custom-call(s32[6,8]{1,0:T(8,128)S(1)} %copy-done.3, bf16[2048,512]{1,0:T(8,128)(2,1)} %bitcast.32, ...), custom_call_target="tpu_custom_call" | custom-call | flops 25769803776 | bytes 1048576 | tf_op jit(solution)/shard_map/feed_forward/pallas_call | solution.py:356
  135.7 1.0 collective-permute-start.39
  136.7 3.7 %conv_weight_backward.2 = (bf16[4,2,2,9,32,256]{5,4,3,2,1,0:T(8,128)(2,1)S(1)}, bf16[4,2,2,9,32,256]{5,4,3,2,1,0:T(8,128)(2,1)S(1)}) custom-call(s32[6,8]{1,0:T(8,128)S(1)} %copy-done.3, bf16[128,512]{1,0:T(8,128)(2,1)S(1)} %collective-permute-done.prev.nxt, bf16[2048,512]{1,0:T(8,128)(2,1)S(1)} %bitcast.34, ...), custom_call_target="tpu_custom_call" | custom-call | flops 2146959360 | bytes 1048576 | tf_op jit(solution)/shard_map/conv_weight_backward/pallas_call | solution.py:435
  140.5 1.0 collective-permute-done.39.prev.nxt
  141.5 1.1 stage.8
  142.5 1.1 collective-permute-start.40
  143.6 1.2 collective-permute-start.41
  144.8 10.3 %conv_weight_backward.3 = (bf16[4,2,2,9,32,256]{5,4,3,2,1,0:T(8,128)(2,1)S(1)}, bf16[4,2,2,9,32,256]{5,4,3,2,1,0:T(8,128)(2,1)S(1)}) custom-call(s32[6,8]{1,0:T(8,128)S(1)} %copy-done.3, bf16[128,512]{1,0:T(8,128)(2,1)S(1)} %collective-permute-done.prev.nxt, bf16[2048,512]{1,0:T(8,128)(2,1)S(1)} %bitcast.35, ...), custom_call_target="tpu_custom_call", output_to_operand_aliasing={{0}: (5, {}), {1}: (6, {})} | custom-call | flops 7511998464 | bytes 1048576 | tf_op jit(solution)/shard_map/conv_weight_backward/pallas_call | solution.py:435
  155.2 1.5 collective-permute-done.41.refs_3_
  156.7 0.8 stage.9
  157.5 1.1 collective-permute-start.43
  158.6 1.2 collective-permute-start.42
  159.8 1.5 collective-permute-done.44.got
  161.2 1.1 stage.10
  162.3 1.1 collective-permute-start.45
  163.5 1.2 collective-permute-start.46
  164.6 12.3 %conv_input_backward.1 = f32[2048,512]{1,0:T(8,128)} custom-call(s32[6,8]{1,0:T(8,128)S(1)} %copy-done.3, bf16[128,512]{1,0:T(8,128)(2,1)S(1)} %collective-permute-done.39.prev.nxt, bf16[2048,512]{1,0:T(8,128)(2,1)S(1)} %get-tuple-element.132.g, bf16[128,512]{1,0:T(8,128)(2,1)S(1)} %collective-permute-done.39.prev.nxt, f32[2048,512]{1,0:T(8,128)S(1)} %copy-done.4, ...), custom_call_target="tpu_custom_call" | custom-call | flops 9663676416 | bytes 1048576 | tf_op jit(solution)/shard_map/conv_input_backward/pallas_call | solution.py:480
  178.6 1.7 collective-permute-done.45.refs_1_
  180.3 0.8 stage.12
  181.1 1.3 collective-permute-start.47
  182.4 1.0 collective-permute-start.48
  183.4 2.3 %collective-permute-done.49.refs_1_ = bf16[2,528,128]{2,1,0:T(8,128)(2,1)S(1)} collective-permute-done((bf16[2,528,128]{2,1,0:T(8,128)(2,1)S(1)}, bf16[2,528,128]{2,1,0:T(8,128)(2,1)S(1)}, u32[]{:S(2)}, u32[]{:S(2)}) %collective-permute-start.49) | collective-permute-done | bytes 270368 | tf_op jit(solution)/shard_map/ppermute | solution.py:568
  186.3 1.4 collective-permute-start.52
  187.8 2.3 %collective-permute-done.48.refs_3_ = bf16[2,2,4,32,256]{4,3,2,1,0:T(8,128)(2,1)S(1)} collective-permute-done((bf16[2,2,4,32,256]{4,3,2,1,0:T(8,128)(2,1)S(1)}, bf16[2,2,4,32,256]{4,3,2,1,0:T(8,128)(2,1)S(1)}, u32[]{:S(2)}, u32[]{:S(2)}) %collective-permute-start.48) | collective-permute-done | bytes 262176 | tf_op jit(solution)/shard_map/ppermute | solution.py:568
  191.7 2.6 %collective-permute-done.52 = bf16[528,128]{1,0:T(8,128)(2,1)S(1)} collective-permute-done((bf16[528,128]{1,0:T(8,128)(2,1)S(1)}, bf16[528,128]{1,0:T(8,128)(2,1)S(1)}, u32[]{:S(2)}, u32[]{:S(2)}) %collective-permute-start.52) | collective-permute-done | bytes 135200 | tf_op jit(solution)/shard_map/ppermute | solution.py:568
  195.0 0.8 copy.27
  196.4 4.2 %collective-permute-done.50.refs_1_ = bf16[2,9,32,256]{3,2,1,0:T(8,128)(2,1)S(1)} collective-permute-done((bf16[2,9,32,256]{3,2,1,0:T(8,128)(2,1)S(1)}, bf16[2,9,32,256]{3,2,1,0:T(8,128)(2,1)S(1)}, u32[]{:S(2)}, u32[]{:S(2)}) %collective-permute-start.50) | collective-permute-done | bytes 294944 | tf_op jit(solution)/shard_map/ppermute | solution.py:568
  201.9 7.6 %collective-permute-done.51 = bf16[9,32,256]{2,1,0:T(8,128)(2,1)S(1)} collective-permute-done((bf16[9,32,256]{2,1,0:T(8,128)(2,1)S(1)}, bf16[9,32,256]{2,1,0:T(8,128)(2,1)S(1)}, u32[]{:S(2)}, u32[]{:S(2)}) %collective-permute-start.51) | collective-permute-done | bytes 147488 | tf_op jit(solution)/shard_map/ppermute | solution.py:568
  209.4 0.7 add_bitcast_fusion
  (105 shorter events, 12.0 us)
Async XLA Ops:
  2.7 44.0 %copy-start.5 = (bf16[1,2,128,256]{3,2,1,0:T(8,128)(2,1)S(1)}, bf16[1,2,128,256]{3,2,1,0:T(8,128)(2,1)}, u32[]{:S(2)}) copy-start(bf16[1,2,128,256]{3,2,1,0:T(8,128)(2,1)} %get-tuple-element.110) | copy-start | bytes 393220
  2.7 55.9 %copy-start = (bf16[1,2048,512]{2,1,0:T(8,128)(2,1)S(1)}, bf16[1,2048,512]{2,1,0:T(8,128)(2,1)}, u32[]{:S(2)}) copy-start(bf16[1,2048,512]{2,1,0:T(8,128)(2,1)} %param.13) | copy-start | bytes 6291460
  2.7 55.8 %copy-start.3 = (s32[6,8]{1,0:T(8,128)S(1)}, s32[6,8]{1,0:T(8,128)}, u32[]{:S(2)}) copy-start(s32[6,8]{1,0:T(8,128)} %get-tuple-element.97.flags) | copy-start | bytes 580
  2.8 14.0 %collective-permute-start.3 = (bf16[1,10,32,256]{3,2,1,0:T(8,128)(2,1)}, bf16[1,10,32,256]{3,2,1,0:T(8,128)(2,1)S(1)}, u32[]{:S(2)}, u32[]{:S(2)}) collective-permute-start(bf16[1,10,32,256]{3,2,1,0:T(8,128)(2,1)} %get-tuple-element.99), channel_id=1, source_target_pairs={{0,16},{8,24},{16,0},{24,8},{1,17},{9,25},{17,1},{25,9},{2,18},{10... | collective-permute-start | bytes 491528 | tf_op jit(solution)/shard_map/ppermute | solution.py:568
  6.9 9.9 %collective-permute-start.2 = (bf16[1,10,32,256]{3,2,1,0:T(8,128)(2,1)}, bf16[1,10,32,256]{3,2,1,0:T(8,128)(2,1)S(1)}, u32[]{:S(2)}, u32[]{:S(2)}) collective-permute-start(bf16[1,10,32,256]{3,2,1,0:T(8,128)(2,1)} %get-tuple-element.99), channel_id=1, source_target_pairs={{0,4},{4,0},{1,5},{5,1},{2,6},{6,2},{3,7},{7,3},{8,12},{12,8},{9,1... | collective-permute-start | bytes 491528 | tf_op jit(solution)/shard_map/ppermute | solution.py:568
  8.4 8.4 %collective-permute-start.1 = (bf16[1,10,32,256]{3,2,1,0:T(8,128)(2,1)}, bf16[1,10,32,256]{3,2,1,0:T(8,128)(2,1)S(1)}, u32[]{:S(2)}, u32[]{:S(2)}) collective-permute-start(bf16[1,10,32,256]{3,2,1,0:T(8,128)(2,1)} %get-tuple-element.99), channel_id=1, source_target_pairs={{0,1},{1,0},{2,3},{3,2},{4,5},{5,4},{6,7},{7,6},{8,9},{9,8},{10,11... | collective-permute-start | bytes 491528 | tf_op jit(solution)/shard_map/ppermute | solution.py:568
  9.9 6.9 %collective-permute-start = (bf16[128,512]{1,0:T(8,128)(2,1)}, bf16[128,512]{1,0:T(8,128)(2,1)S(1)}, u32[]{:S(2)}, u32[]{:S(2)}) collective-permute-start(bf16[128,512]{1,0:T(8,128)(2,1)} %get-tuple-element.98), channel_id=1, source_target_pairs={{0,1},{1,0},{2,3},{3,2},{4,5},{5,4},{6,7},{7,6},{8,9},{9,8},{10,11... | collective-permute-start | bytes 393224 | tf_op jit(solution)/shard_map/ppermute | solution.py:568
  16.8 10.9 %collective-permute-start.4 = (bf16[2,10,32,256]{3,2,1,0:T(8,128)(2,1)S(1)}, bf16[2,10,32,256]{3,2,1,0:T(8,128)(2,1)S(1)}, u32[]{:S(2)}, u32[]{:S(2)}) collective-permute-start(bf16[2,10,32,256]{3,2,1,0:T(8,128)(2,1)S(1)} %constant_dynamic-update-slice_fusion.rest_0_), channel_id=1, source_target_pairs={{0,8},{8,0},{16,24},{24,16},{1,9},{9,1},{17,25},{25,17},{2,10},{10... | collective-permute-start | bytes 983048 | tf_op jit(solution)/shard_map/ppermute | solution.py:568
  18.4 4.8 %collective-permute-start.8 = (bf16[1,5,32,256]{3,2,1,0:T(8,128)(2,1)S(1)}, bf16[1,5,32,256]{3,2,1,0:T(8,128)(2,1)S(1)}, u32[]{:S(2)}, u32[]{:S(2)}) collective-permute-start(bf16[1,5,32,256]{3,2,1,0:T(8,128)(2,1)S(1)} %slice.46), channel_id=1, source_target_pairs={{0,4},{4,0},{1,5},{5,1},{2,6},{6,2},{3,7},{7,3},{8,12},{12,8},{9,1... | collective-permute-start | bytes 245768 | tf_op jit(solution)/shard_map/ppermute | solution.py:568
  19.0 8.7 %collective-permute-start.6 = (bf16[1,10,32,256]{3,2,1,0:T(8,128)(2,1)S(1)}, bf16[1,10,32,256]{3,2,1,0:T(8,128)(2,1)S(1)}, u32[]{:S(2)}, u32[]{:S(2)}) collective-permute-start(bf16[1,10,32,256]{3,2,1,0:T(8,128)(2,1)S(1)} %collective-permute-done.3), channel_id=1, source_target_pairs={{0,1},{1,0},{2,3},{3,2},{4,5},{5,4},{6,7},{7,6},{8,9},{9,8},{10,11... | collective-permute-start | bytes 491528 | tf_op jit(solution)/shard_map/ppermute | solution.py:568
  20.5 7.2 %collective-permute-start.5 = (bf16[1,10,32,256]{3,2,1,0:T(8,128)(2,1)S(1)}, bf16[1,10,32,256]{3,2,1,0:T(8,128)(2,1)S(1)}, u32[]{:S(2)}, u32[]{:S(2)}) collective-permute-start(bf16[1,10,32,256]{3,2,1,0:T(8,128)(2,1)S(1)} %collective-permute-done.3), channel_id=1, source_target_pairs={{0,4},{4,0},{1,5},{5,1},{2,6},{6,2},{3,7},{7,3},{8,12},{12,8},{9,1... | collective-permute-start | bytes 491528 | tf_op jit(solution)/shard_map/ppermute | solution.py:568
  22.0 10.2 %collective-permute-start.16 = (bf16[2,10,32,256]{3,2,1,0:T(8,128)(2,1)S(1)}, bf16[2,10,32,256]{3,2,1,0:T(8,128)(2,1)S(1)}, u32[]{:S(2)}, u32[]{:S(2)}) collective-permute-start(bf16[2,10,32,256]{3,2,1,0:T(8,128)(2,1)S(1)} %constant_dynamic-update-slice_fusion.rest_0_), channel_id=1, source_target_pairs={{0,2},{2,0},{1,3},{3,1},{4,6},{6,4},{5,7},{7,5},{8,10},{10,8},{9,1... | collective-permute-start | bytes 983048 | tf_op jit(solution)/shard_map/ppermute | solution.py:568
  23.2 4.4 %collective-permute-start.7 = (bf16[1,5,32,256]{3,2,1,0:T(8,128)(2,1)S(1)}, bf16[1,5,32,256]{3,2,1,0:T(8,128)(2,1)S(1)}, u32[]{:S(2)}, u32[]{:S(2)}) collective-permute-start(bf16[1,5,32,256]{3,2,1,0:T(8,128)(2,1)S(1)} %slice.45), channel_id=1, source_target_pairs={{0,1},{1,0},{2,3},{3,2},{4,5},{5,4},{6,7},{7,6},{8,9},{9,8},{10,11... | collective-permute-start | bytes 245768 | tf_op jit(solution)/shard_map/ppermute | solution.py:568
  27.7 2.3 %collective-permute-start.18 = (bf16[1,10,32,256]{3,2,1,0:T(8,128)(2,1)S(1)}, bf16[1,10,32,256]{3,2,1,0:T(8,128)(2,1)S(1)}, u32[]{:S(2)}, u32[]{:S(2)}) collective-permute-start(bf16[1,10,32,256]{3,2,1,0:T(8,128)(2,1)S(1)} %collective-permute-done.2.rest_2_), channel_id=1, source_target_pairs={{0,2},{2,0},{1,3},{3,1},{4,6},{6,4},{5,7},{7,5},{8,10},{10,8},{9,1... | collective-permute-start | bytes 491528 | tf_op jit(solution)/shard_map/ppermute | solution.py:568
  27.7 13.7 %collective-permute-start.10 = (bf16[2,10,32,256]{3,2,1,0:T(8,128)(2,1)S(1)}, bf16[2,10,32,256]{3,2,1,0:T(8,128)(2,1)S(1)}, u32[]{:S(2)}, u32[]{:S(2)}) collective-permute-start(bf16[2,10,32,256]{3,2,1,0:T(8,128)(2,1)S(1)} %collective-permute-done.4.rest_1_), channel_id=1, source_target_pairs={{0,1},{1,0},{2,3},{3,2},{4,5},{5,4},{6,7},{7,6},{8,9},{9,8},{10,11... | collective-permute-start | bytes 983048 | tf_op jit(solution)/shard_map/ppermute | solution.py:568
  28.9 2.3 %collective-permute-start.19 = (bf16[1,10,32,256]{3,2,1,0:T(8,128)(2,1)S(1)}, bf16[1,10,32,256]{3,2,1,0:T(8,128)(2,1)S(1)}, u32[]{:S(2)}, u32[]{:S(2)}) collective-permute-start(bf16[1,10,32,256]{3,2,1,0:T(8,128)(2,1)S(1)} %collective-permute-done.1.rest_3_), channel_id=1, source_target_pairs={{0,2},{2,0},{1,3},{3,1},{4,6},{6,4},{5,7},{7,5},{8,10},{10,8},{9,1... | collective-permute-start | bytes 491528 | tf_op jit(solution)/shard_map/ppermute | solution.py:568
  29.1 12.7 %collective-permute-start.9 = (bf16[2,10,32,256]{3,2,1,0:T(8,128)(2,1)S(1)}, bf16[2,10,32,256]{3,2,1,0:T(8,128)(2,1)S(1)}, u32[]{:S(2)}, u32[]{:S(2)}) collective-permute-start(bf16[2,10,32,256]{3,2,1,0:T(8,128)(2,1)S(1)} %collective-permute-done.4.rest_1_), channel_id=1, source_target_pairs={{0,4},{4,0},{1,5},{5,1},{2,6},{6,2},{3,7},{7,3},{8,12},{12,8},{9,1... | collective-permute-start | bytes 983048 | tf_op jit(solution)/shard_map/ppermute | solution.py:568
  30.0 10.8 %collective-permute-start.12 = (bf16[1,5,32,256]{3,2,1,0:T(8,128)(2,1)S(1)}, bf16[1,5,32,256]{3,2,1,0:T(8,128)(2,1)S(1)}, u32[]{:S(2)}, u32[]{:S(2)}) collective-permute-start(bf16[1,5,32,256]{3,2,1,0:T(8,128)(2,1)S(1)} %slice.48), channel_id=1, source_target_pairs={{0,4},{4,0},{1,5},{5,1},{2,6},{6,2},{3,7},{7,3},{8,12},{12,8},{9,1... | collective-permute-start | bytes 245768 | tf_op jit(solution)/shard_map/ppermute | solution.py:568
  31.3 9.6 %collective-permute-start.11 = (bf16[1,5,32,256]{3,2,1,0:T(8,128)(2,1)S(1)}, bf16[1,5,32,256]{3,2,1,0:T(8,128)(2,1)S(1)}, u32[]{:S(2)}, u32[]{:S(2)}) collective-permute-start(bf16[1,5,32,256]{3,2,1,0:T(8,128)(2,1)S(1)} %slice.47), channel_id=1, source_target_pairs={{0,1},{1,0},{2,3},{3,2},{4,5},{5,4},{6,7},{7,6},{8,9},{9,8},{10,11... | collective-permute-start | bytes 245768 | tf_op jit(solution)/shard_map/ppermute | solution.py:568
  32.2 9.1 %collective-permute-start.13 = (bf16[1,2,128,256]{3,2,1,0:T(8,128)(2,1)}, bf16[1,2,128,256]{3,2,1,0:T(8,128)(2,1)S(1)}, u32[]{:S(2)}, u32[]{:S(2)}) collective-permute-start(bf16[1,2,128,256]{3,2,1,0:T(8,128)(2,1)} %get-tuple-element.110), channel_id=1, source_target_pairs={{0,16},{8,24},{16,0},{24,8},{1,17},{9,25},{17,1},{25,9},{2,18},{10... | collective-permute-start | bytes 393224 | tf_op jit(solution)/shard_map/ppermute | solution.py:568
  40.8 5.4 %collective-permute-start.17 = (bf16[2,10,32,256]{3,2,1,0:T(8,128)(2,1)S(1)}, bf16[2,10,32,256]{3,2,1,0:T(8,128)(2,1)S(1)}, u32[]{:S(2)}, u32[]{:S(2)}) collective-permute-start(bf16[2,10,32,256]{3,2,1,0:T(8,128)(2,1)S(1)} %collective-permute-done.4.rest_1_), channel_id=1, source_target_pairs={{0,2},{2,0},{1,3},{3,1},{4,6},{6,4},{5,7},{7,5},{8,10},{10,8},{9,1... | collective-permute-start | bytes 983048 | tf_op jit(solution)/shard_map/ppermute | solution.py:568
  40.8 3.0 %collective-permute-start.22 = (bf16[1,10,32,256]{3,2,1,0:T(8,128)(2,1)S(1)}, bf16[1,10,32,256]{3,2,1,0:T(8,128)(2,1)S(1)}, u32[]{:S(2)}, u32[]{:S(2)}) collective-permute-start(bf16[1,10,32,256]{3,2,1,0:T(8,128)(2,1)S(1)} %collective-permute-done.5.rest_6_), channel_id=1, source_target_pairs={{0,2},{2,0},{1,3},{3,1},{4,6},{6,4},{5,7},{7,5},{8,10},{10,8},{9,1... | collective-permute-start | bytes 491528 | tf_op jit(solution)/shard_map/ppermute | solution.py:568
  41.3 1.5 collective-permute-start.21
  41.4 1.5 collective-permute-start.20
  41.8 3.9 %collective-permute-start.23 = (bf16[1,10,32,256]{3,2,1,0:T(8,128)(2,1)S(1)}, bf16[1,10,32,256]{3,2,1,0:T(8,128)(2,1)S(1)}, u32[]{:S(2)}, u32[]{:S(2)}) collective-permute-start(bf16[1,10,32,256]{3,2,1,0:T(8,128)(2,1)S(1)} %collective-permute-done.6.rest_7_), channel_id=1, source_target_pairs={{0,2},{2,0},{1,3},{3,1},{4,6},{6,4},{5,7},{7,5},{8,10},{10,8},{9,1... | collective-permute-start | bytes 491528 | tf_op jit(solution)/shard_map/ppermute | solution.py:568
  42.8 3.5 %collective-permute-start.24 = (bf16[1,5,32,256]{3,2,1,0:T(8,128)(2,1)S(1)}, bf16[1,5,32,256]{3,2,1,0:T(8,128)(2,1)S(1)}, u32[]{:S(2)}, u32[]{:S(2)}) collective-permute-start(bf16[1,5,32,256]{3,2,1,0:T(8,128)(2,1)S(1)} %collective-permute-done.11.rest_8_), channel_id=1, source_target_pairs={{0,2},{2,0},{1,3},{3,1},{4,6},{6,4},{5,7},{7,5},{8,10},{10,8},{9,1... | collective-permute-start | bytes 245768 | tf_op jit(solution)/shard_map/ppermute | solution.py:568
  42.9 6.5 %collective-permute-start.15 = (bf16[2,5,32,256]{3,2,1,0:T(8,128)(2,1)S(1)}, bf16[2,5,32,256]{3,2,1,0:T(8,128)(2,1)S(1)}, u32[]{:S(2)}, u32[]{:S(2)}) collective-permute-start(bf16[2,5,32,256]{3,2,1,0:T(8,128)(2,1)S(1)} %slice.50), channel_id=1, source_target_pairs={{0,4},{4,0},{1,5},{5,1},{2,6},{6,2},{3,7},{7,3},{8,12},{12,8},{9,1... | collective-permute-start | bytes 491528 | tf_op jit(solution)/shard_map/ppermute | solution.py:568
  43.8 6.2 %collective-permute-start.14 = (bf16[2,5,32,256]{3,2,1,0:T(8,128)(2,1)S(1)}, bf16[2,5,32,256]{3,2,1,0:T(8,128)(2,1)S(1)}, u32[]{:S(2)}, u32[]{:S(2)}) collective-permute-start(bf16[2,5,32,256]{3,2,1,0:T(8,128)(2,1)S(1)} %slice.49), channel_id=1, source_target_pairs={{0,1},{1,0},{2,3},{3,2},{4,5},{5,4},{6,7},{7,6},{8,9},{9,8},{10,11... | collective-permute-start | bytes 491528 | tf_op jit(solution)/shard_map/ppermute | solution.py:568
  45.7 8.1 %collective-permute-start.30 = (bf16[2,2,128,256]{3,2,1,0:T(8,128)(2,1)S(1)}, bf16[2,2,128,256]{3,2,1,0:T(8,128)(2,1)S(1)}, u32[]{:S(2)}, u32[]{:S(2)}) collective-permute-start(bf16[2,2,128,256]{3,2,1,0:T(8,128)(2,1)S(1)} %pad_maximum_fusion), channel_id=1, source_target_pairs={{0,8},{8,0},{16,24},{24,16},{1,9},{9,1},{17,25},{25,17},{2,10},{10... | collective-permute-start | bytes 786440 | tf_op jit(solution)/shard_map/ppermute | solution.py:568
  46.2 12.3 %collective-permute-start.26 = (bf16[2,10,32,256]{3,2,1,0:T(8,128)(2,1)S(1)}, bf16[2,10,32,256]{3,2,1,0:T(8,128)(2,1)S(1)}, u32[]{:S(2)}, u32[]{:S(2)}) collective-permute-start(bf16[2,10,32,256]{3,2,1,0:T(8,128)(2,1)S(1)} %collective-permute-done.9.rest_10_), channel_id=1, source_target_pairs={{0,2},{2,0},{1,3},{3,1},{4,6},{6,4},{5,7},{7,5},{8,10},{10,8},{9,1... | collective-permute-start | bytes 983048 | tf_op jit(solution)/shard_map/ppermute | solution.py:568
  46.3 12.3 %collective-permute-start.27 = (bf16[2,10,32,256]{3,2,1,0:T(8,128)(2,1)S(1)}, bf16[2,10,32,256]{3,2,1,0:T(8,128)(2,1)S(1)}, u32[]{:S(2)}, u32[]{:S(2)}) collective-permute-start(bf16[2,10,32,256]{3,2,1,0:T(8,128)(2,1)S(1)} %collective-permute-done.10.rest_11_), channel_id=1, source_target_pairs={{0,2},{2,0},{1,3},{3,1},{4,6},{6,4},{5,7},{7,5},{8,10},{10,8},{9,1... | collective-permute-start | bytes 983048 | tf_op jit(solution)/shard_map/ppermute | solution.py:568
  49.4 7.3 %collective-permute-start.29 = (bf16[2,5,32,256]{3,2,1,0:T(8,128)(2,1)S(1)}, bf16[2,5,32,256]{3,2,1,0:T(8,128)(2,1)S(1)}, u32[]{:S(2)}, u32[]{:S(2)}) collective-permute-start(bf16[2,5,32,256]{3,2,1,0:T(8,128)(2,1)S(1)} %collective-permute-done.15.rest_13_), channel_id=1, source_target_pairs={{0,2},{2,0},{1,3},{3,1},{4,6},{6,4},{5,7},{7,5},{8,10},{10,8},{9,1... | collective-permute-start | bytes 491528 | tf_op jit(solution)/shard_map/ppermute | solution.py:568
  50.0 7.6 %collective-permute-start.28 = (bf16[2,5,32,256]{3,2,1,0:T(8,128)(2,1)S(1)}, bf16[2,5,32,256]{3,2,1,0:T(8,128)(2,1)S(1)}, u32[]{:S(2)}, u32[]{:S(2)}) collective-permute-start(bf16[2,5,32,256]{3,2,1,0:T(8,128)(2,1)S(1)} %collective-permute-done.14.rest_12_), channel_id=1, source_target_pairs={{0,2},{2,0},{1,3},{3,1},{4,6},{6,4},{5,7},{7,5},{8,10},{10,8},{9,1... | collective-permute-start | bytes 491528 | tf_op jit(solution)/shard_map/ppermute | solution.py:568
  53.8 1.3 collective-permute-start.25
  55.1 22.9 %collective-permute-start.33 = (bf16[4,2,128,256]{3,2,1,0:T(8,128)(2,1)S(1)}, bf16[4,2,128,256]{3,2,1,0:T(8,128)(2,1)S(1)}, u32[]{:S(2)}, u32[]{:S(2)}) collective-permute-start(bf16[4,2,128,256]{3,2,1,0:T(8,128)(2,1)S(1)} %constant_dynamic-update-slice_fusion.2.rest_0_), channel_id=1, source_target_pairs={{0,5},{1,4},{4,1},{5,0},{2,7},{3,6},{6,3},{7,2},{8,13},{9,12},{12,... | collective-permute-start | bytes 1572872 | tf_op jit(solution)/shard_map/ppermute | solution.py:613
  56.7 24.5 %collective-permute-start.32 = (bf16[4,2,128,256]{3,2,1,0:T(8,128)(2,1)S(1)}, bf16[4,2,128,256]{3,2,1,0:T(8,128)(2,1)S(1)}, u32[]{:S(2)}, u32[]{:S(2)}) collective-permute-start(bf16[4,2,128,256]{3,2,1,0:T(8,128)(2,1)S(1)} %constant_dynamic-update-slice_fusion.2.rest_0_), channel_id=1, source_target_pairs={{0,1},{1,0},{2,3},{3,2},{4,5},{5,4},{6,7},{7,6},{8,9},{9,8},{10,11... | collective-permute-start | bytes 1572872 | tf_op jit(solution)/shard_map/ppermute | solution.py:568
  57.6 23.6 %collective-permute-start.31 = (bf16[4,2,128,256]{3,2,1,0:T(8,128)(2,1)S(1)}, bf16[4,2,128,256]{3,2,1,0:T(8,128)(2,1)S(1)}, u32[]{:S(2)}, u32[]{:S(2)}) collective-permute-start(bf16[4,2,128,256]{3,2,1,0:T(8,128)(2,1)S(1)} %constant_dynamic-update-slice_fusion.2.rest_0_), channel_id=1, source_target_pairs={{0,4},{4,0},{1,5},{5,1},{2,6},{6,2},{3,7},{7,3},{8,12},{12,8},{9,1... | collective-permute-start | bytes 1572872 | tf_op jit(solution)/shard_map/ppermute | solution.py:568
  78.0 8.6 %copy-start.6 = (bf16[4,2,128,256]{3,2,1,0:T(8,128)(2,1)}, bf16[4,2,128,256]{3,2,1,0:T(8,128)(2,1)S(1)}, u32[]{:S(2)}) copy-start(bf16[4,2,128,256]{3,2,1,0:T(8,128)(2,1)S(1)} %collective-permute-done.33.rest_3_) | copy-start | bytes 1572868
  81.2 5.4 %copy-start.7 = (bf16[4,2,128,256]{3,2,1,0:T(8,128)(2,1)}, bf16[4,2,128,256]{3,2,1,0:T(8,128)(2,1)S(1)}, u32[]{:S(2)}) copy-start(bf16[4,2,128,256]{3,2,1,0:T(8,128)(2,1)S(1)} %collective-permute-done.32.rest_2_) | copy-start | bytes 1572868
  81.2 5.4 %copy-start.8 = (bf16[4,2,128,256]{3,2,1,0:T(8,128)(2,1)}, bf16[4,2,128,256]{3,2,1,0:T(8,128)(2,1)S(1)}, u32[]{:S(2)}) copy-start(bf16[4,2,128,256]{3,2,1,0:T(8,128)(2,1)S(1)} %collective-permute-done.31.rest_1_) | copy-start | bytes 1572868
  81.2 2.0 collective-permute-start.34
  81.3 2.6 %collective-permute-start.35 = (bf16[4,2,128,256]{3,2,1,0:T(8,128)(2,1)S(1)}, bf16[4,2,128,256]{3,2,1,0:T(8,128)(2,1)S(1)}, u32[]{:S(2)}, u32[]{:S(2)}) collective-permute-start(bf16[4,2,128,256]{3,2,1,0:T(8,128)(2,1)S(1)} %collective-permute-done.31.rest_1_), channel_id=1, source_target_pairs={{0,2},{2,0},{1,3},{3,1},{4,6},{6,4},{5,7},{7,5},{8,10},{10,8},{9,1... | collective-permute-start | bytes 1572872 | tf_op jit(solution)/shard_map/ppermute | solution.py:568
  81.8 2.9 %collective-permute-start.36 = (bf16[4,2,128,256]{3,2,1,0:T(8,128)(2,1)S(1)}, bf16[4,2,128,256]{3,2,1,0:T(8,128)(2,1)S(1)}, u32[]{:S(2)}, u32[]{:S(2)}) collective-permute-start(bf16[4,2,128,256]{3,2,1,0:T(8,128)(2,1)S(1)} %collective-permute-done.32.rest_2_), channel_id=1, source_target_pairs={{0,2},{2,0},{1,3},{3,1},{4,6},{6,4},{5,7},{7,5},{8,10},{10,8},{9,1... | collective-permute-start | bytes 1572872 | tf_op jit(solution)/shard_map/ppermute | solution.py:568
  83.2 3.4 %copy-start.9 = (bf16[4,2,128,256]{3,2,1,0:T(8,128)(2,1)}, bf16[4,2,128,256]{3,2,1,0:T(8,128)(2,1)S(1)}, u32[]{:S(2)}) copy-start(bf16[4,2,128,256]{3,2,1,0:T(8,128)(2,1)S(1)} %collective-permute-done.34.rest_4_) | copy-start | bytes 1572868
  84.7 1.9 collective-permute-start.37
  87.4 49.3 %copy-start.1 = (bf16[1,2048,512]{2,1,0:T(8,128)(2,1)S(1)}, bf16[1,2048,512]{2,1,0:T(8,128)(2,1)}, u32[]{:S(2)}) copy-start(bf16[1,2048,512]{2,1,0:T(8,128)(2,1)} %param.13) | copy-start | bytes 6291460
  135.5 6.0 %collective-permute-start.38 = (bf16[4,2,2,528,128]{4,3,2,1,0:T(8,128)(2,1)}, bf16[4,2,2,528,128]{4,3,2,1,0:T(8,128)(2,1)S(1)}, u32[]{:S(2)}, u32[]{:S(2)}) collective-permute-start(bf16[4,2,2,528,128]{4,3,2,1,0:T(8,128)(2,1)} %get-tuple-element.130), channel_id=1, source_target_pairs={{0,2},{2,0},{1,3},{3,1},{4,6},{6,4},{5,7},{7,5},{8,10},{10,8},{9,1... | collective-permute-start | bytes 6488072 | tf_op jit(solution)/shard_map/ppermute | solution.py:568
  135.7 5.8 %collective-permute-start.39 = (bf16[128,512]{1,0:T(8,128)(2,1)S(1)}, bf16[128,512]{1,0:T(8,128)(2,1)S(1)}, u32[]{:S(2)}, u32[]{:S(2)}) collective-permute-start(bf16[128,512]{1,0:T(8,128)(2,1)S(1)} %get-tuple-element.131), channel_id=1, source_target_pairs={{0,1},{1,0},{2,3},{3,2},{4,5},{5,4},{6,7},{7,6},{8,9},{9,8},{10,11... | collective-permute-start | bytes 393224 | tf_op jit(solution)/shard_map/ppermute | solution.py:568
  136.7 4.7 %copy-start.2 = (bf16[4,2,2,528,128]{4,3,2,1,0:T(8,128)(2,1)S(1)}, bf16[4,2,2,528,128]{4,3,2,1,0:T(8,128)(2,1)}, u32[]{:S(2)}) copy-start(bf16[4,2,2,528,128]{4,3,2,1,0:T(8,128)(2,1)} %get-tuple-element.129.keep) | copy-start | bytes 6488068
  141.5 23.2 %slice-start = ((s8[4718592]{0:T(1024)(128)(4,1)}), s8[4194304]{0:T(1024)(128)(4,1)S(1)}, s32[]{:S(2)}) async-start(s8[4718592]{0:T(1024)(128)(4,1)} %bitcast.36), calls=%async_computation | async-start | bytes 8388608
  142.5 14.2 %collective-permute-start.40 = (bf16[2,2,2,272,128]{4,3,2,1,0:T(8,128)(2,1)S(1)}, bf16[2,2,2,272,128]{4,3,2,1,0:T(8,128)(2,1)S(1)}, u32[]{:S(2)}, u32[]{:S(2)}) collective-permute-start(bf16[2,2,2,272,128]{4,3,2,1,0:T(8,128)(2,1)S(1)} %get-tuple-element.137), channel_id=1, source_target_pairs={{0,4},{4,0},{1,5},{5,1},{2,6},{6,2},{3,7},{7,3},{8,12},{12,8},{9,1... | collective-permute-start | bytes 1671176 | tf_op jit(solution)/shard_map/ppermute | solution.py:568
  143.6 21.0 %slice-start.1 = ((s8[4718592]{0:T(1024)(128)(4,1)}), s8[524288]{0:T(1024)(128)(4,1)S(1)}, s32[]{:S(2)}) async-start(s8[4718592]{0:T(1024)(128)(4,1)} %bitcast.36), calls=%async_computation.1 | async-start | bytes 1048576
  143.6 13.1 %collective-permute-start.41 = (bf16[2,2,2,256,128]{4,3,2,1,0:T(8,128)(2,1)S(1)}, bf16[2,2,2,256,128]{4,3,2,1,0:T(8,128)(2,1)S(1)}, u32[]{:S(2)}, u32[]{:S(2)}) collective-permute-start(bf16[2,2,2,256,128]{4,3,2,1,0:T(8,128)(2,1)S(1)} %get-tuple-element.138), channel_id=1, source_target_pairs={{0,1},{1,0},{2,3},{3,2},{4,5},{5,4},{6,7},{7,6},{8,9},{9,8},{10,11... | collective-permute-start | bytes 1572872 | tf_op jit(solution)/shard_map/ppermute | solution.py:568
  156.7 4.5 %collective-permute-start.44 = (bf16[4,2,2,9,32,256]{5,4,3,2,1,0:T(8,128)(2,1)S(1)}, bf16[4,2,2,9,32,256]{5,4,3,2,1,0:T(8,128)(2,1)S(1)}, u32[]{:S(2)}, u32[]{:S(2)}) collective-permute-start(bf16[4,2,2,9,32,256]{5,4,3,2,1,0:T(8,128)(2,1)S(1)} %get-tuple-element.150), channel_id=1, source_target_pairs={{0,2},{2,0},{1,3},{3,1},{4,6},{6,4},{5,7},{7,5},{8,10},{10,8},{9,1... | collective-permute-start | bytes 7077896 | tf_op jit(solution)/shard_map/ppermute | solution.py:568
  157.5 19.4 %collective-permute-start.43 = (bf16[2,2,256,128]{3,2,1,0:T(8,128)(2,1)S(1)}, bf16[2,2,256,128]{3,2,1,0:T(8,128)(2,1)S(1)}, u32[]{:S(2)}, u32[]{:S(2)}) collective-permute-start(bf16[2,2,256,128]{3,2,1,0:T(8,128)(2,1)S(1)} %get-tuple-element.147), channel_id=1, source_target_pairs={{0,4},{4,0},{1,5},{5,1},{2,6},{6,2},{3,7},{7,3},{8,12},{12,8},{9,1... | collective-permute-start | bytes 786440 | tf_op jit(solution)/shard_map/ppermute | solution.py:568
  158.6 18.3 %collective-permute-start.42 = (bf16[2,2,272,128]{3,2,1,0:T(8,128)(2,1)S(1)}, bf16[2,2,272,128]{3,2,1,0:T(8,128)(2,1)S(1)}, u32[]{:S(2)}, u32[]{:S(2)}) collective-permute-start(bf16[2,2,272,128]{3,2,1,0:T(8,128)(2,1)S(1)} %get-tuple-element.146), channel_id=1, source_target_pairs={{0,1},{1,0},{2,3},{3,2},{4,5},{5,4},{6,7},{7,6},{8,9},{9,8},{10,11... | collective-permute-start | bytes 835592 | tf_op jit(solution)/shard_map/ppermute | solution.py:568
  162.3 18.0 %collective-permute-start.45 = (bf16[2,2,2,5,32,256]{5,4,3,2,1,0:T(8,128)(2,1)S(1)}, bf16[2,2,2,5,32,256]{5,4,3,2,1,0:T(8,128)(2,1)S(1)}, u32[]{:S(2)}, u32[]{:S(2)}) collective-permute-start(bf16[2,2,2,5,32,256]{5,4,3,2,1,0:T(8,128)(2,1)S(1)} %get-tuple-element.152), channel_id=1, source_target_pairs={{0,4},{4,0},{1,5},{5,1},{2,6},{6,2},{3,7},{7,3},{8,12},{12,8},{9,1... | collective-permute-start | bytes 1966088 | tf_op jit(solution)/shard_map/ppermute | solution.py:568
  163.5 15.2 %collective-permute-start.46 = (bf16[2,2,2,4,32,256]{5,4,3,2,1,0:T(8,128)(2,1)S(1)}, bf16[2,2,2,4,32,256]{5,4,3,2,1,0:T(8,128)(2,1)S(1)}, u32[]{:S(2)}, u32[]{:S(2)}) collective-permute-start(bf16[2,2,2,4,32,256]{5,4,3,2,1,0:T(8,128)(2,1)S(1)} %get-tuple-element.158), channel_id=1, source_target_pairs={{0,1},{1,0},{2,3},{3,2},{4,5},{5,4},{6,7},{7,6},{8,9},{9,8},{10,11... | collective-permute-start | bytes 1572872 | tf_op jit(solution)/shard_map/ppermute | solution.py:568
  177.6 8.0 %collective-permute-start.49 = (bf16[2,528,128]{2,1,0:T(8,128)(2,1)S(1)}, bf16[2,528,128]{2,1,0:T(8,128)(2,1)S(1)}, u32[]{:S(2)}, u32[]{:S(2)}) collective-permute-start(bf16[2,528,128]{2,1,0:T(8,128)(2,1)S(1)} %get-tuple-element.163), channel_id=1, source_target_pairs={{0,8},{8,0},{16,24},{24,16},{1,9},{9,1},{17,25},{25,17},{2,10},{10... | collective-permute-start | bytes 811016 | tf_op jit(solution)/shard_map/ppermute | solution.py:568
  181.1 9.4 %collective-permute-start.47 = (bf16[2,2,5,32,256]{4,3,2,1,0:T(8,128)(2,1)S(1)}, bf16[2,2,5,32,256]{4,3,2,1,0:T(8,128)(2,1)S(1)}, u32[]{:S(2)}, u32[]{:S(2)}) collective-permute-start(bf16[2,2,5,32,256]{4,3,2,1,0:T(8,128)(2,1)S(1)} %get-tuple-element.168), channel_id=1, source_target_pairs={{0,1},{1,0},{2,3},{3,2},{4,5},{5,4},{6,7},{7,6},{8,9},{9,8},{10,11... | collective-permute-start | bytes 983048 | tf_op jit(solution)/shard_map/ppermute | solution.py:568
  182.4 7.7 %collective-permute-start.48 = (bf16[2,2,4,32,256]{4,3,2,1,0:T(8,128)(2,1)S(1)}, bf16[2,2,4,32,256]{4,3,2,1,0:T(8,128)(2,1)S(1)}, u32[]{:S(2)}, u32[]{:S(2)}) collective-permute-start(bf16[2,2,4,32,256]{4,3,2,1,0:T(8,128)(2,1)S(1)} %get-tuple-element.169), channel_id=1, source_target_pairs={{0,4},{4,0},{1,5},{5,1},{2,6},{6,2},{3,7},{7,3},{8,12},{12,8},{9,1... | collective-permute-start | bytes 786440 | tf_op jit(solution)/shard_map/ppermute | solution.py:568
  186.3 8.0 %collective-permute-start.52 = (bf16[528,128]{1,0:T(8,128)(2,1)S(1)}, bf16[528,128]{1,0:T(8,128)(2,1)S(1)}, u32[]{:S(2)}, u32[]{:S(2)}) collective-permute-start(bf16[528,128]{1,0:T(8,128)(2,1)S(1)} %get-tuple-element.172), channel_id=1, source_target_pairs={{0,16},{8,24},{16,0},{24,8},{1,17},{9,25},{17,1},{25,9},{2,18},{10... | collective-permute-start | bytes 405512 | tf_op jit(solution)/shard_map/ppermute | solution.py:568
  191.2 9.3 %collective-permute-start.50 = (bf16[2,9,32,256]{3,2,1,0:T(8,128)(2,1)S(1)}, bf16[2,9,32,256]{3,2,1,0:T(8,128)(2,1)S(1)}, u32[]{:S(2)}, u32[]{:S(2)}) collective-permute-start(bf16[2,9,32,256]{3,2,1,0:T(8,128)(2,1)S(1)} %get-tuple-element.177), channel_id=1, source_target_pairs={{0,8},{8,0},{16,24},{24,16},{1,9},{9,1},{17,25},{25,17},{2,10},{10... | collective-permute-start | bytes 884744 | tf_op jit(solution)/shard_map/ppermute | solution.py:568
  201.2 8.3 %collective-permute-start.51 = (bf16[9,32,256]{2,1,0:T(8,128)(2,1)S(1)}, bf16[9,32,256]{2,1,0:T(8,128)(2,1)S(1)}, u32[]{:S(2)}, u32[]{:S(2)}) collective-permute-start(bf16[9,32,256]{2,1,0:T(8,128)(2,1)S(1)} %get-tuple-element.179), channel_id=1, source_target_pairs={{0,16},{8,24},{16,0},{24,8},{1,17},{9,25},{17,1},{25,9},{2,18},{10... | collective-permute-start | bytes 442376 | tf_op jit(solution)/shard_map/ppermute | solution.py:568
  (4 other events, 8.8 us)

commit v4 on v3

--- a/solution.py
+++ b/solution.py
@@ -105,36 +105,27 @@
         pick = (place_of == lax.broadcasted_iota(jnp.int32, (wide, length), 0)).astype(BF)
         values = dot(rows, pick, NN)
         owner = lax.broadcasted_iota(jnp.int32, (devices, length), 1) // each
-        own = owner == lax.broadcasted_iota(jnp.int32, (devices, length), 0)
+        row = lax.broadcasted_iota(jnp.int32, (devices, length), 0)
+        own = owner == 2 * (row % (devices // 2)) + row // (devices // 2)
         out[v : v + 1, :length] = jnp.sum(jnp.where(own, values, 0.0), 0, keepdims=True)
 
 
-def conv_kernel(subs, plan, small, taps, flags, prev, x, nxt, *rest):
+def conv_kernel(subs, plan, small, flags, prev, x, nxt, *rest):
     block = pl.program_id(0)
     width = x.shape[1]
     border = prev.shape[0]
     sources = rest[: len(plan)]
     if small:
-        xhat_out, scale_out, w_out, table, ext, col, w, sems, out_sem, tails, tail_sems = rest[len(plan) :]
+        xhat_out, scale_out, w_out, table, ext, col, w, sems, out_sem = rest[len(plan) :]
+        small_rows = sources[0].shape[2]
     else:
         table, xhat_out, scale_out, w_out, ext, col, w, sems, out_sem = rest[len(plan) :]
 
     def copies_in():
-        copies = place(plan, flags[4, 0], flags[4, 1], sources, w, sems)
-        if small:
-            for source, (offsets, first) in zip(sources, plan):
-                if first + source.shape[1] <= taps:
-                    continue
-                for db, ds in offsets:
-                    n = offsets.index((db, ds))
-                    device = 2 * (flags[4, 0] ^ db) + (flags[4, 1] ^ ds)
-                    k = len(copies) - count_copies(plan)
-                    copies.append(
-                        pltpu.make_async_copy(
-                            source.at[n, taps - first, pl.ds(0, 16)], tails.at[device], tail_sems.at[k]
-                        )
-                    )
-        return copies
+        return place(plan, flags[4, 0], flags[4, 1], sources, w, sems)
+
+    def whole_out():
+        return pltpu.make_async_copy(w.at[pl.ds(0, KERNEL_TAPS)], w_out, out_sem)
 
     @pl.when(block == 0)
     def _():
@@ -146,17 +137,17 @@
 
         for copy in copies_in():
             copy.wait()
-        pltpu.make_async_copy(w, w_out, out_sem).start()
+        whole_out().start()
         if small:
-            devices, high, wide = tails.shape
-            first_row = lax.broadcasted_iota(jnp.int32, (devices, devices * high), 0) * high
-            pick = (first_row == lax.broadcasted_iota(jnp.int32, (devices, devices * high), 1)).astype(BF)
-            rows = dot(pick, tails[...].reshape(devices * high, wide), NN).astype(BF)
-            spread_table(small, rows, table)
+            blocks = width // small_rows
+            first_row = lax.broadcasted_iota(jnp.int32, (blocks, width), 0) * small_rows
+            pick = (first_row == lax.broadcasted_iota(jnp.int32, (blocks, width), 1)).astype(BF)
+            rows = dot(pick, w[KERNEL_TAPS], NN).astype(BF)
+            spread_table(small, jnp.concatenate([rows[:, : width // 2], rows[:, width // 2 :]], 0), table)
 
     @pl.when(block == pl.num_programs(0) - 1)
     def _():
-        pltpu.make_async_copy(w, w_out, out_sem).wait()
+        whole_out().wait()
 
     def load(start, count):
         return ext[pl.ds(pl.multiple_of(start + border, DILATION_STEP), count), :]
@@ -186,7 +177,7 @@
     scratch = [
         pltpu.VMEM((count + 2 * prev.shape[0], width), BF),
         pltpu.VMEM((rows, KERNEL_TAPS * width), BF),
-        pltpu.VMEM((KERNEL_TAPS, width, width), BF),
+        pltpu.VMEM((KERNEL_TAPS + bool(small), width, width), BF),
         pltpu.SemaphoreType.DMA((count_copies(plan),)),
         pltpu.SemaphoreType.DMA,
     ]
@@ -194,12 +185,10 @@
     if small:
         out_specs = out_specs + [whole_block((8, hidden))]
         out_shape = out_shape + [jax.ShapeDtypeStruct((8, hidden), F32)]
-        devices = width // small[0][1]
-        scratch += [pltpu.VMEM((devices, 16, width // 2), BF), pltpu.SemaphoreType.DMA((devices,))]
     else:
         extra_specs, extra = [whole_block(table.shape)], [table]
     outs = pl.pallas_call(
-        functools.partial(conv_kernel, subs, plan, small, KERNEL_TAPS),
+        functools.partial(conv_kernel, subs, plan, small),
         grid_spec=pltpu.PrefetchScalarGridSpec(
             num_scalar_prefetch=1,
             grid=(count // rows,),
@@ -209,7 +198,7 @@
         ),
         out_shape=out_shape,
         compiler_params=pltpu.CompilerParams(vmem_limit_bytes=VMEM_FIRST),
-        cost_estimate=conv_cost(count, width),
+        cost_estimate=pl.CostEstimate(flops=1, bytes_accessed=1, transcendentals=0),
         name="conv_forward",
     )(flags, prev, x, nxt, *sources, *extra)
     return outs if small else (*outs, table)
@@ -603,8 +592,8 @@
         (swap(column, Z0), swap(far, X), swap(far, Y), top(own_x), bottom(own_y))
     )
     pair = after(pair, near, own_top)
-    near_x, near_y, far_top, far_bottom, pair_far = lax.optimization_barrier(
-        (swap(near, X), swap(near, Y), top(far_x), bottom(far_y), swap(pair, Z1))
+    near_y, near_x, far_top, far_bottom, pair_far = lax.optimization_barrier(
+        (swap(near, Y), swap(near, X), top(far_x), bottom(far_y), swap(pair, Z1))
     )
     near_top, near_bottom = top(near_x), bottom(near_y)
     pair = jnp.concatenate([pair, pair_far], 0)

time: 210 us -> 206 us (0.981)
  waiting for transfers between devices: 60 us -> 52 us
  starting transfers between devices: 40.9 us -> 44.5 us
    ppermute x52, waiting for transfers between devices: 60 us -> 52 us  [swap(): lax.ppermute(value, axis, [(i, i ^ bit) for i in range(lax.axis_size(axis...]
    ppermute x52, starting transfers between devices: 39.2 us -> 43.7 us  [swap(): lax.ppermute(value, axis, [(i, i ^ bit) for i in range(lax.axis_size(axis...]
  transfers between devices with their start and end apart: 53 -> 53, of which waited for: 25 -> 26; matrix products, arithmetic and copies ran while one was open for 2% -> 3% of each run, Pallas kernels for 24% -> 24%
where the time goes in v4:
time: 206 us
  Pallas kernels  101 us (49%)
  waiting for transfers between devices  52 us (25%)
  starting transfers between devices  44.5 us (22%)
  local copies, waits for them, and re-layouts  5.28 us (3%)
    ppermute x52, waiting for transfers between devices, swap(): lax.ppermute(value, axis, [(i, i ^ bit) for i in range(lax.axis_size(axis...  52 us
    pallas_call x1, Pallas kernels, ffn(): pl.pallas_call(functools.partial(ffn_kernel, chunk, fast, plan), grid_spe...  48 us
    ppermute x52, starting transfers between devices, swap(): lax.ppermute(value, axis, [(i, i ^ bit) for i in range(lax.axis_size(axis...  43.7 us
    pallas_call x1, Pallas kernels, conv_forward(): pl.pallas_call(functools.partial(conv_kernel, subs, plan, small), grid_sp...  18.5 us
    pallas_call x2, Pallas kernels, conv_weight_backward(): pl.pallas_call(functools.partial(conv_weight_kernel, fast, first), grid_s...  13.8 us
    pallas_call x1, Pallas kernels, conv_input_backward(): pl.pallas_call(functools.partial(conv_input_kernel, subs), grid_spec=pltp...  12.3 us
    pallas_call x6, Pallas kernels, stage(): pl.pallas_call(functools.partial(stage_kernel, columns, joined), grid_spe...  4.29 us
  transfers between devices with their start and end apart: 53, of which 26 were waited for; matrix products, arithmetic and copies ran while one was open for 3% of the time, Pallas kernels for 24%

profile of v4, /device:TPU:0, one launch (start us, length us, event | category | flops | bytes accessed | tf_op | source)
XLA Modules:
  0.0 205.5 jit_solution(8581633131689176626)
XLA Ops:
  0.6 2.1 %pack.1 = (s32[6,8]{1,0:T(8,128)}, bf16[128,512]{1,0:T(8,128)(2,1)}, bf16[1,10,32,256]{3,2,1,0:T(8,128)(2,1)}, bf16[1,2,128,256]{3,2,1,0:T(8,128)(2,1)}) custom-call(s32[1,9]{1,0:T(1,128)} %lengths.1, bf16[2048,512]{1,0:T(8,128)(2,1)} %bitcast.30, bf16[2048,512]{1,0:T(8,128)(2,1)} %bitcast.31, bf16[9,32,256]{2,1,0:T(8,128)(2,1)} %bitcast.38, ...), custom_call_target="tpu_custom_call" | custom-call | tf_op jit(solution)/shard_map/pack/pallas_call | solution.py:544
  2.7 4.1 %collective-permute-start.3 = (bf16[1,10,32,256]{3,2,1,0:T(8,128)(2,1)}, bf16[1,10,32,256]{3,2,1,0:T(8,128)(2,1)S(1)}, u32[]{:S(2)}, u32[]{:S(2)}) collective-permute-start(bf16[1,10,32,256]{3,2,1,0:T(8,128)(2,1)} %get-tuple-element.99), channel_id=1, source_target_pairs={{0,16},{8,24},{16,0},{24,8},{1,17},{9,25},{17,1},{25,9},{2,18},{10... | collective-permute-start | bytes 491528 | tf_op jit(solution)/shard_map/ppermute | solution.py:557
  6.8 1.5 collective-permute-start.2
  8.3 1.5 collective-permute-start.1
  10.4 0.9 constant_dynamic-update-slice_fusion.1
  11.3 5.4 %collective-permute-done.prev.nxt = bf16[128,512]{1,0:T(8,128)(2,1)S(1)} collective-permute-done((bf16[128,512]{1,0:T(8,128)(2,1)}, bf16[128,512]{1,0:T(8,128)(2,1)S(1)}, u32[]{:S(2)}, u32[]{:S(2)}) %collective-permute-start) | collective-permute-done | bytes 131104 | tf_op jit(solution)/shard_map/ppermute | solution.py:557
  16.8 1.6 collective-permute-start.4
  18.4 1.5 collective-permute-start.6
  20.5 1.6 collective-permute-start.8
  22.6 3.6 %collective-permute-done.8.rest_5_ = bf16[1,5,32,256]{3,2,1,0:T(8,128)(2,1)S(1)} collective-permute-done((bf16[1,5,32,256]{3,2,1,0:T(8,128)(2,1)S(1)}, bf16[1,5,32,256]{3,2,1,0:T(8,128)(2,1)S(1)}, u32[]{:S(2)}, u32[]{:S(2)}) %collective-permute-start.8) | collective-permute-done | bytes 81952 | tf_op jit(solution)/shard_map/ppermute | solution.py:557
  27.6 1.7 collective-permute-start.12
  29.3 1.1 collective-permute-start.13
  30.4 4.6 %collective-permute-done.12.rest_9_ = bf16[1,5,32,256]{3,2,1,0:T(8,128)(2,1)S(1)} collective-permute-done((bf16[1,5,32,256]{3,2,1,0:T(8,128)(2,1)S(1)}, bf16[1,5,32,256]{3,2,1,0:T(8,128)(2,1)S(1)}, u32[]{:S(2)}, u32[]{:S(2)}) %collective-permute-start.12) | collective-permute-done | bytes 81952 | tf_op jit(solution)/shard_map/ppermute | solution.py:557
  35.4 4.1 %collective-permute-done.11.rest_8_ = bf16[1,5,32,256]{3,2,1,0:T(8,128)(2,1)S(1)} collective-permute-done((bf16[1,5,32,256]{3,2,1,0:T(8,128)(2,1)S(1)}, bf16[1,5,32,256]{3,2,1,0:T(8,128)(2,1)S(1)}, u32[]{:S(2)}, u32[]{:S(2)}) %collective-permute-start.11) | collective-permute-done | bytes 81952 | tf_op jit(solution)/shard_map/ppermute | solution.py:557
  40.5 0.9 pad_maximum_fusion
  42.6 0.9 constant_dynamic-update-slice_fusion.4
  44.2 1.2 collective-permute-start.14
  45.4 4.4 %collective-permute-done.30 = bf16[2,2,128,256]{3,2,1,0:T(8,128)(2,1)S(1)} collective-permute-done((bf16[2,2,128,256]{3,2,1,0:T(8,128)(2,1)S(1)}, bf16[2,2,128,256]{3,2,1,0:T(8,128)(2,1)S(1)}, u32[]{:S(2)}, u32[]{:S(2)}) %collective-permute-start.30) | collective-permute-done | bytes 262176 | tf_op jit(solution)/shard_map/ppermute | solution.py:557
  49.9 0.8 collective-permute-start.33
  50.7 1.3 collective-permute-start.32
  51.9 1.5 collective-permute-start.31
  54.0 0.9 collective-permute-done.29.rest_27_
  55.3 1.1 collective-permute-done.26.rest_24_
  56.9 18.5 %conv_forward.1 = (f32[2048,512]{1,0:T(8,128)}, f32[2048,512]{1,0:T(8,128)}, bf16[9,512,512]{2,1,0:T(8,128)(2,1)}, f32[8,2048]{1,0:T(8,128)S(1)}) custom-call(s32[6,8]{1,0:T(8,128)S(1)} %copy-done.3, bf16[128,512]{1,0:T(8,128)(2,1)S(1)} %collective-permute-done.prev.nxt, bf16[2048,512]{1,0:T(8,128)(2,1)S(1)} %bitcast.33, ...), custom_call_target="tpu_custom_call" | custom-call | flops 1 | bytes 1 | tf_op jit(solution)/shard_map/conv_forward/pallas_call | solution.py:190
  76.6 1.3 collective-permute-done.34.rest_4_
  77.9 0.7 collective-permute-done.35.rest_5_
  78.7 0.7 collective-permute-done.36.rest_6_
  79.6 1.8 collective-permute-done.37.rest_7_
  81.4 0.8 copy-done.11
  82.1 48.0 %feed_forward.1 = (bf16[2048,512]{1,0:T(8,128)(2,1)}, f32[2048,512]{1,0:T(8,128)}, bf16[2048,512]{1,0:T(8,128)(2,1)S(1)}, bf16[128,512]{1,0:T(8,128)(2,1)S(1)}, ...) custom-call(s32[6,8]{1,0:T(8,128)S(1)} %copy-done.3, bf16[2048,512]{1,0:T(8,128)(2,1)} %bitcast.32, ...), custom_call_target="tpu_custom_call" | custom-call | flops 25769803776 | bytes 1048576 | tf_op jit(solution)/shard_map/feed_forward/pallas_call | solution.py:345
  130.4 1.3 collective-permute-start.39
  131.7 3.7 %conv_weight_backward.2 = (bf16[4,2,2,9,32,256]{5,4,3,2,1,0:T(8,128)(2,1)S(1)}, bf16[4,2,2,9,32,256]{5,4,3,2,1,0:T(8,128)(2,1)S(1)}) custom-call(s32[6,8]{1,0:T(8,128)S(1)} %copy-done.3, bf16[128,512]{1,0:T(8,128)(2,1)S(1)} %collective-permute-done.prev.nxt, bf16[2048,512]{1,0:T(8,128)(2,1)S(1)} %bitcast.34, ...), custom_call_target="tpu_custom_call" | custom-call | flops 2146959360 | bytes 1048576 | tf_op jit(solution)/shard_map/conv_weight_backward/pallas_call | solution.py:424
  135.3 0.8 collective-permute-done.39.prev.nxt
  136.2 1.1 stage.8
  137.3 1.1 collective-permute-start.40
  138.3 0.8 collective-permute-start.41
  139.1 10.1 %conv_weight_backward.3 = (bf16[4,2,2,9,32,256]{5,4,3,2,1,0:T(8,128)(2,1)S(1)}, bf16[4,2,2,9,32,256]{5,4,3,2,1,0:T(8,128)(2,1)S(1)}) custom-call(s32[6,8]{1,0:T(8,128)S(1)} %copy-done.3, bf16[128,512]{1,0:T(8,128)(2,1)S(1)} %collective-permute-done.prev.nxt, bf16[2048,512]{1,0:T(8,128)(2,1)S(1)} %bitcast.35, ...), custom_call_target="tpu_custom_call", output_to_operand_aliasing={{0}: (5, {}), {1}: (6, {})} | custom-call | flops 7511998464 | bytes 1048576 | tf_op jit(solution)/shard_map/conv_weight_backward/pallas_call | solution.py:424
  149.2 2.2 %collective-permute-done.41.refs_3_ = bf16[2,2,2,256,128]{4,3,2,1,0:T(8,128)(2,1)S(1)} collective-permute-done((bf16[2,2,2,256,128]{4,3,2,1,0:T(8,128)(2,1)S(1)}, bf16[2,2,2,256,128]{4,3,2,1,0:T(8,128)(2,1)S(1)}, u32[]{:S(2)}, u32[]{:S(2)}) %collective-permute-start.41) | collective-permute-done | bytes 524320 | tf_op jit(solution)/shard_map/ppermute | solution.py:557
  151.5 0.8 stage.9
  152.2 1.1 collective-permute-start.43
  153.3 1.2 collective-permute-start.42
  154.5 1.5 collective-permute-done.44.got
  156.0 1.1 stage.10
  157.1 1.1 collective-permute-start.45
  158.2 1.2 collective-permute-start.46
  159.4 12.3 %conv_input_backward.1 = f32[2048,512]{1,0:T(8,128)} custom-call(s32[6,8]{1,0:T(8,128)S(1)} %copy-done.3, bf16[128,512]{1,0:T(8,128)(2,1)S(1)} %collective-permute-done.39.prev.nxt, bf16[2048,512]{1,0:T(8,128)(2,1)S(1)} %get-tuple-element.132.g, bf16[128,512]{1,0:T(8,128)(2,1)S(1)} %collective-permute-done.39.prev.nxt, f32[2048,512]{1,0:T(8,128)S(1)} %copy-done.4, ...), custom_call_target="tpu_custom_call" | custom-call | flops 9663676416 | bytes 1048576 | tf_op jit(solution)/shard_map/conv_input_backward/pallas_call | solution.py:469
  171.7 0.7 stage.11
  173.3 1.7 collective-permute-done.45.refs_1_
  175.1 0.8 stage.12
  175.9 1.2 collective-permute-start.47
  177.1 1.1 collective-permute-start.48
  178.2 2.3 %collective-permute-done.49.refs_1_ = bf16[2,528,128]{2,1,0:T(8,128)(2,1)S(1)} collective-permute-done((bf16[2,528,128]{2,1,0:T(8,128)(2,1)S(1)}, bf16[2,528,128]{2,1,0:T(8,128)(2,1)S(1)}, u32[]{:S(2)}, u32[]{:S(2)}) %collective-permute-start.49) | collective-permute-done | bytes 270368 | tf_op jit(solution)/shard_map/ppermute | solution.py:557
  180.4 0.7 stage.13
  181.1 3.3 %collective-permute-start.52 = (bf16[528,128]{1,0:T(8,128)(2,1)S(1)}, bf16[528,128]{1,0:T(8,128)(2,1)S(1)}, u32[]{:S(2)}, u32[]{:S(2)}) collective-permute-start(bf16[528,128]{1,0:T(8,128)(2,1)S(1)} %get-tuple-element.172), channel_id=1, source_target_pairs={{0,16},{8,24},{16,0},{24,8},{1,17},{9,25},{17,1},{25,9},{2,18},{10... | collective-permute-start | bytes 405512 | tf_op jit(solution)/shard_map/ppermute | solution.py:557
  185.3 0.7 stage.14
  186.0 0.9 collective-permute-start.50
  186.9 3.0 %collective-permute-done.52 = bf16[528,128]{1,0:T(8,128)(2,1)S(1)} collective-permute-done((bf16[528,128]{1,0:T(8,128)(2,1)S(1)}, bf16[528,128]{1,0:T(8,128)(2,1)S(1)}, u32[]{:S(2)}, u32[]{:S(2)}) %collective-permute-start.52) | collective-permute-done | bytes 135200 | tf_op jit(solution)/shard_map/ppermute | solution.py:557
  189.9 0.7 slice_bitcast_fusion
  190.5 0.8 copy.27
  191.9 3.1 %collective-permute-done.50.refs_1_ = bf16[2,9,32,256]{3,2,1,0:T(8,128)(2,1)S(1)} collective-permute-done((bf16[2,9,32,256]{3,2,1,0:T(8,128)(2,1)S(1)}, bf16[2,9,32,256]{3,2,1,0:T(8,128)(2,1)S(1)}, u32[]{:S(2)}, u32[]{:S(2)}) %collective-permute-start.50) | collective-permute-done | bytes 294944 | tf_op jit(solution)/shard_map/ppermute | solution.py:557
  195.0 0.7 stage.15
  195.7 2.6 %collective-permute-start.51 = (bf16[9,32,256]{2,1,0:T(8,128)(2,1)S(1)}, bf16[9,32,256]{2,1,0:T(8,128)(2,1)S(1)}, u32[]{:S(2)}, u32[]{:S(2)}) collective-permute-start(bf16[9,32,256]{2,1,0:T(8,128)(2,1)S(1)} %get-tuple-element.179), channel_id=1, source_target_pairs={{0,16},{8,24},{16,0},{24,8},{1,17},{9,25},{17,1},{25,9},{2,18},{10... | collective-permute-start | bytes 442376 | tf_op jit(solution)/shard_map/ppermute | solution.py:557
  198.8 6.0 %collective-permute-done.51 = bf16[9,32,256]{2,1,0:T(8,128)(2,1)S(1)} collective-permute-done((bf16[9,32,256]{2,1,0:T(8,128)(2,1)S(1)}, bf16[9,32,256]{2,1,0:T(8,128)(2,1)S(1)}, u32[]{:S(2)}, u32[]{:S(2)}) %collective-permute-start.51) | collective-permute-done | bytes 147488 | tf_op jit(solution)/shard_map/ppermute | solution.py:557
  204.8 0.8 add_bitcast_fusion
  (103 shorter events, 12.3 us)
Async XLA Ops:
  2.7 54.2 %copy-start = (bf16[1,2048,512]{2,1,0:T(8,128)(2,1)S(1)}, bf16[1,2048,512]{2,1,0:T(8,128)(2,1)}, u32[]{:S(2)}) copy-start(bf16[1,2048,512]{2,1,0:T(8,128)(2,1)} %param.13) | copy-start | bytes 6291460
  2.7 54.2 %copy-start.3 = (s32[6,8]{1,0:T(8,128)S(1)}, s32[6,8]{1,0:T(8,128)}, u32[]{:S(2)}) copy-start(s32[6,8]{1,0:T(8,128)} %get-tuple-element.97.flags) | copy-start | bytes 580
  2.7 14.0 %collective-permute-start.3 = (bf16[1,10,32,256]{3,2,1,0:T(8,128)(2,1)}, bf16[1,10,32,256]{3,2,1,0:T(8,128)(2,1)S(1)}, u32[]{:S(2)}, u32[]{:S(2)}) collective-permute-start(bf16[1,10,32,256]{3,2,1,0:T(8,128)(2,1)} %get-tuple-element.99), channel_id=1, source_target_pairs={{0,16},{8,24},{16,0},{24,8},{1,17},{9,25},{17,1},{25,9},{2,18},{10... | collective-permute-start | bytes 491528 | tf_op jit(solution)/shard_map/ppermute | solution.py:557
  6.8 9.9 %collective-permute-start.2 = (bf16[1,10,32,256]{3,2,1,0:T(8,128)(2,1)}, bf16[1,10,32,256]{3,2,1,0:T(8,128)(2,1)S(1)}, u32[]{:S(2)}, u32[]{:S(2)}) collective-permute-start(bf16[1,10,32,256]{3,2,1,0:T(8,128)(2,1)} %get-tuple-element.99), channel_id=1, source_target_pairs={{0,4},{4,0},{1,5},{5,1},{2,6},{6,2},{3,7},{7,3},{8,12},{12,8},{9,1... | collective-permute-start | bytes 491528 | tf_op jit(solution)/shard_map/ppermute | solution.py:557
  8.3 8.4 %collective-permute-start.1 = (bf16[1,10,32,256]{3,2,1,0:T(8,128)(2,1)}, bf16[1,10,32,256]{3,2,1,0:T(8,128)(2,1)S(1)}, u32[]{:S(2)}, u32[]{:S(2)}) collective-permute-start(bf16[1,10,32,256]{3,2,1,0:T(8,128)(2,1)} %get-tuple-element.99), channel_id=1, source_target_pairs={{0,1},{1,0},{2,3},{3,2},{4,5},{5,4},{6,7},{7,6},{8,9},{9,8},{10,11... | collective-permute-start | bytes 491528 | tf_op jit(solution)/shard_map/ppermute | solution.py:557
  9.9 6.9 %collective-permute-start = (bf16[128,512]{1,0:T(8,128)(2,1)}, bf16[128,512]{1,0:T(8,128)(2,1)S(1)}, u32[]{:S(2)}, u32[]{:S(2)}) collective-permute-start(bf16[128,512]{1,0:T(8,128)(2,1)} %get-tuple-element.98), channel_id=1, source_target_pairs={{0,1},{1,0},{2,3},{3,2},{4,5},{5,4},{6,7},{7,6},{8,9},{9,8},{10,11... | collective-permute-start | bytes 393224 | tf_op jit(solution)/shard_map/ppermute | solution.py:557
  16.8 9.7 %collective-permute-start.4 = (bf16[2,10,32,256]{3,2,1,0:T(8,128)(2,1)S(1)}, bf16[2,10,32,256]{3,2,1,0:T(8,128)(2,1)S(1)}, u32[]{:S(2)}, u32[]{:S(2)}) collective-permute-start(bf16[2,10,32,256]{3,2,1,0:T(8,128)(2,1)S(1)} %constant_dynamic-update-slice_fusion.rest_0_), channel_id=1, source_target_pairs={{0,8},{8,0},{16,24},{24,16},{1,9},{9,1},{17,25},{25,17},{2,10},{10... | collective-permute-start | bytes 983048 | tf_op jit(solution)/shard_map/ppermute | solution.py:557
  18.4 8.1 %collective-permute-start.6 = (bf16[1,10,32,256]{3,2,1,0:T(8,128)(2,1)S(1)}, bf16[1,10,32,256]{3,2,1,0:T(8,128)(2,1)S(1)}, u32[]{:S(2)}, u32[]{:S(2)}) collective-permute-start(bf16[1,10,32,256]{3,2,1,0:T(8,128)(2,1)S(1)} %collective-permute-done.3), channel_id=1, source_target_pairs={{0,1},{1,0},{2,3},{3,2},{4,5},{5,4},{6,7},{7,6},{8,9},{9,8},{10,11... | collective-permute-start | bytes 491528 | tf_op jit(solution)/shard_map/ppermute | solution.py:557
  19.9 6.6 %collective-permute-start.5 = (bf16[1,10,32,256]{3,2,1,0:T(8,128)(2,1)S(1)}, bf16[1,10,32,256]{3,2,1,0:T(8,128)(2,1)S(1)}, u32[]{:S(2)}, u32[]{:S(2)}) collective-permute-start(bf16[1,10,32,256]{3,2,1,0:T(8,128)(2,1)S(1)} %collective-permute-done.3), channel_id=1, source_target_pairs={{0,4},{4,0},{1,5},{5,1},{2,6},{6,2},{3,7},{7,3},{8,12},{12,8},{9,1... | collective-permute-start | bytes 491528 | tf_op jit(solution)/shard_map/ppermute | solution.py:557
  20.5 5.6 %collective-permute-start.8 = (bf16[1,5,32,256]{3,2,1,0:T(8,128)(2,1)S(1)}, bf16[1,5,32,256]{3,2,1,0:T(8,128)(2,1)S(1)}, u32[]{:S(2)}, u32[]{:S(2)}) collective-permute-start(bf16[1,5,32,256]{3,2,1,0:T(8,128)(2,1)S(1)} %slice.46), channel_id=1, source_target_pairs={{0,4},{4,0},{1,5},{5,1},{2,6},{6,2},{3,7},{7,3},{8,12},{12,8},{9,1... | collective-permute-start | bytes 245768 | tf_op jit(solution)/shard_map/ppermute | solution.py:557
  22.0 4.4 %collective-permute-start.7 = (bf16[1,5,32,256]{3,2,1,0:T(8,128)(2,1)S(1)}, bf16[1,5,32,256]{3,2,1,0:T(8,128)(2,1)S(1)}, u32[]{:S(2)}, u32[]{:S(2)}) collective-permute-start(bf16[1,5,32,256]{3,2,1,0:T(8,128)(2,1)S(1)} %slice.45), channel_id=1, source_target_pairs={{0,1},{1,0},{2,3},{3,2},{4,5},{5,4},{6,7},{7,6},{8,9},{9,8},{10,11... | collective-permute-start | bytes 245768 | tf_op jit(solution)/shard_map/ppermute | solution.py:557
  26.5 13.5 %collective-permute-start.10 = (bf16[2,10,32,256]{3,2,1,0:T(8,128)(2,1)S(1)}, bf16[2,10,32,256]{3,2,1,0:T(8,128)(2,1)S(1)}, u32[]{:S(2)}, u32[]{:S(2)}) collective-permute-start(bf16[2,10,32,256]{3,2,1,0:T(8,128)(2,1)S(1)} %collective-permute-done.4.rest_1_), channel_id=1, source_target_pairs={{0,4},{4,0},{1,5},{5,1},{2,6},{6,2},{3,7},{7,3},{8,12},{12,8},{9,1... | collective-permute-start | bytes 983048 | tf_op jit(solution)/shard_map/ppermute | solution.py:557
  27.1 13.0 %collective-permute-start.9 = (bf16[2,10,32,256]{3,2,1,0:T(8,128)(2,1)S(1)}, bf16[2,10,32,256]{3,2,1,0:T(8,128)(2,1)S(1)}, u32[]{:S(2)}, u32[]{:S(2)}) collective-permute-start(bf16[2,10,32,256]{3,2,1,0:T(8,128)(2,1)S(1)} %collective-permute-done.4.rest_1_), channel_id=1, source_target_pairs={{0,1},{1,0},{2,3},{3,2},{4,5},{5,4},{6,7},{7,6},{8,9},{9,8},{10,11... | collective-permute-start | bytes 983048 | tf_op jit(solution)/shard_map/ppermute | solution.py:557
  27.6 7.5 %collective-permute-start.12 = (bf16[1,5,32,256]{3,2,1,0:T(8,128)(2,1)S(1)}, bf16[1,5,32,256]{3,2,1,0:T(8,128)(2,1)S(1)}, u32[]{:S(2)}, u32[]{:S(2)}) collective-permute-start(bf16[1,5,32,256]{3,2,1,0:T(8,128)(2,1)S(1)} %slice.48), channel_id=1, source_target_pairs={{0,4},{4,0},{1,5},{5,1},{2,6},{6,2},{3,7},{7,3},{8,12},{12,8},{9,1... | collective-permute-start | bytes 245768 | tf_op jit(solution)/shard_map/ppermute | solution.py:557
  29.3 12.7 %collective-permute-start.16 = (bf16[2,10,32,256]{3,2,1,0:T(8,128)(2,1)S(1)}, bf16[2,10,32,256]{3,2,1,0:T(8,128)(2,1)S(1)}, u32[]{:S(2)}, u32[]{:S(2)}) collective-permute-start(bf16[2,10,32,256]{3,2,1,0:T(8,128)(2,1)S(1)} %constant_dynamic-update-slice_fusion.rest_0_), channel_id=1, source_target_pairs={{0,2},{2,0},{1,3},{3,1},{4,6},{6,4},{5,7},{7,5},{8,10},{10,8},{9,1... | collective-permute-start | bytes 983048 | tf_op jit(solution)/shard_map/ppermute | solution.py:557
  29.3 10.2 %collective-permute-start.13 = (bf16[1,2,128,256]{3,2,1,0:T(8,128)(2,1)}, bf16[1,2,128,256]{3,2,1,0:T(8,128)(2,1)S(1)}, u32[]{:S(2)}, u32[]{:S(2)}) collective-permute-start(bf16[1,2,128,256]{3,2,1,0:T(8,128)(2,1)} %get-tuple-element.110), channel_id=1, source_target_pairs={{0,16},{8,24},{16,0},{24,8},{1,17},{9,25},{17,1},{25,9},{2,18},{10... | collective-permute-start | bytes 393224 | tf_op jit(solution)/shard_map/ppermute | solution.py:557
  35.1 4.4 %collective-permute-start.11 = (bf16[1,5,32,256]{3,2,1,0:T(8,128)(2,1)S(1)}, bf16[1,5,32,256]{3,2,1,0:T(8,128)(2,1)S(1)}, u32[]{:S(2)}, u32[]{:S(2)}) collective-permute-start(bf16[1,5,32,256]{3,2,1,0:T(8,128)(2,1)S(1)} %slice.47), channel_id=1, source_target_pairs={{0,1},{1,0},{2,3},{3,2},{4,5},{5,4},{6,7},{7,6},{8,9},{9,8},{10,11... | collective-permute-start | bytes 245768 | tf_op jit(solution)/shard_map/ppermute | solution.py:557
  39.5 2.0 collective-permute-start.18
  39.5 2.5 %collective-permute-start.19 = (bf16[1,10,32,256]{3,2,1,0:T(8,128)(2,1)S(1)}, bf16[1,10,32,256]{3,2,1,0:T(8,128)(2,1)S(1)}, u32[]{:S(2)}, u32[]{:S(2)}) collective-permute-start(bf16[1,10,32,256]{3,2,1,0:T(8,128)(2,1)S(1)} %collective-permute-done.1.rest_3_), channel_id=1, source_target_pairs={{0,2},{2,0},{1,3},{3,1},{4,6},{6,4},{5,7},{7,5},{8,10},{10,8},{9,1... | collective-permute-start | bytes 491528 | tf_op jit(solution)/shard_map/ppermute | solution.py:557
  40.0 4.1 %collective-permute-start.22 = (bf16[1,10,32,256]{3,2,1,0:T(8,128)(2,1)S(1)}, bf16[1,10,32,256]{3,2,1,0:T(8,128)(2,1)S(1)}, u32[]{:S(2)}, u32[]{:S(2)}) collective-permute-start(bf16[1,10,32,256]{3,2,1,0:T(8,128)(2,1)S(1)} %collective-permute-done.5.rest_6_), channel_id=1, source_target_pairs={{0,2},{2,0},{1,3},{3,1},{4,6},{6,4},{5,7},{7,5},{8,10},{10,8},{9,1... | collective-permute-start | bytes 491528 | tf_op jit(solution)/shard_map/ppermute | solution.py:557
  40.1 2.4 %collective-permute-start.21 = (bf16[1,5,32,256]{3,2,1,0:T(8,128)(2,1)S(1)}, bf16[1,5,32,256]{3,2,1,0:T(8,128)(2,1)S(1)}, u32[]{:S(2)}, u32[]{:S(2)}) collective-permute-start(bf16[1,5,32,256]{3,2,1,0:T(8,128)(2,1)S(1)} %collective-permute-done.8.rest_5_), channel_id=1, source_target_pairs={{0,2},{2,0},{1,3},{3,1},{4,6},{6,4},{5,7},{7,5},{8,10},{10,8},{9,1... | collective-permute-start | bytes 245768 | tf_op jit(solution)/shard_map/ppermute | solution.py:557
  41.5 8.3 %collective-permute-start.30 = (bf16[2,2,128,256]{3,2,1,0:T(8,128)(2,1)S(1)}, bf16[2,2,128,256]{3,2,1,0:T(8,128)(2,1)S(1)}, u32[]{:S(2)}, u32[]{:S(2)}) collective-permute-start(bf16[2,2,128,256]{3,2,1,0:T(8,128)(2,1)S(1)} %pad_maximum_fusion), channel_id=1, source_target_pairs={{0,8},{8,0},{16,24},{24,16},{1,9},{9,1},{17,25},{25,17},{2,10},{10... | collective-permute-start | bytes 786440 | tf_op jit(solution)/shard_map/ppermute | solution.py:557
  42.0 1.5 collective-permute-start.20
  42.0 3.3 %collective-permute-start.23 = (bf16[1,10,32,256]{3,2,1,0:T(8,128)(2,1)S(1)}, bf16[1,10,32,256]{3,2,1,0:T(8,128)(2,1)S(1)}, u32[]{:S(2)}, u32[]{:S(2)}) collective-permute-start(bf16[1,10,32,256]{3,2,1,0:T(8,128)(2,1)S(1)} %collective-permute-done.6.rest_7_), channel_id=1, source_target_pairs={{0,2},{2,0},{1,3},{3,1},{4,6},{6,4},{5,7},{7,5},{8,10},{10,8},{9,1... | collective-permute-start | bytes 491528 | tf_op jit(solution)/shard_map/ppermute | solution.py:557
  42.5 7.3 %collective-permute-start.17 = (bf16[2,10,32,256]{3,2,1,0:T(8,128)(2,1)S(1)}, bf16[2,10,32,256]{3,2,1,0:T(8,128)(2,1)S(1)}, u32[]{:S(2)}, u32[]{:S(2)}) collective-permute-start(bf16[2,10,32,256]{3,2,1,0:T(8,128)(2,1)S(1)} %collective-permute-done.4.rest_1_), channel_id=1, source_target_pairs={{0,2},{2,0},{1,3},{3,1},{4,6},{6,4},{5,7},{7,5},{8,10},{10,8},{9,1... | collective-permute-start | bytes 983048 | tf_op jit(solution)/shard_map/ppermute | solution.py:557
  43.6 9.9 %collective-permute-start.15 = (bf16[2,5,32,256]{3,2,1,0:T(8,128)(2,1)S(1)}, bf16[2,5,32,256]{3,2,1,0:T(8,128)(2,1)S(1)}, u32[]{:S(2)}, u32[]{:S(2)}) collective-permute-start(bf16[2,5,32,256]{3,2,1,0:T(8,128)(2,1)S(1)} %slice.50), channel_id=1, source_target_pairs={{0,4},{4,0},{1,5},{5,1},{2,6},{6,2},{3,7},{7,3},{8,12},{12,8},{9,1... | collective-permute-start | bytes 491528 | tf_op jit(solution)/shard_map/ppermute | solution.py:557
  44.2 9.3 %collective-permute-start.14 = (bf16[2,5,32,256]{3,2,1,0:T(8,128)(2,1)S(1)}, bf16[2,5,32,256]{3,2,1,0:T(8,128)(2,1)S(1)}, u32[]{:S(2)}, u32[]{:S(2)}) collective-permute-start(bf16[2,5,32,256]{3,2,1,0:T(8,128)(2,1)S(1)} %slice.49), channel_id=1, source_target_pairs={{0,1},{1,0},{2,3},{3,2},{4,5},{5,4},{6,7},{7,6},{8,9},{9,8},{10,11... | collective-permute-start | bytes 491528 | tf_op jit(solution)/shard_map/ppermute | solution.py:557
  45.4 5.3 %collective-permute-start.24 = (bf16[1,5,32,256]{3,2,1,0:T(8,128)(2,1)S(1)}, bf16[1,5,32,256]{3,2,1,0:T(8,128)(2,1)S(1)}, u32[]{:S(2)}, u32[]{:S(2)}) collective-permute-start(bf16[1,5,32,256]{3,2,1,0:T(8,128)(2,1)S(1)} %collective-permute-done.11.rest_8_), channel_id=1, source_target_pairs={{0,2},{2,0},{1,3},{3,1},{4,6},{6,4},{5,7},{7,5},{8,10},{10,8},{9,1... | collective-permute-start | bytes 245768 | tf_op jit(solution)/shard_map/ppermute | solution.py:557
  49.8 2.1 %collective-permute-start.25 = (bf16[1,5,32,256]{3,2,1,0:T(8,128)(2,1)S(1)}, bf16[1,5,32,256]{3,2,1,0:T(8,128)(2,1)S(1)}, u32[]{:S(2)}, u32[]{:S(2)}) collective-permute-start(bf16[1,5,32,256]{3,2,1,0:T(8,128)(2,1)S(1)} %collective-permute-done.12.rest_9_), channel_id=1, source_target_pairs={{0,2},{2,0},{1,3},{3,1},{4,6},{6,4},{5,7},{7,5},{8,10},{10,8},{9,1... | collective-permute-start | bytes 245768 | tf_op jit(solution)/shard_map/ppermute | solution.py:557
  49.9 25.6 %collective-permute-start.33 = (bf16[4,2,128,256]{3,2,1,0:T(8,128)(2,1)S(1)}, bf16[4,2,128,256]{3,2,1,0:T(8,128)(2,1)S(1)}, u32[]{:S(2)}, u32[]{:S(2)}) collective-permute-start(bf16[4,2,128,256]{3,2,1,0:T(8,128)(2,1)S(1)} %constant_dynamic-update-slice_fusion.2.rest_0_), channel_id=1, source_target_pairs={{0,5},{1,4},{4,1},{5,0},{2,7},{3,6},{6,3},{7,2},{8,13},{9,12},{12,... | collective-permute-start | bytes 1572872 | tf_op jit(solution)/shard_map/ppermute | solution.py:602
  50.7 25.3 %collective-permute-start.32 = (bf16[4,2,128,256]{3,2,1,0:T(8,128)(2,1)S(1)}, bf16[4,2,128,256]{3,2,1,0:T(8,128)(2,1)S(1)}, u32[]{:S(2)}, u32[]{:S(2)}) collective-permute-start(bf16[4,2,128,256]{3,2,1,0:T(8,128)(2,1)S(1)} %constant_dynamic-update-slice_fusion.2.rest_0_), channel_id=1, source_target_pairs={{0,1},{1,0},{2,3},{3,2},{4,5},{5,4},{6,7},{7,6},{8,9},{9,8},{10,11... | collective-permute-start | bytes 1572872 | tf_op jit(solution)/shard_map/ppermute | solution.py:557
  51.9 24.0 %collective-permute-start.31 = (bf16[4,2,128,256]{3,2,1,0:T(8,128)(2,1)S(1)}, bf16[4,2,128,256]{3,2,1,0:T(8,128)(2,1)S(1)}, u32[]{:S(2)}, u32[]{:S(2)}) collective-permute-start(bf16[4,2,128,256]{3,2,1,0:T(8,128)(2,1)S(1)} %constant_dynamic-update-slice_fusion.2.rest_0_), channel_id=1, source_target_pairs={{0,4},{4,0},{1,5},{5,1},{2,6},{6,2},{3,7},{7,3},{8,12},{12,8},{9,1... | collective-permute-start | bytes 1572872 | tf_op jit(solution)/shard_map/ppermute | solution.py:557
  53.4 1.4 collective-permute-start.29
  53.4 1.6 collective-permute-start.28
  54.8 1.6 collective-permute-start.26
  55.1 1.9 collective-permute-start.27
  75.5 5.9 %copy-start.5 = (bf16[4,2,128,256]{3,2,1,0:T(8,128)(2,1)}, bf16[4,2,128,256]{3,2,1,0:T(8,128)(2,1)S(1)}, u32[]{:S(2)}) copy-start(bf16[4,2,128,256]{3,2,1,0:T(8,128)(2,1)S(1)} %collective-permute-done.33.rest_3_) | copy-start | bytes 1572868
  76.0 5.4 %copy-start.6 = (bf16[4,2,128,256]{3,2,1,0:T(8,128)(2,1)}, bf16[4,2,128,256]{3,2,1,0:T(8,128)(2,1)S(1)}, u32[]{:S(2)}) copy-start(bf16[4,2,128,256]{3,2,1,0:T(8,128)(2,1)S(1)} %collective-permute-done.32.rest_2_) | copy-start | bytes 1572868
  76.0 5.4 %copy-start.7 = (bf16[4,2,128,256]{3,2,1,0:T(8,128)(2,1)}, bf16[4,2,128,256]{3,2,1,0:T(8,128)(2,1)S(1)}, u32[]{:S(2)}) copy-start(bf16[4,2,128,256]{3,2,1,0:T(8,128)(2,1)S(1)} %collective-permute-done.31.rest_1_) | copy-start | bytes 1572868
  76.0 2.0 collective-permute-start.34
  76.0 2.6 %collective-permute-start.35 = (bf16[4,2,128,256]{3,2,1,0:T(8,128)(2,1)S(1)}, bf16[4,2,128,256]{3,2,1,0:T(8,128)(2,1)S(1)}, u32[]{:S(2)}, u32[]{:S(2)}) collective-permute-start(bf16[4,2,128,256]{3,2,1,0:T(8,128)(2,1)S(1)} %collective-permute-done.31.rest_1_), channel_id=1, source_target_pairs={{0,2},{2,0},{1,3},{3,1},{4,6},{6,4},{5,7},{7,5},{8,10},{10,8},{9,1... | collective-permute-start | bytes 1572872 | tf_op jit(solution)/shard_map/ppermute | solution.py:557
  76.5 2.9 %collective-permute-start.36 = (bf16[4,2,128,256]{3,2,1,0:T(8,128)(2,1)S(1)}, bf16[4,2,128,256]{3,2,1,0:T(8,128)(2,1)S(1)}, u32[]{:S(2)}, u32[]{:S(2)}) collective-permute-start(bf16[4,2,128,256]{3,2,1,0:T(8,128)(2,1)S(1)} %collective-permute-done.32.rest_2_), channel_id=1, source_target_pairs={{0,2},{2,0},{1,3},{3,1},{4,6},{6,4},{5,7},{7,5},{8,10},{10,8},{9,1... | collective-permute-start | bytes 1572872 | tf_op jit(solution)/shard_map/ppermute | solution.py:557
  77.9 3.4 %copy-start.8 = (bf16[4,2,128,256]{3,2,1,0:T(8,128)(2,1)}, bf16[4,2,128,256]{3,2,1,0:T(8,128)(2,1)S(1)}, u32[]{:S(2)}) copy-start(bf16[4,2,128,256]{3,2,1,0:T(8,128)(2,1)S(1)} %collective-permute-done.34.rest_4_) | copy-start | bytes 1572868
  79.4 1.9 collective-permute-start.37
  82.1 49.5 %copy-start.1 = (bf16[1,2048,512]{2,1,0:T(8,128)(2,1)S(1)}, bf16[1,2048,512]{2,1,0:T(8,128)(2,1)}, u32[]{:S(2)}) copy-start(bf16[1,2048,512]{2,1,0:T(8,128)(2,1)} %param.13) | copy-start | bytes 6291460
  130.2 6.0 %collective-permute-start.38 = (bf16[4,2,2,528,128]{4,3,2,1,0:T(8,128)(2,1)}, bf16[4,2,2,528,128]{4,3,2,1,0:T(8,128)(2,1)S(1)}, u32[]{:S(2)}, u32[]{:S(2)}) collective-permute-start(bf16[4,2,2,528,128]{4,3,2,1,0:T(8,128)(2,1)} %get-tuple-element.130), channel_id=1, source_target_pairs={{0,2},{2,0},{1,3},{3,1},{4,6},{6,4},{5,7},{7,5},{8,10},{10,8},{9,1... | collective-permute-start | bytes 6488072 | tf_op jit(solution)/shard_map/ppermute | solution.py:557
  130.4 5.8 %collective-permute-start.39 = (bf16[128,512]{1,0:T(8,128)(2,1)S(1)}, bf16[128,512]{1,0:T(8,128)(2,1)S(1)}, u32[]{:S(2)}, u32[]{:S(2)}) collective-permute-start(bf16[128,512]{1,0:T(8,128)(2,1)S(1)} %get-tuple-element.131), channel_id=1, source_target_pairs={{0,1},{1,0},{2,3},{3,2},{4,5},{5,4},{6,7},{7,6},{8,9},{9,8},{10,11... | collective-permute-start | bytes 393224 | tf_op jit(solution)/shard_map/ppermute | solution.py:557
  131.7 4.5 %copy-start.2 = (bf16[4,2,2,528,128]{4,3,2,1,0:T(8,128)(2,1)S(1)}, bf16[4,2,2,528,128]{4,3,2,1,0:T(8,128)(2,1)}, u32[]{:S(2)}) copy-start(bf16[4,2,2,528,128]{4,3,2,1,0:T(8,128)(2,1)} %get-tuple-element.129.keep) | copy-start | bytes 6488068
  136.2 23.2 %slice-start = ((s8[4718592]{0:T(1024)(128)(4,1)}), s8[4194304]{0:T(1024)(128)(4,1)S(1)}, s32[]{:S(2)}) async-start(s8[4718592]{0:T(1024)(128)(4,1)} %bitcast.36), calls=%async_computation | async-start | bytes 8388608
  137.3 14.2 %collective-permute-start.40 = (bf16[2,2,2,272,128]{4,3,2,1,0:T(8,128)(2,1)S(1)}, bf16[2,2,2,272,128]{4,3,2,1,0:T(8,128)(2,1)S(1)}, u32[]{:S(2)}, u32[]{:S(2)}) collective-permute-start(bf16[2,2,2,272,128]{4,3,2,1,0:T(8,128)(2,1)S(1)} %get-tuple-element.137), channel_id=1, source_target_pairs={{0,4},{4,0},{1,5},{5,1},{2,6},{6,2},{3,7},{7,3},{8,12},{12,8},{9,1... | collective-permute-start | bytes 1671176 | tf_op jit(solution)/shard_map/ppermute | solution.py:557
  138.3 21.0 %slice-start.1 = ((s8[4718592]{0:T(1024)(128)(4,1)}), s8[524288]{0:T(1024)(128)(4,1)S(1)}, s32[]{:S(2)}) async-start(s8[4718592]{0:T(1024)(128)(4,1)} %bitcast.36), calls=%async_computation.1 | async-start | bytes 1048576
  138.3 13.1 %collective-permute-start.41 = (bf16[2,2,2,256,128]{4,3,2,1,0:T(8,128)(2,1)S(1)}, bf16[2,2,2,256,128]{4,3,2,1,0:T(8,128)(2,1)S(1)}, u32[]{:S(2)}, u32[]{:S(2)}) collective-permute-start(bf16[2,2,2,256,128]{4,3,2,1,0:T(8,128)(2,1)S(1)} %get-tuple-element.138), channel_id=1, source_target_pairs={{0,1},{1,0},{2,3},{3,2},{4,5},{5,4},{6,7},{7,6},{8,9},{9,8},{10,11... | collective-permute-start | bytes 1572872 | tf_op jit(solution)/shard_map/ppermute | solution.py:557
  151.5 4.5 %collective-permute-start.44 = (bf16[4,2,2,9,32,256]{5,4,3,2,1,0:T(8,128)(2,1)S(1)}, bf16[4,2,2,9,32,256]{5,4,3,2,1,0:T(8,128)(2,1)S(1)}, u32[]{:S(2)}, u32[]{:S(2)}) collective-permute-start(bf16[4,2,2,9,32,256]{5,4,3,2,1,0:T(8,128)(2,1)S(1)} %get-tuple-element.150), channel_id=1, source_target_pairs={{0,2},{2,0},{1,3},{3,1},{4,6},{6,4},{5,7},{7,5},{8,10},{10,8},{9,1... | collective-permute-start | bytes 7077896 | tf_op jit(solution)/shard_map/ppermute | solution.py:557
  152.2 19.4 %collective-permute-start.43 = (bf16[2,2,256,128]{3,2,1,0:T(8,128)(2,1)S(1)}, bf16[2,2,256,128]{3,2,1,0:T(8,128)(2,1)S(1)}, u32[]{:S(2)}, u32[]{:S(2)}) collective-permute-start(bf16[2,2,256,128]{3,2,1,0:T(8,128)(2,1)S(1)} %get-tuple-element.147), channel_id=1, source_target_pairs={{0,4},{4,0},{1,5},{5,1},{2,6},{6,2},{3,7},{7,3},{8,12},{12,8},{9,1... | collective-permute-start | bytes 786440 | tf_op jit(solution)/shard_map/ppermute | solution.py:557
  153.3 18.4 %collective-permute-start.42 = (bf16[2,2,272,128]{3,2,1,0:T(8,128)(2,1)S(1)}, bf16[2,2,272,128]{3,2,1,0:T(8,128)(2,1)S(1)}, u32[]{:S(2)}, u32[]{:S(2)}) collective-permute-start(bf16[2,2,272,128]{3,2,1,0:T(8,128)(2,1)S(1)} %get-tuple-element.146), channel_id=1, source_target_pairs={{0,1},{1,0},{2,3},{3,2},{4,5},{5,4},{6,7},{7,6},{8,9},{9,8},{10,11... | collective-permute-start | bytes 835592 | tf_op jit(solution)/shard_map/ppermute | solution.py:557
  156.0 3.4 %copy-start.4 = (f32[2048,512]{1,0:T(8,128)S(1)}, f32[2048,512]{1,0:T(8,128)}, u32[]{:S(2)}) copy-start(f32[2048,512]{1,0:T(8,128)} %get-tuple-element.154.gh) | copy-start | bytes 12582916
  157.1 18.0 %collective-permute-start.45 = (bf16[2,2,2,5,32,256]{5,4,3,2,1,0:T(8,128)(2,1)S(1)}, bf16[2,2,2,5,32,256]{5,4,3,2,1,0:T(8,128)(2,1)S(1)}, u32[]{:S(2)}, u32[]{:S(2)}) collective-permute-start(bf16[2,2,2,5,32,256]{5,4,3,2,1,0:T(8,128)(2,1)S(1)} %get-tuple-element.152), channel_id=1, source_target_pairs={{0,4},{4,0},{1,5},{5,1},{2,6},{6,2},{3,7},{7,3},{8,12},{12,8},{9,1... | collective-permute-start | bytes 1966088 | tf_op jit(solution)/shard_map/ppermute | solution.py:557
  158.2 15.2 %collective-permute-start.46 = (bf16[2,2,2,4,32,256]{5,4,3,2,1,0:T(8,128)(2,1)S(1)}, bf16[2,2,2,4,32,256]{5,4,3,2,1,0:T(8,128)(2,1)S(1)}, u32[]{:S(2)}, u32[]{:S(2)}) collective-permute-start(bf16[2,2,2,4,32,256]{5,4,3,2,1,0:T(8,128)(2,1)S(1)} %get-tuple-element.158), channel_id=1, source_target_pairs={{0,1},{1,0},{2,3},{3,2},{4,5},{5,4},{6,7},{7,6},{8,9},{9,8},{10,11... | collective-permute-start | bytes 1572872 | tf_op jit(solution)/shard_map/ppermute | solution.py:557
  172.4 8.0 %collective-permute-start.49 = (bf16[2,528,128]{2,1,0:T(8,128)(2,1)S(1)}, bf16[2,528,128]{2,1,0:T(8,128)(2,1)S(1)}, u32[]{:S(2)}, u32[]{:S(2)}) collective-permute-start(bf16[2,528,128]{2,1,0:T(8,128)(2,1)S(1)} %get-tuple-element.163), channel_id=1, source_target_pairs={{0,8},{8,0},{16,24},{24,16},{1,9},{9,1},{17,25},{25,17},{2,10},{10... | collective-permute-start | bytes 811016 | tf_op jit(solution)/shard_map/ppermute | solution.py:557
  175.9 9.4 %collective-permute-start.47 = (bf16[2,2,5,32,256]{4,3,2,1,0:T(8,128)(2,1)S(1)}, bf16[2,2,5,32,256]{4,3,2,1,0:T(8,128)(2,1)S(1)}, u32[]{:S(2)}, u32[]{:S(2)}) collective-permute-start(bf16[2,2,5,32,256]{4,3,2,1,0:T(8,128)(2,1)S(1)} %get-tuple-element.168), channel_id=1, source_target_pairs={{0,1},{1,0},{2,3},{3,2},{4,5},{5,4},{6,7},{7,6},{8,9},{9,8},{10,11... | collective-permute-start | bytes 983048 | tf_op jit(solution)/shard_map/ppermute | solution.py:557
  177.1 7.7 %collective-permute-start.48 = (bf16[2,2,4,32,256]{4,3,2,1,0:T(8,128)(2,1)S(1)}, bf16[2,2,4,32,256]{4,3,2,1,0:T(8,128)(2,1)S(1)}, u32[]{:S(2)}, u32[]{:S(2)}) collective-permute-start(bf16[2,2,4,32,256]{4,3,2,1,0:T(8,128)(2,1)S(1)} %get-tuple-element.169), channel_id=1, source_target_pairs={{0,4},{4,0},{1,5},{5,1},{2,6},{6,2},{3,7},{7,3},{8,12},{12,8},{9,1... | collective-permute-start | bytes 786440 | tf_op jit(solution)/shard_map/ppermute | solution.py:557
  181.1 8.7 %collective-permute-start.52 = (bf16[528,128]{1,0:T(8,128)(2,1)S(1)}, bf16[528,128]{1,0:T(8,128)(2,1)S(1)}, u32[]{:S(2)}, u32[]{:S(2)}) collective-permute-start(bf16[528,128]{1,0:T(8,128)(2,1)S(1)} %get-tuple-element.172), channel_id=1, source_target_pairs={{0,16},{8,24},{16,0},{24,8},{1,17},{9,25},{17,1},{25,9},{2,18},{10... | collective-permute-start | bytes 405512 | tf_op jit(solution)/shard_map/ppermute | solution.py:557
  186.0 9.0 %collective-permute-start.50 = (bf16[2,9,32,256]{3,2,1,0:T(8,128)(2,1)S(1)}, bf16[2,9,32,256]{3,2,1,0:T(8,128)(2,1)S(1)}, u32[]{:S(2)}, u32[]{:S(2)}) collective-permute-start(bf16[2,9,32,256]{3,2,1,0:T(8,128)(2,1)S(1)} %get-tuple-element.177), channel_id=1, source_target_pairs={{0,8},{8,0},{16,24},{24,16},{1,9},{9,1},{17,25},{25,17},{2,10},{10... | collective-permute-start | bytes 884744 | tf_op jit(solution)/shard_map/ppermute | solution.py:557
  195.7 9.1 %collective-permute-start.51 = (bf16[9,32,256]{2,1,0:T(8,128)(2,1)S(1)}, bf16[9,32,256]{2,1,0:T(8,128)(2,1)S(1)}, u32[]{:S(2)}, u32[]{:S(2)}) collective-permute-start(bf16[9,32,256]{2,1,0:T(8,128)(2,1)S(1)} %get-tuple-element.179), channel_id=1, source_target_pairs={{0,16},{8,24},{16,0},{24,8},{1,17},{9,25},{17,1},{25,9},{2,18},{10... | collective-permute-start | bytes 442376 | tf_op jit(solution)/shard_map/ppermute | solution.py:557
  (3 other events, 5.4 us)

commit v5 on v4

--- a/solution.py
+++ b/solution.py
@@ -586,7 +586,7 @@
     cut = own.shape[1] // 2
     top = lambda value: swap(value[:, :cut], Y)
     bottom = lambda value: swap(value[:, cut:], X)
-    halo, own_y, own_x, far = lax.optimization_barrier((swap(halo, Y), swap(own, Y), swap(own, X), swap(own, Z1)))
+    own_y, own_x, far = lax.optimization_barrier((swap(own, Y), swap(own, X), swap(own, Z1)))
     column = jnp.concatenate([own, far], 0)
     near, far_x, far_y, own_top, own_bottom = lax.optimization_barrier(
         (swap(column, Z0), swap(far, X), swap(far, Y), top(own_x), bottom(own_y))
@@ -595,6 +595,7 @@
     near_y, near_x, far_top, far_bottom, pair_far = lax.optimization_barrier(
         (swap(near, Y), swap(near, X), top(far_x), bottom(far_y), swap(pair, Z1))
     )
+    halo = swap(after(halo, far_top), Y)
     near_top, near_bottom = top(near_x), bottom(near_y)
     pair = jnp.concatenate([pair, pair_far], 0)
     pair = jnp.concatenate([pair, swap(pair, Z0)], 0)
@@ -720,11 +721,8 @@
     conv_pieces, conv_plan = list(conv_pieces), tuple((None if o is None else tuple(o), f) for o, f in conv_plan)
     xhat, scale, conv_full, table = conv_forward(flags, prev, x, nxt, conv_pieces, conv_plan, small, table, 2, hidden)
     if fast:
-        (column, over_x, over_y, across), table = lax.optimization_barrier((pair_pieces, table))
-        others = [swap(a, CORE) for a in (column, over_x, over_y)]
-        others, across = lax.optimization_barrier((others, across))
-        pair_pieces = [column, over_x, over_y, across] + others + [swap(across, CORE)]
-        pair_plan = tuple(pair_plan) + tuple((shifted(o, 1, 0), first) for o, first in pair_plan)
+        pair_pieces, table = lax.optimization_barrier((pair_pieces, table))
+        pair_pieces, pair_plan = both_cores(pair_pieces, pair_plan)
     pair_plan = tuple((None if o is None else tuple(o), f) for o, f in pair_plan)
     block_output, grad_hidden, grad_conv, *ffn_grads = ffn(
         flags, x, xhat, scale, og, table, pair_pieces, pair_plan, 2 * SUB, min(1024, hidden), batch, fast

time: 206 us -> 203 us (0.985)
  waiting for transfers between devices: 52 us -> 45 us
  starting transfers between devices: 44.5 us -> 49.1 us
    ppermute x52, waiting for transfers between devices: 52 us -> 45 us  [swap(): lax.ppermute(value, axis, [(i, i ^ bit) for i in range(lax.axis_size(axis...]
    ppermute x52, starting transfers between devices: 43.7 us -> 47.5 us  [swap(): lax.ppermute(value, axis, [(i, i ^ bit) for i in range(lax.axis_size(axis...]
  transfers between devices with their start and end apart: 53 -> 53, of which waited for: 26 -> 29; matrix products, arithmetic and copies ran while one was open for 3% -> 3% of each run, Pallas kernels for 24% -> 24%
where the time goes in v5:
time: 203 us
  Pallas kernels  101 us (50%)
  starting transfers between devices  49.1 us (24%)
  waiting for transfers between devices  45 us (22%)
  local copies, waits for them, and re-layouts  5.33 us (3%)
    pallas_call x1, Pallas kernels, ffn(): pl.pallas_call(functools.partial(ffn_kernel, chunk, fast, plan), grid_spe...  48.1 us
    ppermute x52, starting transfers between devices, swap(): lax.ppermute(value, axis, [(i, i ^ bit) for i in range(lax.axis_size(axis...  47.5 us
    ppermute x52, waiting for transfers between devices, swap(): lax.ppermute(value, axis, [(i, i ^ bit) for i in range(lax.axis_size(axis...  45 us
    pallas_call x1, Pallas kernels, conv_forward(): pl.pallas_call(functools.partial(conv_kernel, subs, plan, small), grid_sp...  18.5 us
    pallas_call x2, Pallas kernels, conv_weight_backward(): pl.pallas_call(functools.partial(conv_weight_kernel, fast, first), grid_s...  13.8 us
    pallas_call x1, Pallas kernels, conv_input_backward(): pl.pallas_call(functools.partial(conv_input_kernel, subs), grid_spec=pltp...  12.3 us
    pallas_call x6, Pallas kernels, stage(): pl.pallas_call(functools.partial(stage_kernel, columns, joined), grid_spe...  4.29 us
  transfers between devices with their start and end apart: 53, of which 29 were waited for; matrix products, arithmetic and copies ran while one was open for 3% of the time, Pallas kernels for 24%

profile of v5, /device:TPU:0, one launch (start us, length us, event | category | flops | bytes accessed | tf_op | source)
XLA Modules:
  0.0 203.2 jit_solution(3180221489962506302)
XLA Ops:
  0.6 2.1 %pack.1 = (s32[6,8]{1,0:T(8,128)}, bf16[128,512]{1,0:T(8,128)(2,1)}, bf16[1,10,32,256]{3,2,1,0:T(8,128)(2,1)}, bf16[1,2,128,256]{3,2,1,0:T(8,128)(2,1)}) custom-call(s32[1,9]{1,0:T(1,128)} %lengths.1, bf16[2048,512]{1,0:T(8,128)(2,1)} %bitcast.30, bf16[2048,512]{1,0:T(8,128)(2,1)} %bitcast.31, bf16[9,32,256]{2,1,0:T(8,128)(2,1)} %bitcast.38, ...), custom_call_target="tpu_custom_call" | custom-call | tf_op jit(solution)/shard_map/pack/pallas_call | solution.py:544
  2.8 4.1 %collective-permute-start.2 = (bf16[1,10,32,256]{3,2,1,0:T(8,128)(2,1)}, bf16[1,10,32,256]{3,2,1,0:T(8,128)(2,1)S(1)}, u32[]{:S(2)}, u32[]{:S(2)}) collective-permute-start(bf16[1,10,32,256]{3,2,1,0:T(8,128)(2,1)} %get-tuple-element.95), channel_id=1, source_target_pairs={{0,16},{8,24},{16,0},{24,8},{1,17},{9,25},{17,1},{25,9},{2,18},{10... | collective-permute-start | bytes 491528 | tf_op jit(solution)/shard_map/ppermute | solution.py:557
  6.9 1.5 collective-permute-start.1
  8.4 1.5 collective-permute-start
  9.9 1.0 constant_dynamic-update-slice_fusion.1
  10.8 3.9 %collective-permute-done.2 = bf16[1,10,32,256]{3,2,1,0:T(8,128)(2,1)S(1)} collective-permute-done((bf16[1,10,32,256]{3,2,1,0:T(8,128)(2,1)}, bf16[1,10,32,256]{3,2,1,0:T(8,128)(2,1)S(1)}, u32[]{:S(2)}, u32[]{:S(2)}) %collective-permute-start.2) | collective-permute-done | bytes 163872 | tf_op jit(solution)/shard_map/ppermute | solution.py:557
  14.8 0.9 collective-permute-start.3
  15.7 1.5 collective-permute-start.5
  17.2 1.5 collective-permute-start.4
  19.8 4.7 %collective-permute-done.7.rest_5_ = bf16[1,5,32,256]{3,2,1,0:T(8,128)(2,1)S(1)} collective-permute-done((bf16[1,5,32,256]{3,2,1,0:T(8,128)(2,1)S(1)}, bf16[1,5,32,256]{3,2,1,0:T(8,128)(2,1)S(1)}, u32[]{:S(2)}, u32[]{:S(2)}) %collective-permute-start.7) | collective-permute-done | bytes 81952 | tf_op jit(solution)/shard_map/ppermute | solution.py:557
  24.6 1.6 collective-permute-start.9
  26.6 3.3 %collective-permute-start.12 = (bf16[1,2,128,256]{3,2,1,0:T(8,128)(2,1)}, bf16[1,2,128,256]{3,2,1,0:T(8,128)(2,1)S(1)}, u32[]{:S(2)}, u32[]{:S(2)}) collective-permute-start(bf16[1,2,128,256]{3,2,1,0:T(8,128)(2,1)} %get-tuple-element.104), channel_id=1, source_target_pairs={{0,16},{8,24},{16,0},{24,8},{1,17},{9,25},{17,1},{25,9},{2,18},{10... | collective-permute-start | bytes 393224 | tf_op jit(solution)/shard_map/ppermute | solution.py:557
  30.4 1.5 collective-permute-start.10
  32.0 2.6 %collective-permute-done.11.rest_9_ = bf16[1,5,32,256]{3,2,1,0:T(8,128)(2,1)S(1)} collective-permute-done((bf16[1,5,32,256]{3,2,1,0:T(8,128)(2,1)S(1)}, bf16[1,5,32,256]{3,2,1,0:T(8,128)(2,1)S(1)}, u32[]{:S(2)}, u32[]{:S(2)}) %collective-permute-start.11) | collective-permute-done | bytes 81952 | tf_op jit(solution)/shard_map/ppermute | solution.py:557
  34.5 1.2 collective-permute-done.10.rest_8_
  37.7 0.9 pad_maximum_fusion
  38.6 1.4 collective-permute-start.30
  40.0 0.9 constant_dynamic-update-slice_fusion.4
  41.3 1.5 collective-permute-start.13
  42.8 0.7 collective-permute-start.15
  43.6 0.8 collective-permute-start.14
  44.4 2.7 %collective-permute-done.30 = bf16[2,2,128,256]{3,2,1,0:T(8,128)(2,1)S(1)} collective-permute-done((bf16[2,2,128,256]{3,2,1,0:T(8,128)(2,1)S(1)}, bf16[2,2,128,256]{3,2,1,0:T(8,128)(2,1)S(1)}, u32[]{:S(2)}, u32[]{:S(2)}) %collective-permute-start.30) | collective-permute-done | bytes 262176 | tf_op jit(solution)/shard_map/ppermute | solution.py:557
  47.1 1.3 collective-permute-done.25.rest_23_
  48.4 1.6 collective-permute-start.33
  50.6 1.3 collective-permute-start.31
  52.4 0.9 collective-permute-done.29.rest_27_
  53.8 1.1 collective-permute-done.26.rest_24_
  55.4 18.5 %conv_forward.1 = (f32[2048,512]{1,0:T(8,128)}, f32[2048,512]{1,0:T(8,128)}, bf16[9,512,512]{2,1,0:T(8,128)(2,1)}, f32[8,2048]{1,0:T(8,128)S(1)}) custom-call(s32[6,8]{1,0:T(8,128)S(1)} %copy-done.3, bf16[128,512]{1,0:T(8,128)(2,1)S(1)} %collective-permute-done.13.prev.nxt, bf16[2048,512]{1,0:T(8,128)(2,1)S(1)} %bitcast.33, ...), custom_call_target="tpu_custom_call" | custom-call | flops 1 | bytes 1 | tf_op jit(solution)/shard_map/conv_forward/pallas_call | solution.py:190
  75.6 0.9 collective-permute-done.34.rest_4_
  76.5 0.7 collective-permute-done.35.rest_5_
  77.2 0.7 collective-permute-done.36.rest_6_
  78.0 0.7 collective-permute-done.37.rest_7_
  78.8 0.7 copy-done.11
  79.5 48.1 %feed_forward.1 = (bf16[2048,512]{1,0:T(8,128)(2,1)}, f32[2048,512]{1,0:T(8,128)}, bf16[2048,512]{1,0:T(8,128)(2,1)S(1)}, bf16[128,512]{1,0:T(8,128)(2,1)S(1)}, ...) custom-call(s32[6,8]{1,0:T(8,128)S(1)} %copy-done.3, bf16[2048,512]{1,0:T(8,128)(2,1)} %bitcast.32, ...), custom_call_target="tpu_custom_call" | custom-call | flops 25769803776 | bytes 1048576 | tf_op jit(solution)/shard_map/feed_forward/pallas_call | solution.py:345
  127.8 1.1 collective-permute-start.39
  128.9 3.7 %conv_weight_backward.2 = (bf16[4,2,2,9,32,256]{5,4,3,2,1,0:T(8,128)(2,1)S(1)}, bf16[4,2,2,9,32,256]{5,4,3,2,1,0:T(8,128)(2,1)S(1)}) custom-call(s32[6,8]{1,0:T(8,128)S(1)} %copy-done.3, bf16[128,512]{1,0:T(8,128)(2,1)S(1)} %collective-permute-done.13.prev.nxt, bf16[2048,512]{1,0:T(8,128)(2,1)S(1)} %bitcast.34, ...), custom_call_target="tpu_custom_call" | custom-call | flops 2146959360 | bytes 1048576 | tf_op jit(solution)/shard_map/conv_weight_backward/pallas_call | solution.py:424
  132.6 1.1 collective-permute-done.39.prev.nxt
  133.6 1.1 stage.8
  134.7 0.8 collective-permute-start.40
  135.5 1.4 collective-permute-start.41
  136.9 10.1 %conv_weight_backward.3 = (bf16[4,2,2,9,32,256]{5,4,3,2,1,0:T(8,128)(2,1)S(1)}, bf16[4,2,2,9,32,256]{5,4,3,2,1,0:T(8,128)(2,1)S(1)}) custom-call(s32[6,8]{1,0:T(8,128)S(1)} %copy-done.3, bf16[128,512]{1,0:T(8,128)(2,1)S(1)} %collective-permute-done.13.prev.nxt, bf16[2048,512]{1,0:T(8,128)(2,1)S(1)} %bitcast.35, ...), custom_call_target="tpu_custom_call", output_to_operand_aliasing={{0}: (5, {}), {1}: (6, {})} | custom-call | flops 7511998464 | bytes 1048576 | tf_op jit(solution)/shard_map/conv_weight_backward/pallas_call | solution.py:424
  147.0 1.7 collective-permute-done.41.refs_3_
  148.9 0.8 stage.9
  149.7 1.1 collective-permute-start.43
  150.8 1.0 collective-permute-start.42
  151.8 1.6 collective-permute-done.44.got
  153.5 1.1 stage.10
  154.6 1.1 collective-permute-start.45
  155.7 1.0 collective-permute-start.46
  156.7 12.3 %conv_input_backward.1 = f32[2048,512]{1,0:T(8,128)} custom-call(s32[6,8]{1,0:T(8,128)S(1)} %copy-done.3, bf16[128,512]{1,0:T(8,128)(2,1)S(1)} %collective-permute-done.39.prev.nxt, bf16[2048,512]{1,0:T(8,128)(2,1)S(1)} %get-tuple-element.124.g, bf16[128,512]{1,0:T(8,128)(2,1)S(1)} %collective-permute-done.39.prev.nxt, f32[2048,512]{1,0:T(8,128)S(1)} %copy-done.4, ...), custom_call_target="tpu_custom_call" | custom-call | flops 9663676416 | bytes 1048576 | tf_op jit(solution)/shard_map/conv_input_backward/pallas_call | solution.py:469
  169.7 1.5 collective-permute-start.49
  171.2 1.3 collective-permute-done.45.refs_1_
  172.6 0.8 stage.12
  173.4 1.1 collective-permute-start.47
  174.5 1.0 collective-permute-start.48
  175.5 2.3 %collective-permute-done.49.refs_1_ = bf16[2,528,128]{2,1,0:T(8,128)(2,1)S(1)} collective-permute-done((bf16[2,528,128]{2,1,0:T(8,128)(2,1)S(1)}, bf16[2,528,128]{2,1,0:T(8,128)(2,1)S(1)}, u32[]{:S(2)}, u32[]{:S(2)}) %collective-permute-start.49) | collective-permute-done | bytes 270368 | tf_op jit(solution)/shard_map/ppermute | solution.py:557
  178.4 3.4 %collective-permute-start.52 = (bf16[528,128]{1,0:T(8,128)(2,1)S(1)}, bf16[528,128]{1,0:T(8,128)(2,1)S(1)}, u32[]{:S(2)}, u32[]{:S(2)}) collective-permute-start(bf16[528,128]{1,0:T(8,128)(2,1)S(1)} %get-tuple-element.164), channel_id=1, source_target_pairs={{0,16},{8,24},{16,0},{24,8},{1,17},{9,25},{17,1},{25,9},{2,18},{10... | collective-permute-start | bytes 405512 | tf_op jit(solution)/shard_map/ppermute | solution.py:557
  183.5 1.2 collective-permute-start.50
  184.7 2.5 %collective-permute-done.52 = bf16[528,128]{1,0:T(8,128)(2,1)S(1)} collective-permute-done((bf16[528,128]{1,0:T(8,128)(2,1)S(1)}, bf16[528,128]{1,0:T(8,128)(2,1)S(1)}, u32[]{:S(2)}, u32[]{:S(2)}) %collective-permute-start.52) | collective-permute-done | bytes 135200 | tf_op jit(solution)/shard_map/ppermute | solution.py:557
  187.9 0.8 copy.27
  189.2 3.4 %collective-permute-done.50.refs_1_ = bf16[2,9,32,256]{3,2,1,0:T(8,128)(2,1)S(1)} collective-permute-done((bf16[2,9,32,256]{3,2,1,0:T(8,128)(2,1)S(1)}, bf16[2,9,32,256]{3,2,1,0:T(8,128)(2,1)S(1)}, u32[]{:S(2)}, u32[]{:S(2)}) %collective-permute-start.50) | collective-permute-done | bytes 294944 | tf_op jit(solution)/shard_map/ppermute | solution.py:557
  193.3 2.2 %collective-permute-start.51 = (bf16[9,32,256]{2,1,0:T(8,128)(2,1)S(1)}, bf16[9,32,256]{2,1,0:T(8,128)(2,1)S(1)}, u32[]{:S(2)}, u32[]{:S(2)}) collective-permute-start(bf16[9,32,256]{2,1,0:T(8,128)(2,1)S(1)} %get-tuple-element.171), channel_id=1, source_target_pairs={{0,16},{8,24},{16,0},{24,8},{1,17},{9,25},{17,1},{25,9},{2,18},{10... | collective-permute-start | bytes 442376 | tf_op jit(solution)/shard_map/ppermute | solution.py:557
  196.0 6.4 %collective-permute-done.51 = bf16[9,32,256]{2,1,0:T(8,128)(2,1)S(1)} collective-permute-done((bf16[9,32,256]{2,1,0:T(8,128)(2,1)S(1)}, bf16[9,32,256]{2,1,0:T(8,128)(2,1)S(1)}, u32[]{:S(2)}, u32[]{:S(2)}) %collective-permute-start.51) | collective-permute-done | bytes 147488 | tf_op jit(solution)/shard_map/ppermute | solution.py:557
  202.4 0.8 add_bitcast_fusion
  (105 shorter events, 14.4 us)
Async XLA Ops:
  2.7 38.6 %copy-start.12 = (bf16[128,512]{1,0:T(8,128)(2,1)S(1)}, bf16[128,512]{1,0:T(8,128)(2,1)}, u32[]{:S(2)}) copy-start(bf16[128,512]{1,0:T(8,128)(2,1)} %get-tuple-element.106) | copy-start | bytes 393220
  2.7 52.6 %copy-start = (bf16[1,2048,512]{2,1,0:T(8,128)(2,1)S(1)}, bf16[1,2048,512]{2,1,0:T(8,128)(2,1)}, u32[]{:S(2)}) copy-start(bf16[1,2048,512]{2,1,0:T(8,128)(2,1)} %param.13) | copy-start | bytes 6291460
  2.7 52.6 %copy-start.3 = (s32[6,8]{1,0:T(8,128)S(1)}, s32[6,8]{1,0:T(8,128)}, u32[]{:S(2)}) copy-start(s32[6,8]{1,0:T(8,128)} %get-tuple-element.93.flags) | copy-start | bytes 580
  2.8 12.0 %collective-permute-start.2 = (bf16[1,10,32,256]{3,2,1,0:T(8,128)(2,1)}, bf16[1,10,32,256]{3,2,1,0:T(8,128)(2,1)S(1)}, u32[]{:S(2)}, u32[]{:S(2)}) collective-permute-start(bf16[1,10,32,256]{3,2,1,0:T(8,128)(2,1)} %get-tuple-element.95), channel_id=1, source_target_pairs={{0,16},{8,24},{16,0},{24,8},{1,17},{9,25},{17,1},{25,9},{2,18},{10... | collective-permute-start | bytes 491528 | tf_op jit(solution)/shard_map/ppermute | solution.py:557
  6.9 7.9 %collective-permute-start.1 = (bf16[1,10,32,256]{3,2,1,0:T(8,128)(2,1)}, bf16[1,10,32,256]{3,2,1,0:T(8,128)(2,1)S(1)}, u32[]{:S(2)}, u32[]{:S(2)}) collective-permute-start(bf16[1,10,32,256]{3,2,1,0:T(8,128)(2,1)} %get-tuple-element.95), channel_id=1, source_target_pairs={{0,4},{4,0},{1,5},{5,1},{2,6},{6,2},{3,7},{7,3},{8,12},{12,8},{9,1... | collective-permute-start | bytes 491528 | tf_op jit(solution)/shard_map/ppermute | solution.py:557
  8.4 6.4 %collective-permute-start = (bf16[1,10,32,256]{3,2,1,0:T(8,128)(2,1)}, bf16[1,10,32,256]{3,2,1,0:T(8,128)(2,1)S(1)}, u32[]{:S(2)}, u32[]{:S(2)}) collective-permute-start(bf16[1,10,32,256]{3,2,1,0:T(8,128)(2,1)} %get-tuple-element.95), channel_id=1, source_target_pairs={{0,1},{1,0},{2,3},{3,2},{4,5},{5,4},{6,7},{7,6},{8,9},{9,8},{10,11... | collective-permute-start | bytes 491528 | tf_op jit(solution)/shard_map/ppermute | solution.py:557
  14.8 9.7 %collective-permute-start.3 = (bf16[2,10,32,256]{3,2,1,0:T(8,128)(2,1)S(1)}, bf16[2,10,32,256]{3,2,1,0:T(8,128)(2,1)S(1)}, u32[]{:S(2)}, u32[]{:S(2)}) collective-permute-start(bf16[2,10,32,256]{3,2,1,0:T(8,128)(2,1)S(1)} %constant_dynamic-update-slice_fusion.rest_0_), channel_id=1, source_target_pairs={{0,8},{8,0},{16,24},{24,16},{1,9},{9,1},{17,25},{25,17},{2,10},{10... | collective-permute-start | bytes 983048 | tf_op jit(solution)/shard_map/ppermute | solution.py:557
  15.7 8.8 %collective-permute-start.5 = (bf16[1,10,32,256]{3,2,1,0:T(8,128)(2,1)S(1)}, bf16[1,10,32,256]{3,2,1,0:T(8,128)(2,1)S(1)}, u32[]{:S(2)}, u32[]{:S(2)}) collective-permute-start(bf16[1,10,32,256]{3,2,1,0:T(8,128)(2,1)S(1)} %collective-permute-done.2), channel_id=1, source_target_pairs={{0,1},{1,0},{2,3},{3,2},{4,5},{5,4},{6,7},{7,6},{8,9},{9,8},{10,11... | collective-permute-start | bytes 491528 | tf_op jit(solution)/shard_map/ppermute | solution.py:557
  17.2 7.3 %collective-permute-start.4 = (bf16[1,10,32,256]{3,2,1,0:T(8,128)(2,1)S(1)}, bf16[1,10,32,256]{3,2,1,0:T(8,128)(2,1)S(1)}, u32[]{:S(2)}, u32[]{:S(2)}) collective-permute-start(bf16[1,10,32,256]{3,2,1,0:T(8,128)(2,1)S(1)} %collective-permute-done.2), channel_id=1, source_target_pairs={{0,4},{4,0},{1,5},{5,1},{2,6},{6,2},{3,7},{7,3},{8,12},{12,8},{9,1... | collective-permute-start | bytes 491528 | tf_op jit(solution)/shard_map/ppermute | solution.py:557
  18.7 5.8 %collective-permute-start.7 = (bf16[1,5,32,256]{3,2,1,0:T(8,128)(2,1)S(1)}, bf16[1,5,32,256]{3,2,1,0:T(8,128)(2,1)S(1)}, u32[]{:S(2)}, u32[]{:S(2)}) collective-permute-start(bf16[1,5,32,256]{3,2,1,0:T(8,128)(2,1)S(1)} %slice.46), channel_id=1, source_target_pairs={{0,4},{4,0},{1,5},{5,1},{2,6},{6,2},{3,7},{7,3},{8,12},{12,8},{9,1... | collective-permute-start | bytes 245768 | tf_op jit(solution)/shard_map/ppermute | solution.py:557
  19.3 5.2 %collective-permute-start.6 = (bf16[1,5,32,256]{3,2,1,0:T(8,128)(2,1)S(1)}, bf16[1,5,32,256]{3,2,1,0:T(8,128)(2,1)S(1)}, u32[]{:S(2)}, u32[]{:S(2)}) collective-permute-start(bf16[1,5,32,256]{3,2,1,0:T(8,128)(2,1)S(1)} %slice.45), channel_id=1, source_target_pairs={{0,1},{1,0},{2,3},{3,2},{4,5},{5,4},{6,7},{7,6},{8,9},{9,8},{10,11... | collective-permute-start | bytes 245768 | tf_op jit(solution)/shard_map/ppermute | solution.py:557
  24.6 11.7 %collective-permute-start.9 = (bf16[2,10,32,256]{3,2,1,0:T(8,128)(2,1)S(1)}, bf16[2,10,32,256]{3,2,1,0:T(8,128)(2,1)S(1)}, u32[]{:S(2)}, u32[]{:S(2)}) collective-permute-start(bf16[2,10,32,256]{3,2,1,0:T(8,128)(2,1)S(1)} %collective-permute-done.3.rest_1_), channel_id=1, source_target_pairs={{0,4},{4,0},{1,5},{5,1},{2,6},{6,2},{3,7},{7,3},{8,12},{12,8},{9,1... | collective-permute-start | bytes 983048 | tf_op jit(solution)/shard_map/ppermute | solution.py:557
  26.1 10.2 %collective-permute-start.8 = (bf16[2,10,32,256]{3,2,1,0:T(8,128)(2,1)S(1)}, bf16[2,10,32,256]{3,2,1,0:T(8,128)(2,1)S(1)}, u32[]{:S(2)}, u32[]{:S(2)}) collective-permute-start(bf16[2,10,32,256]{3,2,1,0:T(8,128)(2,1)S(1)} %collective-permute-done.3.rest_1_), channel_id=1, source_target_pairs={{0,1},{1,0},{2,3},{3,2},{4,5},{5,4},{6,7},{7,6},{8,9},{9,8},{10,11... | collective-permute-start | bytes 983048 | tf_op jit(solution)/shard_map/ppermute | solution.py:557
  26.6 9.1 %collective-permute-start.12 = (bf16[1,2,128,256]{3,2,1,0:T(8,128)(2,1)}, bf16[1,2,128,256]{3,2,1,0:T(8,128)(2,1)S(1)}, u32[]{:S(2)}, u32[]{:S(2)}) collective-permute-start(bf16[1,2,128,256]{3,2,1,0:T(8,128)(2,1)} %get-tuple-element.104), channel_id=1, source_target_pairs={{0,16},{8,24},{16,0},{24,8},{1,17},{9,25},{17,1},{25,9},{2,18},{10... | collective-permute-start | bytes 393224 | tf_op jit(solution)/shard_map/ppermute | solution.py:557
  29.9 4.6 %collective-permute-start.11 = (bf16[1,5,32,256]{3,2,1,0:T(8,128)(2,1)S(1)}, bf16[1,5,32,256]{3,2,1,0:T(8,128)(2,1)S(1)}, u32[]{:S(2)}, u32[]{:S(2)}) collective-permute-start(bf16[1,5,32,256]{3,2,1,0:T(8,128)(2,1)S(1)} %slice.48), channel_id=1, source_target_pairs={{0,4},{4,0},{1,5},{5,1},{2,6},{6,2},{3,7},{7,3},{8,12},{12,8},{9,1... | collective-permute-start | bytes 245768 | tf_op jit(solution)/shard_map/ppermute | solution.py:557
  30.4 5.3 %collective-permute-start.10 = (bf16[1,5,32,256]{3,2,1,0:T(8,128)(2,1)S(1)}, bf16[1,5,32,256]{3,2,1,0:T(8,128)(2,1)S(1)}, u32[]{:S(2)}, u32[]{:S(2)}) collective-permute-start(bf16[1,5,32,256]{3,2,1,0:T(8,128)(2,1)S(1)} %slice.47), channel_id=1, source_target_pairs={{0,1},{1,0},{2,3},{3,2},{4,5},{5,4},{6,7},{7,6},{8,9},{9,8},{10,11... | collective-permute-start | bytes 245768 | tf_op jit(solution)/shard_map/ppermute | solution.py:557
  34.5 4.1 %collective-permute-start.16 = (bf16[2,10,32,256]{3,2,1,0:T(8,128)(2,1)S(1)}, bf16[2,10,32,256]{3,2,1,0:T(8,128)(2,1)S(1)}, u32[]{:S(2)}, u32[]{:S(2)}) collective-permute-start(bf16[2,10,32,256]{3,2,1,0:T(8,128)(2,1)S(1)} %constant_dynamic-update-slice_fusion.rest_0_), channel_id=1, source_target_pairs={{0,2},{2,0},{1,3},{3,1},{4,6},{6,4},{5,7},{7,5},{8,10},{10,8},{9,1... | collective-permute-start | bytes 983048 | tf_op jit(solution)/shard_map/ppermute | solution.py:557
  35.7 1.4 collective-permute-start.18
  35.7 1.6 collective-permute-start.19
  36.3 6.6 %collective-permute-start.22 = (bf16[1,10,32,256]{3,2,1,0:T(8,128)(2,1)S(1)}, bf16[1,10,32,256]{3,2,1,0:T(8,128)(2,1)S(1)}, u32[]{:S(2)}, u32[]{:S(2)}) collective-permute-start(bf16[1,10,32,256]{3,2,1,0:T(8,128)(2,1)S(1)} %collective-permute-done.4.rest_6_), channel_id=1, source_target_pairs={{0,2},{2,0},{1,3},{3,1},{4,6},{6,4},{5,7},{7,5},{8,10},{10,8},{9,1... | collective-permute-start | bytes 491528 | tf_op jit(solution)/shard_map/ppermute | solution.py:557
  36.3 7.2 %collective-permute-start.23 = (bf16[1,10,32,256]{3,2,1,0:T(8,128)(2,1)S(1)}, bf16[1,10,32,256]{3,2,1,0:T(8,128)(2,1)S(1)}, u32[]{:S(2)}, u32[]{:S(2)}) collective-permute-start(bf16[1,10,32,256]{3,2,1,0:T(8,128)(2,1)S(1)} %collective-permute-done.5.rest_7_), channel_id=1, source_target_pairs={{0,2},{2,0},{1,3},{3,1},{4,6},{6,4},{5,7},{7,5},{8,10},{10,8},{9,1... | collective-permute-start | bytes 491528 | tf_op jit(solution)/shard_map/ppermute | solution.py:557
  37.1 7.2 %collective-permute-start.17 = (bf16[2,10,32,256]{3,2,1,0:T(8,128)(2,1)S(1)}, bf16[2,10,32,256]{3,2,1,0:T(8,128)(2,1)S(1)}, u32[]{:S(2)}, u32[]{:S(2)}) collective-permute-start(bf16[2,10,32,256]{3,2,1,0:T(8,128)(2,1)S(1)} %collective-permute-done.3.rest_1_), channel_id=1, source_target_pairs={{0,2},{2,0},{1,3},{3,1},{4,6},{6,4},{5,7},{7,5},{8,10},{10,8},{9,1... | collective-permute-start | bytes 983048 | tf_op jit(solution)/shard_map/ppermute | solution.py:557
  37.4 2.6 %collective-permute-start.21 = (bf16[1,5,32,256]{3,2,1,0:T(8,128)(2,1)S(1)}, bf16[1,5,32,256]{3,2,1,0:T(8,128)(2,1)S(1)}, u32[]{:S(2)}, u32[]{:S(2)}) collective-permute-start(bf16[1,5,32,256]{3,2,1,0:T(8,128)(2,1)S(1)} %collective-permute-done.7.rest_5_), channel_id=1, source_target_pairs={{0,2},{2,0},{1,3},{3,1},{4,6},{6,4},{5,7},{7,5},{8,10},{10,8},{9,1... | collective-permute-start | bytes 245768 | tf_op jit(solution)/shard_map/ppermute | solution.py:557
  38.6 8.5 %collective-permute-start.30 = (bf16[2,2,128,256]{3,2,1,0:T(8,128)(2,1)S(1)}, bf16[2,2,128,256]{3,2,1,0:T(8,128)(2,1)S(1)}, u32[]{:S(2)}, u32[]{:S(2)}) collective-permute-start(bf16[2,2,128,256]{3,2,1,0:T(8,128)(2,1)S(1)} %pad_maximum_fusion), channel_id=1, source_target_pairs={{0,8},{8,0},{16,24},{24,16},{1,9},{9,1},{17,25},{25,17},{2,10},{10... | collective-permute-start | bytes 786440 | tf_op jit(solution)/shard_map/ppermute | solution.py:557
  40.0 1.3 collective-permute-start.20
  41.3 9.3 %collective-permute-start.13 = (bf16[128,512]{1,0:T(8,128)(2,1)S(1)}, bf16[128,512]{1,0:T(8,128)(2,1)S(1)}, u32[]{:S(2)}, u32[]{:S(2)}) collective-permute-start(bf16[128,512]{1,0:T(8,128)(2,1)S(1)} %copy-done.12), channel_id=1, source_target_pairs={{0,1},{1,0},{2,3},{3,2},{4,5},{5,4},{6,7},{7,6},{8,9},{9,8},{10,11... | collective-permute-start | bytes 393224 | tf_op jit(solution)/shard_map/ppermute | solution.py:557
  42.8 9.1 %collective-permute-start.15 = (bf16[2,5,32,256]{3,2,1,0:T(8,128)(2,1)S(1)}, bf16[2,5,32,256]{3,2,1,0:T(8,128)(2,1)S(1)}, u32[]{:S(2)}, u32[]{:S(2)}) collective-permute-start(bf16[2,5,32,256]{3,2,1,0:T(8,128)(2,1)S(1)} %slice.50), channel_id=1, source_target_pairs={{0,4},{4,0},{1,5},{5,1},{2,6},{6,2},{3,7},{7,3},{8,12},{12,8},{9,1... | collective-permute-start | bytes 491528 | tf_op jit(solution)/shard_map/ppermute | solution.py:557
  43.6 8.3 %collective-permute-start.14 = (bf16[2,5,32,256]{3,2,1,0:T(8,128)(2,1)S(1)}, bf16[2,5,32,256]{3,2,1,0:T(8,128)(2,1)S(1)}, u32[]{:S(2)}, u32[]{:S(2)}) collective-permute-start(bf16[2,5,32,256]{3,2,1,0:T(8,128)(2,1)S(1)} %slice.49), channel_id=1, source_target_pairs={{0,1},{1,0},{2,3},{3,2},{4,5},{5,4},{6,7},{7,6},{8,9},{9,8},{10,11... | collective-permute-start | bytes 491528 | tf_op jit(solution)/shard_map/ppermute | solution.py:557
  44.4 5.6 %collective-permute-start.24 = (bf16[1,5,32,256]{3,2,1,0:T(8,128)(2,1)S(1)}, bf16[1,5,32,256]{3,2,1,0:T(8,128)(2,1)S(1)}, u32[]{:S(2)}, u32[]{:S(2)}) collective-permute-start(bf16[1,5,32,256]{3,2,1,0:T(8,128)(2,1)S(1)} %collective-permute-done.10.rest_8_), channel_id=1, source_target_pairs={{0,2},{2,0},{1,3},{3,1},{4,6},{6,4},{5,7},{7,5},{8,10},{10,8},{9,1... | collective-permute-start | bytes 245768 | tf_op jit(solution)/shard_map/ppermute | solution.py:557
  47.1 1.3 collective-permute-start.25
  48.4 25.5 %collective-permute-start.33 = (bf16[4,2,128,256]{3,2,1,0:T(8,128)(2,1)S(1)}, bf16[4,2,128,256]{3,2,1,0:T(8,128)(2,1)S(1)}, u32[]{:S(2)}, u32[]{:S(2)}) collective-permute-start(bf16[4,2,128,256]{3,2,1,0:T(8,128)(2,1)S(1)} %constant_dynamic-update-slice_fusion.2.rest_0_), channel_id=1, source_target_pairs={{0,5},{1,4},{4,1},{5,0},{2,7},{3,6},{6,3},{7,2},{8,13},{9,12},{12,... | collective-permute-start | bytes 1572872 | tf_op jit(solution)/shard_map/ppermute | solution.py:603
  50.0 24.5 %collective-permute-start.32 = (bf16[4,2,128,256]{3,2,1,0:T(8,128)(2,1)S(1)}, bf16[4,2,128,256]{3,2,1,0:T(8,128)(2,1)S(1)}, u32[]{:S(2)}, u32[]{:S(2)}) collective-permute-start(bf16[4,2,128,256]{3,2,1,0:T(8,128)(2,1)S(1)} %constant_dynamic-update-slice_fusion.2.rest_0_), channel_id=1, source_target_pairs={{0,1},{1,0},{2,3},{3,2},{4,5},{5,4},{6,7},{7,6},{8,9},{9,8},{10,11... | collective-permute-start | bytes 1572872 | tf_op jit(solution)/shard_map/ppermute | solution.py:557
  50.6 23.9 %collective-permute-start.31 = (bf16[4,2,128,256]{3,2,1,0:T(8,128)(2,1)S(1)}, bf16[4,2,128,256]{3,2,1,0:T(8,128)(2,1)S(1)}, u32[]{:S(2)}, u32[]{:S(2)}) collective-permute-start(bf16[4,2,128,256]{3,2,1,0:T(8,128)(2,1)S(1)} %constant_dynamic-update-slice_fusion.2.rest_0_), channel_id=1, source_target_pairs={{0,4},{4,0},{1,5},{5,1},{2,6},{6,2},{3,7},{7,3},{8,12},{12,8},{9,1... | collective-permute-start | bytes 1572872 | tf_op jit(solution)/shard_map/ppermute | solution.py:557
  51.9 1.4 collective-permute-start.29
  51.9 1.6 collective-permute-start.28
  53.3 1.6 collective-permute-start.26
  53.5 1.9 collective-permute-start.27
  73.9 4.8 %copy-start.5 = (bf16[4,2,128,256]{3,2,1,0:T(8,128)(2,1)}, bf16[4,2,128,256]{3,2,1,0:T(8,128)(2,1)S(1)}, u32[]{:S(2)}) copy-start(bf16[4,2,128,256]{3,2,1,0:T(8,128)(2,1)S(1)} %collective-permute-done.33.rest_3_) | copy-start | bytes 1572868
  74.5 4.2 %copy-start.6 = (bf16[4,2,128,256]{3,2,1,0:T(8,128)(2,1)}, bf16[4,2,128,256]{3,2,1,0:T(8,128)(2,1)S(1)}, u32[]{:S(2)}) copy-start(bf16[4,2,128,256]{3,2,1,0:T(8,128)(2,1)S(1)} %collective-permute-done.32.rest_2_) | copy-start | bytes 1572868
  74.5 4.2 %copy-start.7 = (bf16[4,2,128,256]{3,2,1,0:T(8,128)(2,1)}, bf16[4,2,128,256]{3,2,1,0:T(8,128)(2,1)S(1)}, u32[]{:S(2)}) copy-start(bf16[4,2,128,256]{3,2,1,0:T(8,128)(2,1)S(1)} %collective-permute-done.31.rest_1_) | copy-start | bytes 1572868
  74.5 2.0 collective-permute-start.34
  74.6 2.6 %collective-permute-start.35 = (bf16[4,2,128,256]{3,2,1,0:T(8,128)(2,1)S(1)}, bf16[4,2,128,256]{3,2,1,0:T(8,128)(2,1)S(1)}, u32[]{:S(2)}, u32[]{:S(2)}) collective-permute-start(bf16[4,2,128,256]{3,2,1,0:T(8,128)(2,1)S(1)} %collective-permute-done.31.rest_1_), channel_id=1, source_target_pairs={{0,2},{2,0},{1,3},{3,1},{4,6},{6,4},{5,7},{7,5},{8,10},{10,8},{9,1... | collective-permute-start | bytes 1572872 | tf_op jit(solution)/shard_map/ppermute | solution.py:557
  75.1 2.9 %collective-permute-start.36 = (bf16[4,2,128,256]{3,2,1,0:T(8,128)(2,1)S(1)}, bf16[4,2,128,256]{3,2,1,0:T(8,128)(2,1)S(1)}, u32[]{:S(2)}, u32[]{:S(2)}) collective-permute-start(bf16[4,2,128,256]{3,2,1,0:T(8,128)(2,1)S(1)} %collective-permute-done.32.rest_2_), channel_id=1, source_target_pairs={{0,2},{2,0},{1,3},{3,1},{4,6},{6,4},{5,7},{7,5},{8,10},{10,8},{9,1... | collective-permute-start | bytes 1572872 | tf_op jit(solution)/shard_map/ppermute | solution.py:557
  75.2 3.6 %collective-permute-start.37 = (bf16[4,2,128,256]{3,2,1,0:T(8,128)(2,1)S(1)}, bf16[4,2,128,256]{3,2,1,0:T(8,128)(2,1)S(1)}, u32[]{:S(2)}, u32[]{:S(2)}) collective-permute-start(bf16[4,2,128,256]{3,2,1,0:T(8,128)(2,1)S(1)} %collective-permute-done.33.rest_3_), channel_id=1, source_target_pairs={{0,2},{2,0},{1,3},{3,1},{4,6},{6,4},{5,7},{7,5},{8,10},{10,8},{9,1... | collective-permute-start | bytes 1572872 | tf_op jit(solution)/shard_map/ppermute | solution.py:557
  79.5 49.3 %copy-start.1 = (bf16[1,2048,512]{2,1,0:T(8,128)(2,1)S(1)}, bf16[1,2048,512]{2,1,0:T(8,128)(2,1)}, u32[]{:S(2)}) copy-start(bf16[1,2048,512]{2,1,0:T(8,128)(2,1)} %param.13) | copy-start | bytes 6291460
  127.6 6.0 %collective-permute-start.38 = (bf16[4,2,2,528,128]{4,3,2,1,0:T(8,128)(2,1)}, bf16[4,2,2,528,128]{4,3,2,1,0:T(8,128)(2,1)S(1)}, u32[]{:S(2)}, u32[]{:S(2)}) collective-permute-start(bf16[4,2,2,528,128]{4,3,2,1,0:T(8,128)(2,1)} %get-tuple-element.122), channel_id=1, source_target_pairs={{0,2},{2,0},{1,3},{3,1},{4,6},{6,4},{5,7},{7,5},{8,10},{10,8},{9,1... | collective-permute-start | bytes 6488072 | tf_op jit(solution)/shard_map/ppermute | solution.py:557
  127.8 5.8 %collective-permute-start.39 = (bf16[128,512]{1,0:T(8,128)(2,1)S(1)}, bf16[128,512]{1,0:T(8,128)(2,1)S(1)}, u32[]{:S(2)}, u32[]{:S(2)}) collective-permute-start(bf16[128,512]{1,0:T(8,128)(2,1)S(1)} %get-tuple-element.123), channel_id=1, source_target_pairs={{0,1},{1,0},{2,3},{3,2},{4,5},{5,4},{6,7},{7,6},{8,9},{9,8},{10,11... | collective-permute-start | bytes 393224 | tf_op jit(solution)/shard_map/ppermute | solution.py:557
  128.9 4.7 %copy-start.2 = (bf16[4,2,2,528,128]{4,3,2,1,0:T(8,128)(2,1)S(1)}, bf16[4,2,2,528,128]{4,3,2,1,0:T(8,128)(2,1)}, u32[]{:S(2)}) copy-start(bf16[4,2,2,528,128]{4,3,2,1,0:T(8,128)(2,1)} %get-tuple-element.121.keep) | copy-start | bytes 6488068
  133.6 23.1 %slice-start = ((s8[4718592]{0:T(1024)(128)(4,1)}), s8[4194304]{0:T(1024)(128)(4,1)S(1)}, s32[]{:S(2)}) async-start(s8[4718592]{0:T(1024)(128)(4,1)} %bitcast.36), calls=%async_computation | async-start | bytes 8388608
  134.7 14.2 %collective-permute-start.40 = (bf16[2,2,2,272,128]{4,3,2,1,0:T(8,128)(2,1)S(1)}, bf16[2,2,2,272,128]{4,3,2,1,0:T(8,128)(2,1)S(1)}, u32[]{:S(2)}, u32[]{:S(2)}) collective-permute-start(bf16[2,2,2,272,128]{4,3,2,1,0:T(8,128)(2,1)S(1)} %get-tuple-element.129), channel_id=1, source_target_pairs={{0,4},{4,0},{1,5},{5,1},{2,6},{6,2},{3,7},{7,3},{8,12},{12,8},{9,1... | collective-permute-start | bytes 1671176 | tf_op jit(solution)/shard_map/ppermute | solution.py:557
  135.5 21.2 %slice-start.1 = ((s8[4718592]{0:T(1024)(128)(4,1)}), s8[524288]{0:T(1024)(128)(4,1)S(1)}, s32[]{:S(2)}) async-start(s8[4718592]{0:T(1024)(128)(4,1)} %bitcast.36), calls=%async_computation.1 | async-start | bytes 1048576
  135.5 13.2 %collective-permute-start.41 = (bf16[2,2,2,256,128]{4,3,2,1,0:T(8,128)(2,1)S(1)}, bf16[2,2,2,256,128]{4,3,2,1,0:T(8,128)(2,1)S(1)}, u32[]{:S(2)}, u32[]{:S(2)}) collective-permute-start(bf16[2,2,2,256,128]{4,3,2,1,0:T(8,128)(2,1)S(1)} %get-tuple-element.130), channel_id=1, source_target_pairs={{0,1},{1,0},{2,3},{3,2},{4,5},{5,4},{6,7},{7,6},{8,9},{9,8},{10,11... | collective-permute-start | bytes 1572872 | tf_op jit(solution)/shard_map/ppermute | solution.py:557
  148.9 4.5 %collective-permute-start.44 = (bf16[4,2,2,9,32,256]{5,4,3,2,1,0:T(8,128)(2,1)S(1)}, bf16[4,2,2,9,32,256]{5,4,3,2,1,0:T(8,128)(2,1)S(1)}, u32[]{:S(2)}, u32[]{:S(2)}) collective-permute-start(bf16[4,2,2,9,32,256]{5,4,3,2,1,0:T(8,128)(2,1)S(1)} %get-tuple-element.142), channel_id=1, source_target_pairs={{0,2},{2,0},{1,3},{3,1},{4,6},{6,4},{5,7},{7,5},{8,10},{10,8},{9,1... | collective-permute-start | bytes 7077896 | tf_op jit(solution)/shard_map/ppermute | solution.py:557
  149.7 19.3 %collective-permute-start.43 = (bf16[2,2,256,128]{3,2,1,0:T(8,128)(2,1)S(1)}, bf16[2,2,256,128]{3,2,1,0:T(8,128)(2,1)S(1)}, u32[]{:S(2)}, u32[]{:S(2)}) collective-permute-start(bf16[2,2,256,128]{3,2,1,0:T(8,128)(2,1)S(1)} %get-tuple-element.139), channel_id=1, source_target_pairs={{0,4},{4,0},{1,5},{5,1},{2,6},{6,2},{3,7},{7,3},{8,12},{12,8},{9,1... | collective-permute-start | bytes 786440 | tf_op jit(solution)/shard_map/ppermute | solution.py:557
  150.8 18.2 %collective-permute-start.42 = (bf16[2,2,272,128]{3,2,1,0:T(8,128)(2,1)S(1)}, bf16[2,2,272,128]{3,2,1,0:T(8,128)(2,1)S(1)}, u32[]{:S(2)}, u32[]{:S(2)}) collective-permute-start(bf16[2,2,272,128]{3,2,1,0:T(8,128)(2,1)S(1)} %get-tuple-element.138), channel_id=1, source_target_pairs={{0,1},{1,0},{2,3},{3,2},{4,5},{5,4},{6,7},{7,6},{8,9},{9,8},{10,11... | collective-permute-start | bytes 835592 | tf_op jit(solution)/shard_map/ppermute | solution.py:557
  153.5 3.2 %copy-start.4 = (f32[2048,512]{1,0:T(8,128)S(1)}, f32[2048,512]{1,0:T(8,128)}, u32[]{:S(2)}) copy-start(f32[2048,512]{1,0:T(8,128)} %get-tuple-element.146.gh) | copy-start | bytes 12582916
  154.6 18.0 %collective-permute-start.45 = (bf16[2,2,2,5,32,256]{5,4,3,2,1,0:T(8,128)(2,1)S(1)}, bf16[2,2,2,5,32,256]{5,4,3,2,1,0:T(8,128)(2,1)S(1)}, u32[]{:S(2)}, u32[]{:S(2)}) collective-permute-start(bf16[2,2,2,5,32,256]{5,4,3,2,1,0:T(8,128)(2,1)S(1)} %get-tuple-element.144), channel_id=1, source_target_pairs={{0,4},{4,0},{1,5},{5,1},{2,6},{6,2},{3,7},{7,3},{8,12},{12,8},{9,1... | collective-permute-start | bytes 1966088 | tf_op jit(solution)/shard_map/ppermute | solution.py:557
  155.7 15.5 %collective-permute-start.46 = (bf16[2,2,2,4,32,256]{5,4,3,2,1,0:T(8,128)(2,1)S(1)}, bf16[2,2,2,4,32,256]{5,4,3,2,1,0:T(8,128)(2,1)S(1)}, u32[]{:S(2)}, u32[]{:S(2)}) collective-permute-start(bf16[2,2,2,4,32,256]{5,4,3,2,1,0:T(8,128)(2,1)S(1)} %get-tuple-element.150), channel_id=1, source_target_pairs={{0,1},{1,0},{2,3},{3,2},{4,5},{5,4},{6,7},{7,6},{8,9},{9,8},{10,11... | collective-permute-start | bytes 1572872 | tf_op jit(solution)/shard_map/ppermute | solution.py:557
  169.7 8.0 %collective-permute-start.49 = (bf16[2,528,128]{2,1,0:T(8,128)(2,1)S(1)}, bf16[2,528,128]{2,1,0:T(8,128)(2,1)S(1)}, u32[]{:S(2)}, u32[]{:S(2)}) collective-permute-start(bf16[2,528,128]{2,1,0:T(8,128)(2,1)S(1)} %get-tuple-element.155), channel_id=1, source_target_pairs={{0,8},{8,0},{16,24},{24,16},{1,9},{9,1},{17,25},{25,17},{2,10},{10... | collective-permute-start | bytes 811016 | tf_op jit(solution)/shard_map/ppermute | solution.py:557
  173.4 9.4 %collective-permute-start.47 = (bf16[2,2,5,32,256]{4,3,2,1,0:T(8,128)(2,1)S(1)}, bf16[2,2,5,32,256]{4,3,2,1,0:T(8,128)(2,1)S(1)}, u32[]{:S(2)}, u32[]{:S(2)}) collective-permute-start(bf16[2,2,5,32,256]{4,3,2,1,0:T(8,128)(2,1)S(1)} %get-tuple-element.160), channel_id=1, source_target_pairs={{0,1},{1,0},{2,3},{3,2},{4,5},{5,4},{6,7},{7,6},{8,9},{9,8},{10,11... | collective-permute-start | bytes 983048 | tf_op jit(solution)/shard_map/ppermute | solution.py:557
  174.5 7.7 %collective-permute-start.48 = (bf16[2,2,4,32,256]{4,3,2,1,0:T(8,128)(2,1)S(1)}, bf16[2,2,4,32,256]{4,3,2,1,0:T(8,128)(2,1)S(1)}, u32[]{:S(2)}, u32[]{:S(2)}) collective-permute-start(bf16[2,2,4,32,256]{4,3,2,1,0:T(8,128)(2,1)S(1)} %get-tuple-element.161), channel_id=1, source_target_pairs={{0,4},{4,0},{1,5},{5,1},{2,6},{6,2},{3,7},{7,3},{8,12},{12,8},{9,1... | collective-permute-start | bytes 786440 | tf_op jit(solution)/shard_map/ppermute | solution.py:557
  178.4 8.8 %collective-permute-start.52 = (bf16[528,128]{1,0:T(8,128)(2,1)S(1)}, bf16[528,128]{1,0:T(8,128)(2,1)S(1)}, u32[]{:S(2)}, u32[]{:S(2)}) collective-permute-start(bf16[528,128]{1,0:T(8,128)(2,1)S(1)} %get-tuple-element.164), channel_id=1, source_target_pairs={{0,16},{8,24},{16,0},{24,8},{1,17},{9,25},{17,1},{25,9},{2,18},{10... | collective-permute-start | bytes 405512 | tf_op jit(solution)/shard_map/ppermute | solution.py:557
  183.5 9.2 %collective-permute-start.50 = (bf16[2,9,32,256]{3,2,1,0:T(8,128)(2,1)S(1)}, bf16[2,9,32,256]{3,2,1,0:T(8,128)(2,1)S(1)}, u32[]{:S(2)}, u32[]{:S(2)}) collective-permute-start(bf16[2,9,32,256]{3,2,1,0:T(8,128)(2,1)S(1)} %get-tuple-element.169), channel_id=1, source_target_pairs={{0,8},{8,0},{16,24},{24,16},{1,9},{9,1},{17,25},{25,17},{2,10},{10... | collective-permute-start | bytes 884744 | tf_op jit(solution)/shard_map/ppermute | solution.py:557
  193.3 9.1 %collective-permute-start.51 = (bf16[9,32,256]{2,1,0:T(8,128)(2,1)S(1)}, bf16[9,32,256]{2,1,0:T(8,128)(2,1)S(1)}, u32[]{:S(2)}, u32[]{:S(2)}) collective-permute-start(bf16[9,32,256]{2,1,0:T(8,128)(2,1)S(1)} %get-tuple-element.171), channel_id=1, source_target_pairs={{0,16},{8,24},{16,0},{24,8},{1,17},{9,25},{17,1},{25,9},{2,18},{10... | collective-permute-start | bytes 442376 | tf_op jit(solution)/shard_map/ppermute | solution.py:557
  (4 other events, 5.4 us)

commit v6 on v5

--- a/solution.py
+++ b/solution.py
@@ -13,7 +13,7 @@
 BF = jnp.bfloat16
 F32 = jnp.float32
 VMEM_CONV = 28 * 2**20
-VMEM_FFN = 51 * 2**20
+VMEM_FFN = 50 * 2**20
 VMEM_FIRST = 30 * 2**20
 VMEM_PACK = 60 * 2**20
 VMEM_SUM = 24 * 2**20
@@ -595,7 +595,8 @@
     near_y, near_x, far_top, far_bottom, pair_far = lax.optimization_barrier(
         (swap(near, Y), swap(near, X), top(far_x), bottom(far_y), swap(pair, Z1))
     )
-    halo = swap(after(halo, far_top), Y)
+    pair_far, near_x, near_y = lax.optimization_barrier((pair_far, near_x, near_y))
+    halo = swap(after(halo, near_x), Y)
     near_top, near_bottom = top(near_x), bottom(near_y)
     pair = jnp.concatenate([pair, pair_far], 0)
     pair = jnp.concatenate([pair, swap(pair, Z0)], 0)

time: 203 us -> 202 us (level)
  waiting for transfers between devices: 45 us -> 42 us
    ppermute x52, waiting for transfers between devices: 45 us -> 42 us  [swap(): lax.ppermute(value, axis, [(i, i ^ bit) for i in range(lax.axis_size(axis...]
  transfers between devices with their start and end apart: 53 -> 53, of which waited for: 29 -> 28; matrix products, arithmetic and copies ran while one was open for 3% -> 3% of each run, Pallas kernels for 24% -> 25%
where the time goes in v6:
time: 202 us
  Pallas kernels  101 us (50%)
  starting transfers between devices  50.7 us (25%)
  waiting for transfers between devices  42 us (21%)
  local copies, waits for them, and re-layouts  5.32 us (3%)
    ppermute x52, starting transfers between devices, swap(): lax.ppermute(value, axis, [(i, i ^ bit) for i in range(lax.axis_size(axis...  49.1 us
    pallas_call x1, Pallas kernels, ffn(): pl.pallas_call(functools.partial(ffn_kernel, chunk, fast, plan), grid_spe...  47.8 us
    ppermute x52, waiting for transfers between devices, swap(): lax.ppermute(value, axis, [(i, i ^ bit) for i in range(lax.axis_size(axis...  42 us
    pallas_call x1, Pallas kernels, conv_forward(): pl.pallas_call(functools.partial(conv_kernel, subs, plan, small), grid_sp...  18.5 us
    pallas_call x2, Pallas kernels, conv_weight_backward(): pl.pallas_call(functools.partial(conv_weight_kernel, fast, first), grid_s...  14 us
    pallas_call x1, Pallas kernels, conv_input_backward(): pl.pallas_call(functools.partial(conv_input_kernel, subs), grid_spec=pltp...  12.3 us
    pallas_call x6, Pallas kernels, stage(): pl.pallas_call(functools.partial(stage_kernel, columns, joined), grid_spe...  4.29 us
  transfers between devices with their start and end apart: 53, of which 28 were waited for; matrix products, arithmetic and copies ran while one was open for 3% of the time, Pallas kernels for 25%

profile of v6, /device:TPU:0, one launch (start us, length us, event | category | flops | bytes accessed | tf_op | source)
XLA Modules:
  0.0 201.9 jit_solution(2818067709845213006)
XLA Ops:
  0.6 2.1 %pack.1 = (s32[6,8]{1,0:T(8,128)}, bf16[128,512]{1,0:T(8,128)(2,1)}, bf16[1,10,32,256]{3,2,1,0:T(8,128)(2,1)}, bf16[1,2,128,256]{3,2,1,0:T(8,128)(2,1)}) custom-call(s32[1,9]{1,0:T(1,128)} %lengths.1, bf16[2048,512]{1,0:T(8,128)(2,1)} %bitcast.30, bf16[2048,512]{1,0:T(8,128)(2,1)} %bitcast.31, bf16[9,32,256]{2,1,0:T(8,128)(2,1)} %bitcast.38, ...), custom_call_target="tpu_custom_call" | custom-call | tf_op jit(solution)/shard_map/pack/pallas_call | solution.py:544
  2.8 4.1 %collective-permute-start.2 = (bf16[1,10,32,256]{3,2,1,0:T(8,128)(2,1)}, bf16[1,10,32,256]{3,2,1,0:T(8,128)(2,1)S(1)}, u32[]{:S(2)}, u32[]{:S(2)}) collective-permute-start(bf16[1,10,32,256]{3,2,1,0:T(8,128)(2,1)} %get-tuple-element.98), channel_id=1, source_target_pairs={{0,16},{8,24},{16,0},{24,8},{1,17},{9,25},{17,1},{25,9},{2,18},{10... | collective-permute-start | bytes 491528 | tf_op jit(solution)/shard_map/ppermute | solution.py:557
  6.9 1.5 collective-permute-start.1
  8.4 1.5 collective-permute-start
  9.9 1.0 constant_dynamic-update-slice_fusion.1
  10.8 3.9 %collective-permute-done.2 = bf16[1,10,32,256]{3,2,1,0:T(8,128)(2,1)S(1)} collective-permute-done((bf16[1,10,32,256]{3,2,1,0:T(8,128)(2,1)}, bf16[1,10,32,256]{3,2,1,0:T(8,128)(2,1)S(1)}, u32[]{:S(2)}, u32[]{:S(2)}) %collective-permute-start.2) | collective-permute-done | bytes 163872 | tf_op jit(solution)/shard_map/ppermute | solution.py:557
  14.8 0.9 collective-permute-start.3
  15.7 1.5 collective-permute-start.5
  17.2 1.5 collective-permute-start.4
  19.8 4.7 %collective-permute-done.7.rest_5_ = bf16[1,5,32,256]{3,2,1,0:T(8,128)(2,1)S(1)} collective-permute-done((bf16[1,5,32,256]{3,2,1,0:T(8,128)(2,1)S(1)}, bf16[1,5,32,256]{3,2,1,0:T(8,128)(2,1)S(1)}, u32[]{:S(2)}, u32[]{:S(2)}) %collective-permute-start.7) | collective-permute-done | bytes 81952 | tf_op jit(solution)/shard_map/ppermute | solution.py:557
  24.6 1.6 collective-permute-start.9
  26.6 3.3 %collective-permute-start.12 = (bf16[1,2,128,256]{3,2,1,0:T(8,128)(2,1)}, bf16[1,2,128,256]{3,2,1,0:T(8,128)(2,1)S(1)}, u32[]{:S(2)}, u32[]{:S(2)}) collective-permute-start(bf16[1,2,128,256]{3,2,1,0:T(8,128)(2,1)} %get-tuple-element.107), channel_id=1, source_target_pairs={{0,16},{8,24},{16,0},{24,8},{1,17},{9,25},{17,1},{25,9},{2,18},{10... | collective-permute-start | bytes 393224 | tf_op jit(solution)/shard_map/ppermute | solution.py:557
  30.4 1.5 collective-permute-start.10
  32.0 2.6 %collective-permute-done.11.rest_9_ = bf16[1,5,32,256]{3,2,1,0:T(8,128)(2,1)S(1)} collective-permute-done((bf16[1,5,32,256]{3,2,1,0:T(8,128)(2,1)S(1)}, bf16[1,5,32,256]{3,2,1,0:T(8,128)(2,1)S(1)}, u32[]{:S(2)}, u32[]{:S(2)}) %collective-permute-start.11) | collective-permute-done | bytes 81952 | tf_op jit(solution)/shard_map/ppermute | solution.py:557
  34.5 1.2 collective-permute-done.10.rest_8_
  37.7 0.9 pad_maximum_fusion
  38.6 1.4 collective-permute-start.30
  40.0 0.9 constant_dynamic-update-slice_fusion.4
  41.3 1.5 collective-permute-start.13
  43.3 1.0 collective-permute-start.15
  44.4 2.7 %collective-permute-done.30 = bf16[2,2,128,256]{3,2,1,0:T(8,128)(2,1)S(1)} collective-permute-done((bf16[2,2,128,256]{3,2,1,0:T(8,128)(2,1)S(1)}, bf16[2,2,128,256]{3,2,1,0:T(8,128)(2,1)S(1)}, u32[]{:S(2)}, u32[]{:S(2)}) %collective-permute-start.30) | collective-permute-done | bytes 262176 | tf_op jit(solution)/shard_map/ppermute | solution.py:557
  47.1 1.7 collective-permute-start.33
  49.5 1.2 collective-permute-start.31
  51.2 0.9 collective-permute-done.28.rest_26_
  52.6 1.1 collective-permute-done.27.rest_25_
  54.2 18.5 %conv_forward.1 = (f32[2048,512]{1,0:T(8,128)}, f32[2048,512]{1,0:T(8,128)}, bf16[9,512,512]{2,1,0:T(8,128)(2,1)}, f32[8,2048]{1,0:T(8,128)S(1)}) custom-call(s32[6,8]{1,0:T(8,128)S(1)} %copy-done.3, bf16[128,512]{1,0:T(8,128)(2,1)S(1)} %collective-permute-done.13.prev.nxt, bf16[2048,512]{1,0:T(8,128)(2,1)S(1)} %bitcast.33, ...), custom_call_target="tpu_custom_call" | custom-call | flops 1 | bytes 1 | tf_op jit(solution)/shard_map/conv_forward/pallas_call | solution.py:190
  72.7 0.9 collective-permute-done.32.rest_2_
  74.7 0.9 collective-permute-done.34.rest_4_
  75.6 0.7 collective-permute-done.35.rest_5_
  76.3 0.7 collective-permute-done.36.rest_6_
  77.1 0.7 collective-permute-done.37.rest_7_
  77.9 0.7 copy-done.9
  78.6 47.8 %feed_forward.1 = (bf16[2048,512]{1,0:T(8,128)(2,1)}, f32[2048,512]{1,0:T(8,128)}, bf16[2048,512]{1,0:T(8,128)(2,1)S(1)}, bf16[128,512]{1,0:T(8,128)(2,1)S(1)}, ...) custom-call(s32[6,8]{1,0:T(8,128)S(1)} %copy-done.3, bf16[2048,512]{1,0:T(8,128)(2,1)} %bitcast.32, ...), custom_call_target="tpu_custom_call" | custom-call | flops 25769803776 | bytes 1048576 | tf_op jit(solution)/shard_map/feed_forward/pallas_call | solution.py:345
  126.6 1.1 collective-permute-start.39
  127.7 3.7 %conv_weight_backward.2 = (bf16[4,2,2,9,32,256]{5,4,3,2,1,0:T(8,128)(2,1)S(1)}, bf16[4,2,2,9,32,256]{5,4,3,2,1,0:T(8,128)(2,1)S(1)}) custom-call(s32[6,8]{1,0:T(8,128)S(1)} %copy-done.3, bf16[128,512]{1,0:T(8,128)(2,1)S(1)} %collective-permute-done.13.prev.nxt, bf16[2048,512]{1,0:T(8,128)(2,1)S(1)} %bitcast.34, ...), custom_call_target="tpu_custom_call" | custom-call | flops 2146959360 | bytes 1048576 | tf_op jit(solution)/shard_map/conv_weight_backward/pallas_call | solution.py:424
  131.4 1.0 collective-permute-done.39.prev.nxt
  132.4 1.1 stage.8
  133.5 0.8 collective-permute-start.40
  134.3 1.5 collective-permute-start.41
  135.7 10.3 %conv_weight_backward.3 = (bf16[4,2,2,9,32,256]{5,4,3,2,1,0:T(8,128)(2,1)S(1)}, bf16[4,2,2,9,32,256]{5,4,3,2,1,0:T(8,128)(2,1)S(1)}) custom-call(s32[6,8]{1,0:T(8,128)S(1)} %copy-done.3, bf16[128,512]{1,0:T(8,128)(2,1)S(1)} %collective-permute-done.13.prev.nxt, bf16[2048,512]{1,0:T(8,128)(2,1)S(1)} %bitcast.35, ...), custom_call_target="tpu_custom_call", output_to_operand_aliasing={{0}: (5, {}), {1}: (6, {})} | custom-call | flops 7511998464 | bytes 1048576 | tf_op jit(solution)/shard_map/conv_weight_backward/pallas_call | solution.py:424
  146.1 1.3 collective-permute-done.41.refs_3_
  147.6 0.8 stage.9
  148.4 1.1 collective-permute-start.43
  149.5 1.2 collective-permute-start.42
  150.8 1.4 collective-permute-done.44.got
  152.2 1.1 stage.10
  153.3 1.1 collective-permute-start.45
  154.4 1.2 collective-permute-start.46
  155.6 12.3 %conv_input_backward.1 = f32[2048,512]{1,0:T(8,128)} custom-call(s32[6,8]{1,0:T(8,128)S(1)} %copy-done.3, bf16[128,512]{1,0:T(8,128)(2,1)S(1)} %collective-permute-done.39.prev.nxt, bf16[2048,512]{1,0:T(8,128)(2,1)S(1)} %get-tuple-element.130.g, bf16[128,512]{1,0:T(8,128)(2,1)S(1)} %collective-permute-done.39.prev.nxt, f32[2048,512]{1,0:T(8,128)S(1)} %copy-done.4, ...), custom_call_target="tpu_custom_call" | custom-call | flops 9663676416 | bytes 1048576 | tf_op jit(solution)/shard_map/conv_input_backward/pallas_call | solution.py:469
  168.6 1.6 collective-permute-start.49
  170.3 1.0 collective-permute-done.45.refs_1_
  171.2 0.8 stage.12
  172.0 1.4 collective-permute-start.47
  173.4 1.0 collective-permute-start.48
  174.4 2.3 %collective-permute-done.49.refs_1_ = bf16[2,528,128]{2,1,0:T(8,128)(2,1)S(1)} collective-permute-done((bf16[2,528,128]{2,1,0:T(8,128)(2,1)S(1)}, bf16[2,528,128]{2,1,0:T(8,128)(2,1)S(1)}, u32[]{:S(2)}, u32[]{:S(2)}) %collective-permute-start.49) | collective-permute-done | bytes 270368 | tf_op jit(solution)/shard_map/ppermute | solution.py:557
  177.3 3.4 %collective-permute-start.52 = (bf16[528,128]{1,0:T(8,128)(2,1)S(1)}, bf16[528,128]{1,0:T(8,128)(2,1)S(1)}, u32[]{:S(2)}, u32[]{:S(2)}) collective-permute-start(bf16[528,128]{1,0:T(8,128)(2,1)S(1)} %get-tuple-element.170), channel_id=1, source_target_pairs={{0,16},{8,24},{16,0},{24,8},{1,17},{9,25},{17,1},{25,9},{2,18},{10... | collective-permute-start | bytes 405512 | tf_op jit(solution)/shard_map/ppermute | solution.py:557
  181.4 0.7 stage.14
  182.1 1.5 collective-permute-start.50
  183.6 2.5 %collective-permute-done.52 = bf16[528,128]{1,0:T(8,128)(2,1)S(1)} collective-permute-done((bf16[528,128]{1,0:T(8,128)(2,1)S(1)}, bf16[528,128]{1,0:T(8,128)(2,1)S(1)}, u32[]{:S(2)}, u32[]{:S(2)}) %collective-permute-start.52) | collective-permute-done | bytes 135200 | tf_op jit(solution)/shard_map/ppermute | solution.py:557
  186.9 0.8 copy.27
  188.2 2.9 %collective-permute-done.50.refs_1_ = bf16[2,9,32,256]{3,2,1,0:T(8,128)(2,1)S(1)} collective-permute-done((bf16[2,9,32,256]{3,2,1,0:T(8,128)(2,1)S(1)}, bf16[2,9,32,256]{3,2,1,0:T(8,128)(2,1)S(1)}, u32[]{:S(2)}, u32[]{:S(2)}) %collective-permute-start.50) | collective-permute-done | bytes 294944 | tf_op jit(solution)/shard_map/ppermute | solution.py:557
  191.8 2.6 %collective-permute-start.51 = (bf16[9,32,256]{2,1,0:T(8,128)(2,1)S(1)}, bf16[9,32,256]{2,1,0:T(8,128)(2,1)S(1)}, u32[]{:S(2)}, u32[]{:S(2)}) collective-permute-start(bf16[9,32,256]{2,1,0:T(8,128)(2,1)S(1)} %get-tuple-element.177), channel_id=1, source_target_pairs={{0,16},{8,24},{16,0},{24,8},{1,17},{9,25},{17,1},{25,9},{2,18},{10... | collective-permute-start | bytes 442376 | tf_op jit(solution)/shard_map/ppermute | solution.py:557
  195.0 6.1 %collective-permute-done.51 = bf16[9,32,256]{2,1,0:T(8,128)(2,1)S(1)} collective-permute-done((bf16[9,32,256]{2,1,0:T(8,128)(2,1)S(1)}, bf16[9,32,256]{2,1,0:T(8,128)(2,1)S(1)}, u32[]{:S(2)}, u32[]{:S(2)}) %collective-permute-start.51) | collective-permute-done | bytes 147488 | tf_op jit(solution)/shard_map/ppermute | solution.py:557
  201.1 0.8 add_bitcast_fusion
  (101 shorter events, 13.4 us)
Async XLA Ops:
  2.7 38.6 %copy-start.10 = (bf16[128,512]{1,0:T(8,128)(2,1)S(1)}, bf16[128,512]{1,0:T(8,128)(2,1)}, u32[]{:S(2)}) copy-start(bf16[128,512]{1,0:T(8,128)(2,1)} %get-tuple-element.112) | copy-start | bytes 393220
  2.7 51.5 %copy-start = (bf16[1,2048,512]{2,1,0:T(8,128)(2,1)S(1)}, bf16[1,2048,512]{2,1,0:T(8,128)(2,1)}, u32[]{:S(2)}) copy-start(bf16[1,2048,512]{2,1,0:T(8,128)(2,1)} %param.13) | copy-start | bytes 6291460
  2.7 51.5 %copy-start.3 = (s32[6,8]{1,0:T(8,128)S(1)}, s32[6,8]{1,0:T(8,128)}, u32[]{:S(2)}) copy-start(s32[6,8]{1,0:T(8,128)} %get-tuple-element.96.flags) | copy-start | bytes 580
  2.8 12.0 %collective-permute-start.2 = (bf16[1,10,32,256]{3,2,1,0:T(8,128)(2,1)}, bf16[1,10,32,256]{3,2,1,0:T(8,128)(2,1)S(1)}, u32[]{:S(2)}, u32[]{:S(2)}) collective-permute-start(bf16[1,10,32,256]{3,2,1,0:T(8,128)(2,1)} %get-tuple-element.98), channel_id=1, source_target_pairs={{0,16},{8,24},{16,0},{24,8},{1,17},{9,25},{17,1},{25,9},{2,18},{10... | collective-permute-start | bytes 491528 | tf_op jit(solution)/shard_map/ppermute | solution.py:557
  6.9 7.9 %collective-permute-start.1 = (bf16[1,10,32,256]{3,2,1,0:T(8,128)(2,1)}, bf16[1,10,32,256]{3,2,1,0:T(8,128)(2,1)S(1)}, u32[]{:S(2)}, u32[]{:S(2)}) collective-permute-start(bf16[1,10,32,256]{3,2,1,0:T(8,128)(2,1)} %get-tuple-element.98), channel_id=1, source_target_pairs={{0,4},{4,0},{1,5},{5,1},{2,6},{6,2},{3,7},{7,3},{8,12},{12,8},{9,1... | collective-permute-start | bytes 491528 | tf_op jit(solution)/shard_map/ppermute | solution.py:557
  8.4 6.4 %collective-permute-start = (bf16[1,10,32,256]{3,2,1,0:T(8,128)(2,1)}, bf16[1,10,32,256]{3,2,1,0:T(8,128)(2,1)S(1)}, u32[]{:S(2)}, u32[]{:S(2)}) collective-permute-start(bf16[1,10,32,256]{3,2,1,0:T(8,128)(2,1)} %get-tuple-element.98), channel_id=1, source_target_pairs={{0,1},{1,0},{2,3},{3,2},{4,5},{5,4},{6,7},{7,6},{8,9},{9,8},{10,11... | collective-permute-start | bytes 491528 | tf_op jit(solution)/shard_map/ppermute | solution.py:557
  14.8 9.7 %collective-permute-start.3 = (bf16[2,10,32,256]{3,2,1,0:T(8,128)(2,1)S(1)}, bf16[2,10,32,256]{3,2,1,0:T(8,128)(2,1)S(1)}, u32[]{:S(2)}, u32[]{:S(2)}) collective-permute-start(bf16[2,10,32,256]{3,2,1,0:T(8,128)(2,1)S(1)} %constant_dynamic-update-slice_fusion.rest_0_), channel_id=1, source_target_pairs={{0,8},{8,0},{16,24},{24,16},{1,9},{9,1},{17,25},{25,17},{2,10},{10... | collective-permute-start | bytes 983048 | tf_op jit(solution)/shard_map/ppermute | solution.py:557
  15.7 8.8 %collective-permute-start.5 = (bf16[1,10,32,256]{3,2,1,0:T(8,128)(2,1)S(1)}, bf16[1,10,32,256]{3,2,1,0:T(8,128)(2,1)S(1)}, u32[]{:S(2)}, u32[]{:S(2)}) collective-permute-start(bf16[1,10,32,256]{3,2,1,0:T(8,128)(2,1)S(1)} %collective-permute-done.2), channel_id=1, source_target_pairs={{0,1},{1,0},{2,3},{3,2},{4,5},{5,4},{6,7},{7,6},{8,9},{9,8},{10,11... | collective-permute-start | bytes 491528 | tf_op jit(solution)/shard_map/ppermute | solution.py:557
  17.2 7.3 %collective-permute-start.4 = (bf16[1,10,32,256]{3,2,1,0:T(8,128)(2,1)S(1)}, bf16[1,10,32,256]{3,2,1,0:T(8,128)(2,1)S(1)}, u32[]{:S(2)}, u32[]{:S(2)}) collective-permute-start(bf16[1,10,32,256]{3,2,1,0:T(8,128)(2,1)S(1)} %collective-permute-done.2), channel_id=1, source_target_pairs={{0,4},{4,0},{1,5},{5,1},{2,6},{6,2},{3,7},{7,3},{8,12},{12,8},{9,1... | collective-permute-start | bytes 491528 | tf_op jit(solution)/shard_map/ppermute | solution.py:557
  18.7 5.8 %collective-permute-start.7 = (bf16[1,5,32,256]{3,2,1,0:T(8,128)(2,1)S(1)}, bf16[1,5,32,256]{3,2,1,0:T(8,128)(2,1)S(1)}, u32[]{:S(2)}, u32[]{:S(2)}) collective-permute-start(bf16[1,5,32,256]{3,2,1,0:T(8,128)(2,1)S(1)} %slice.46), channel_id=1, source_target_pairs={{0,4},{4,0},{1,5},{5,1},{2,6},{6,2},{3,7},{7,3},{8,12},{12,8},{9,1... | collective-permute-start | bytes 245768 | tf_op jit(solution)/shard_map/ppermute | solution.py:557
  19.3 5.2 %collective-permute-start.6 = (bf16[1,5,32,256]{3,2,1,0:T(8,128)(2,1)S(1)}, bf16[1,5,32,256]{3,2,1,0:T(8,128)(2,1)S(1)}, u32[]{:S(2)}, u32[]{:S(2)}) collective-permute-start(bf16[1,5,32,256]{3,2,1,0:T(8,128)(2,1)S(1)} %slice.45), channel_id=1, source_target_pairs={{0,1},{1,0},{2,3},{3,2},{4,5},{5,4},{6,7},{7,6},{8,9},{9,8},{10,11... | collective-permute-start | bytes 245768 | tf_op jit(solution)/shard_map/ppermute | solution.py:557
  24.6 11.7 %collective-permute-start.9 = (bf16[2,10,32,256]{3,2,1,0:T(8,128)(2,1)S(1)}, bf16[2,10,32,256]{3,2,1,0:T(8,128)(2,1)S(1)}, u32[]{:S(2)}, u32[]{:S(2)}) collective-permute-start(bf16[2,10,32,256]{3,2,1,0:T(8,128)(2,1)S(1)} %collective-permute-done.3.rest_1_), channel_id=1, source_target_pairs={{0,4},{4,0},{1,5},{5,1},{2,6},{6,2},{3,7},{7,3},{8,12},{12,8},{9,1... | collective-permute-start | bytes 983048 | tf_op jit(solution)/shard_map/ppermute | solution.py:557
  26.1 10.2 %collective-permute-start.8 = (bf16[2,10,32,256]{3,2,1,0:T(8,128)(2,1)S(1)}, bf16[2,10,32,256]{3,2,1,0:T(8,128)(2,1)S(1)}, u32[]{:S(2)}, u32[]{:S(2)}) collective-permute-start(bf16[2,10,32,256]{3,2,1,0:T(8,128)(2,1)S(1)} %collective-permute-done.3.rest_1_), channel_id=1, source_target_pairs={{0,1},{1,0},{2,3},{3,2},{4,5},{5,4},{6,7},{7,6},{8,9},{9,8},{10,11... | collective-permute-start | bytes 983048 | tf_op jit(solution)/shard_map/ppermute | solution.py:557
  26.6 9.1 %collective-permute-start.12 = (bf16[1,2,128,256]{3,2,1,0:T(8,128)(2,1)}, bf16[1,2,128,256]{3,2,1,0:T(8,128)(2,1)S(1)}, u32[]{:S(2)}, u32[]{:S(2)}) collective-permute-start(bf16[1,2,128,256]{3,2,1,0:T(8,128)(2,1)} %get-tuple-element.107), channel_id=1, source_target_pairs={{0,16},{8,24},{16,0},{24,8},{1,17},{9,25},{17,1},{25,9},{2,18},{10... | collective-permute-start | bytes 393224 | tf_op jit(solution)/shard_map/ppermute | solution.py:557
  29.9 4.6 %collective-permute-start.11 = (bf16[1,5,32,256]{3,2,1,0:T(8,128)(2,1)S(1)}, bf16[1,5,32,256]{3,2,1,0:T(8,128)(2,1)S(1)}, u32[]{:S(2)}, u32[]{:S(2)}) collective-permute-start(bf16[1,5,32,256]{3,2,1,0:T(8,128)(2,1)S(1)} %slice.48), channel_id=1, source_target_pairs={{0,4},{4,0},{1,5},{5,1},{2,6},{6,2},{3,7},{7,3},{8,12},{12,8},{9,1... | collective-permute-start | bytes 245768 | tf_op jit(solution)/shard_map/ppermute | solution.py:557
  30.4 5.3 %collective-permute-start.10 = (bf16[1,5,32,256]{3,2,1,0:T(8,128)(2,1)S(1)}, bf16[1,5,32,256]{3,2,1,0:T(8,128)(2,1)S(1)}, u32[]{:S(2)}, u32[]{:S(2)}) collective-permute-start(bf16[1,5,32,256]{3,2,1,0:T(8,128)(2,1)S(1)} %slice.47), channel_id=1, source_target_pairs={{0,1},{1,0},{2,3},{3,2},{4,5},{5,4},{6,7},{7,6},{8,9},{9,8},{10,11... | collective-permute-start | bytes 245768 | tf_op jit(solution)/shard_map/ppermute | solution.py:557
  34.5 4.1 %collective-permute-start.16 = (bf16[2,10,32,256]{3,2,1,0:T(8,128)(2,1)S(1)}, bf16[2,10,32,256]{3,2,1,0:T(8,128)(2,1)S(1)}, u32[]{:S(2)}, u32[]{:S(2)}) collective-permute-start(bf16[2,10,32,256]{3,2,1,0:T(8,128)(2,1)S(1)} %constant_dynamic-update-slice_fusion.rest_0_), channel_id=1, source_target_pairs={{0,2},{2,0},{1,3},{3,1},{4,6},{6,4},{5,7},{7,5},{8,10},{10,8},{9,1... | collective-permute-start | bytes 983048 | tf_op jit(solution)/shard_map/ppermute | solution.py:557
  35.7 1.4 collective-permute-start.18
  35.7 1.6 collective-permute-start.19
  36.3 6.6 %collective-permute-start.22 = (bf16[1,10,32,256]{3,2,1,0:T(8,128)(2,1)S(1)}, bf16[1,10,32,256]{3,2,1,0:T(8,128)(2,1)S(1)}, u32[]{:S(2)}, u32[]{:S(2)}) collective-permute-start(bf16[1,10,32,256]{3,2,1,0:T(8,128)(2,1)S(1)} %collective-permute-done.4.rest_6_), channel_id=1, source_target_pairs={{0,2},{2,0},{1,3},{3,1},{4,6},{6,4},{5,7},{7,5},{8,10},{10,8},{9,1... | collective-permute-start | bytes 491528 | tf_op jit(solution)/shard_map/ppermute | solution.py:557
  36.3 7.0 %collective-permute-start.23 = (bf16[1,10,32,256]{3,2,1,0:T(8,128)(2,1)S(1)}, bf16[1,10,32,256]{3,2,1,0:T(8,128)(2,1)S(1)}, u32[]{:S(2)}, u32[]{:S(2)}) collective-permute-start(bf16[1,10,32,256]{3,2,1,0:T(8,128)(2,1)S(1)} %collective-permute-done.5.rest_7_), channel_id=1, source_target_pairs={{0,2},{2,0},{1,3},{3,1},{4,6},{6,4},{5,7},{7,5},{8,10},{10,8},{9,1... | collective-permute-start | bytes 491528 | tf_op jit(solution)/shard_map/ppermute | solution.py:557
  37.1 7.2 %collective-permute-start.17 = (bf16[2,10,32,256]{3,2,1,0:T(8,128)(2,1)S(1)}, bf16[2,10,32,256]{3,2,1,0:T(8,128)(2,1)S(1)}, u32[]{:S(2)}, u32[]{:S(2)}) collective-permute-start(bf16[2,10,32,256]{3,2,1,0:T(8,128)(2,1)S(1)} %collective-permute-done.3.rest_1_), channel_id=1, source_target_pairs={{0,2},{2,0},{1,3},{3,1},{4,6},{6,4},{5,7},{7,5},{8,10},{10,8},{9,1... | collective-permute-start | bytes 983048 | tf_op jit(solution)/shard_map/ppermute | solution.py:557
  37.4 2.6 %collective-permute-start.21 = (bf16[1,5,32,256]{3,2,1,0:T(8,128)(2,1)S(1)}, bf16[1,5,32,256]{3,2,1,0:T(8,128)(2,1)S(1)}, u32[]{:S(2)}, u32[]{:S(2)}) collective-permute-start(bf16[1,5,32,256]{3,2,1,0:T(8,128)(2,1)S(1)} %collective-permute-done.7.rest_5_), channel_id=1, source_target_pairs={{0,2},{2,0},{1,3},{3,1},{4,6},{6,4},{5,7},{7,5},{8,10},{10,8},{9,1... | collective-permute-start | bytes 245768 | tf_op jit(solution)/shard_map/ppermute | solution.py:557
  38.6 8.5 %collective-permute-start.30 = (bf16[2,2,128,256]{3,2,1,0:T(8,128)(2,1)S(1)}, bf16[2,2,128,256]{3,2,1,0:T(8,128)(2,1)S(1)}, u32[]{:S(2)}, u32[]{:S(2)}) collective-permute-start(bf16[2,2,128,256]{3,2,1,0:T(8,128)(2,1)S(1)} %pad_maximum_fusion), channel_id=1, source_target_pairs={{0,8},{8,0},{16,24},{24,16},{1,9},{9,1},{17,25},{25,17},{2,10},{10... | collective-permute-start | bytes 786440 | tf_op jit(solution)/shard_map/ppermute | solution.py:557
  40.0 1.3 collective-permute-start.20
  41.3 8.2 %collective-permute-start.13 = (bf16[128,512]{1,0:T(8,128)(2,1)S(1)}, bf16[128,512]{1,0:T(8,128)(2,1)S(1)}, u32[]{:S(2)}, u32[]{:S(2)}) collective-permute-start(bf16[128,512]{1,0:T(8,128)(2,1)S(1)} %copy-done.10), channel_id=1, source_target_pairs={{0,1},{1,0},{2,3},{3,2},{4,5},{5,4},{6,7},{7,6},{8,9},{9,8},{10,11... | collective-permute-start | bytes 393224 | tf_op jit(solution)/shard_map/ppermute | solution.py:557
  42.8 7.9 %collective-permute-start.14 = (bf16[2,5,32,256]{3,2,1,0:T(8,128)(2,1)S(1)}, bf16[2,5,32,256]{3,2,1,0:T(8,128)(2,1)S(1)}, u32[]{:S(2)}, u32[]{:S(2)}) collective-permute-start(bf16[2,5,32,256]{3,2,1,0:T(8,128)(2,1)S(1)} %slice.49), channel_id=1, source_target_pairs={{0,1},{1,0},{2,3},{3,2},{4,5},{5,4},{6,7},{7,6},{8,9},{9,8},{10,11... | collective-permute-start | bytes 491528 | tf_op jit(solution)/shard_map/ppermute | solution.py:557
  43.3 7.4 %collective-permute-start.15 = (bf16[2,5,32,256]{3,2,1,0:T(8,128)(2,1)S(1)}, bf16[2,5,32,256]{3,2,1,0:T(8,128)(2,1)S(1)}, u32[]{:S(2)}, u32[]{:S(2)}) collective-permute-start(bf16[2,5,32,256]{3,2,1,0:T(8,128)(2,1)S(1)} %slice.50), channel_id=1, source_target_pairs={{0,4},{4,0},{1,5},{5,1},{2,6},{6,2},{3,7},{7,3},{8,12},{12,8},{9,1... | collective-permute-start | bytes 491528 | tf_op jit(solution)/shard_map/ppermute | solution.py:557
  44.4 2.8 %collective-permute-start.24 = (bf16[1,5,32,256]{3,2,1,0:T(8,128)(2,1)S(1)}, bf16[1,5,32,256]{3,2,1,0:T(8,128)(2,1)S(1)}, u32[]{:S(2)}, u32[]{:S(2)}) collective-permute-start(bf16[1,5,32,256]{3,2,1,0:T(8,128)(2,1)S(1)} %collective-permute-done.10.rest_8_), channel_id=1, source_target_pairs={{0,2},{2,0},{1,3},{3,1},{4,6},{6,4},{5,7},{7,5},{8,10},{10,8},{9,1... | collective-permute-start | bytes 245768 | tf_op jit(solution)/shard_map/ppermute | solution.py:557
  47.1 1.7 collective-permute-start.25
  47.1 25.6 %collective-permute-start.33 = (bf16[4,2,128,256]{3,2,1,0:T(8,128)(2,1)S(1)}, bf16[4,2,128,256]{3,2,1,0:T(8,128)(2,1)S(1)}, u32[]{:S(2)}, u32[]{:S(2)}) collective-permute-start(bf16[4,2,128,256]{3,2,1,0:T(8,128)(2,1)S(1)} %constant_dynamic-update-slice_fusion.2.rest_0_), channel_id=1, source_target_pairs={{0,5},{1,4},{4,1},{5,0},{2,7},{3,6},{6,3},{7,2},{8,13},{9,12},{12,... | collective-permute-start | bytes 1572872 | tf_op jit(solution)/shard_map/ppermute | solution.py:604
  48.8 24.9 %collective-permute-start.32 = (bf16[4,2,128,256]{3,2,1,0:T(8,128)(2,1)S(1)}, bf16[4,2,128,256]{3,2,1,0:T(8,128)(2,1)S(1)}, u32[]{:S(2)}, u32[]{:S(2)}) collective-permute-start(bf16[4,2,128,256]{3,2,1,0:T(8,128)(2,1)S(1)} %constant_dynamic-update-slice_fusion.2.rest_0_), channel_id=1, source_target_pairs={{0,1},{1,0},{2,3},{3,2},{4,5},{5,4},{6,7},{7,6},{8,9},{9,8},{10,11... | collective-permute-start | bytes 1572872 | tf_op jit(solution)/shard_map/ppermute | solution.py:557
  49.5 24.2 %collective-permute-start.31 = (bf16[4,2,128,256]{3,2,1,0:T(8,128)(2,1)S(1)}, bf16[4,2,128,256]{3,2,1,0:T(8,128)(2,1)S(1)}, u32[]{:S(2)}, u32[]{:S(2)}) collective-permute-start(bf16[4,2,128,256]{3,2,1,0:T(8,128)(2,1)S(1)} %constant_dynamic-update-slice_fusion.2.rest_0_), channel_id=1, source_target_pairs={{0,4},{4,0},{1,5},{5,1},{2,6},{6,2},{3,7},{7,3},{8,12},{12,8},{9,1... | collective-permute-start | bytes 1572872 | tf_op jit(solution)/shard_map/ppermute | solution.py:557
  50.7 1.4 collective-permute-start.28
  50.7 1.6 collective-permute-start.29
  52.1 1.6 collective-permute-start.27
  52.3 1.9 collective-permute-start.26
  72.7 5.1 %copy-start.5 = (bf16[4,2,128,256]{3,2,1,0:T(8,128)(2,1)}, bf16[4,2,128,256]{3,2,1,0:T(8,128)(2,1)S(1)}, u32[]{:S(2)}) copy-start(bf16[4,2,128,256]{3,2,1,0:T(8,128)(2,1)S(1)} %collective-permute-done.33.rest_3_) | copy-start | bytes 1572868
  73.7 1.9 collective-permute-start.34
  73.7 2.6 %collective-permute-start.35 = (bf16[4,2,128,256]{3,2,1,0:T(8,128)(2,1)S(1)}, bf16[4,2,128,256]{3,2,1,0:T(8,128)(2,1)S(1)}, u32[]{:S(2)}, u32[]{:S(2)}) collective-permute-start(bf16[4,2,128,256]{3,2,1,0:T(8,128)(2,1)S(1)} %collective-permute-done.31.rest_1_), channel_id=1, source_target_pairs={{0,2},{2,0},{1,3},{3,1},{4,6},{6,4},{5,7},{7,5},{8,10},{10,8},{9,1... | collective-permute-start | bytes 1572872 | tf_op jit(solution)/shard_map/ppermute | solution.py:557
  74.2 2.9 %collective-permute-start.36 = (bf16[4,2,128,256]{3,2,1,0:T(8,128)(2,1)S(1)}, bf16[4,2,128,256]{3,2,1,0:T(8,128)(2,1)S(1)}, u32[]{:S(2)}, u32[]{:S(2)}) collective-permute-start(bf16[4,2,128,256]{3,2,1,0:T(8,128)(2,1)S(1)} %collective-permute-done.32.rest_2_), channel_id=1, source_target_pairs={{0,2},{2,0},{1,3},{3,1},{4,6},{6,4},{5,7},{7,5},{8,10},{10,8},{9,1... | collective-permute-start | bytes 1572872 | tf_op jit(solution)/shard_map/ppermute | solution.py:557
  74.2 3.6 %collective-permute-start.37 = (bf16[4,2,128,256]{3,2,1,0:T(8,128)(2,1)S(1)}, bf16[4,2,128,256]{3,2,1,0:T(8,128)(2,1)S(1)}, u32[]{:S(2)}, u32[]{:S(2)}) collective-permute-start(bf16[4,2,128,256]{3,2,1,0:T(8,128)(2,1)S(1)} %collective-permute-done.33.rest_3_), channel_id=1, source_target_pairs={{0,2},{2,0},{1,3},{3,1},{4,6},{6,4},{5,7},{7,5},{8,10},{10,8},{9,1... | collective-permute-start | bytes 1572872 | tf_op jit(solution)/shard_map/ppermute | solution.py:557
  75.6 2.3 %copy-start.6 = (bf16[4,2,128,256]{3,2,1,0:T(8,128)(2,1)}, bf16[4,2,128,256]{3,2,1,0:T(8,128)(2,1)S(1)}, u32[]{:S(2)}) copy-start(bf16[4,2,128,256]{3,2,1,0:T(8,128)(2,1)S(1)} %collective-permute-done.34.rest_4_) | copy-start | bytes 1572868
  76.3 1.5 copy-start.7
  78.6 49.1 %copy-start.1 = (bf16[1,2048,512]{2,1,0:T(8,128)(2,1)S(1)}, bf16[1,2048,512]{2,1,0:T(8,128)(2,1)}, u32[]{:S(2)}) copy-start(bf16[1,2048,512]{2,1,0:T(8,128)(2,1)} %param.13) | copy-start | bytes 6291460
  126.4 6.0 %collective-permute-start.38 = (bf16[4,2,2,528,128]{4,3,2,1,0:T(8,128)(2,1)}, bf16[4,2,2,528,128]{4,3,2,1,0:T(8,128)(2,1)S(1)}, u32[]{:S(2)}, u32[]{:S(2)}) collective-permute-start(bf16[4,2,2,528,128]{4,3,2,1,0:T(8,128)(2,1)} %get-tuple-element.128), channel_id=1, source_target_pairs={{0,2},{2,0},{1,3},{3,1},{4,6},{6,4},{5,7},{7,5},{8,10},{10,8},{9,1... | collective-permute-start | bytes 6488072 | tf_op jit(solution)/shard_map/ppermute | solution.py:557
  126.6 5.8 %collective-permute-start.39 = (bf16[128,512]{1,0:T(8,128)(2,1)S(1)}, bf16[128,512]{1,0:T(8,128)(2,1)S(1)}, u32[]{:S(2)}, u32[]{:S(2)}) collective-permute-start(bf16[128,512]{1,0:T(8,128)(2,1)S(1)} %get-tuple-element.129), channel_id=1, source_target_pairs={{0,1},{1,0},{2,3},{3,2},{4,5},{5,4},{6,7},{7,6},{8,9},{9,8},{10,11... | collective-permute-start | bytes 393224 | tf_op jit(solution)/shard_map/ppermute | solution.py:557
  127.7 4.7 %copy-start.2 = (bf16[4,2,2,528,128]{4,3,2,1,0:T(8,128)(2,1)S(1)}, bf16[4,2,2,528,128]{4,3,2,1,0:T(8,128)(2,1)}, u32[]{:S(2)}) copy-start(bf16[4,2,2,528,128]{4,3,2,1,0:T(8,128)(2,1)} %get-tuple-element.127.keep) | copy-start | bytes 6488068
  132.4 23.2 %slice-start = ((s8[4718592]{0:T(1024)(128)(4,1)}), s8[4194304]{0:T(1024)(128)(4,1)S(1)}, s32[]{:S(2)}) async-start(s8[4718592]{0:T(1024)(128)(4,1)} %bitcast.36), calls=%async_computation | async-start | bytes 8388608
  133.5 14.2 %collective-permute-start.40 = (bf16[2,2,2,272,128]{4,3,2,1,0:T(8,128)(2,1)S(1)}, bf16[2,2,2,272,128]{4,3,2,1,0:T(8,128)(2,1)S(1)}, u32[]{:S(2)}, u32[]{:S(2)}) collective-permute-start(bf16[2,2,2,272,128]{4,3,2,1,0:T(8,128)(2,1)S(1)} %get-tuple-element.135), channel_id=1, source_target_pairs={{0,4},{4,0},{1,5},{5,1},{2,6},{6,2},{3,7},{7,3},{8,12},{12,8},{9,1... | collective-permute-start | bytes 1671176 | tf_op jit(solution)/shard_map/ppermute | solution.py:557
  134.3 21.3 %slice-start.1 = ((s8[4718592]{0:T(1024)(128)(4,1)}), s8[524288]{0:T(1024)(128)(4,1)S(1)}, s32[]{:S(2)}) async-start(s8[4718592]{0:T(1024)(128)(4,1)} %bitcast.36), calls=%async_computation.1 | async-start | bytes 1048576
  134.3 13.1 %collective-permute-start.41 = (bf16[2,2,2,256,128]{4,3,2,1,0:T(8,128)(2,1)S(1)}, bf16[2,2,2,256,128]{4,3,2,1,0:T(8,128)(2,1)S(1)}, u32[]{:S(2)}, u32[]{:S(2)}) collective-permute-start(bf16[2,2,2,256,128]{4,3,2,1,0:T(8,128)(2,1)S(1)} %get-tuple-element.136), channel_id=1, source_target_pairs={{0,1},{1,0},{2,3},{3,2},{4,5},{5,4},{6,7},{7,6},{8,9},{9,8},{10,11... | collective-permute-start | bytes 1572872 | tf_op jit(solution)/shard_map/ppermute | solution.py:557
  147.6 4.5 %collective-permute-start.44 = (bf16[4,2,2,9,32,256]{5,4,3,2,1,0:T(8,128)(2,1)S(1)}, bf16[4,2,2,9,32,256]{5,4,3,2,1,0:T(8,128)(2,1)S(1)}, u32[]{:S(2)}, u32[]{:S(2)}) collective-permute-start(bf16[4,2,2,9,32,256]{5,4,3,2,1,0:T(8,128)(2,1)S(1)} %get-tuple-element.148), channel_id=1, source_target_pairs={{0,2},{2,0},{1,3},{3,1},{4,6},{6,4},{5,7},{7,5},{8,10},{10,8},{9,1... | collective-permute-start | bytes 7077896 | tf_op jit(solution)/shard_map/ppermute | solution.py:557
  148.4 19.5 %collective-permute-start.43 = (bf16[2,2,256,128]{3,2,1,0:T(8,128)(2,1)S(1)}, bf16[2,2,256,128]{3,2,1,0:T(8,128)(2,1)S(1)}, u32[]{:S(2)}, u32[]{:S(2)}) collective-permute-start(bf16[2,2,256,128]{3,2,1,0:T(8,128)(2,1)S(1)} %get-tuple-element.145), channel_id=1, source_target_pairs={{0,4},{4,0},{1,5},{5,1},{2,6},{6,2},{3,7},{7,3},{8,12},{12,8},{9,1... | collective-permute-start | bytes 786440 | tf_op jit(solution)/shard_map/ppermute | solution.py:557
  149.5 18.4 %collective-permute-start.42 = (bf16[2,2,272,128]{3,2,1,0:T(8,128)(2,1)S(1)}, bf16[2,2,272,128]{3,2,1,0:T(8,128)(2,1)S(1)}, u32[]{:S(2)}, u32[]{:S(2)}) collective-permute-start(bf16[2,2,272,128]{3,2,1,0:T(8,128)(2,1)S(1)} %get-tuple-element.144), channel_id=1, source_target_pairs={{0,1},{1,0},{2,3},{3,2},{4,5},{5,4},{6,7},{7,6},{8,9},{9,8},{10,11... | collective-permute-start | bytes 835592 | tf_op jit(solution)/shard_map/ppermute | solution.py:557
  152.2 3.5 %copy-start.4 = (f32[2048,512]{1,0:T(8,128)S(1)}, f32[2048,512]{1,0:T(8,128)}, u32[]{:S(2)}) copy-start(f32[2048,512]{1,0:T(8,128)} %get-tuple-element.152.gh) | copy-start | bytes 12582916
  153.3 18.0 %collective-permute-start.45 = (bf16[2,2,2,5,32,256]{5,4,3,2,1,0:T(8,128)(2,1)S(1)}, bf16[2,2,2,5,32,256]{5,4,3,2,1,0:T(8,128)(2,1)S(1)}, u32[]{:S(2)}, u32[]{:S(2)}) collective-permute-start(bf16[2,2,2,5,32,256]{5,4,3,2,1,0:T(8,128)(2,1)S(1)} %get-tuple-element.150), channel_id=1, source_target_pairs={{0,4},{4,0},{1,5},{5,1},{2,6},{6,2},{3,7},{7,3},{8,12},{12,8},{9,1... | collective-permute-start | bytes 1966088 | tf_op jit(solution)/shard_map/ppermute | solution.py:557
  154.4 15.9 %collective-permute-start.46 = (bf16[2,2,2,4,32,256]{5,4,3,2,1,0:T(8,128)(2,1)S(1)}, bf16[2,2,2,4,32,256]{5,4,3,2,1,0:T(8,128)(2,1)S(1)}, u32[]{:S(2)}, u32[]{:S(2)}) collective-permute-start(bf16[2,2,2,4,32,256]{5,4,3,2,1,0:T(8,128)(2,1)S(1)} %get-tuple-element.156), channel_id=1, source_target_pairs={{0,1},{1,0},{2,3},{3,2},{4,5},{5,4},{6,7},{7,6},{8,9},{9,8},{10,11... | collective-permute-start | bytes 1572872 | tf_op jit(solution)/shard_map/ppermute | solution.py:557
  168.6 8.0 %collective-permute-start.49 = (bf16[2,528,128]{2,1,0:T(8,128)(2,1)S(1)}, bf16[2,528,128]{2,1,0:T(8,128)(2,1)S(1)}, u32[]{:S(2)}, u32[]{:S(2)}) collective-permute-start(bf16[2,528,128]{2,1,0:T(8,128)(2,1)S(1)} %get-tuple-element.161), channel_id=1, source_target_pairs={{0,8},{8,0},{16,24},{24,16},{1,9},{9,1},{17,25},{25,17},{2,10},{10... | collective-permute-start | bytes 811016 | tf_op jit(solution)/shard_map/ppermute | solution.py:557
  172.0 9.4 %collective-permute-start.47 = (bf16[2,2,5,32,256]{4,3,2,1,0:T(8,128)(2,1)S(1)}, bf16[2,2,5,32,256]{4,3,2,1,0:T(8,128)(2,1)S(1)}, u32[]{:S(2)}, u32[]{:S(2)}) collective-permute-start(bf16[2,2,5,32,256]{4,3,2,1,0:T(8,128)(2,1)S(1)} %get-tuple-element.166), channel_id=1, source_target_pairs={{0,1},{1,0},{2,3},{3,2},{4,5},{5,4},{6,7},{7,6},{8,9},{9,8},{10,11... | collective-permute-start | bytes 983048 | tf_op jit(solution)/shard_map/ppermute | solution.py:557
  173.4 7.7 %collective-permute-start.48 = (bf16[2,2,4,32,256]{4,3,2,1,0:T(8,128)(2,1)S(1)}, bf16[2,2,4,32,256]{4,3,2,1,0:T(8,128)(2,1)S(1)}, u32[]{:S(2)}, u32[]{:S(2)}) collective-permute-start(bf16[2,2,4,32,256]{4,3,2,1,0:T(8,128)(2,1)S(1)} %get-tuple-element.167), channel_id=1, source_target_pairs={{0,4},{4,0},{1,5},{5,1},{2,6},{6,2},{3,7},{7,3},{8,12},{12,8},{9,1... | collective-permute-start | bytes 786440 | tf_op jit(solution)/shard_map/ppermute | solution.py:557
  177.3 8.8 %collective-permute-start.52 = (bf16[528,128]{1,0:T(8,128)(2,1)S(1)}, bf16[528,128]{1,0:T(8,128)(2,1)S(1)}, u32[]{:S(2)}, u32[]{:S(2)}) collective-permute-start(bf16[528,128]{1,0:T(8,128)(2,1)S(1)} %get-tuple-element.170), channel_id=1, source_target_pairs={{0,16},{8,24},{16,0},{24,8},{1,17},{9,25},{17,1},{25,9},{2,18},{10... | collective-permute-start | bytes 405512 | tf_op jit(solution)/shard_map/ppermute | solution.py:557
  182.1 9.0 %collective-permute-start.50 = (bf16[2,9,32,256]{3,2,1,0:T(8,128)(2,1)S(1)}, bf16[2,9,32,256]{3,2,1,0:T(8,128)(2,1)S(1)}, u32[]{:S(2)}, u32[]{:S(2)}) collective-permute-start(bf16[2,9,32,256]{3,2,1,0:T(8,128)(2,1)S(1)} %get-tuple-element.175), channel_id=1, source_target_pairs={{0,8},{8,0},{16,24},{24,16},{1,9},{9,1},{17,25},{25,17},{2,10},{10... | collective-permute-start | bytes 884744 | tf_op jit(solution)/shard_map/ppermute | solution.py:557
  191.8 9.3 %collective-permute-start.51 = (bf16[9,32,256]{2,1,0:T(8,128)(2,1)S(1)}, bf16[9,32,256]{2,1,0:T(8,128)(2,1)S(1)}, u32[]{:S(2)}, u32[]{:S(2)}) collective-permute-start(bf16[9,32,256]{2,1,0:T(8,128)(2,1)S(1)} %get-tuple-element.177), channel_id=1, source_target_pairs={{0,16},{8,24},{16,0},{24,8},{1,17},{9,25},{17,1},{25,9},{2,18},{10... | collective-permute-start | bytes 442376 | tf_op jit(solution)/shard_map/ppermute | solution.py:557
  (2 other events, 1.6 us)

commit v7 on v6

--- a/solution.py
+++ b/solution.py
@@ -538,7 +538,7 @@
     outs = [
         sds((6, count // SUB), jnp.int32),
         sds((border, width), BF),
-        sds((1, taps + 1, rows, wide), BF),
+        pltpu.VMEM((1, taps + 1, rows, wide), BF),
         sds((1, 2) + down.shape, BF),
     ]
     return pl.pallas_call(

time: 202 us -> 202 us (level)
  transfers between devices with their start and end apart: 53 -> 53, of which waited for: 28 -> 28; matrix products, arithmetic and copies ran while one was open for 3% -> 2% of each run, Pallas kernels for 25% -> 25%
where the time goes in v7:
time: 202 us
  Pallas kernels  101 us (50%)
  starting transfers between devices  51 us (25%)
  waiting for transfers between devices  42.5 us (21%)
  local copies, waits for them, and re-layouts  4.37 us (2%)
    ppermute x52, starting transfers between devices, swap(): lax.ppermute(value, axis, [(i, i ^ bit) for i in range(lax.axis_size(axis...  49.2 us
    pallas_call x1, Pallas kernels, ffn(): pl.pallas_call(functools.partial(ffn_kernel, chunk, fast, plan), grid_spe...  47.8 us
    ppermute x52, waiting for transfers between devices, swap(): lax.ppermute(value, axis, [(i, i ^ bit) for i in range(lax.axis_size(axis...  42.5 us
    pallas_call x1, Pallas kernels, conv_forward(): pl.pallas_call(functools.partial(conv_kernel, subs, plan, small), grid_sp...  18.5 us
    pallas_call x2, Pallas kernels, conv_weight_backward(): pl.pallas_call(functools.partial(conv_weight_kernel, fast, first), grid_s...  14 us
    pallas_call x1, Pallas kernels, conv_input_backward(): pl.pallas_call(functools.partial(conv_input_kernel, subs), grid_spec=pltp...  12.3 us
    pallas_call x6, Pallas kernels, stage(): pl.pallas_call(functools.partial(stage_kernel, columns, joined), grid_spe...  4.29 us
  transfers between devices with their start and end apart: 53, of which 28 were waited for; matrix products, arithmetic and copies ran while one was open for 2% of the time, Pallas kernels for 25%

profile of v7, /device:TPU:0, one launch (start us, length us, event | category | flops | bytes accessed | tf_op | source)
XLA Modules:
  0.0 201.7 jit_solution(7029838877572716792)
XLA Ops:
  0.6 2.1 %pack.1 = (s32[6,8]{1,0:T(8,128)}, bf16[128,512]{1,0:T(8,128)(2,1)}, bf16[1,10,32,256]{3,2,1,0:T(8,128)(2,1)S(1)}, bf16[1,2,128,256]{3,2,1,0:T(8,128)(2,1)}) custom-call(s32[1,9]{1,0:T(1,128)} %lengths.1, bf16[2048,512]{1,0:T(8,128)(2,1)} %bitcast.30, bf16[2048,512]{1,0:T(8,128)(2,1)} %bitcast.31, bf16[9,32,256]{2,1,0:T(8,128)(2,1)} %bitcast.38, ...), custom_call_target="tpu_custom_call" | custom-call | tf_op jit(solution)/shard_map/pack/pallas_call | solution.py:544
  2.8 4.1 %collective-permute-start.2 = (bf16[1,10,32,256]{3,2,1,0:T(8,128)(2,1)S(1)}, bf16[1,10,32,256]{3,2,1,0:T(8,128)(2,1)S(1)}, u32[]{:S(2)}, u32[]{:S(2)}) collective-permute-start(bf16[1,10,32,256]{3,2,1,0:T(8,128)(2,1)S(1)} %get-tuple-element.98), channel_id=1, source_target_pairs={{0,16},{8,24},{16,0},{24,8},{1,17},{9,25},{17,1},{25,9},{2,18},{10... | collective-permute-start | bytes 491528 | tf_op jit(solution)/shard_map/ppermute | solution.py:557
  6.9 1.5 collective-permute-start.1
  8.3 1.5 collective-permute-start
  9.9 4.7 %collective-permute-done.2 = bf16[1,10,32,256]{3,2,1,0:T(8,128)(2,1)S(1)} collective-permute-done((bf16[1,10,32,256]{3,2,1,0:T(8,128)(2,1)S(1)}, bf16[1,10,32,256]{3,2,1,0:T(8,128)(2,1)S(1)}, u32[]{:S(2)}, u32[]{:S(2)}) %collective-permute-start.2) | collective-permute-done | bytes 163872 | tf_op jit(solution)/shard_map/ppermute | solution.py:557
  14.6 0.8 collective-permute-start.3
  15.4 1.5 collective-permute-start.5
  16.9 1.5 collective-permute-start.4
  19.5 4.7 %collective-permute-done.7.rest_5_ = bf16[1,5,32,256]{3,2,1,0:T(8,128)(2,1)S(1)} collective-permute-done((bf16[1,5,32,256]{3,2,1,0:T(8,128)(2,1)S(1)}, bf16[1,5,32,256]{3,2,1,0:T(8,128)(2,1)S(1)}, u32[]{:S(2)}, u32[]{:S(2)}) %collective-permute-start.7) | collective-permute-done | bytes 81952 | tf_op jit(solution)/shard_map/ppermute | solution.py:557
  24.2 1.6 collective-permute-start.9
  26.3 3.4 %collective-permute-start.12 = (bf16[1,2,128,256]{3,2,1,0:T(8,128)(2,1)}, bf16[1,2,128,256]{3,2,1,0:T(8,128)(2,1)S(1)}, u32[]{:S(2)}, u32[]{:S(2)}) collective-permute-start(bf16[1,2,128,256]{3,2,1,0:T(8,128)(2,1)} %get-tuple-element.107), channel_id=1, source_target_pairs={{0,16},{8,24},{16,0},{24,8},{1,17},{9,25},{17,1},{25,9},{2,18},{10... | collective-permute-start | bytes 393224 | tf_op jit(solution)/shard_map/ppermute | solution.py:557
  30.2 1.5 collective-permute-start.10
  31.7 2.4 %collective-permute-done.11.rest_9_ = bf16[1,5,32,256]{3,2,1,0:T(8,128)(2,1)S(1)} collective-permute-done((bf16[1,5,32,256]{3,2,1,0:T(8,128)(2,1)S(1)}, bf16[1,5,32,256]{3,2,1,0:T(8,128)(2,1)S(1)}, u32[]{:S(2)}, u32[]{:S(2)}) %collective-permute-start.11) | collective-permute-done | bytes 81952 | tf_op jit(solution)/shard_map/ppermute | solution.py:557
  34.2 1.2 collective-permute-done.10.rest_8_
  37.3 0.9 pad_maximum_fusion
  38.3 1.4 collective-permute-start.30
  39.7 0.9 constant_dynamic-update-slice_fusion.4
  41.0 1.5 collective-permute-start.13
  43.0 1.1 collective-permute-start.15
  44.2 2.6 %collective-permute-done.30 = bf16[2,2,128,256]{3,2,1,0:T(8,128)(2,1)S(1)} collective-permute-done((bf16[2,2,128,256]{3,2,1,0:T(8,128)(2,1)S(1)}, bf16[2,2,128,256]{3,2,1,0:T(8,128)(2,1)S(1)}, u32[]{:S(2)}, u32[]{:S(2)}) %collective-permute-start.30) | collective-permute-done | bytes 262176 | tf_op jit(solution)/shard_map/ppermute | solution.py:557
  46.8 1.8 collective-permute-start.33
  49.2 1.2 collective-permute-start.31
  50.9 0.9 collective-permute-done.28.rest_26_
  52.3 1.1 collective-permute-done.27.rest_25_
  53.9 18.5 %conv_forward.1 = (f32[2048,512]{1,0:T(8,128)}, f32[2048,512]{1,0:T(8,128)}, bf16[9,512,512]{2,1,0:T(8,128)(2,1)}, f32[8,2048]{1,0:T(8,128)S(1)}) custom-call(s32[6,8]{1,0:T(8,128)S(1)} %copy-done.3, bf16[128,512]{1,0:T(8,128)(2,1)S(1)} %collective-permute-done.13.prev.nxt, bf16[2048,512]{1,0:T(8,128)(2,1)S(1)} %bitcast.33, ...), custom_call_target="tpu_custom_call" | custom-call | flops 1 | bytes 1 | tf_op jit(solution)/shard_map/conv_forward/pallas_call | solution.py:190
  72.4 0.9 collective-permute-done.32.rest_2_
  74.4 0.9 collective-permute-done.34.rest_4_
  75.3 0.7 collective-permute-done.35.rest_5_
  76.0 0.7 collective-permute-done.36.rest_6_
  76.8 0.7 collective-permute-done.37.rest_7_
  77.6 0.7 copy-done.9
  78.3 47.8 %feed_forward.1 = (bf16[2048,512]{1,0:T(8,128)(2,1)}, f32[2048,512]{1,0:T(8,128)}, bf16[2048,512]{1,0:T(8,128)(2,1)S(1)}, bf16[128,512]{1,0:T(8,128)(2,1)S(1)}, ...) custom-call(s32[6,8]{1,0:T(8,128)S(1)} %copy-done.3, bf16[2048,512]{1,0:T(8,128)(2,1)} %bitcast.32, ...), custom_call_target="tpu_custom_call" | custom-call | flops 25769803776 | bytes 1048576 | tf_op jit(solution)/shard_map/feed_forward/pallas_call | solution.py:345
  126.3 1.1 collective-permute-start.39
  127.4 3.7 %conv_weight_backward.2 = (bf16[4,2,2,9,32,256]{5,4,3,2,1,0:T(8,128)(2,1)S(1)}, bf16[4,2,2,9,32,256]{5,4,3,2,1,0:T(8,128)(2,1)S(1)}) custom-call(s32[6,8]{1,0:T(8,128)S(1)} %copy-done.3, bf16[128,512]{1,0:T(8,128)(2,1)S(1)} %collective-permute-done.13.prev.nxt, bf16[2048,512]{1,0:T(8,128)(2,1)S(1)} %bitcast.34, ...), custom_call_target="tpu_custom_call" | custom-call | flops 2146959360 | bytes 1048576 | tf_op jit(solution)/shard_map/conv_weight_backward/pallas_call | solution.py:424
  131.1 1.0 collective-permute-done.39.prev.nxt
  132.1 1.1 stage.8
  133.1 0.9 collective-permute-start.40
  134.0 1.5 collective-permute-start.41
  135.5 10.3 %conv_weight_backward.3 = (bf16[4,2,2,9,32,256]{5,4,3,2,1,0:T(8,128)(2,1)S(1)}, bf16[4,2,2,9,32,256]{5,4,3,2,1,0:T(8,128)(2,1)S(1)}) custom-call(s32[6,8]{1,0:T(8,128)S(1)} %copy-done.3, bf16[128,512]{1,0:T(8,128)(2,1)S(1)} %collective-permute-done.13.prev.nxt, bf16[2048,512]{1,0:T(8,128)(2,1)S(1)} %bitcast.35, ...), custom_call_target="tpu_custom_call", output_to_operand_aliasing={{0}: (5, {}), {1}: (6, {})} | custom-call | flops 7511998464 | bytes 1048576 | tf_op jit(solution)/shard_map/conv_weight_backward/pallas_call | solution.py:424
  145.8 1.3 collective-permute-done.41.refs_3_
  147.3 0.8 stage.9
  148.1 1.1 collective-permute-start.43
  149.2 1.2 collective-permute-start.42
  150.4 1.4 collective-permute-done.44.got
  151.8 1.1 stage.10
  152.9 1.1 collective-permute-start.45
  154.1 1.2 collective-permute-start.46
  155.3 12.3 %conv_input_backward.1 = f32[2048,512]{1,0:T(8,128)} custom-call(s32[6,8]{1,0:T(8,128)S(1)} %copy-done.3, bf16[128,512]{1,0:T(8,128)(2,1)S(1)} %collective-permute-done.39.prev.nxt, bf16[2048,512]{1,0:T(8,128)(2,1)S(1)} %get-tuple-element.130.g, bf16[128,512]{1,0:T(8,128)(2,1)S(1)} %collective-permute-done.39.prev.nxt, f32[2048,512]{1,0:T(8,128)S(1)} %copy-done.4, ...), custom_call_target="tpu_custom_call" | custom-call | flops 9663676416 | bytes 1048576 | tf_op jit(solution)/shard_map/conv_input_backward/pallas_call | solution.py:469
  167.6 0.7 stage.11
  168.3 1.6 collective-permute-start.49
  169.9 1.0 collective-permute-done.45.refs_1_
  170.9 0.8 stage.12
  171.7 1.4 collective-permute-start.47
  173.1 1.0 collective-permute-start.48
  174.1 2.3 %collective-permute-done.49.refs_1_ = bf16[2,528,128]{2,1,0:T(8,128)(2,1)S(1)} collective-permute-done((bf16[2,528,128]{2,1,0:T(8,128)(2,1)S(1)}, bf16[2,528,128]{2,1,0:T(8,128)(2,1)S(1)}, u32[]{:S(2)}, u32[]{:S(2)}) %collective-permute-start.49) | collective-permute-done | bytes 270368 | tf_op jit(solution)/shard_map/ppermute | solution.py:557
  177.0 3.6 %collective-permute-start.52 = (bf16[528,128]{1,0:T(8,128)(2,1)S(1)}, bf16[528,128]{1,0:T(8,128)(2,1)S(1)}, u32[]{:S(2)}, u32[]{:S(2)}) collective-permute-start(bf16[528,128]{1,0:T(8,128)(2,1)S(1)} %get-tuple-element.170), channel_id=1, source_target_pairs={{0,16},{8,24},{16,0},{24,8},{1,17},{9,25},{17,1},{25,9},{2,18},{10... | collective-permute-start | bytes 405512 | tf_op jit(solution)/shard_map/ppermute | solution.py:557
  181.1 0.7 stage.14
  181.8 1.6 collective-permute-start.50
  183.4 2.6 %collective-permute-done.52 = bf16[528,128]{1,0:T(8,128)(2,1)S(1)} collective-permute-done((bf16[528,128]{1,0:T(8,128)(2,1)S(1)}, bf16[528,128]{1,0:T(8,128)(2,1)S(1)}, u32[]{:S(2)}, u32[]{:S(2)}) %collective-permute-start.52) | collective-permute-done | bytes 135200 | tf_op jit(solution)/shard_map/ppermute | solution.py:557
  186.7 0.8 copy.27
  188.0 2.9 %collective-permute-done.50.refs_1_ = bf16[2,9,32,256]{3,2,1,0:T(8,128)(2,1)S(1)} collective-permute-done((bf16[2,9,32,256]{3,2,1,0:T(8,128)(2,1)S(1)}, bf16[2,9,32,256]{3,2,1,0:T(8,128)(2,1)S(1)}, u32[]{:S(2)}, u32[]{:S(2)}) %collective-permute-start.50) | collective-permute-done | bytes 294944 | tf_op jit(solution)/shard_map/ppermute | solution.py:557
  191.7 2.5 %collective-permute-start.51 = (bf16[9,32,256]{2,1,0:T(8,128)(2,1)S(1)}, bf16[9,32,256]{2,1,0:T(8,128)(2,1)S(1)}, u32[]{:S(2)}, u32[]{:S(2)}) collective-permute-start(bf16[9,32,256]{2,1,0:T(8,128)(2,1)S(1)} %get-tuple-element.177), channel_id=1, source_target_pairs={{0,16},{8,24},{16,0},{24,8},{1,17},{9,25},{17,1},{25,9},{2,18},{10... | collective-permute-start | bytes 442376 | tf_op jit(solution)/shard_map/ppermute | solution.py:557
  194.7 6.2 %collective-permute-done.51 = bf16[9,32,256]{2,1,0:T(8,128)(2,1)S(1)} collective-permute-done((bf16[9,32,256]{2,1,0:T(8,128)(2,1)S(1)}, bf16[9,32,256]{2,1,0:T(8,128)(2,1)S(1)}, u32[]{:S(2)}, u32[]{:S(2)}) %collective-permute-start.51) | collective-permute-done | bytes 147488 | tf_op jit(solution)/shard_map/ppermute | solution.py:557
  200.9 0.8 add_bitcast_fusion
  (101 shorter events, 12.4 us)
Async XLA Ops:
  2.7 38.3 %copy-start.10 = (bf16[128,512]{1,0:T(8,128)(2,1)S(1)}, bf16[128,512]{1,0:T(8,128)(2,1)}, u32[]{:S(2)}) copy-start(bf16[128,512]{1,0:T(8,128)(2,1)} %get-tuple-element.112) | copy-start | bytes 393220
  2.7 51.2 %copy-start = (bf16[1,2048,512]{2,1,0:T(8,128)(2,1)S(1)}, bf16[1,2048,512]{2,1,0:T(8,128)(2,1)}, u32[]{:S(2)}) copy-start(bf16[1,2048,512]{2,1,0:T(8,128)(2,1)} %param.13) | copy-start | bytes 6291460
  2.7 51.1 %copy-start.3 = (s32[6,8]{1,0:T(8,128)S(1)}, s32[6,8]{1,0:T(8,128)}, u32[]{:S(2)}) copy-start(s32[6,8]{1,0:T(8,128)} %get-tuple-element.96.flags) | copy-start | bytes 580
  2.8 11.8 %collective-permute-start.2 = (bf16[1,10,32,256]{3,2,1,0:T(8,128)(2,1)S(1)}, bf16[1,10,32,256]{3,2,1,0:T(8,128)(2,1)S(1)}, u32[]{:S(2)}, u32[]{:S(2)}) collective-permute-start(bf16[1,10,32,256]{3,2,1,0:T(8,128)(2,1)S(1)} %get-tuple-element.98), channel_id=1, source_target_pairs={{0,16},{8,24},{16,0},{24,8},{1,17},{9,25},{17,1},{25,9},{2,18},{10... | collective-permute-start | bytes 491528 | tf_op jit(solution)/shard_map/ppermute | solution.py:557
  6.9 7.7 %collective-permute-start.1 = (bf16[1,10,32,256]{3,2,1,0:T(8,128)(2,1)S(1)}, bf16[1,10,32,256]{3,2,1,0:T(8,128)(2,1)S(1)}, u32[]{:S(2)}, u32[]{:S(2)}) collective-permute-start(bf16[1,10,32,256]{3,2,1,0:T(8,128)(2,1)S(1)} %get-tuple-element.98), channel_id=1, source_target_pairs={{0,4},{4,0},{1,5},{5,1},{2,6},{6,2},{3,7},{7,3},{8,12},{12,8},{9,1... | collective-permute-start | bytes 491528 | tf_op jit(solution)/shard_map/ppermute | solution.py:557
  8.3 6.2 %collective-permute-start = (bf16[1,10,32,256]{3,2,1,0:T(8,128)(2,1)S(1)}, bf16[1,10,32,256]{3,2,1,0:T(8,128)(2,1)S(1)}, u32[]{:S(2)}, u32[]{:S(2)}) collective-permute-start(bf16[1,10,32,256]{3,2,1,0:T(8,128)(2,1)S(1)} %get-tuple-element.98), channel_id=1, source_target_pairs={{0,1},{1,0},{2,3},{3,2},{4,5},{5,4},{6,7},{7,6},{8,9},{9,8},{10,11... | collective-permute-start | bytes 491528 | tf_op jit(solution)/shard_map/ppermute | solution.py:557
  14.6 9.6 %collective-permute-start.3 = (bf16[2,10,32,256]{3,2,1,0:T(8,128)(2,1)S(1)}, bf16[2,10,32,256]{3,2,1,0:T(8,128)(2,1)S(1)}, u32[]{:S(2)}, u32[]{:S(2)}) collective-permute-start(bf16[2,10,32,256]{3,2,1,0:T(8,128)(2,1)S(1)} %constant_dynamic-update-slice_fusion.rest_0_), channel_id=1, source_target_pairs={{0,8},{8,0},{16,24},{24,16},{1,9},{9,1},{17,25},{25,17},{2,10},{10... | collective-permute-start | bytes 983048 | tf_op jit(solution)/shard_map/ppermute | solution.py:557
  15.4 8.8 %collective-permute-start.5 = (bf16[1,10,32,256]{3,2,1,0:T(8,128)(2,1)S(1)}, bf16[1,10,32,256]{3,2,1,0:T(8,128)(2,1)S(1)}, u32[]{:S(2)}, u32[]{:S(2)}) collective-permute-start(bf16[1,10,32,256]{3,2,1,0:T(8,128)(2,1)S(1)} %collective-permute-done.2), channel_id=1, source_target_pairs={{0,1},{1,0},{2,3},{3,2},{4,5},{5,4},{6,7},{7,6},{8,9},{9,8},{10,11... | collective-permute-start | bytes 491528 | tf_op jit(solution)/shard_map/ppermute | solution.py:557
  16.9 7.3 %collective-permute-start.4 = (bf16[1,10,32,256]{3,2,1,0:T(8,128)(2,1)S(1)}, bf16[1,10,32,256]{3,2,1,0:T(8,128)(2,1)S(1)}, u32[]{:S(2)}, u32[]{:S(2)}) collective-permute-start(bf16[1,10,32,256]{3,2,1,0:T(8,128)(2,1)S(1)} %collective-permute-done.2), channel_id=1, source_target_pairs={{0,4},{4,0},{1,5},{5,1},{2,6},{6,2},{3,7},{7,3},{8,12},{12,8},{9,1... | collective-permute-start | bytes 491528 | tf_op jit(solution)/shard_map/ppermute | solution.py:557
  18.4 5.8 %collective-permute-start.7 = (bf16[1,5,32,256]{3,2,1,0:T(8,128)(2,1)S(1)}, bf16[1,5,32,256]{3,2,1,0:T(8,128)(2,1)S(1)}, u32[]{:S(2)}, u32[]{:S(2)}) collective-permute-start(bf16[1,5,32,256]{3,2,1,0:T(8,128)(2,1)S(1)} %slice.46), channel_id=1, source_target_pairs={{0,4},{4,0},{1,5},{5,1},{2,6},{6,2},{3,7},{7,3},{8,12},{12,8},{9,1... | collective-permute-start | bytes 245768 | tf_op jit(solution)/shard_map/ppermute | solution.py:557
  19.0 5.2 %collective-permute-start.6 = (bf16[1,5,32,256]{3,2,1,0:T(8,128)(2,1)S(1)}, bf16[1,5,32,256]{3,2,1,0:T(8,128)(2,1)S(1)}, u32[]{:S(2)}, u32[]{:S(2)}) collective-permute-start(bf16[1,5,32,256]{3,2,1,0:T(8,128)(2,1)S(1)} %slice.45), channel_id=1, source_target_pairs={{0,1},{1,0},{2,3},{3,2},{4,5},{5,4},{6,7},{7,6},{8,9},{9,8},{10,11... | collective-permute-start | bytes 245768 | tf_op jit(solution)/shard_map/ppermute | solution.py:557
  24.2 11.7 %collective-permute-start.9 = (bf16[2,10,32,256]{3,2,1,0:T(8,128)(2,1)S(1)}, bf16[2,10,32,256]{3,2,1,0:T(8,128)(2,1)S(1)}, u32[]{:S(2)}, u32[]{:S(2)}) collective-permute-start(bf16[2,10,32,256]{3,2,1,0:T(8,128)(2,1)S(1)} %collective-permute-done.3.rest_1_), channel_id=1, source_target_pairs={{0,4},{4,0},{1,5},{5,1},{2,6},{6,2},{3,7},{7,3},{8,12},{12,8},{9,1... | collective-permute-start | bytes 983048 | tf_op jit(solution)/shard_map/ppermute | solution.py:557
  25.8 10.2 %collective-permute-start.8 = (bf16[2,10,32,256]{3,2,1,0:T(8,128)(2,1)S(1)}, bf16[2,10,32,256]{3,2,1,0:T(8,128)(2,1)S(1)}, u32[]{:S(2)}, u32[]{:S(2)}) collective-permute-start(bf16[2,10,32,256]{3,2,1,0:T(8,128)(2,1)S(1)} %collective-permute-done.3.rest_1_), channel_id=1, source_target_pairs={{0,1},{1,0},{2,3},{3,2},{4,5},{5,4},{6,7},{7,6},{8,9},{9,8},{10,11... | collective-permute-start | bytes 983048 | tf_op jit(solution)/shard_map/ppermute | solution.py:557
  26.3 9.1 %collective-permute-start.12 = (bf16[1,2,128,256]{3,2,1,0:T(8,128)(2,1)}, bf16[1,2,128,256]{3,2,1,0:T(8,128)(2,1)S(1)}, u32[]{:S(2)}, u32[]{:S(2)}) collective-permute-start(bf16[1,2,128,256]{3,2,1,0:T(8,128)(2,1)} %get-tuple-element.107), channel_id=1, source_target_pairs={{0,16},{8,24},{16,0},{24,8},{1,17},{9,25},{17,1},{25,9},{2,18},{10... | collective-permute-start | bytes 393224 | tf_op jit(solution)/shard_map/ppermute | solution.py:557
  29.7 4.5 %collective-permute-start.11 = (bf16[1,5,32,256]{3,2,1,0:T(8,128)(2,1)S(1)}, bf16[1,5,32,256]{3,2,1,0:T(8,128)(2,1)S(1)}, u32[]{:S(2)}, u32[]{:S(2)}) collective-permute-start(bf16[1,5,32,256]{3,2,1,0:T(8,128)(2,1)S(1)} %slice.48), channel_id=1, source_target_pairs={{0,4},{4,0},{1,5},{5,1},{2,6},{6,2},{3,7},{7,3},{8,12},{12,8},{9,1... | collective-permute-start | bytes 245768 | tf_op jit(solution)/shard_map/ppermute | solution.py:557
  30.2 5.2 %collective-permute-start.10 = (bf16[1,5,32,256]{3,2,1,0:T(8,128)(2,1)S(1)}, bf16[1,5,32,256]{3,2,1,0:T(8,128)(2,1)S(1)}, u32[]{:S(2)}, u32[]{:S(2)}) collective-permute-start(bf16[1,5,32,256]{3,2,1,0:T(8,128)(2,1)S(1)} %slice.47), channel_id=1, source_target_pairs={{0,1},{1,0},{2,3},{3,2},{4,5},{5,4},{6,7},{7,6},{8,9},{9,8},{10,11... | collective-permute-start | bytes 245768 | tf_op jit(solution)/shard_map/ppermute | solution.py:557
  34.2 4.1 %collective-permute-start.16 = (bf16[2,10,32,256]{3,2,1,0:T(8,128)(2,1)S(1)}, bf16[2,10,32,256]{3,2,1,0:T(8,128)(2,1)S(1)}, u32[]{:S(2)}, u32[]{:S(2)}) collective-permute-start(bf16[2,10,32,256]{3,2,1,0:T(8,128)(2,1)S(1)} %constant_dynamic-update-slice_fusion.rest_0_), channel_id=1, source_target_pairs={{0,2},{2,0},{1,3},{3,1},{4,6},{6,4},{5,7},{7,5},{8,10},{10,8},{9,1... | collective-permute-start | bytes 983048 | tf_op jit(solution)/shard_map/ppermute | solution.py:557
  35.4 1.4 collective-permute-start.18
  35.4 1.6 collective-permute-start.19
  35.9 6.6 %collective-permute-start.22 = (bf16[1,10,32,256]{3,2,1,0:T(8,128)(2,1)S(1)}, bf16[1,10,32,256]{3,2,1,0:T(8,128)(2,1)S(1)}, u32[]{:S(2)}, u32[]{:S(2)}) collective-permute-start(bf16[1,10,32,256]{3,2,1,0:T(8,128)(2,1)S(1)} %collective-permute-done.4.rest_6_), channel_id=1, source_target_pairs={{0,2},{2,0},{1,3},{3,1},{4,6},{6,4},{5,7},{7,5},{8,10},{10,8},{9,1... | collective-permute-start | bytes 491528 | tf_op jit(solution)/shard_map/ppermute | solution.py:557
  36.0 7.0 %collective-permute-start.23 = (bf16[1,10,32,256]{3,2,1,0:T(8,128)(2,1)S(1)}, bf16[1,10,32,256]{3,2,1,0:T(8,128)(2,1)S(1)}, u32[]{:S(2)}, u32[]{:S(2)}) collective-permute-start(bf16[1,10,32,256]{3,2,1,0:T(8,128)(2,1)S(1)} %collective-permute-done.5.rest_7_), channel_id=1, source_target_pairs={{0,2},{2,0},{1,3},{3,1},{4,6},{6,4},{5,7},{7,5},{8,10},{10,8},{9,1... | collective-permute-start | bytes 491528 | tf_op jit(solution)/shard_map/ppermute | solution.py:557
  36.8 7.3 %collective-permute-start.17 = (bf16[2,10,32,256]{3,2,1,0:T(8,128)(2,1)S(1)}, bf16[2,10,32,256]{3,2,1,0:T(8,128)(2,1)S(1)}, u32[]{:S(2)}, u32[]{:S(2)}) collective-permute-start(bf16[2,10,32,256]{3,2,1,0:T(8,128)(2,1)S(1)} %collective-permute-done.3.rest_1_), channel_id=1, source_target_pairs={{0,2},{2,0},{1,3},{3,1},{4,6},{6,4},{5,7},{7,5},{8,10},{10,8},{9,1... | collective-permute-start | bytes 983048 | tf_op jit(solution)/shard_map/ppermute | solution.py:557
  37.0 2.6 %collective-permute-start.21 = (bf16[1,5,32,256]{3,2,1,0:T(8,128)(2,1)S(1)}, bf16[1,5,32,256]{3,2,1,0:T(8,128)(2,1)S(1)}, u32[]{:S(2)}, u32[]{:S(2)}) collective-permute-start(bf16[1,5,32,256]{3,2,1,0:T(8,128)(2,1)S(1)} %collective-permute-done.7.rest_5_), channel_id=1, source_target_pairs={{0,2},{2,0},{1,3},{3,1},{4,6},{6,4},{5,7},{7,5},{8,10},{10,8},{9,1... | collective-permute-start | bytes 245768 | tf_op jit(solution)/shard_map/ppermute | solution.py:557
  38.3 8.5 %collective-permute-start.30 = (bf16[2,2,128,256]{3,2,1,0:T(8,128)(2,1)S(1)}, bf16[2,2,128,256]{3,2,1,0:T(8,128)(2,1)S(1)}, u32[]{:S(2)}, u32[]{:S(2)}) collective-permute-start(bf16[2,2,128,256]{3,2,1,0:T(8,128)(2,1)S(1)} %pad_maximum_fusion), channel_id=1, source_target_pairs={{0,8},{8,0},{16,24},{24,16},{1,9},{9,1},{17,25},{25,17},{2,10},{10... | collective-permute-start | bytes 786440 | tf_op jit(solution)/shard_map/ppermute | solution.py:557
  39.7 1.3 collective-permute-start.20
  41.0 8.2 %collective-permute-start.13 = (bf16[128,512]{1,0:T(8,128)(2,1)S(1)}, bf16[128,512]{1,0:T(8,128)(2,1)S(1)}, u32[]{:S(2)}, u32[]{:S(2)}) collective-permute-start(bf16[128,512]{1,0:T(8,128)(2,1)S(1)} %copy-done.10), channel_id=1, source_target_pairs={{0,1},{1,0},{2,3},{3,2},{4,5},{5,4},{6,7},{7,6},{8,9},{9,8},{10,11... | collective-permute-start | bytes 393224 | tf_op jit(solution)/shard_map/ppermute | solution.py:557
  42.5 7.9 %collective-permute-start.14 = (bf16[2,5,32,256]{3,2,1,0:T(8,128)(2,1)S(1)}, bf16[2,5,32,256]{3,2,1,0:T(8,128)(2,1)S(1)}, u32[]{:S(2)}, u32[]{:S(2)}) collective-permute-start(bf16[2,5,32,256]{3,2,1,0:T(8,128)(2,1)S(1)} %slice.49), channel_id=1, source_target_pairs={{0,1},{1,0},{2,3},{3,2},{4,5},{5,4},{6,7},{7,6},{8,9},{9,8},{10,11... | collective-permute-start | bytes 491528 | tf_op jit(solution)/shard_map/ppermute | solution.py:557
  43.0 7.4 %collective-permute-start.15 = (bf16[2,5,32,256]{3,2,1,0:T(8,128)(2,1)S(1)}, bf16[2,5,32,256]{3,2,1,0:T(8,128)(2,1)S(1)}, u32[]{:S(2)}, u32[]{:S(2)}) collective-permute-start(bf16[2,5,32,256]{3,2,1,0:T(8,128)(2,1)S(1)} %slice.50), channel_id=1, source_target_pairs={{0,4},{4,0},{1,5},{5,1},{2,6},{6,2},{3,7},{7,3},{8,12},{12,8},{9,1... | collective-permute-start | bytes 491528 | tf_op jit(solution)/shard_map/ppermute | solution.py:557
  44.1 2.7 %collective-permute-start.24 = (bf16[1,5,32,256]{3,2,1,0:T(8,128)(2,1)S(1)}, bf16[1,5,32,256]{3,2,1,0:T(8,128)(2,1)S(1)}, u32[]{:S(2)}, u32[]{:S(2)}) collective-permute-start(bf16[1,5,32,256]{3,2,1,0:T(8,128)(2,1)S(1)} %collective-permute-done.10.rest_8_), channel_id=1, source_target_pairs={{0,2},{2,0},{1,3},{3,1},{4,6},{6,4},{5,7},{7,5},{8,10},{10,8},{9,1... | collective-permute-start | bytes 245768 | tf_op jit(solution)/shard_map/ppermute | solution.py:557
  46.8 1.8 collective-permute-start.25
  46.8 25.6 %collective-permute-start.33 = (bf16[4,2,128,256]{3,2,1,0:T(8,128)(2,1)S(1)}, bf16[4,2,128,256]{3,2,1,0:T(8,128)(2,1)S(1)}, u32[]{:S(2)}, u32[]{:S(2)}) collective-permute-start(bf16[4,2,128,256]{3,2,1,0:T(8,128)(2,1)S(1)} %constant_dynamic-update-slice_fusion.2.rest_0_), channel_id=1, source_target_pairs={{0,5},{1,4},{4,1},{5,0},{2,7},{3,6},{6,3},{7,2},{8,13},{9,12},{12,... | collective-permute-start | bytes 1572872 | tf_op jit(solution)/shard_map/ppermute | solution.py:604
  48.6 24.8 %collective-permute-start.32 = (bf16[4,2,128,256]{3,2,1,0:T(8,128)(2,1)S(1)}, bf16[4,2,128,256]{3,2,1,0:T(8,128)(2,1)S(1)}, u32[]{:S(2)}, u32[]{:S(2)}) collective-permute-start(bf16[4,2,128,256]{3,2,1,0:T(8,128)(2,1)S(1)} %constant_dynamic-update-slice_fusion.2.rest_0_), channel_id=1, source_target_pairs={{0,1},{1,0},{2,3},{3,2},{4,5},{5,4},{6,7},{7,6},{8,9},{9,8},{10,11... | collective-permute-start | bytes 1572872 | tf_op jit(solution)/shard_map/ppermute | solution.py:557
  49.2 24.2 %collective-permute-start.31 = (bf16[4,2,128,256]{3,2,1,0:T(8,128)(2,1)S(1)}, bf16[4,2,128,256]{3,2,1,0:T(8,128)(2,1)S(1)}, u32[]{:S(2)}, u32[]{:S(2)}) collective-permute-start(bf16[4,2,128,256]{3,2,1,0:T(8,128)(2,1)S(1)} %constant_dynamic-update-slice_fusion.2.rest_0_), channel_id=1, source_target_pairs={{0,4},{4,0},{1,5},{5,1},{2,6},{6,2},{3,7},{7,3},{8,12},{12,8},{9,1... | collective-permute-start | bytes 1572872 | tf_op jit(solution)/shard_map/ppermute | solution.py:557
  50.4 1.4 collective-permute-start.28
  50.4 1.6 collective-permute-start.29
  51.8 1.6 collective-permute-start.27
  52.0 1.9 collective-permute-start.26
  72.4 5.1 %copy-start.5 = (bf16[4,2,128,256]{3,2,1,0:T(8,128)(2,1)}, bf16[4,2,128,256]{3,2,1,0:T(8,128)(2,1)S(1)}, u32[]{:S(2)}) copy-start(bf16[4,2,128,256]{3,2,1,0:T(8,128)(2,1)S(1)} %collective-permute-done.33.rest_3_) | copy-start | bytes 1572868
  73.4 1.9 collective-permute-start.34
  73.4 2.6 %collective-permute-start.35 = (bf16[4,2,128,256]{3,2,1,0:T(8,128)(2,1)S(1)}, bf16[4,2,128,256]{3,2,1,0:T(8,128)(2,1)S(1)}, u32[]{:S(2)}, u32[]{:S(2)}) collective-permute-start(bf16[4,2,128,256]{3,2,1,0:T(8,128)(2,1)S(1)} %collective-permute-done.31.rest_1_), channel_id=1, source_target_pairs={{0,2},{2,0},{1,3},{3,1},{4,6},{6,4},{5,7},{7,5},{8,10},{10,8},{9,1... | collective-permute-start | bytes 1572872 | tf_op jit(solution)/shard_map/ppermute | solution.py:557
  73.9 2.9 %collective-permute-start.36 = (bf16[4,2,128,256]{3,2,1,0:T(8,128)(2,1)S(1)}, bf16[4,2,128,256]{3,2,1,0:T(8,128)(2,1)S(1)}, u32[]{:S(2)}, u32[]{:S(2)}) collective-permute-start(bf16[4,2,128,256]{3,2,1,0:T(8,128)(2,1)S(1)} %collective-permute-done.32.rest_2_), channel_id=1, source_target_pairs={{0,2},{2,0},{1,3},{3,1},{4,6},{6,4},{5,7},{7,5},{8,10},{10,8},{9,1... | collective-permute-start | bytes 1572872 | tf_op jit(solution)/shard_map/ppermute | solution.py:557
  73.9 3.6 %collective-permute-start.37 = (bf16[4,2,128,256]{3,2,1,0:T(8,128)(2,1)S(1)}, bf16[4,2,128,256]{3,2,1,0:T(8,128)(2,1)S(1)}, u32[]{:S(2)}, u32[]{:S(2)}) collective-permute-start(bf16[4,2,128,256]{3,2,1,0:T(8,128)(2,1)S(1)} %collective-permute-done.33.rest_3_), channel_id=1, source_target_pairs={{0,2},{2,0},{1,3},{3,1},{4,6},{6,4},{5,7},{7,5},{8,10},{10,8},{9,1... | collective-permute-start | bytes 1572872 | tf_op jit(solution)/shard_map/ppermute | solution.py:557
  75.3 2.3 %copy-start.6 = (bf16[4,2,128,256]{3,2,1,0:T(8,128)(2,1)}, bf16[4,2,128,256]{3,2,1,0:T(8,128)(2,1)S(1)}, u32[]{:S(2)}) copy-start(bf16[4,2,128,256]{3,2,1,0:T(8,128)(2,1)S(1)} %collective-permute-done.34.rest_4_) | copy-start | bytes 1572868
  76.0 1.5 copy-start.7
  78.3 49.1 %copy-start.1 = (bf16[1,2048,512]{2,1,0:T(8,128)(2,1)S(1)}, bf16[1,2048,512]{2,1,0:T(8,128)(2,1)}, u32[]{:S(2)}) copy-start(bf16[1,2048,512]{2,1,0:T(8,128)(2,1)} %param.13) | copy-start | bytes 6291460
  126.1 6.0 %collective-permute-start.38 = (bf16[4,2,2,528,128]{4,3,2,1,0:T(8,128)(2,1)}, bf16[4,2,2,528,128]{4,3,2,1,0:T(8,128)(2,1)S(1)}, u32[]{:S(2)}, u32[]{:S(2)}) collective-permute-start(bf16[4,2,2,528,128]{4,3,2,1,0:T(8,128)(2,1)} %get-tuple-element.128), channel_id=1, source_target_pairs={{0,2},{2,0},{1,3},{3,1},{4,6},{6,4},{5,7},{7,5},{8,10},{10,8},{9,1... | collective-permute-start | bytes 6488072 | tf_op jit(solution)/shard_map/ppermute | solution.py:557
  126.3 5.8 %collective-permute-start.39 = (bf16[128,512]{1,0:T(8,128)(2,1)S(1)}, bf16[128,512]{1,0:T(8,128)(2,1)S(1)}, u32[]{:S(2)}, u32[]{:S(2)}) collective-permute-start(bf16[128,512]{1,0:T(8,128)(2,1)S(1)} %get-tuple-element.129), channel_id=1, source_target_pairs={{0,1},{1,0},{2,3},{3,2},{4,5},{5,4},{6,7},{7,6},{8,9},{9,8},{10,11... | collective-permute-start | bytes 393224 | tf_op jit(solution)/shard_map/ppermute | solution.py:557
  127.4 4.7 %copy-start.2 = (bf16[4,2,2,528,128]{4,3,2,1,0:T(8,128)(2,1)S(1)}, bf16[4,2,2,528,128]{4,3,2,1,0:T(8,128)(2,1)}, u32[]{:S(2)}) copy-start(bf16[4,2,2,528,128]{4,3,2,1,0:T(8,128)(2,1)} %get-tuple-element.127.keep) | copy-start | bytes 6488068
  132.1 23.2 %slice-start = ((s8[4718592]{0:T(1024)(128)(4,1)}), s8[4194304]{0:T(1024)(128)(4,1)S(1)}, s32[]{:S(2)}) async-start(s8[4718592]{0:T(1024)(128)(4,1)} %bitcast.36), calls=%async_computation | async-start | bytes 8388608
  133.1 14.2 %collective-permute-start.40 = (bf16[2,2,2,272,128]{4,3,2,1,0:T(8,128)(2,1)S(1)}, bf16[2,2,2,272,128]{4,3,2,1,0:T(8,128)(2,1)S(1)}, u32[]{:S(2)}, u32[]{:S(2)}) collective-permute-start(bf16[2,2,2,272,128]{4,3,2,1,0:T(8,128)(2,1)S(1)} %get-tuple-element.135), channel_id=1, source_target_pairs={{0,4},{4,0},{1,5},{5,1},{2,6},{6,2},{3,7},{7,3},{8,12},{12,8},{9,1... | collective-permute-start | bytes 1671176 | tf_op jit(solution)/shard_map/ppermute | solution.py:557
  134.0 21.3 %slice-start.1 = ((s8[4718592]{0:T(1024)(128)(4,1)}), s8[524288]{0:T(1024)(128)(4,1)S(1)}, s32[]{:S(2)}) async-start(s8[4718592]{0:T(1024)(128)(4,1)} %bitcast.36), calls=%async_computation.1 | async-start | bytes 1048576
  134.0 13.1 %collective-permute-start.41 = (bf16[2,2,2,256,128]{4,3,2,1,0:T(8,128)(2,1)S(1)}, bf16[2,2,2,256,128]{4,3,2,1,0:T(8,128)(2,1)S(1)}, u32[]{:S(2)}, u32[]{:S(2)}) collective-permute-start(bf16[2,2,2,256,128]{4,3,2,1,0:T(8,128)(2,1)S(1)} %get-tuple-element.136), channel_id=1, source_target_pairs={{0,1},{1,0},{2,3},{3,2},{4,5},{5,4},{6,7},{7,6},{8,9},{9,8},{10,11... | collective-permute-start | bytes 1572872 | tf_op jit(solution)/shard_map/ppermute | solution.py:557
  147.3 4.5 %collective-permute-start.44 = (bf16[4,2,2,9,32,256]{5,4,3,2,1,0:T(8,128)(2,1)S(1)}, bf16[4,2,2,9,32,256]{5,4,3,2,1,0:T(8,128)(2,1)S(1)}, u32[]{:S(2)}, u32[]{:S(2)}) collective-permute-start(bf16[4,2,2,9,32,256]{5,4,3,2,1,0:T(8,128)(2,1)S(1)} %get-tuple-element.148), channel_id=1, source_target_pairs={{0,2},{2,0},{1,3},{3,1},{4,6},{6,4},{5,7},{7,5},{8,10},{10,8},{9,1... | collective-permute-start | bytes 7077896 | tf_op jit(solution)/shard_map/ppermute | solution.py:557
  148.1 19.5 %collective-permute-start.43 = (bf16[2,2,256,128]{3,2,1,0:T(8,128)(2,1)S(1)}, bf16[2,2,256,128]{3,2,1,0:T(8,128)(2,1)S(1)}, u32[]{:S(2)}, u32[]{:S(2)}) collective-permute-start(bf16[2,2,256,128]{3,2,1,0:T(8,128)(2,1)S(1)} %get-tuple-element.145), channel_id=1, source_target_pairs={{0,4},{4,0},{1,5},{5,1},{2,6},{6,2},{3,7},{7,3},{8,12},{12,8},{9,1... | collective-permute-start | bytes 786440 | tf_op jit(solution)/shard_map/ppermute | solution.py:557
  149.2 18.4 %collective-permute-start.42 = (bf16[2,2,272,128]{3,2,1,0:T(8,128)(2,1)S(1)}, bf16[2,2,272,128]{3,2,1,0:T(8,128)(2,1)S(1)}, u32[]{:S(2)}, u32[]{:S(2)}) collective-permute-start(bf16[2,2,272,128]{3,2,1,0:T(8,128)(2,1)S(1)} %get-tuple-element.144), channel_id=1, source_target_pairs={{0,1},{1,0},{2,3},{3,2},{4,5},{5,4},{6,7},{7,6},{8,9},{9,8},{10,11... | collective-permute-start | bytes 835592 | tf_op jit(solution)/shard_map/ppermute | solution.py:557
  151.8 3.5 %copy-start.4 = (f32[2048,512]{1,0:T(8,128)S(1)}, f32[2048,512]{1,0:T(8,128)}, u32[]{:S(2)}) copy-start(f32[2048,512]{1,0:T(8,128)} %get-tuple-element.152.gh) | copy-start | bytes 12582916
  152.9 18.0 %collective-permute-start.45 = (bf16[2,2,2,5,32,256]{5,4,3,2,1,0:T(8,128)(2,1)S(1)}, bf16[2,2,2,5,32,256]{5,4,3,2,1,0:T(8,128)(2,1)S(1)}, u32[]{:S(2)}, u32[]{:S(2)}) collective-permute-start(bf16[2,2,2,5,32,256]{5,4,3,2,1,0:T(8,128)(2,1)S(1)} %get-tuple-element.150), channel_id=1, source_target_pairs={{0,4},{4,0},{1,5},{5,1},{2,6},{6,2},{3,7},{7,3},{8,12},{12,8},{9,1... | collective-permute-start | bytes 1966088 | tf_op jit(solution)/shard_map/ppermute | solution.py:557
  154.1 15.8 %collective-permute-start.46 = (bf16[2,2,2,4,32,256]{5,4,3,2,1,0:T(8,128)(2,1)S(1)}, bf16[2,2,2,4,32,256]{5,4,3,2,1,0:T(8,128)(2,1)S(1)}, u32[]{:S(2)}, u32[]{:S(2)}) collective-permute-start(bf16[2,2,2,4,32,256]{5,4,3,2,1,0:T(8,128)(2,1)S(1)} %get-tuple-element.156), channel_id=1, source_target_pairs={{0,1},{1,0},{2,3},{3,2},{4,5},{5,4},{6,7},{7,6},{8,9},{9,8},{10,11... | collective-permute-start | bytes 1572872 | tf_op jit(solution)/shard_map/ppermute | solution.py:557
  168.3 8.0 %collective-permute-start.49 = (bf16[2,528,128]{2,1,0:T(8,128)(2,1)S(1)}, bf16[2,528,128]{2,1,0:T(8,128)(2,1)S(1)}, u32[]{:S(2)}, u32[]{:S(2)}) collective-permute-start(bf16[2,528,128]{2,1,0:T(8,128)(2,1)S(1)} %get-tuple-element.161), channel_id=1, source_target_pairs={{0,8},{8,0},{16,24},{24,16},{1,9},{9,1},{17,25},{25,17},{2,10},{10... | collective-permute-start | bytes 811016 | tf_op jit(solution)/shard_map/ppermute | solution.py:557
  171.7 9.4 %collective-permute-start.47 = (bf16[2,2,5,32,256]{4,3,2,1,0:T(8,128)(2,1)S(1)}, bf16[2,2,5,32,256]{4,3,2,1,0:T(8,128)(2,1)S(1)}, u32[]{:S(2)}, u32[]{:S(2)}) collective-permute-start(bf16[2,2,5,32,256]{4,3,2,1,0:T(8,128)(2,1)S(1)} %get-tuple-element.166), channel_id=1, source_target_pairs={{0,1},{1,0},{2,3},{3,2},{4,5},{5,4},{6,7},{7,6},{8,9},{9,8},{10,11... | collective-permute-start | bytes 983048 | tf_op jit(solution)/shard_map/ppermute | solution.py:557
  173.1 7.7 %collective-permute-start.48 = (bf16[2,2,4,32,256]{4,3,2,1,0:T(8,128)(2,1)S(1)}, bf16[2,2,4,32,256]{4,3,2,1,0:T(8,128)(2,1)S(1)}, u32[]{:S(2)}, u32[]{:S(2)}) collective-permute-start(bf16[2,2,4,32,256]{4,3,2,1,0:T(8,128)(2,1)S(1)} %get-tuple-element.167), channel_id=1, source_target_pairs={{0,4},{4,0},{1,5},{5,1},{2,6},{6,2},{3,7},{7,3},{8,12},{12,8},{9,1... | collective-permute-start | bytes 786440 | tf_op jit(solution)/shard_map/ppermute | solution.py:557
  177.0 9.0 %collective-permute-start.52 = (bf16[528,128]{1,0:T(8,128)(2,1)S(1)}, bf16[528,128]{1,0:T(8,128)(2,1)S(1)}, u32[]{:S(2)}, u32[]{:S(2)}) collective-permute-start(bf16[528,128]{1,0:T(8,128)(2,1)S(1)} %get-tuple-element.170), channel_id=1, source_target_pairs={{0,16},{8,24},{16,0},{24,8},{1,17},{9,25},{17,1},{25,9},{2,18},{10... | collective-permute-start | bytes 405512 | tf_op jit(solution)/shard_map/ppermute | solution.py:557
  181.8 9.2 %collective-permute-start.50 = (bf16[2,9,32,256]{3,2,1,0:T(8,128)(2,1)S(1)}, bf16[2,9,32,256]{3,2,1,0:T(8,128)(2,1)S(1)}, u32[]{:S(2)}, u32[]{:S(2)}) collective-permute-start(bf16[2,9,32,256]{3,2,1,0:T(8,128)(2,1)S(1)} %get-tuple-element.175), channel_id=1, source_target_pairs={{0,8},{8,0},{16,24},{24,16},{1,9},{9,1},{17,25},{25,17},{2,10},{10... | collective-permute-start | bytes 884744 | tf_op jit(solution)/shard_map/ppermute | solution.py:557
  191.7 9.3 %collective-permute-start.51 = (bf16[9,32,256]{2,1,0:T(8,128)(2,1)S(1)}, bf16[9,32,256]{2,1,0:T(8,128)(2,1)S(1)}, u32[]{:S(2)}, u32[]{:S(2)}) collective-permute-start(bf16[9,32,256]{2,1,0:T(8,128)(2,1)S(1)} %get-tuple-element.177), channel_id=1, source_target_pairs={{0,16},{8,24},{16,0},{24,8},{1,17},{9,25},{17,1},{25,9},{2,18},{10... | collective-permute-start | bytes 442376 | tf_op jit(solution)/shard_map/ppermute | solution.py:557
  (2 other events, 1.6 us)
